TPU v7x, 32 devices: a whole 2x2x4 slice. The times are simulated.
32 devices in a mesh: fsdp: 4 (over z), context: 4 (over y, x), tensor: 2 (over core).
Axes of the slice: x: 2, y: 2, z: 4, core: 2. Of those that a mesh axis runs over, the one named last changes fastest.
Arguments:
- tokens: bfloat16 [10240, 2048], P(('fsdp', 'context')), may hold values from -6 to 6
- cotangent: bfloat16 [10240, 2048], P(('fsdp', 'context')), may hold values from -6 to 6
- attn_gain: bfloat16 [2048], P(('fsdp', 'context')), may hold values from 0.099609375 to 1.8984375
- w_query: bfloat16 [2048, 2048], P(('fsdp', 'context'), 'tensor'), may hold values from -0.5 to 0.5
- w_key: bfloat16 [2048, 512], P(('fsdp', 'context'), 'tensor'), may hold values from -0.5 to 0.5
- w_value: bfloat16 [2048, 512], P(('fsdp', 'context'), 'tensor'), may hold values from -0.125 to 0.125
- w_out: bfloat16 [2048, 2048], P('tensor', ('fsdp', 'context')), may hold values from -1 to 1
- ffn_gain: bfloat16 [2048], P(('fsdp', 'context')), may hold values from 0.099609375 to 1.8984375
- w_gate: bfloat16 [2048, 8192], P(('fsdp', 'context'), 'tensor'), may hold values from -0.125 to 0.125
- w_up: bfloat16 [2048, 8192], P(('fsdp', 'context'), 'tensor'), may hold values from -0.125 to 0.125
- w_down: bfloat16 [8192, 2048], P('tensor', ('fsdp', 'context')), may hold values from -0.25 to 0.25
- piece_segment: int32 [4, 20], P('fsdp'), may hold values from 0 to 12, as said below
- piece_parent: int32 [4, 20], P('fsdp'), may hold values from -1 to 4, as said below
- piece_start: int32 [4, 20], P('fsdp'), may hold values from 0 to 1152, as said below
Outputs:
- output: bfloat16 [10240, 2048], P(('fsdp', 'context'))
- grad_tokens: float32 [10240, 2048], P(('fsdp', 'context'))
- grad_attn_gain: float32 [2048], P(('fsdp', 'context'))
- grad_query: float32 [2048, 2048], P(('fsdp', 'context'), 'tensor')
- grad_key: float32 [2048, 512], P(('fsdp', 'context'), 'tensor')
- grad_value: float32 [2048, 512], P(('fsdp', 'context'), 'tensor')
- grad_out: float32 [2048, 2048], P('tensor', ('fsdp', 'context'))
- grad_ffn_gain: float32 [2048], P(('fsdp', 'context'))
- grad_gate: float32 [2048, 8192], P(('fsdp', 'context'), 'tensor')
- grad_up: float32 [2048, 8192], P(('fsdp', 'context'), 'tensor')
- grad_down: float32 [8192, 2048], P('tensor', ('fsdp', 'context'))
Inputs may be any that keep to these rules, and one draw needn't show every extreme that they name: `piece_segment`: tree t's trunk is segment 13 t, its branches 13 t + 1 to 13 t + 4, its leaves 13 t + 5 to 13 t + 12, leaves 13 t + 5 + 2 b and 13 t + 6 + 2 b under branch 13 t + 1 + b. Within each row (one fsdp group) every tree 0 to 0 has 20 pieces: 8 trunk pieces, and 1 pieces for each of four branches and eight leaves. Pieces are placed in any order; one tree of each group has a trunk piece first on every device of the context axis. `piece_parent`: the trunk's segment for a branch's pieces, the branch's for a leaf's, -1 for trunk pieces. `piece_start`: trunk pieces start at multiples of 128 below 1024, branch pieces at 1024 + multiples of 128, leaf pieces at 1152 + multiples of 128; the pieces of one segment cover its positions once.
All inputs are finite; a program needn't handle non-finite values.
Results may differ from a plain program's by a relative error of at most 0.019.
Values may be sent and summed in bfloat16 or wider, within the bound.
A program may use at most 320 MiB of HBM per device.

v0:
```python
import jax
import jax.numpy as jnp
from jax import lax
from jax.sharding import PartitionSpec as P

HEAD = 64
SEG = 128


epsilon = 1e-05
rope_base = 10000000.0
residual_scale = 0.22
score_scale = 0.015625
masked_score = -1e30


def plain_dot(left_side, right_side):
    return jnp.dot(left_side, right_side, preferred_element_type=jnp.float32)


def transpose_dot(left_side, right_side):
    return lax.dot_general(
        left_side, right_side, (((0,), (0,)), ((), ())), preferred_element_type=jnp.float32
    )


def dot_against(left_side, right_side):
    return lax.dot_general(
        left_side, right_side, (((1,), (1,)), ((), ())), preferred_element_type=jnp.float32
    )


def rope_tables(positions, head_width):
    frequency = rope_base ** (-(jnp.arange(head_width // 2).astype(jnp.float32) * 2.0) / head_width)
    angles = positions.astype(jnp.float32)[:, None] * frequency[None, :]
    angles = jnp.concatenate([angles, angles], axis=-1)
    return (jnp.cos(angles), jnp.sin(angles))


def rotate_pairs(values, cosine_table, sine_table):
    half_width = values.shape[-1] // 2
    turned = jnp.concatenate([-values[..., half_width:], values[..., :half_width]], axis=-1)
    return values * cosine_table[:, None, :] + turned * sine_table[:, None, :]


def visible_mask(
    tree_query, segment_query, parent_query, position_query, tree_key, segment_key, position_key
):
    same_tree = tree_query[:, None] == tree_key[None, :]
    on_path = (
        (position_key[None, :] < 8 * SEG)
        | (segment_query[:, None] == segment_key[None, :])
        | (parent_query[:, None] == segment_key[None, :])
    )
    causal = position_key[None, :] <= position_query[:, None]
    return same_tree & on_path & causal


def norm_backward(gradient, normed, inv_root):
    return inv_root * (gradient - normed * jnp.mean(gradient * normed, axis=-1, keepdims=True))


def local(
    tokens,
    cotangent,
    attn_gain,
    w_query,
    w_key,
    w_value,
    w_out,
    ffn_gain,
    w_gate,
    w_up,
    w_down,
    piece_segment,
    piece_parent,
    piece_start,
):
    row_count = tokens.shape[0]
    groups = lax.axis_size("context")
    per_device = piece_segment.shape[1] // groups
    piece_len = row_count // per_device
    head_count = w_query.shape[1] // HEAD
    kv_count = w_key.shape[1] // HEAD
    repeat_count = head_count // kv_count
    context_rank = lax.axis_index("context")
    query_full, key_full, value_full, gate_full, up_full, attn_gain_full, ffn_gain_full = (
        lax.all_gather(w_query, ("fsdp", "context"), axis=0, tiled=True),
        lax.all_gather(w_key, ("fsdp", "context"), axis=0, tiled=True),
        lax.all_gather(w_value, ("fsdp", "context"), axis=0, tiled=True),
        lax.all_gather(w_gate, ("fsdp", "context"), axis=0, tiled=True),
        lax.all_gather(w_up, ("fsdp", "context"), axis=0, tiled=True),
        lax.all_gather(attn_gain, ("fsdp", "context"), axis=0, tiled=True),
        lax.all_gather(ffn_gain, ("fsdp", "context"), axis=0, tiled=True),
    )
    out_full, down_full = (
        lax.all_gather(w_out, ("fsdp", "context"), axis=1, tiled=True),
        lax.all_gather(w_down, ("fsdp", "context"), axis=1, tiled=True),
    )
    attn_scale = attn_gain_full.astype(jnp.float32)
    ffn_scale = ffn_gain_full.astype(jnp.float32)
    residual_in = tokens.astype(jnp.float32)
    offsets = jnp.tile(jnp.arange(piece_len, dtype=jnp.int32), piece_segment.shape[1])
    key_segment = jnp.repeat(piece_segment[0], piece_len)
    key_tree = key_segment // 13
    key_parent = jnp.repeat(piece_parent[0], piece_len)
    key_position = jnp.repeat(piece_start[0], piece_len) + offsets
    start_row = context_rank * row_count
    query_tree = lax.dynamic_slice_in_dim(key_tree, start_row, row_count)
    query_segment = lax.dynamic_slice_in_dim(key_segment, start_row, row_count)
    query_parent = lax.dynamic_slice_in_dim(key_parent, start_row, row_count)
    query_position = lax.dynamic_slice_in_dim(key_position, start_row, row_count)
    visible = visible_mask(
        query_tree, query_segment, query_parent, query_position, key_tree, key_segment, key_position
    )
    cosine_table, sine_table = rope_tables(query_position, HEAD)
    norm_first = lax.rsqrt(jnp.mean(residual_in * residual_in, axis=-1, keepdims=True) + epsilon)
    normed_first = residual_in * norm_first
    hidden_first = (normed_first * attn_scale).astype(jnp.bfloat16)
    query_raw = plain_dot(hidden_first, query_full)
    key_raw = plain_dot(hidden_first, key_full)
    value_raw = plain_dot(hidden_first, value_full)
    queries = (
        rotate_pairs(query_raw.reshape(row_count, head_count, HEAD), cosine_table, sine_table)
        .reshape(row_count, head_count * HEAD)
        .astype(jnp.bfloat16)
    )
    key_vectors = (
        rotate_pairs(key_raw.reshape(row_count, kv_count, HEAD), cosine_table, sine_table)
        .reshape(row_count, kv_count * HEAD)
        .astype(jnp.bfloat16)
    )
    value_vectors = value_raw.astype(jnp.bfloat16)
    key_rows, value_rows = (
        lax.all_gather(key_vectors, "context", axis=0, tiled=True),
        lax.all_gather(value_vectors, "context", axis=0, tiled=True),
    )

    def head_slices(head_index):
        query_head = lax.dynamic_slice_in_dim(queries, head_index * HEAD, HEAD, 1)
        column = head_index // repeat_count * HEAD
        key_head = lax.dynamic_slice_in_dim(key_rows, column, HEAD, 1)
        value_head = lax.dynamic_slice_in_dim(value_rows, column, HEAD, 1)
        return (query_head, key_head, value_head)

    def head_scores(query_head, key_head):
        scores = score_scale * dot_against(query_head, key_head)
        return jnp.where(visible, scores, masked_score)

    def forward_head(head_index):
        query_head, key_head, value_head = head_slices(head_index)
        scores = head_scores(query_head, key_head)
        largest = jnp.max(scores, axis=-1, keepdims=True)
        exponent = jnp.exp(scores - largest)
        denominator = jnp.sum(exponent, axis=-1, keepdims=True)
        weights = (exponent / denominator).astype(jnp.bfloat16)
        return (plain_dot(weights, value_head), largest + jnp.log(denominator))

    head_outputs, log_totals = lax.map(forward_head, jnp.arange(head_count))
    attended = (
        jnp.transpose(head_outputs, (1, 0, 2))
        .reshape(row_count, head_count * HEAD)
        .astype(jnp.bfloat16)
    )
    branch = lax.psum(plain_dot(attended, out_full).astype(jnp.bfloat16), "tensor").astype(
        jnp.float32
    )
    middle = residual_in + residual_scale * branch
    norm_second = lax.rsqrt(jnp.mean(middle * middle, axis=-1, keepdims=True) + epsilon)
    normed_second = middle * norm_second
    hidden_second = (normed_second * ffn_scale).astype(jnp.bfloat16)
    gate_proj = plain_dot(hidden_second, gate_full)
    up_proj = plain_dot(hidden_second, up_full)
    sigmoid_gate = jax.nn.sigmoid(gate_proj)
    silu_gate = gate_proj * sigmoid_gate
    hidden = (silu_gate * up_proj).astype(jnp.bfloat16)
    ffn_out = lax.psum(plain_dot(hidden, down_full).astype(jnp.bfloat16), "tensor").astype(
        jnp.float32
    )
    result = middle + residual_scale * ffn_out
    refreshed = lax.optimization_barrier(
        (ffn_out, w_query, w_key, w_value, w_gate, w_up, w_out, w_down)
    )
    later_out, shard_query, shard_key, shard_value, shard_gate, shard_up, shard_out, shard_down = (
        refreshed
    )
    query_full, key_full, value_full, gate_full, up_full = (
        lax.all_gather(shard_query, ("fsdp", "context"), axis=0, tiled=True),
        lax.all_gather(shard_key, ("fsdp", "context"), axis=0, tiled=True),
        lax.all_gather(shard_value, ("fsdp", "context"), axis=0, tiled=True),
        lax.all_gather(shard_gate, ("fsdp", "context"), axis=0, tiled=True),
        lax.all_gather(shard_up, ("fsdp", "context"), axis=0, tiled=True),
    )
    out_full, down_full = (
        lax.all_gather(shard_out, ("fsdp", "context"), axis=1, tiled=True),
        lax.all_gather(shard_down, ("fsdp", "context"), axis=1, tiled=True),
    )
    grad_result = cotangent.astype(jnp.float32)
    ffn_grad = (residual_scale * grad_result).astype(jnp.bfloat16)
    grad_down = transpose_dot(hidden, ffn_grad)
    grad_hidden = dot_against(ffn_grad, down_full)
    silu_slope = sigmoid_gate * (1.0 + gate_proj * (1.0 - sigmoid_gate))
    grad_gate_proj = (grad_hidden * up_proj * silu_slope).astype(jnp.bfloat16)
    grad_up_proj = (grad_hidden * silu_gate).astype(jnp.bfloat16)
    grad_gate_w = transpose_dot(hidden_second, grad_gate_proj)
    grad_up_w = transpose_dot(hidden_second, grad_up_proj)
    second_partial = dot_against(grad_gate_proj, gate_full) + dot_against(grad_up_proj, up_full)
    grad_second = lax.psum(second_partial.astype(jnp.bfloat16), "tensor").astype(jnp.float32)
    grad_ffn_gain = jnp.sum(grad_second * normed_second, axis=0)
    grad_middle = grad_result + norm_backward(grad_second * ffn_scale, normed_second, norm_second)
    attn_grad = (residual_scale * grad_middle).astype(jnp.bfloat16)
    grad_out_w = transpose_dot(attended, attn_grad)
    grad_attended = dot_against(attn_grad, out_full).astype(jnp.bfloat16)
    zero_keys = jnp.zeros((key_rows.shape[0], kv_count * HEAD), jnp.float32)

    def backward_head(running, head_index):
        key_grads, value_grads = running
        query_head, key_head, value_head = head_slices(head_index)
        scores = head_scores(query_head, key_head)
        probabilities = jnp.exp(scores - log_totals[head_index])
        out_grad_head = lax.dynamic_slice_in_dim(grad_attended, head_index * HEAD, HEAD, 1)
        prob_grad = dot_against(out_grad_head, value_head)
        inner_sum = jnp.sum(probabilities * prob_grad, axis=-1, keepdims=True)
        score_grad = (probabilities * (prob_grad - inner_sum)).astype(jnp.bfloat16)
        query_grad = score_scale * plain_dot(score_grad, key_head)
        key_grad = score_scale * transpose_dot(score_grad, query_head)
        value_grad = transpose_dot(probabilities.astype(jnp.bfloat16), out_grad_head)
        column = head_index // repeat_count * HEAD
        key_grads = lax.dynamic_update_slice_in_dim(
            key_grads, lax.dynamic_slice_in_dim(key_grads, column, HEAD, 1) + key_grad, column, 1
        )
        value_grads = lax.dynamic_update_slice_in_dim(
            value_grads,
            lax.dynamic_slice_in_dim(value_grads, column, HEAD, 1) + value_grad,
            column,
            1,
        )
        return ((key_grads, value_grads), query_grad)

    (key_grads, value_grads), query_grads = lax.scan(
        backward_head, (zero_keys, zero_keys), jnp.arange(head_count)
    )
    key_sum, value_sum = (
        lax.psum_scatter(
            key_grads.astype(jnp.bfloat16), "context", scatter_dimension=0, tiled=True
        ).astype(jnp.float32),
        lax.psum_scatter(
            value_grads.astype(jnp.bfloat16), "context", scatter_dimension=0, tiled=True
        ).astype(jnp.float32),
    )
    query_back = (
        rotate_pairs(jnp.transpose(query_grads, (1, 0, 2)), cosine_table, -sine_table)
        .reshape(row_count, head_count * HEAD)
        .astype(jnp.bfloat16)
    )
    key_back = (
        rotate_pairs(key_sum.reshape(row_count, kv_count, HEAD), cosine_table, -sine_table)
        .reshape(row_count, kv_count * HEAD)
        .astype(jnp.bfloat16)
    )
    value_back = value_sum.astype(jnp.bfloat16)
    grad_query_w = transpose_dot(hidden_first, query_back)
    grad_key_w = transpose_dot(hidden_first, key_back)
    grad_value_w = transpose_dot(hidden_first, value_back)
    first_partial = (
        dot_against(query_back, query_full)
        + dot_against(key_back, key_full)
        + dot_against(value_back, value_full)
    )
    grad_first = lax.psum(first_partial.astype(jnp.bfloat16), "tensor").astype(jnp.float32)
    grad_attn_gain = jnp.sum(grad_first * normed_first, axis=0)
    grad_tokens = grad_middle + norm_backward(grad_first * attn_scale, normed_first, norm_first)
    row_grads = (
        lax.psum_scatter(grad_query_w, ("fsdp", "context"), scatter_dimension=0, tiled=True),
        lax.psum_scatter(grad_key_w, ("fsdp", "context"), scatter_dimension=0, tiled=True),
        lax.psum_scatter(grad_value_w, ("fsdp", "context"), scatter_dimension=0, tiled=True),
        lax.psum_scatter(grad_gate_w, ("fsdp", "context"), scatter_dimension=0, tiled=True),
        lax.psum_scatter(grad_up_w, ("fsdp", "context"), scatter_dimension=0, tiled=True),
        lax.psum_scatter(grad_attn_gain, ("fsdp", "context"), scatter_dimension=0, tiled=True),
        lax.psum_scatter(grad_ffn_gain, ("fsdp", "context"), scatter_dimension=0, tiled=True),
    )
    col_grads = (
        lax.psum_scatter(grad_out_w, ("fsdp", "context"), scatter_dimension=1, tiled=True),
        lax.psum_scatter(grad_down, ("fsdp", "context"), scatter_dimension=1, tiled=True),
    )
    return (
        result.astype(jnp.bfloat16),
        grad_tokens,
        row_grads[5],
        row_grads[0],
        row_grads[1],
        row_grads[2],
        col_grads[0],
        row_grads[6],
        row_grads[3],
        row_grads[4],
        col_grads[1],
    )


def solution(mesh):
    return jax.shard_map(
        local,
        mesh=mesh,
        in_specs=(
            P(("fsdp", "context"), None),
            P(("fsdp", "context"), None),
            P(("fsdp", "context")),
            P(("fsdp", "context"), "tensor"),
            P(("fsdp", "context"), "tensor"),
            P(("fsdp", "context"), "tensor"),
            P("tensor", ("fsdp", "context")),
            P(("fsdp", "context")),
            P(("fsdp", "context"), "tensor"),
            P(("fsdp", "context"), "tensor"),
            P("tensor", ("fsdp", "context")),
            P("fsdp", None),
            P("fsdp", None),
            P("fsdp", None),
        ),
        out_specs=(
            P(("fsdp", "context"), None),
            P(("fsdp", "context"), None),
            P(("fsdp", "context")),
            P(("fsdp", "context"), "tensor"),
            P(("fsdp", "context"), "tensor"),
            P(("fsdp", "context"), "tensor"),
            P("tensor", ("fsdp", "context")),
            P(("fsdp", "context")),
            P(("fsdp", "context"), "tensor"),
            P(("fsdp", "context"), "tensor"),
            P("tensor", ("fsdp", "context")),
        ),
        check_vma=False,
    )
```

profile of v0, /device:TPU:0, one launch (start us, length us, event | category | flops | bytes accessed | tf_op | source)
XLA Modules:
  0.0 4919.3 jit_solution(6098114791909330306)
XLA Ops:
  9.5 42.4 all-gather
  73.7 51.9 %all-gather.25.cloned.1.call-done = bf16[2048,256]{1,0:T(8,128)(2,1)} async-done(((bf16[128,256]{1,0:T(8,128)(2,1)}), bf16[2048,256]{1,0:T(8,128)(2,1)}) %all-gather.25.cloned.1.call-update) | async-done | bytes 1048592 | tf_op jit(solution)/shard_map/all_gather | solution.py:90
  158.2 76.3 %all-gather.19.cloned.1.call-done = bf16[2048,1024]{1,0:T(8,128)(2,1)} async-done(((bf16[128,1024]{1,0:T(8,128)(2,1)}), bf16[2048,1024]{1,0:T(8,128)(2,1)}) %all-gather.19.cloned.1.call-update) | async-done | bytes 4194320 | tf_op jit(solution)/shard_map/all_gather | solution.py:88
  264.2 201.9 %while.34 = (s32[]{:T(128)}, bf16[16,640,64]{1,2,0:T(8,128)(2,1)}, f32[16,640,1]{1,2,0:T(1,128)}, s32[16]{0:T(128)S(1)}, bf16[640,1024]{1,0:T(8,128)(2,1)}, /*in...) while((s32[]{:T(128)}, bf16[16,640,64]{1,2,0:T(8,128)(2,1)}, ...), condition=%wide.region_4.5_spmd.clone.clone, body=%wide.region_1.4_spmd.clone.sunk.clone | while | flops 445644192 | bytes 26615732 | solution.py:159
  476.7 39.6 all-gather.1
  522.5 169.1 %all-gather.31.cloned.1.call-done = bf16[2048,4096]{1,0:T(8,128)(2,1)} async-done(((bf16[128,4096]{1,0:T(8,128)(2,1)}), bf16[2048,4096]{1,0:T(8,128)(2,1)}) %all-gather.31.cloned.1.call-update) | async-done | bytes 16777232 | tf_op jit(solution)/shard_map/all_gather | solution.py:91
  709.3 175.2 %all-gather.33.cloned.1.call-done = bf16[2048,4096]{1,0:T(8,128)(2,1)} async-done(((bf16[128,4096]{1,0:T(8,128)(2,1)}), bf16[2048,4096]{1,0:T(8,128)(2,1)}) %all-gather.33.cloned.1.call-update) | async-done | bytes 16777232 | tf_op jit(solution)/shard_map/all_gather | solution.py:92
  902.1 233.2 %all-gather.37.cloned.1.call-done = bf16[4096,2048]{1,0:T(8,128)(2,1)} async-done(((bf16[4096,128]{1,0:T(8,128)(2,1)}), bf16[4096,2048]{1,0:T(8,128)(2,1)}) %all-gather.37.cloned.1.call-update) | async-done | bytes 16777232 | tf_op jit(solution)/shard_map/all_gather | solution.py:196
  1135.4 25.3 multiply_convert_fusion.1
  1160.6 167.7 %all-gather.39.cloned.1.call-done = bf16[2048,4096]{1,0:T(8,128)(2,1)} async-done(((bf16[128,4096]{1,0:T(8,128)(2,1)}), bf16[2048,4096]{1,0:T(8,128)(2,1)}) %all-gather.39.cloned.1.call-update) | async-done | bytes 16777232 | tf_op jit(solution)/shard_map/all_gather | solution.py:191
  1346.2 175.0 %all-gather.41.cloned.1.call-done = bf16[2048,4096]{1,0:T(8,128)(2,1)} async-done(((bf16[128,4096]{1,0:T(8,128)(2,1)}), bf16[2048,4096]{1,0:T(8,128)(2,1)}) %all-gather.41.cloned.1.call-update) | async-done | bytes 16777232 | tf_op jit(solution)/shard_map/all_gather | solution.py:192
  1565.5 87.7 %all-gather.43.cloned.1.call-done = bf16[1024,2048]{1,0:T(8,128)(2,1)} async-done(((bf16[1024,128]{1,0:T(8,128)(2,1)}), bf16[1024,2048]{1,0:T(8,128)(2,1)}) %all-gather.43.cloned.1.call-update) | async-done | bytes 4194320 | tf_op jit(solution)/shard_map/all_gather | solution.py:195
  1666.9 429.4 %while.35 = (s32[]{:T(128)}, f32[2560,256]{0,1:T(8,128)}, f32[2560,256]{0,1:T(8,128)}, f32[16,640,64]{1,2,0:T(8,128)}, s32[16]{0:T(128)S(1)}, /*index=5*/bf16[64...) while((s32[]{:T(128)}, f32[2560,256]{0,1:T(8,128)}, ...), condition=%wide.region_12.13_spmd.clone.clone, body=%wide.region_10.12_spmd.clone.sunk.clone | while | flops 1076960640 | bytes 80844808 | solution.py:240
  2135.6 51.9 %all-gather.47.cloned.1.call-done = bf16[2048,256]{1,0:T(8,128)(2,1)} async-done(((bf16[128,256]{1,0:T(8,128)(2,1)}), bf16[2048,256]{1,0:T(8,128)(2,1)}) %all-gather.47.cloned.1.call-update) | async-done | bytes 1048592 | tf_op jit(solution)/shard_map/all_gather | solution.py:189
  2192.0 52.4 %all-gather.49.cloned.1.call-done = bf16[2048,256]{1,0:T(8,128)(2,1)} async-done(((bf16[128,256]{1,0:T(8,128)(2,1)}), bf16[2048,256]{1,0:T(8,128)(2,1)}) %all-gather.49.cloned.1.call-update) | async-done | bytes 1048592 | tf_op jit(solution)/shard_map/all_gather | solution.py:190
  2244.4 30.9 reduce-scatter.30.cloned.1.call-done
  2310.4 22.3 fusion.89
  2333.0 22.2 fusion.90
  2383.1 76.5 %all-reduce.2 = (f32[2048]{0:T(1024)S(1)}, f32[2048]{0:T(1024)S(1)}) all-reduce(f32[2048]{0:T(1024)S(1)} %get-tuple-element.460, f32[2048]{0:T(1024)S(1)} %copy-done.23), channel_id=4, replica_groups=mesh['fsdp'=4,'context'=4,'tensor'=2] {'fsdp','context'}, use_global_device_ids=true, to_apply=%region_18.19.clone | all-reduce | flops 4096 | bytes 32768
  2478.3 177.8 %reduce-scatter.20.cloned.1.call-done = f32[1024,128]{1,0:T(8,128)} async-done(((f32[1024,2048]{1,0:T(8,128)}), f32[1024,128]{1,0:T(8,128)}) %reduce-scatter.20.cloned.1.call-update) | async-done | bytes 524304 | tf_op jit(solution)/shard_map/reduce_scatter | solution.py:283
  2656.1 183.2 %reduce-scatter.14.cloned.1.call-done = f32[128,1024]{1,0:T(8,128)} async-done(((f32[2048,1024]{1,0:T(8,128)}), f32[128,1024]{1,0:T(8,128)}) %reduce-scatter.14.cloned.1.call-update) | async-done | bytes 524304 | tf_op jit(solution)/shard_map/reduce_scatter | solution.py:274
  2839.3 688.8 %reduce-scatter.22.cloned.1.call-done = f32[128,4096]{1,0:T(8,128)} async-done(((f32[2048,4096]{1,0:T(8,128)}), f32[128,4096]{1,0:T(8,128)}) %reduce-scatter.22.cloned.1.call-update) | async-done | bytes 2097168 | tf_op jit(solution)/shard_map/reduce_scatter | solution.py:277
  3528.1 692.0 %reduce-scatter.24.cloned.1.call-done = f32[128,4096]{1,0:T(8,128)} async-done(((f32[2048,4096]{1,0:T(8,128)}), f32[128,4096]{1,0:T(8,128)}) %reduce-scatter.24.cloned.1.call-update) | async-done | bytes 2097168 | tf_op jit(solution)/shard_map/reduce_scatter | solution.py:278
  4220.1 692.2 %reduce-scatter.26.cloned.1.call-done = f32[4096,128]{1,0:T(8,128)} async-done(((f32[4096,2048]{1,0:T(8,128)}), f32[4096,128]{1,0:T(8,128)}) %reduce-scatter.26.cloned.1.call-update) | async-done | bytes 2097168 | tf_op jit(solution)/shard_map/reduce_scatter | solution.py:284
  (519 shorter events, 843.4 us)
Async XLA Ops:
  8.7 147.1 %all-gather.23.cloned.1.call-start = ((), (), s32[]{:S(2)}) async-start(), calls=%async_computation.11 | async-start | bytes 1638400 | tf_op jit(solution)/shard_map/all_gather | solution.py:135
  73.1 161.4 %all-gather.19.cloned.1.call-start = ((), (), s32[]{:S(2)}) async-start(), calls=%async_computation.9 | async-start | bytes 4456448 | tf_op jit(solution)/shard_map/all_gather | solution.py:88
  73.7 190.5 %all-gather.27.cloned.1.call-start = ((), (), s32[]{:S(2)}) async-start(), calls=%async_computation.13 | async-start | bytes 1638400 | tf_op jit(solution)/shard_map/all_gather | solution.py:136
  128.6 337.6 %all-gather.29.cloned.1.call-start = ((), (), s32[]{:S(2)}) async-start(), calls=%async_computation.14 | async-start | bytes 4456448 | tf_op jit(solution)/shard_map/all_gather | solution.py:97
  129.2 387.2 %all-reduce.8.cloned.1.call-start = ((), (), s32[]{:S(2)}) async-start(), calls=%async_computation.15 | async-start | bytes 5242880 | tf_op jit(solution)/shard_map/psum | solution.py:165
  473.3 218.3 %all-gather.31.cloned.1.call-start = ((), (), s32[]{:S(2)}) async-start(), calls=%async_computation.16 | async-start | bytes 17825792 | tf_op jit(solution)/shard_map/all_gather | solution.py:91
  474.0 410.6 %all-gather.33.cloned.1.call-start = ((), (), s32[]{:S(2)}) async-start(), calls=%async_computation.17 | async-start | bytes 17825792 | tf_op jit(solution)/shard_map/all_gather | solution.py:92
  474.8 660.6 %all-gather.37.cloned.1.call-start = ((), (), s32[]{:S(2)}) async-start(), calls=%async_computation.19 | async-start | bytes 17825792 | tf_op jit(solution)/shard_map/all_gather | solution.py:196
  475.4 853.0 %all-gather.39.cloned.1.call-start = ((), (), s32[]{:S(2)}) async-start(), calls=%async_computation.20 | async-start | bytes 17825792 | tf_op jit(solution)/shard_map/all_gather | solution.py:191
  476.1 1045.1 %all-gather.41.cloned.1.call-start = ((), (), s32[]{:S(2)}) async-start(), calls=%async_computation.21 | async-start | bytes 17825792 | tf_op jit(solution)/shard_map/all_gather | solution.py:192
  476.7 1083.5 %all-reduce.10.cloned.1.call-start = ((), (), s32[]{:S(2)}) async-start(), calls=%async_computation.22 | async-start | bytes 5242880 | tf_op jit(solution)/shard_map/psum | solution.py:208
  1540.3 566.7 %all-gather.35.cloned.1.call-start = ((), (), s32[]{:S(2)}) async-start(), calls=%async_computation.18 | async-start | bytes 17825792 | tf_op jit(solution)/shard_map/all_gather | solution.py:98
  1540.8 585.4 %all-gather.45.cloned.1.call-start = ((), (), s32[]{:S(2)}) async-start(), calls=%async_computation.24 | async-start | bytes 4456448 | tf_op jit(solution)/shard_map/all_gather | solution.py:188
  1541.4 592.8 %reduce-scatter.28.cloned.1.call-start = ((), (), s32[]{:S(2)}) async-start(), calls=%async_computation.34 | async-start | bytes 1638400
  2102.4 142.1 %all-gather.49.cloned.1.call-start = ((), (), s32[]{:S(2)}) async-start(), calls=%async_computation.26 | async-start | bytes 1114112 | tf_op jit(solution)/shard_map/all_gather | solution.py:190
  2103.1 172.2 %reduce-scatter.30.cloned.1.call-start = ((), (), s32[]{:S(2)}) async-start(), calls=%async_computation.35 | async-start | bytes 1638400
  2106.9 272.7 %all-reduce.12.cloned.1.call-start = ((), (), s32[]{:S(2)}) async-start(), calls=%async_computation.36 | async-start | bytes 10485760 | tf_op jit(solution)/shard_map/psum | solution.py:177
  2282.2 188.6 %reduce-scatter.16.cloned.1.call-start = ((), (), s32[]{:S(2)}) async-start(), calls=%async_computation.28 | async-start | bytes 2228224 | tf_op jit(solution)/shard_map/reduce_scatter | solution.py:275
  2286.7 191.5 %reduce-scatter.18.cloned.1.call-start = ((), (), s32[]{:S(2)}) async-start(), calls=%async_computation.29 | async-start | bytes 2228224 | tf_op jit(solution)/shard_map/reduce_scatter | solution.py:276
  2289.8 366.3 %reduce-scatter.20.cloned.1.call-start = ((), (), s32[]{:S(2)}) async-start(), calls=%async_computation.30 | async-start | bytes 8912896 | tf_op jit(solution)/shard_map/reduce_scatter | solution.py:283
  2302.2 537.1 %reduce-scatter.14.cloned.1.call-start = ((), (), s32[]{:S(2)}) async-start(), calls=%async_computation.27 | async-start | bytes 8912896 | tf_op jit(solution)/shard_map/reduce_scatter | solution.py:274
  2309.9 1218.2 %reduce-scatter.22.cloned.1.call-start = ((), (), s32[]{:S(2)}) async-start(), calls=%async_computation.31 | async-start | bytes 35651584 | tf_op jit(solution)/shard_map/reduce_scatter | solution.py:277
  2332.7 1887.4 %reduce-scatter.24.cloned.1.call-start = ((), (), s32[]{:S(2)}) async-start(), calls=%async_computation.32 | async-start | bytes 35651584 | tf_op jit(solution)/shard_map/reduce_scatter | solution.py:278
  2355.2 2557.1 %reduce-scatter.26.cloned.1.call-start = ((), (), s32[]{:S(2)}) async-start(), calls=%async_computation.33 | async-start | bytes 35651584 | tf_op jit(solution)/shard_map/reduce_scatter | solution.py:284
  (80 other events, 6237.1 us)
Sparse Core Ops, SparseCore 0:
  10.8 57.9 all-gather.20
  71.6 54.0 all-gather.24
  158.4 76.0 all-gather.18
  266.7 89.2 all-gather.28
  498.8 192.7 all-gather.30
  694.7 189.7 all-gather.32
  887.5 247.8 all-gather.36
  1138.5 189.7 all-gather.38
  1331.4 189.7 all-gather.40
  1562.8 90.3 all-gather.42
  1655.7 247.8 all-gather.34
  1906.2 74.2 all-gather.44
  2101.9 27.6 reduce-scatter.27
  2132.3 55.2 all-gather.46
  2190.3 54.0 all-gather.48
  2247.2 28.1 reduce-scatter.29
  2282.3 30.1 all-reduce.11
  2315.5 81.4 reduce-scatter.15
  2399.9 78.2 reduce-scatter.17
  2481.1 174.9 reduce-scatter.19
  2659.0 180.1 reduce-scatter.13
  2842.2 685.8 reduce-scatter.21
  3531.0 689.0 reduce-scatter.23
  4223.2 689.0 reduce-scatter.25
  (4 shorter events, 97.4 us)
where the time goes:
time: 4930 us; the launch traced here: 4920 us
  waiting for transfers between devices  3780 us (77%)
  matrix products  695 us (14%)
  blocking collectives  158 us (3%)
  loops' own time  126 us (3%)
  other arithmetic  71.8 us (1%)
  local copies, waits for them, and re-layouts  68.6 us (1%)
    reduce_scatter x1, waiting for transfers between devices, local(): lax.psum_scatter(grad_down, ('fsdp', 'context'), scatter_dimension=1, til...  692 us
    reduce_scatter x1, waiting for transfers between devices, local(): lax.psum_scatter(grad_up_w, ('fsdp', 'context'), scatter_dimension=0, til...  692 us
    reduce_scatter x1, waiting for transfers between devices, local(): lax.psum_scatter(grad_gate_w, ('fsdp', 'context'), scatter_dimension=0, t...  689 us
    dot_general x55, matrix products, dot_against(): lax.dot_general(left_side, right_side, (((1,), (1,)), ((), ())), preferre...  377 us
    all_gather x1, waiting for transfers between devices, local(): lax.all_gather(shard_down, ('fsdp', 'context'), axis=1, tiled=True)  233 us
    reduce_scatter x1, waiting for transfers between devices, local(): lax.psum_scatter(grad_query_w, ('fsdp', 'context'), scatter_dimension=0,...  183 us
    dot_general x39, matrix products, transpose_dot(): lax.dot_general(left_side, right_side, (((0,), (0,)), ((), ())), preferre...  183 us
    reduce_scatter x1, waiting for transfers between devices, local(): lax.psum_scatter(grad_out_w, ('fsdp', 'context'), scatter_dimension=1, ti...  178 us
  transfers between devices with their start and end apart: 28, of which 21 were waited for; matrix products, arithmetic and copies ran while one was open for 16% of the time, Pallas kernels for 0%

commit v1 on v0

v1 whole, which is shorter than its diff:
```python
import functools

import jax
import jax.numpy as jnp
from jax import lax
from jax.experimental import pallas as pl
from jax.experimental.pallas import tpu as pltpu
from jax.sharding import PartitionSpec as P

HEAD = 64
SEG = 128
TRUNK = 8 * SEG
BRANCHES = 4
LEAVES = 8
GROUP = TRUNK + (BRANCHES + LEAVES) * SEG
DEPTH = TRUNK + 2 * SEG
TILE = 2 * SEG

epsilon = 1e-05
rope_base = 10000000.0
residual_scale = 0.22
score_scale = 0.015625
masked_score = -1e30

FIRST = (((0,), (0,)), ((), ()))
LAST = (((1,), (1,)), ((), ()))
PLAIN = (((1,), (0,)), ((), ()))


def dot(left_side, right_side, dims=PLAIN):
    return lax.dot_general(left_side, right_side, dims, preferred_element_type=jnp.float32)


def rope_tables():
    frequency = rope_base ** (-(jnp.arange(HEAD // 2).astype(jnp.float32) * 2.0) / HEAD)
    angles = jnp.arange(DEPTH).astype(jnp.float32)[:, None] * frequency[None, :]
    sine = jnp.sin(angles)
    cosine = jnp.cos(angles)
    return (
        jnp.concatenate([cosine] * 4, axis=-1),
        jnp.concatenate([-sine, sine, -sine, sine], axis=-1),
    )


def lanes(values):
    return lax.broadcasted_iota(jnp.int32, values.shape, 1)


def swap_halves(values):
    return jnp.where(
        lanes(values) % HEAD < HEAD // 2,
        pltpu.roll(values, 128 - HEAD // 2, 1),
        pltpu.roll(values, HEAD // 2, 1),
    )


def only_head(values, head):
    return jnp.where(lanes(values) // HEAD == head, values, jnp.zeros_like(values))


def query_tiles(work):
    for j in range(TRUNK // TILE):
        prefix = [(0, j * TILE, False)] if j else []
        work(j * TILE, prefix + [(j * TILE, TILE, True)], False)

    def branch(i, carry):
        row = pl.multiple_of(TRUNK + i * TILE, TILE)
        work(row, [(0, TRUNK, False), (row, TILE, True)], True)
        return carry

    lax.fori_loop(0, BRANCHES * SEG // TILE, branch, 0)

    def leaf(i, carry):
        row = pl.multiple_of(TRUNK + BRANCHES * SEG + i * TILE, TILE)
        parent = pl.multiple_of(TRUNK + i * SEG, SEG)
        work(row, [(0, TRUNK, False), (parent, SEG, False), (row, TILE, True)], True)
        return carry

    lax.fori_loop(0, LEAVES * SEG // TILE, leaf, 0)


def visible_scores(keys, query, own, one_segment):
    scores = dot(keys, query, LAST)
    if not own:
        return scores
    key_at = lax.broadcasted_iota(jnp.int32, scores.shape, 0)
    query_at = lax.broadcasted_iota(jnp.int32, scores.shape, 1)
    seen = key_at <= query_at
    if one_segment:
        seen = seen & (key_at // SEG == query_at // SEG)
    return jnp.where(seen, scores, masked_score)


def attention_forward_kernel(
    to_ref, start_ref, raw_ref, cos_ref, sin_ref, out_ref, q_ref, k_ref, v_ref, log_ref, held
):
    width = q_ref.shape[1]
    pieces = to_ref.shape[0]
    piece = raw_ref.shape[0] // pieces

    def place(p, carry):
        rows = pl.ds(pl.multiple_of(p * piece, piece), piece)
        to = pl.ds(pl.multiple_of(to_ref[p], piece), piece)
        at = pl.ds(pl.multiple_of(start_ref[p], piece), piece)
        cosine, sine = cos_ref[at, :], sin_ref[at, :]

        def turn(values):
            return values * cosine + swap_halves(values) * sine

        for g in range(width // 128):
            cut = slice(g * 128, g * 128 + 128)
            turned = turn(raw_ref[rows, cut]).astype(jnp.bfloat16)
            q_ref[to, cut] = turned * jnp.bfloat16(score_scale)
        pair = raw_ref[rows, width : width + 128]
        low = lanes(pair) < HEAD
        key = turn(pair)
        key = jnp.where(low, key, pltpu.roll(key, HEAD, 1)).astype(jnp.bfloat16)
        value = jnp.where(low, pltpu.roll(pair, HEAD, 1), pair).astype(jnp.bfloat16)
        for g in range(width // 128):
            cut = slice(g * 128, g * 128 + 128)
            k_ref[to, cut] = key
            v_ref[to, cut] = value
        return carry

    lax.fori_loop(0, pieces, place, 0)

    def work(row, parts, one_segment):
        rows = pl.ds(row, TILE)

        def one_head(head, carry):
            query = only_head(q_ref[rows, :], head)
            scores = [
                visible_scores(k_ref[pl.ds(first, count), :], query, own, one_segment)
                for first, count, own in parts
            ]
            largest = functools.reduce(
                jnp.maximum, [jnp.max(s, axis=0, keepdims=True) for s in scores]
            )
            exponent = [jnp.exp(s - largest) for s in scores]
            total = functools.reduce(
                jnp.add, [jnp.sum(e, axis=0, keepdims=True) for e in exponent]
            )
            inverse = 1.0 / total
            result = functools.reduce(
                jnp.add,
                [
                    dot((e * inverse).astype(jnp.bfloat16), v_ref[pl.ds(first, count), :], FIRST)
                    for e, (first, count, own) in zip(exponent, parts)
                ],
            )
            log_ref[head, :, rows] = largest + jnp.log(total)
            before = held[rows, :]
            held[rows, :] = jnp.where(
                lanes(before) // HEAD == head, result.astype(jnp.bfloat16), before
            )
            return carry

        lax.fori_loop(0, width // HEAD, one_head, 0)

    query_tiles(work)

    def back(p, carry):
        rows = pl.ds(pl.multiple_of(p * piece, piece), piece)
        to = pl.ds(pl.multiple_of(to_ref[p], piece), piece)
        out_ref[rows, :] = held[to, :]
        return carry

    lax.fori_loop(0, pieces, back, 0)


def attention_backward_kernel(
    to_ref,
    start_ref,
    grad_ref,
    q_ref,
    k_ref,
    v_ref,
    log_ref,
    cos_ref,
    sin_ref,
    out_ref,
    og_ref,
    dq_ref,
    dk_ref,
    dv_ref,
):
    width = q_ref.shape[1]
    pieces = to_ref.shape[0]
    piece = grad_ref.shape[0] // pieces

    def place(p, carry):
        rows = pl.ds(pl.multiple_of(p * piece, piece), piece)
        to = pl.ds(pl.multiple_of(to_ref[p], piece), piece)
        og_ref[to, :] = grad_ref[rows, :]
        return carry

    lax.fori_loop(0, pieces, place, 0)
    dk_ref[...] = jnp.zeros_like(dk_ref)
    dv_ref[...] = jnp.zeros_like(dv_ref)

    def work(row, parts, one_segment):
        rows = pl.ds(row, TILE)
        dq_ref[rows, :] = jnp.zeros((TILE, width), jnp.float32)

        def one_head(head, carry):
            query = only_head(q_ref[rows, :], head)
            out_grad = only_head(og_ref[rows, :], head)
            log_total = log_ref[head, :, rows]
            weights, products = [], []
            for first, count, own in parts:
                keys = pl.ds(first, count)
                scores = visible_scores(k_ref[keys, :], query, own, one_segment)
                weights.append(jnp.exp(scores - log_total))
                products.append(dot(v_ref[keys, :], out_grad, LAST))
            inner = functools.reduce(
                jnp.add,
                [jnp.sum(w * d, axis=0, keepdims=True) for w, d in zip(weights, products)],
            )
            query_grad = jnp.zeros((TILE, width), jnp.float32)
            for (first, count, own), w, d in zip(parts, weights, products):
                keys = pl.ds(first, count)
                score_grad = (w * (d - inner)).astype(jnp.bfloat16)
                dv_ref[keys, :] += dot(w.astype(jnp.bfloat16), out_grad)
                dk_ref[keys, :] += dot(score_grad, query)
                query_grad += dot(score_grad, k_ref[keys, :], FIRST)
            dq_ref[rows, :] += only_head(query_grad, head)
            return carry

        lax.fori_loop(0, width // HEAD, one_head, 0)

    query_tiles(work)

    def back(p, carry):
        rows = pl.ds(pl.multiple_of(p * piece, piece), piece)
        to = pl.ds(pl.multiple_of(to_ref[p], piece), piece)
        at = pl.ds(pl.multiple_of(start_ref[p], piece), piece)
        cosine, sine = cos_ref[at, :], sin_ref[at, :]

        def turn_back(values):
            return values * cosine - swap_halves(values) * sine

        def over_heads(ref):
            total = functools.reduce(
                jnp.add, [ref[to, g * 128 : g * 128 + 128] for g in range(width // 128)]
            )
            return total + pltpu.roll(total, HEAD, 1)

        for g in range(width // 128):
            cut = slice(g * 128, g * 128 + 128)
            turned = turn_back(score_scale * dq_ref[to, cut])
            out_ref[rows, cut] = turned.astype(jnp.bfloat16)
        key = turn_back(over_heads(dk_ref))
        value = over_heads(dv_ref)
        pair = jnp.where(lanes(key) < HEAD, key, value)
        out_ref[rows, width : width + 128] = pair.astype(jnp.bfloat16)
        return carry

    lax.fori_loop(0, pieces, back, 0)


SMEM = pl.BlockSpec(memory_space=pltpu.SMEM)
VMEM = pl.BlockSpec(memory_space=pltpu.VMEM)
VMEM_LIMIT = 48 * 1024 * 1024


def attention_cost(width, products):
    flops = products * 2 * GROUP * (GROUP * 2 // 5) * width
    return pl.CostEstimate(
        flops=flops, bytes_accessed=16 * GROUP * width, transcendentals=GROUP * GROUP * width // 128
    )


def attention_forward(places, starts, raw, tables):
    width = raw.shape[1] - 2 * HEAD
    rows = raw.shape[0]
    kept = jax.ShapeDtypeStruct((rows, width), jnp.bfloat16)
    return pl.pallas_call(
        attention_forward_kernel,
        out_shape=[kept] * 4 + [jax.ShapeDtypeStruct((width // HEAD, 1, rows), jnp.float32)],
        in_specs=[SMEM, SMEM, VMEM, VMEM, VMEM],
        out_specs=[VMEM] * 5,
        scratch_shapes=[pltpu.VMEM((rows, width), jnp.bfloat16)],
        compiler_params=pltpu.CompilerParams(vmem_limit_bytes=VMEM_LIMIT),
        cost_estimate=attention_cost(width, 4),
        name="attention_forward",
    )(places, starts, raw, *tables)


def attention_backward(places, starts, out_grad, kept, tables):
    rows, width = out_grad.shape
    return pl.pallas_call(
        attention_backward_kernel,
        out_shape=jax.ShapeDtypeStruct((rows, width + 2 * HEAD), jnp.bfloat16),
        in_specs=[SMEM, SMEM] + [VMEM] * 7,
        out_specs=VMEM,
        scratch_shapes=[
            pltpu.VMEM((rows, width), jnp.bfloat16),
            pltpu.VMEM((rows, width), jnp.float32),
            pltpu.VMEM((rows, width), jnp.float32),
            pltpu.VMEM((rows, width), jnp.float32),
        ],
        compiler_params=pltpu.CompilerParams(vmem_limit_bytes=VMEM_LIMIT),
        cost_estimate=attention_cost(width, 10),
        name="attention_backward",
    )(places, starts, out_grad, *kept, *tables)


def norm_backward(gradient, normed, inv_root):
    return inv_root * (gradient - normed * jnp.mean(gradient * normed, axis=-1, keepdims=True))


def inverse_root(values):
    return lax.rsqrt(jnp.mean(values * values, axis=-1, keepdims=True) + epsilon)


PLANE = ("context", "tensor")


def gather_rows(values):
    return lax.all_gather(values, PLANE, axis=0, tiled=True)


def scatter_rows(partial):
    return lax.psum_scatter(
        partial.astype(jnp.bfloat16), PLANE, scatter_dimension=0, tiled=True
    ).astype(jnp.float32)


def local(
    tokens,
    cotangent,
    attn_gain,
    w_query,
    w_key,
    w_value,
    w_out,
    ffn_gain,
    w_gate,
    w_up,
    w_down,
    piece_segment,
    piece_parent,
    piece_start,
):
    groups = lax.axis_size("context")
    cores = lax.axis_size("tensor")
    depth = w_query.shape[0]
    kv_count = w_key.shape[1] // HEAD
    sharing = groups // kv_count
    share = tokens.shape[0] // cores
    first_row = lax.axis_index("tensor") * share

    def my_rows(values):
        return lax.dynamic_slice_in_dim(values, first_row, share, 0)

    def blocks(weight):
        return jnp.transpose(weight.reshape(depth, groups, -1), (1, 0, 2))

    def kv_blocks(weight):
        return jnp.repeat(jnp.transpose(weight.reshape(depth, kv_count, HEAD), (1, 0, 2)), sharing, 0)

    def spread(weight_blocks):
        mine = lax.all_to_all(weight_blocks, "context", 0, 0)
        mine = mine.reshape(groups * depth, -1)
        return lax.all_gather(mine, "fsdp", axis=0, tiled=True)

    gains = jnp.stack([attn_gain, ffn_gain], axis=1)
    gains = jnp.broadcast_to(jnp.pad(gains, ((0, 0), (0, 126))), (groups, depth, 128))
    packed = spread(
        jnp.concatenate(
            [blocks(w_query), kv_blocks(w_key), kv_blocks(w_value), blocks(w_out.T), gains], axis=2
        )
    )
    width = w_query.shape[1] // groups
    qkv_full = packed[:, : width + 2 * HEAD]
    out_full = packed[:, width + 2 * HEAD : 2 * width + 2 * HEAD]
    gains_full = packed[:, 2 * width + 2 * HEAD :].astype(jnp.float32)
    attn_scale, ffn_scale = gains_full[:, 0], gains_full[:, 1]
    gate_full = spread(blocks(w_gate))
    up_full = spread(blocks(w_up))
    down_full = spread(blocks(w_down.T))

    segment, starts = piece_segment[0] % 13, piece_start[0]
    places = jnp.where(
        segment == 0,
        starts,
        jnp.where(
            segment <= BRANCHES,
            starts + (segment - 1) * SEG,
            starts + (segment - 1 - BRANCHES) * SEG + (BRANCHES - 1) * SEG,
        ),
    )
    tables = rope_tables()

    inputs_full = gather_rows(my_rows(tokens)).astype(jnp.float32)
    hidden_first = (inputs_full * inverse_root(inputs_full) * attn_scale).astype(jnp.bfloat16)
    residual_in = my_rows(tokens).astype(jnp.float32)
    grad_result = my_rows(cotangent).astype(jnp.float32)
    ffn_grad = gather_rows((residual_scale * grad_result).astype(jnp.bfloat16))

    raw = dot(hidden_first, qkv_full)
    attended, *kept = attention_forward(places, starts, raw, tables)
    branch = scatter_rows(dot(attended, out_full, LAST))
    middle = residual_in + residual_scale * branch
    norm_second = inverse_root(middle)
    normed_second = middle * norm_second
    hidden_second = gather_rows((normed_second * ffn_scale).astype(jnp.bfloat16))

    gate_proj = dot(hidden_second, gate_full)
    up_proj = dot(hidden_second, up_full)
    sigmoid_gate = jax.nn.sigmoid(gate_proj)
    silu_gate = gate_proj * sigmoid_gate
    hidden = (silu_gate * up_proj).astype(jnp.bfloat16)
    grad_hidden = dot(ffn_grad, down_full)
    silu_slope = sigmoid_gate * (1.0 + gate_proj * (1.0 - sigmoid_gate))
    grad_gate_proj = (grad_hidden * up_proj * silu_slope).astype(jnp.bfloat16)
    grad_up_proj = (grad_hidden * silu_gate).astype(jnp.bfloat16)
    grad_second = scatter_rows(
        dot(grad_gate_proj, gate_full, LAST) + dot(grad_up_proj, up_full, LAST)
    )
    ffn_out = scatter_rows(dot(hidden, down_full, LAST))
    result = (middle + residual_scale * ffn_out).astype(jnp.bfloat16)
    result = lax.all_gather(result, "tensor", axis=0, tiled=True)

    def collect(gradient):
        mine = lax.psum_scatter(
            gradient.astype(jnp.bfloat16), "fsdp", scatter_dimension=0, tiled=True
        )
        return lax.all_to_all(mine.reshape(groups, depth, -1), "context", 0, 0)

    def columns(gradient):
        return jnp.transpose(gradient, (1, 0, 2)).reshape(depth, -1).astype(jnp.float32)

    grad_down = collect(dot(ffn_grad, hidden, FIRST))
    grad_gate = collect(dot(hidden_second, grad_gate_proj, FIRST))
    grad_up = collect(dot(hidden_second, grad_up_proj, FIRST))

    grad_ffn_gain = jnp.sum(grad_second * normed_second, axis=0)
    grad_middle = grad_result + norm_backward(grad_second * ffn_scale, normed_second, norm_second)
    attn_grad = gather_rows((residual_scale * grad_middle).astype(jnp.bfloat16))
    grad_attended = dot(attn_grad, out_full).astype(jnp.bfloat16)
    back = attention_backward(places, starts, grad_attended, kept, tables)
    grad_first = scatter_rows(dot(back, qkv_full, LAST))
    grad_attn = collect(
        jnp.concatenate([dot(hidden_first, back, FIRST), dot(attn_grad, attended, FIRST)], axis=1)
    )
    norm_first = inverse_root(residual_in)
    normed_first = residual_in * norm_first
    grad_attn_gain = jnp.sum(grad_first * normed_first, axis=0)
    grad_tokens = grad_middle + norm_backward(grad_first * attn_scale, normed_first, norm_first)
    grad_tokens = lax.all_gather(grad_tokens, "tensor", axis=0, tiled=True)

    gain_grads = lax.psum(
        jnp.stack([grad_attn_gain, grad_ffn_gain]), ("fsdp", "context", "tensor")
    )
    rank = lax.axis_index("fsdp") * groups + lax.axis_index("context")
    gain_grads = lax.dynamic_slice_in_dim(gain_grads, rank * depth, depth, 1)

    def kv_columns(gradient):
        gradient = gradient.astype(jnp.float32).reshape(kv_count, sharing, depth, HEAD)
        return jnp.transpose(jnp.sum(gradient, axis=1), (1, 0, 2)).reshape(depth, -1)

    return (
        result,
        grad_tokens,
        gain_grads[0],
        columns(grad_attn[:, :, :width]),
        kv_columns(grad_attn[:, :, width : width + HEAD]),
        kv_columns(grad_attn[:, :, width + HEAD : width + 2 * HEAD]),
        columns(grad_attn[:, :, width + 2 * HEAD :]).T,
        gain_grads[1],
        columns(grad_gate),
        columns(grad_up),
        columns(grad_down).T,
    )


ROWS = ("fsdp", "context")


def solution(mesh):
    return jax.shard_map(
        local,
        mesh=mesh,
        in_specs=(
            P(ROWS, None),
            P(ROWS, None),
            P(ROWS),
            P(ROWS, "tensor"),
            P(ROWS, "tensor"),
            P(ROWS, "tensor"),
            P("tensor", ROWS),
            P(ROWS),
            P(ROWS, "tensor"),
            P(ROWS, "tensor"),
            P("tensor", ROWS),
            P("fsdp", None),
            P("fsdp", None),
            P("fsdp", None),
        ),
        out_specs=(
            P(ROWS, None),
            P(ROWS, None),
            P(ROWS),
            P(ROWS, "tensor"),
            P(ROWS, "tensor"),
            P(ROWS, "tensor"),
            P("tensor", ROWS),
            P(ROWS),
            P(ROWS, "tensor"),
            P(ROWS, "tensor"),
            P("tensor", ROWS),
        ),
        check_vma=False,
    )
```

time: 4930 us -> 1520 us (0.31)
  waiting for transfers between devices: 3780 us -> 967 us
  matrix products: 695 us -> 216 us
  loops' own time: 126 us -> 0 us
  Pallas kernels: 0 us -> 106 us
    reduce_scatter x7 -> x8, waiting for transfers between devices: 2440 us -> 487 us  [the longest x4 273 us: collect(): lax.psum_scatter(gradient.astype(jnp.bfloat16), 'fsdp', scatter_dimension...]
    all_gather x16 -> x10, waiting for transfers between devices: 1280 us -> 474 us  [the longest x4 254 us: gather_rows(): return lax.all_gather(values, PLANE, axis=0, tiled=True)]
    dot_general x133 -> x15, matrix products: 695 us -> 216 us  [dot(): lax.dot_general(left_side, right_side, dims, preferred_element_type=jnp.f...]
    another operation x2 -> x0, loops' own time: 126 us -> none  [the longest x1 73.6 us: local(): lax.scan(backward_head, (zero_keys, zero_keys), jnp.arange(head_count))]
    pallas_call x0 -> x2, Pallas kernels: none -> 106 us  [the longest x1 55.5 us: attention_backward(): pl.pallas_call(attention_backward_kernel, out_shape=jax.ShapeDtypeStruct(...]
    all_gather x2 -> x0, blocking collectives: 82 us -> none  [the longest x1 42.4 us: local(): lax.all_gather(attn_gain, ('fsdp', 'context'), axis=0, tiled=True)]
    unnamed x1 -> x0, blocking collectives: 76.5 us -> none
    all_to_all x0 -> x4, blocking collectives: none -> 71.7 us  [spread(): mine = lax.all_to_all(weight_blocks, 'context', 0, 0)]
  transfers between devices with their start and end apart: 28 -> 22, of which waited for: 21 -> 16; matrix products, arithmetic and copies ran while one was open for 16% -> 11% of each run, Pallas kernels for 0% -> 0%
where the time goes in v1:
time: 1520 us; the launch traced here: 1510 us
  waiting for transfers between devices  967 us (64%)
  matrix products  216 us (14%)
  blocking collectives  111 us (7%)
  Pallas kernels  106 us (7%)
  other arithmetic  42 us (3%)
  local copies, waits for them, and re-layouts  37.8 us (2%)
  starting transfers between devices  16.1 us (1%)
    reduce_scatter x4, waiting for transfers between devices, collect(): lax.psum_scatter(gradient.astype(jnp.bfloat16), 'fsdp', scatter_dimension...  273 us
    all_gather x4, waiting for transfers between devices, gather_rows(): return lax.all_gather(values, PLANE, axis=0, tiled=True)  254 us
    all_gather x4, waiting for transfers between devices, spread(): return lax.all_gather(mine, 'fsdp', axis=0, tiled=True)  220 us
    dot_general x15, matrix products, dot(): lax.dot_general(left_side, right_side, dims, preferred_element_type=jnp.f...  216 us
    reduce_scatter x4, waiting for transfers between devices, scatter_rows(): lax.psum_scatter(partial.astype(jnp.bfloat16), PLANE, scatter_dimension=0...  215 us
    all_to_all x4, blocking collectives, spread(): mine = lax.all_to_all(weight_blocks, 'context', 0, 0)  71.7 us
    pallas_call x1, Pallas kernels, attention_backward(): pl.pallas_call(attention_backward_kernel, out_shape=jax.ShapeDtypeStruct(...  55.5 us
    pallas_call x1, Pallas kernels, attention_forward(): pl.pallas_call(attention_forward_kernel, out_shape=[kept] * 4 + [jax.Shap...  50.3 us
  transfers between devices with their start and end apart: 22, of which 16 were waited for; matrix products, arithmetic and copies ran while one was open for 11% of the time, Pallas kernels for 0%

profile of v1, /device:TPU:0, one launch (start us, length us, event | category | flops | bytes accessed | tf_op | source)
XLA Modules:
  0.0 1510.6 jit_solution(7911137459574156044)
XLA Ops:
  34.5 58.6 %all-gather.13.cloned.1.call-done = bf16[2048,768]{1,0:T(8,128)(2,1)} async-done(((bf16[512,768]{1,0:T(8,128)(2,1)}), bf16[2048,768]{1,0:T(8,128)(2,1)}) %all-gather.13.cloned.1.call-update) | async-done | bytes 3145744 | tf_op jit(solution)/shard_map/all_gather | solution.py:365
  95.1 62.4 %all-gather.11.cloned.1.call-done = bf16[2560,2048]{1,0:T(8,128)(2,1)} async-done(((bf16[320,2048]{1,0:T(8,128)(2,1)}), bf16[2560,2048]{1,0:T(8,128)(2,1)}) %all-gather.11.cloned.1.call-update) | async-done | bytes 10485776 | tf_op jit(solution)/shard_map/all_gather | solution.py:320
  174.3 50.3 %attention_forward.1 = (bf16[2560,256]{1,0:T(8,128)(2,1)S(1)}, bf16[2560,256]{1,0:T(8,128)(2,1)S(1)}, bf16[2560,256]{1,0:T(8,128)(2,1)S(1)}, bf16[2560,256]{1,0:T(8,128)(2,1)}, f32[4,1,2560]{2,1,0:T(1,128)S(1)}) custom-call(s32[20]{0:T(128)S(1)} %compare_select_fusion.1.to_ref, s32[20]{0:T(128)S(1)} %bitcast.102, f32[2560,384]{1,0:T(8,128)} %fusion.12.raw_ref, ...), custom_call_target="tpu_custom_call" | custom-call | flops 5368709120 | bytes 10485760 | tf_op jit(solution)/shard_map/attention_forward/pallas_call | solution.py:277
  234.6 19.1 %all_to_all.41 = bf16[4,128,1024]{1,2,0:T(8,128)(2,1)} all-to-all(bf16[4,128,1024]{1,2,0:T(8,128)(2,1)} %bitcast.107), channel_id=1, replica_groups=mesh['fsdp'=4,'context'=4,'tensor'=2] {'context'}, dimensions={0} | all-to-all | bytes 2097152 | tf_op jit(solution)/shard_map/all_to_all | solution.py:363
  256.1 57.9 %reduce-scatter.9.cloned.1.call-done = bf16[320,2048]{1,0:T(8,128)(2,1)} async-done(((bf16[2560,2048]{1,0:T(8,128)(2,1)}), bf16[320,2048]{1,0:T(8,128)(2,1)}) %reduce-scatter.9.cloned.1.call-update) | async-done | bytes 1310736 | tf_op jit(solution)/shard_map/reduce_scatter | solution.py:324
  321.8 18.8 %all_to_all.42 = bf16[4,128,1024]{1,2,0:T(8,128)(2,1)} all-to-all(bf16[4,128,1024]{1,2,0:T(8,128)(2,1)} %bitcast.108), channel_id=1, replica_groups=mesh['fsdp'=4,'context'=4,'tensor'=2] {'context'}, dimensions={0} | all-to-all | bytes 2097152 | tf_op jit(solution)/shard_map/all_to_all | solution.py:363
  365.5 30.6 %all-gather.19.cloned.1.call-done = bf16[2048,1024]{1,0:T(8,128)(2,1)} async-done(((bf16[512,1024]{1,0:T(8,128)(2,1)}), bf16[2048,1024]{1,0:T(8,128)(2,1)}) %all-gather.19.cloned.1.call-update) | async-done | bytes 4194320 | tf_op jit(solution)/shard_map/all_gather | solution.py:365
  396.2 64.1 %all-gather.15.cloned.1.call-done = bf16[2560,2048]{1,0:T(8,128)(2,1)} async-done(((bf16[320,2048]{1,0:T(8,128)(2,1)}), bf16[2560,2048]{1,0:T(8,128)(2,1)}) %all-gather.15.cloned.1.call-update) | async-done | bytes 10485776 | tf_op jit(solution)/shard_map/all_gather | solution.py:320
  476.9 66.2 %all-gather.17.cloned.1.call-done = bf16[2048,1024]{1,0:T(8,128)(2,1)} async-done(((bf16[512,1024]{1,0:T(8,128)(2,1)}), bf16[2048,1024]{1,0:T(8,128)(2,1)}) %all-gather.17.cloned.1.call-update) | async-done | bytes 4194320 | tf_op jit(solution)/shard_map/all_gather | solution.py:365
  559.6 64.4 %all-gather.21.cloned.1.call-done = bf16[2048,1024]{1,0:T(8,128)(2,1)} async-done(((bf16[512,1024]{1,0:T(8,128)(2,1)}), bf16[2048,1024]{1,0:T(8,128)(2,1)}) %all-gather.21.cloned.1.call-update) | async-done | bytes 4194320 | tf_op jit(solution)/shard_map/all_gather | solution.py:365
  624.0 64.3 %all-gather.25.cloned.1.call-done = bf16[2560,2048]{1,0:T(8,128)(2,1)} async-done(((bf16[320,2048]{1,0:T(8,128)(2,1)}), bf16[2560,2048]{1,0:T(8,128)(2,1)}) %all-gather.25.cloned.1.call-update) | async-done | bytes 10485776 | tf_op jit(solution)/shard_map/all_gather | solution.py:320
  688.3 26.7 %multiply_convert_fusion = (bf16[2560,1024]{1,0:T(8,128)(2,1)}, bf16[2560,1024]{1,0:T(8,128)(2,1)}, bf16[2560,1024]{1,0:T(8,128)(2,1)}) fusion(f32[2560,1024]{1,0:T(8,128)} %fusion.34, f32[2560,1024]{1,0:T(8,128)} %fusion.35, bf16[2560,2048]{1,0:T(8,128)(2,1)} %all-gather.25.cloned.1.call-done, bf16[2048,1024]{1,0:T(8,128)(2,1)} %all-gather.21.cloned.1.call-done), kind=kOutput, calls=%fused_computation.9 | convolution fusion | flops 10776739840 | bytes 51380224 | tf_op jit(solution)/shard_map/dot_general | solution.py:31
  715.0 18.2 %fusion.36 = f32[2560,2048]{1,0:T(8,128)} fusion(bf16[2560,1024]{1,0:T(8,128)(2,1)} %get-tuple-element.62, bf16[2048,1024]{1,0:T(8,128)(2,1)} %all-gather.17.cloned.1.call-done), kind=kOutput, calls=%fused_computation.96 | convolution fusion | flops 10737418240 | bytes 30408704 | tf_op jit(solution)/shard_map/dot_general | solution.py:31
  733.1 20.2 %add_convert_fusion = bf16[2560,2048]{1,0:T(8,128)(2,1)} fusion(f32[2560,2048]{1,0:T(8,128)} %fusion.36, bf16[2560,1024]{1,0:T(8,128)(2,1)} %get-tuple-element.61, bf16[2048,1024]{1,0:T(8,128)(2,1)} %all-gather.19.cloned.1.call-done), kind=kOutput, calls=%fused_computation.5 | convolution fusion | flops 10747904000 | bytes 40894464 | tf_op jit(solution)/shard_map/dot_general | solution.py:31
  753.4 81.7 %reduce-scatter.13.cloned.1.call-done = bf16[320,2048]{1,0:T(8,128)(2,1)} async-done(((bf16[2560,2048]{1,0:T(8,128)(2,1)}), bf16[320,2048]{1,0:T(8,128)(2,1)}) %reduce-scatter.13.cloned.1.call-update) | async-done | bytes 1310736 | tf_op jit(solution)/shard_map/reduce_scatter | solution.py:324
  843.0 63.4 %all-gather.27.cloned.1.call-done = bf16[2560,2048]{1,0:T(8,128)(2,1)} async-done(((bf16[320,2048]{1,0:T(8,128)(2,1)}), bf16[2560,2048]{1,0:T(8,128)(2,1)}) %all-gather.27.cloned.1.call-update) | async-done | bytes 10485776 | tf_op jit(solution)/shard_map/all_gather | solution.py:320
  913.6 55.5 %attention_backward.1 = bf16[2560,384]{1,0:T(8,128)(2,1)} custom-call(s32[20]{0:T(128)S(1)} %compare_select_fusion.1.to_ref, s32[20]{0:T(128)S(1)} %bitcast.103, bf16[2560,256]{1,0:T(8,128)(2,1)S(1)} %convolution_convert_fusion.3.grad_ref, bf16[2560,256]{1,0:T(8,128)(2,1)S(1)} %get-tuple-element.17.q_ref, bf16[2560,256]{1,0:T(8,128)(2,1)S(1)} %copy-done.4, ...), custom_call_target="tpu_custom_call" | custom-call | flops 13421772800 | bytes 10485760 | tf_op jit(solution)/shard_map/attention_backward/pallas_call | solution.py:291
  1013.4 17.6 %convolution_convert_fusion.5 = bf16[2048,1024]{1,0:T(8,128)(2,1)} fusion(bf16[2560,2048]{1,0:T(8,128)(2,1)} %all-gather.15.cloned.1.call-done, bf16[2560,1024]{1,0:T(8,128)(2,1)} %get-tuple-element.61), kind=kOutput, calls=%fused_computation.19 | convolution fusion | flops 10739515392 | bytes 19922944 | tf_op jit(solution)/shard_map/dot_general | solution.py:31
  1070.5 75.1 %reduce-scatter.11.cloned.1.call-done = bf16[320,2048]{1,0:T(8,128)(2,1)} async-done(((bf16[2560,2048]{1,0:T(8,128)(2,1)}), bf16[320,2048]{1,0:T(8,128)(2,1)}) %reduce-scatter.11.cloned.1.call-update) | async-done | bytes 1310736 | tf_op jit(solution)/shard_map/reduce_scatter | solution.py:324
  1151.6 73.0 %reduce-scatter.23.cloned.1.call-done = bf16[512,1024]{1,0:T(8,128)(2,1)} async-done(((bf16[2048,1024]{1,0:T(8,128)(2,1)}), bf16[512,1024]{1,0:T(8,128)(2,1)}) %reduce-scatter.23.cloned.1.call-update) | async-done | bytes 1048592 | tf_op jit(solution)/shard_map/reduce_scatter | solution.py:426
  1228.3 75.9 %reduce-scatter.21.cloned.1.call-done = bf16[512,1024]{1,0:T(8,128)(2,1)} async-done(((bf16[2048,1024]{1,0:T(8,128)(2,1)}), bf16[512,1024]{1,0:T(8,128)(2,1)}) %reduce-scatter.21.cloned.1.call-update) | async-done | bytes 1048592 | tf_op jit(solution)/shard_map/reduce_scatter | solution.py:426
  1307.9 76.4 %reduce-scatter.19.cloned.1.call-done = bf16[512,1024]{1,0:T(8,128)(2,1)} async-done(((bf16[2048,1024]{1,0:T(8,128)(2,1)}), bf16[512,1024]{1,0:T(8,128)(2,1)}) %reduce-scatter.19.cloned.1.call-update) | async-done | bytes 1048592 | tf_op jit(solution)/shard_map/reduce_scatter | solution.py:426
  1391.8 47.3 %reduce-scatter.17.cloned.1.call-done = bf16[512,640]{0,1:T(8,128)(2,1)} async-done(((bf16[2048,640]{0,1:T(8,128)(2,1)}), bf16[512,640]{0,1:T(8,128)(2,1)}) %reduce-scatter.17.cloned.1.call-update) | async-done | bytes 655376 | tf_op jit(solution)/shard_map/reduce_scatter | solution.py:426
  1457.6 39.3 %psum.7 = f32[2,2048]{1,0:T(2,128)S(1)} all-reduce(f32[2,2048]{1,0:T(2,128)S(1)} %pad_maximum_fusion.3), channel_id=1, replica_groups=mesh['fsdp'=4,'context'=4,'tensor'=2] {'fsdp','context','tensor'}, use_global_device_ids=true, to_apply=%region_11.12 | all-reduce | flops 4096 | bytes 32768 | tf_op jit(solution)/shard_map/psum | solution.py:453
  (156 shorter events, 268.8 us)
Async XLA Ops:
  7.2 85.9 %all-gather.13.cloned.1.call-start = ((), (), s32[]{:S(2)}) async-start(), calls=%async_computation.17 | async-start | bytes 3932160 | tf_op jit(solution)/shard_map/all_gather | solution.py:365
  29.7 127.8 %all-gather.11.cloned.1.call-start = ((), (), s32[]{:S(2)}) async-start(), calls=%async_computation.16 | async-start | bytes 11796480 | tf_op jit(solution)/shard_map/all_gather | solution.py:320
  31.0 283.0 %reduce-scatter.9.cloned.1.call-start = ((), (), s32[]{:S(2)}) async-start(), calls=%async_computation.18 | async-start | bytes 11796480 | tf_op jit(solution)/shard_map/reduce_scatter | solution.py:324
  232.3 163.9 %all-gather.19.cloned.1.call-start = ((), (), s32[]{:S(2)}) async-start(), calls=%async_computation.21 | async-start | bytes 5242880 | tf_op jit(solution)/shard_map/all_gather | solution.py:365
  256.0 204.3 %all-gather.15.cloned.1.call-start = ((), (), s32[]{:S(2)}) async-start(), calls=%async_computation.19 | async-start | bytes 11796480 | tf_op jit(solution)/shard_map/all_gather | solution.py:320
  319.5 223.6 %all-gather.17.cloned.1.call-start = ((), (), s32[]{:S(2)}) async-start(), calls=%async_computation.20 | async-start | bytes 5242880 | tf_op jit(solution)/shard_map/all_gather | solution.py:365
  342.9 281.1 %all-gather.21.cloned.1.call-start = ((), (), s32[]{:S(2)}) async-start(), calls=%async_computation.22 | async-start | bytes 5242880 | tf_op jit(solution)/shard_map/all_gather | solution.py:365
  362.7 325.5 %all-gather.25.cloned.1.call-start = ((), (), s32[]{:S(2)}) async-start(), calls=%async_computation.25 | async-start | bytes 11796480 | tf_op jit(solution)/shard_map/all_gather | solution.py:320
  365.5 469.6 %reduce-scatter.13.cloned.1.call-start = ((), (), s32[]{:S(2)}) async-start(), calls=%async_computation.26 | async-start | bytes 11796480 | tf_op jit(solution)/shard_map/reduce_scatter | solution.py:324
  753.4 153.0 %all-gather.27.cloned.1.call-start = ((), (), s32[]{:S(2)}) async-start(), calls=%async_computation.27 | async-start | bytes 11796480 | tf_op jit(solution)/shard_map/all_gather | solution.py:320
  843.0 224.6 %reduce-scatter.15.cloned.1.call-start = ((), (), s32[]{:S(2)}) async-start(), calls=%async_computation.28 | async-start | bytes 11796480 | tf_op jit(solution)/shard_map/reduce_scatter | solution.py:324
  979.0 166.6 %reduce-scatter.11.cloned.1.call-start = ((), (), s32[]{:S(2)}) async-start(), calls=%async_computation.23 | async-start | bytes 11796480 | tf_op jit(solution)/shard_map/reduce_scatter | solution.py:324
  996.2 228.4 %reduce-scatter.23.cloned.1.call-start = ((), (), s32[]{:S(2)}) async-start(), calls=%async_computation.33 | async-start | bytes 5242880 | tf_op jit(solution)/shard_map/reduce_scatter | solution.py:426
  1013.3 290.9 %reduce-scatter.21.cloned.1.call-start = ((), (), s32[]{:S(2)}) async-start(), calls=%async_computation.32 | async-start | bytes 5242880 | tf_op jit(solution)/shard_map/reduce_scatter | solution.py:426
  1031.0 353.3 %reduce-scatter.19.cloned.1.call-start = ((), (), s32[]{:S(2)}) async-start(), calls=%async_computation.31 | async-start | bytes 5242880 | tf_op jit(solution)/shard_map/reduce_scatter | solution.py:426
  1048.0 391.2 %reduce-scatter.17.cloned.1.call-start = ((), (), s32[]{:S(2)}) async-start(), calls=%async_computation.30 | async-start | bytes 3276800 | tf_op jit(solution)/shard_map/reduce_scatter | solution.py:426
  1067.4 78.2 %copy-start.10 = (bf16[320,2048]{1,0:T(8,128)(2,1)S(1)}, bf16[320,2048]{1,0:T(8,128)(2,1)}, u32[]{:S(2)}) copy-start(bf16[320,2048]{1,0:T(8,128)(2,1)} %reduce-scatter.13.cloned.1.call-done) | copy-start | bytes 3932164
  1067.5 430.0 %all-gather.23.cloned.1.call-start = ((), (), s32[]{:S(2)}) async-start(), calls=%async_computation.24 | async-start | bytes 3932160 | tf_op jit(solution)/shard_map/all_gather | solution.py:423
  1151.1 346.4 %all-gather.29.cloned.1.call-start = ((), (), s32[]{:S(2)}) async-start(), calls=%async_computation.29 | async-start | bytes 7864320 | tf_op jit(solution)/shard_map/all_gather | solution.py:451
  1224.7 79.6 %all-to-all-start.7 = ((bf16[4,128,1024]{2,1,0:T(8,128)(2,1)}), bf16[4,128,1024]{2,1,0:T(8,128)(2,1)S(1)}, u32[]{:S(2)}, u32[]{:S(2)}) async-start(bf16[4,128,1024]{2,1,0:T(8,128)(2,1)} %bitcast.117), calls=%async_computation.15 | async-start | bytes 2097152 | tf_op jit(solution)/shard_map/all_to_all | solution.py:429
  1304.2 84.3 %copy-start.12 = (bf16[4,128,1024]{2,1,0:T(8,128)(2,1)}, bf16[4,128,1024]{2,1,0:T(8,128)(2,1)S(1)}, u32[]{:S(2)}) copy-start(bf16[4,128,1024]{2,1,0:T(8,128)(2,1)S(1)} %all-to-all-done.7) | copy-start | bytes 3145732
  1304.2 80.0 %all-to-all-start.6 = ((bf16[4,128,1024]{2,1,0:T(8,128)(2,1)}), bf16[4,128,1024]{2,1,0:T(8,128)(2,1)S(1)}, u32[]{:S(2)}, u32[]{:S(2)}) async-start(bf16[4,128,1024]{2,1,0:T(8,128)(2,1)} %bitcast.116), calls=%async_computation.13 | async-start | bytes 2097152 | tf_op jit(solution)/shard_map/all_to_all | solution.py:429
  1384.3 56.9 %all-to-all-start.5 = ((bf16[4,128,1024]{2,1,0:T(8,128)(2,1)}), bf16[4,128,1024]{2,1,0:T(8,128)(2,1)}, u32[]{:S(2)}, u32[]{:S(2)}) async-start(bf16[4,128,1024]{2,1,0:T(8,128)(2,1)} %bitcast.115), calls=%async_computation.11 | async-start | bytes 2097152 | tf_op jit(solution)/shard_map/all_to_all | solution.py:429
  1441.2 13.0 all-to-all-start.4
  (19 other events, 289.6 us)
Sparse Core Ops, SparseCore 0:
  29.8 63.2 all-gather.12
  95.6 61.8 all-gather.10
  232.4 81.5 reduce-scatter.8
  315.4 80.7 all-gather.18
  398.5 61.7 all-gather.14
  462.3 80.7 all-gather.16
  544.7 79.2 all-gather.20
  626.4 61.7 all-gather.24
  753.5 81.5 reduce-scatter.12
  843.1 63.2 all-gather.26
  979.1 81.5 reduce-scatter.14
  1064.0 81.5 reduce-scatter.10
  1147.9 76.7 reduce-scatter.22
  1226.9 77.2 reduce-scatter.20
  1306.9 77.2 reduce-scatter.18
  1386.5 52.5 reduce-scatter.16
  1440.6 11.0 all-gather.22
  1453.7 16.3 all-gather.28

commit v2 on v1

--- a/solution.py
+++ b/solution.py
@@ -305,6 +305,427 @@
     )(places, starts, out_grad, *kept, *tables)
 
 
+MESH = pl.DeviceIdType.MESH
+ANY = pl.BlockSpec(memory_space=pl.ANY)
+CHUNKS = 4
+SLAB = 16
+
+
+def lasting(microseconds):
+    return pl.CostEstimate(
+        flops=0, bytes_accessed=int(microseconds * 3_000_000), transcendentals=0
+    )
+
+
+class Plane:
+    def __init__(self, sent, landed, diagonal=False):
+        self.sent, self.landed = sent, landed
+        self.copies = []
+        self.rank = lax.axis_index("context")
+        self.core = lax.axis_index("tensor")
+        self.at_x = self.rank + 1 - 2 * lax.rem(self.rank, 2)
+        self.at_y = lax.rem(self.rank + 2, 4)
+        self.at_both = 3 - self.rank
+        self.x = {"context": self.at_x}
+        self.y = {"context": self.at_y}
+        self.both = {"context": self.at_both}
+        self.sibling = {"tensor": 1 - self.core}
+        barrier = pltpu.get_barrier_semaphore()
+        partners = [self.x, self.y, self.sibling] + ([self.both] if diagonal else [])
+        for partner in partners:
+            pl.semaphore_signal(barrier, inc=1, device_id=partner, device_id_type=MESH)
+        pl.semaphore_wait(barrier, len(partners))
+
+    def copy(self, number, source, target, partner):
+        return pltpu.make_async_remote_copy(
+            src_ref=source,
+            dst_ref=target,
+            send_sem=self.sent.at[number],
+            recv_sem=self.landed.at[number],
+            device_id=partner,
+            device_id_type=MESH,
+        )
+
+    def send(self, source, target, partner):
+        number = len(self.copies)
+        started = self.copy(number, source, target, partner)
+        started.start()
+        self.copies.append(started)
+        return number
+
+    def arrive(self, number, target):
+        self.copy(number, target, target, self.sibling).wait_recv()
+
+    def finish(self):
+        for started in self.copies:
+            started.wait_send()
+
+
+def chunk(index, rows):
+    return pl.ds(index * (rows // CHUNKS), rows // CHUNKS)
+
+
+class Gather:
+    def __init__(self, plane, block, out):
+        self.plane, self.block, self.out = plane, block, out
+        self.rows = block.shape[0]
+        self.to_x, self.to_y, self.across = {}, {}, {}
+
+    def start(self, k):
+        p, cut = self.plane, chunk(k, self.rows)
+        target = self.out.at[p.rank, p.core, cut]
+        self.to_x[k] = p.send(self.block.at[cut], target, p.x)
+        self.to_y[k] = p.send(self.block.at[cut], target, p.y)
+        self.across[0, k] = p.send(self.block.at[cut], target, p.sibling)
+
+    def forward(self):
+        p, out = self.plane, self.out
+        onward = {}
+        for k in range(CHUNKS):
+            cut = chunk(k, self.rows)
+            from_x, from_y = out.at[p.at_x, p.core, cut], out.at[p.at_y, p.core, cut]
+            p.arrive(self.to_x[k], from_x)
+            if k < CHUNKS // 2:
+                onward[k] = p.send(from_x, from_x, p.y)
+            self.across[1, k] = p.send(from_x, from_x, p.sibling)
+            p.arrive(self.to_y[k], from_y)
+            if k >= CHUNKS // 2:
+                onward[k] = p.send(from_y, from_y, p.x)
+            self.across[2, k] = p.send(from_y, from_y, p.sibling)
+        for k in range(CHUNKS):
+            far = out.at[p.at_both, p.core, chunk(k, self.rows)]
+            p.arrive(onward[k], far)
+            self.across[3, k] = p.send(far, far, p.sibling)
+
+    def finish(self):
+        p = self.plane
+        for i, rank in enumerate((p.rank, p.at_x, p.at_y, p.at_both)):
+            for k in range(CHUNKS):
+                p.arrive(
+                    self.across[i, k], self.out.at[rank, 1 - p.core, chunk(k, self.rows)]
+                )
+
+
+GATHER_COPIES = CHUNKS * 8
+
+
+def add_rows(target, source, first, count):
+    def step(i, carry):
+        rows = pl.ds(first + i * SLAB, SLAB)
+        target[rows, :] = (
+            target[rows, :].astype(jnp.float32) + source[rows, :].astype(jnp.float32)
+        ).astype(jnp.bfloat16)
+        return carry
+
+    lax.fori_loop(0, count // SLAB, step, 0)
+
+
+class Scatter:
+    def __init__(self, plane, partial, held, other, near_x, near_y, far_x, far_y, local):
+        p = plane
+        rows = near_x.shape[0]
+        half = rows // 2
+        top, low = pl.ds(0, half), pl.ds(half, half)
+        order = (p.at_both, p.at_x, p.at_y, p.rank)
+        across, kept = [], []
+        for i, rank in enumerate(order):
+            across.append(p.send(partial.at[rank, 1 - p.core], other.at[i], p.sibling))
+            kept.append(pltpu.make_async_copy(partial.at[rank, p.core], held.at[i], local.at[i]))
+            kept[i].start()
+
+        def pair(i):
+            p.arrive(across[i], other.at[i])
+            kept[i].wait()
+            add_rows(held.at[i], other.at[i], 0, rows)
+
+        pair(0)
+        first = p.send(held.at[0, top], far_x, p.x)
+        second = p.send(held.at[0, low], far_y, p.y)
+        pair(1)
+        third = p.send(held.at[1, top], near_x.at[top], p.x)
+        pair(2)
+        fourth = p.send(held.at[2, low], near_y.at[low], p.y)
+        p.arrive(first, far_x)
+        add_rows(held.at[2], far_x, 0, half)
+        fifth = p.send(held.at[2, top], near_y.at[top], p.y)
+        p.arrive(second, far_y)
+
+        def step(i, carry):
+            rows, at = pl.ds(half + i * SLAB, SLAB), pl.ds(i * SLAB, SLAB)
+            held[1, rows, :] = (
+                held[1, rows, :].astype(jnp.float32) + far_y[at, :].astype(jnp.float32)
+            ).astype(jnp.bfloat16)
+            return carry
+
+        lax.fori_loop(0, half // SLAB, step, 0)
+        sixth = p.send(held.at[1, low], near_x.at[low], p.x)
+        pair(3)
+        p.arrive(third, near_x.at[top])
+        p.arrive(fourth, near_y.at[low])
+        p.arrive(fifth, near_y.at[top])
+        p.arrive(sixth, near_x.at[low])
+        self.parts = (held.at[3], near_x, near_y)
+
+    def rows(self, rows):
+        return sum(part[rows, :].astype(jnp.float32) for part in self.parts)
+
+
+SCATTER_COPIES = 4 + 6
+
+
+def scatter_scratch(share, width):
+    kind = jnp.bfloat16
+    return [
+        pltpu.VMEM((4, share, width), kind),
+        pltpu.VMEM((4, share, width), kind),
+        pltpu.VMEM((share, width), kind),
+        pltpu.VMEM((share, width), kind),
+        pltpu.VMEM((share // 2, width), kind),
+        pltpu.VMEM((share // 2, width), kind),
+        pltpu.SemaphoreType.DMA((4,)),
+    ]
+
+
+def wires(count):
+    return [pltpu.SemaphoreType.DMA((count,)), pltpu.SemaphoreType.DMA((count,))]
+
+
+def row_root(values):
+    return lax.rsqrt(jnp.mean(values * values, axis=-1, keepdims=True) + epsilon)
+
+
+def slabs(first, count, work):
+    def step(i, carry):
+        work(pl.ds(first + i * SLAB, SLAB))
+        return carry
+
+    lax.fori_loop(0, count // SLAB, step, 0)
+
+
+def start_kernel(
+    block, gate, up, down, out, gate_out, up_out, down_out, sent, landed, local
+):
+    p = Plane(sent, landed, diagonal=True)
+    gather = Gather(p, block, out)
+    mine = [pltpu.make_async_copy(block, out.at[p.rank, p.core], local.at[0])]
+    for k in range(CHUNKS):
+        gather.start(k)
+    moves = []
+    for i, (source, target) in enumerate(((gate, gate_out), (up, up_out), (down, down_out))):
+        mine.append(pltpu.make_async_copy(source.at[p.rank], target.at[p.rank], local.at[i + 1]))
+        for partner, rank in ((p.x, p.at_x), (p.y, p.at_y), (p.both, p.at_both)):
+            number = p.send(source.at[rank], target.at[p.rank], partner)
+            moves.append((number, target.at[rank]))
+    for started in mine:
+        started.start()
+    gather.forward()
+    gather.finish()
+    for number, target in moves:
+        p.arrive(number, target)
+    p.finish()
+    for started in mine:
+        started.wait()
+
+
+def start_plane(block, gate, up, down):
+    share, width = block.shape
+    full = jax.ShapeDtypeStruct((4, 2, share, width), block.dtype)
+    weight = jax.ShapeDtypeStruct(gate.shape, gate.dtype)
+    full, *weights = pl.pallas_call(
+        start_kernel,
+        out_shape=[full, weight, weight, weight],
+        in_specs=[ANY] * 4,
+        out_specs=[ANY] * 4,
+        scratch_shapes=wires(GATHER_COPIES + 9) + [pltpu.SemaphoreType.DMA((4,))],
+        compiler_params=pltpu.CompilerParams(collective_id=1, has_side_effects=True),
+        cost_estimate=lasting(80),
+        name="gather_tokens",
+    )(block, gate, up, down)
+    return full.reshape(8 * share, width), weights
+
+
+def middle_kernel(
+    partial, residual, gain, out, middle, sent, landed, own_copy, hidden, *scratch
+):
+    p = Plane(sent, landed)
+    total = Scatter(p, partial, *scratch)
+    share = hidden.shape[0]
+    gather = Gather(p, hidden, out)
+
+    def work(rows):
+        value = residual[rows, :].astype(jnp.float32) + residual_scale * total.rows(rows)
+        middle[rows, :] = value
+        hidden[rows, :] = (value * row_root(value) * gain[...]).astype(jnp.bfloat16)
+
+    for k in range(CHUNKS):
+        slabs(k * (share // CHUNKS), share // CHUNKS, work)
+        gather.start(k)
+    mine = pltpu.make_async_copy(hidden, out.at[p.rank, p.core], own_copy)
+    mine.start()
+    gather.forward()
+    gather.finish()
+    p.finish()
+    mine.wait()
+
+
+def middle_plane(partial, residual, gain):
+    share, width = residual.shape
+    full = jax.ShapeDtypeStruct((4, 2, share, width), jnp.bfloat16)
+    out, middle = pl.pallas_call(
+        middle_kernel,
+        out_shape=[full, jax.ShapeDtypeStruct((share, width), jnp.float32)],
+        in_specs=[ANY, VMEM, VMEM],
+        out_specs=[ANY, VMEM],
+        scratch_shapes=wires(GATHER_COPIES + SCATTER_COPIES)
+        + [pltpu.SemaphoreType.DMA, pltpu.VMEM((share, width), jnp.bfloat16)]
+        + scatter_scratch(share, width),
+        compiler_params=pltpu.CompilerParams(
+            collective_id=2, has_side_effects=True, vmem_limit_bytes=VMEM_LIMIT
+        ),
+        cost_estimate=lasting(100),
+        name="middle_rows",
+    )(partial.reshape(full.shape), residual, gain)
+    return out.reshape(8 * share, width), middle
+
+
+def second_kernel(
+    partial, middle, cotangent, gain, out, grad_middle, sent, landed, own_copy, hidden, *scratch
+):
+    p = Plane(sent, landed)
+    total = Scatter(p, partial, *scratch)
+    share = hidden.shape[0]
+    gather = Gather(p, hidden, out)
+
+    def work(rows):
+        value = middle[rows, :]
+        root = row_root(value)
+        normed = value * root
+        slope = total.rows(rows) * gain[...]
+        mean = jnp.mean(slope * normed, axis=-1, keepdims=True)
+        gradient = cotangent[rows, :].astype(jnp.float32) + root * (slope - normed * mean)
+        grad_middle[rows, :] = gradient
+        hidden[rows, :] = (residual_scale * gradient).astype(jnp.bfloat16)
+
+    for k in range(CHUNKS):
+        slabs(k * (share // CHUNKS), share // CHUNKS, work)
+        gather.start(k)
+    mine = pltpu.make_async_copy(hidden, out.at[p.rank, p.core], own_copy)
+    mine.start()
+    gather.forward()
+    gather.finish()
+    p.finish()
+    mine.wait()
+
+
+def second_plane(partial, middle, cotangent, gain):
+    share, width = middle.shape
+    full = jax.ShapeDtypeStruct((4, 2, share, width), jnp.bfloat16)
+    out, grad_middle = pl.pallas_call(
+        second_kernel,
+        out_shape=[full, jax.ShapeDtypeStruct((share, width), jnp.float32)],
+        in_specs=[ANY, VMEM, VMEM, VMEM],
+        out_specs=[ANY, VMEM],
+        scratch_shapes=wires(GATHER_COPIES + SCATTER_COPIES)
+        + [pltpu.SemaphoreType.DMA, pltpu.VMEM((share, width), jnp.bfloat16)]
+        + scatter_scratch(share, width),
+        compiler_params=pltpu.CompilerParams(
+            collective_id=3, has_side_effects=True, vmem_limit_bytes=VMEM_LIMIT
+        ),
+        cost_estimate=lasting(100),
+        name="second_rows",
+    )(partial.reshape(full.shape), middle, cotangent, gain)
+    return out.reshape(8 * share, width), grad_middle
+
+
+def last_kernel(
+    partial, residual, grad_middle, gain, result, out, result_out, sent, landed, local_copy, held, *scratch
+):
+    p = Plane(sent, landed)
+    kept = [pltpu.make_async_copy(result, result_out.at[p.core], local_copy.at[0])]
+    kept[0].start()
+    given = p.send(result, result_out.at[p.core], p.sibling)
+    total = Scatter(p, partial, *scratch)
+    share = held.shape[0]
+
+    def work(rows):
+        value = residual[rows, :].astype(jnp.float32)
+        root = row_root(value)
+        normed = value * root
+        slope = total.rows(rows) * gain[...]
+        mean = jnp.mean(slope * normed, axis=-1, keepdims=True)
+        held[rows, :] = grad_middle[rows, :] + root * (slope - normed * mean)
+
+    across = []
+    for k in range(CHUNKS):
+        cut = chunk(k, share)
+        slabs(k * (share // CHUNKS), share // CHUNKS, work)
+        across.append(p.send(held.at[cut], out.at[p.core, cut], p.sibling))
+    kept.append(pltpu.make_async_copy(held, out.at[p.core], local_copy.at[1]))
+    kept[1].start()
+    p.arrive(given, result_out.at[1 - p.core])
+    for k in range(CHUNKS):
+        p.arrive(across[k], out.at[1 - p.core, chunk(k, share)])
+    p.finish()
+    for started in kept:
+        started.wait()
+
+
+def last_plane(partial, residual, grad_middle, gain, result):
+    share, width = residual.shape
+    out, result_out = pl.pallas_call(
+        last_kernel,
+        out_shape=[
+            jax.ShapeDtypeStruct((2, share, width), jnp.float32),
+            jax.ShapeDtypeStruct((2, share, width), jnp.bfloat16),
+        ],
+        in_specs=[ANY, VMEM, VMEM, VMEM, ANY],
+        out_specs=[ANY, ANY],
+        scratch_shapes=wires(CHUNKS + 1 + SCATTER_COPIES)
+        + [pltpu.SemaphoreType.DMA((2,)), pltpu.VMEM((share, width), jnp.float32)]
+        + scatter_scratch(share, width),
+        compiler_params=pltpu.CompilerParams(
+            collective_id=4, has_side_effects=True, vmem_limit_bytes=VMEM_LIMIT
+        ),
+        cost_estimate=lasting(70),
+        name="last_rows",
+    )(partial.reshape(4, 2, share, width), residual, grad_middle, gain, result)
+    return out.reshape(2 * share, width), result_out.reshape(2 * share, width)
+
+
+def context_pairs(step):
+    return [(i, i ^ step) for i in range(4)]
+
+
+def swap_cores(values):
+    return lax.ppermute(values, "tensor", [(0, 1), (1, 0)])
+
+
+def gather_beside(block):
+    rank, core = lax.axis_index("context"), lax.axis_index("tensor")
+    share, width = block.shape
+    mine = jnp.zeros((4, share, width), block.dtype)
+    for step in range(4):
+        got = lax.ppermute(block, "context", context_pairs(step)) if step else block
+        mine = lax.dynamic_update_slice(mine, got[None], (rank ^ step, 0, 0))
+    theirs = swap_cores(mine)
+    first = jnp.where(core == 0, mine, theirs)
+    second = jnp.where(core == 0, theirs, mine)
+    return jnp.stack([first, second], axis=1).reshape(8 * share, width)
+
+
+def scatter_beside(partial, share):
+    rank, core = lax.axis_index("context"), lax.axis_index("tensor")
+    blocks = partial.reshape(4, 2, share, -1)
+    keep = lax.dynamic_index_in_dim(blocks, core, 1, False)
+    give = lax.dynamic_index_in_dim(blocks, 1 - core, 1, False)
+    both = (keep.astype(jnp.float32) + swap_cores(give).astype(jnp.float32)).astype(jnp.bfloat16)
+    total = lax.dynamic_index_in_dim(both, rank, 0, False).astype(jnp.float32)
+    for step in range(1, 4):
+        block = lax.dynamic_index_in_dim(both, rank ^ step, 0, False)
+        total += lax.ppermute(block, "context", context_pairs(step)).astype(jnp.float32)
+    return total
+
+
 def norm_backward(gradient, normed, inv_root):
     return inv_root * (gradient - normed * jnp.mean(gradient * normed, axis=-1, keepdims=True))
 
@@ -376,9 +797,18 @@
     out_full = packed[:, width + 2 * HEAD : 2 * width + 2 * HEAD]
     gains_full = packed[:, 2 * width + 2 * HEAD :].astype(jnp.float32)
     attn_scale, ffn_scale = gains_full[:, 0], gains_full[:, 1]
-    gate_full = spread(blocks(w_gate))
-    up_full = spread(blocks(w_up))
-    down_full = spread(blocks(w_down.T))
+    square = groups == 4 and cores == 2
+    ffn_blocks = blocks(w_gate), blocks(w_up), blocks(w_down.T)
+    tokens_half, cotangent_half = my_rows(tokens), my_rows(cotangent)
+    if square:
+        inputs_full, ffn_blocks = start_plane(tokens_half, *ffn_blocks)
+    else:
+        inputs_full = gather_rows(tokens_half)
+        ffn_blocks = [lax.all_to_all(w, "context", 0, 0) for w in ffn_blocks]
+    gate_full, up_full, down_full = (
+        lax.all_gather(w.reshape(groups * depth, -1), "fsdp", axis=0, tiled=True)
+        for w in ffn_blocks
+    )
 
     segment, starts = piece_segment[0] % 13, piece_start[0]
     places = jnp.where(
@@ -392,19 +822,21 @@
     )
     tables = rope_tables()
 
-    inputs_full = gather_rows(my_rows(tokens)).astype(jnp.float32)
+    inputs_full = inputs_full.astype(jnp.float32)
     hidden_first = (inputs_full * inverse_root(inputs_full) * attn_scale).astype(jnp.bfloat16)
-    residual_in = my_rows(tokens).astype(jnp.float32)
-    grad_result = my_rows(cotangent).astype(jnp.float32)
-    ffn_grad = gather_rows((residual_scale * grad_result).astype(jnp.bfloat16))
+    residual_in = tokens_half.astype(jnp.float32)
+    grad_result = cotangent_half.astype(jnp.float32)
+    ffn_grad = (residual_scale * grad_result).astype(jnp.bfloat16)
+    ffn_grad = gather_beside(ffn_grad) if square else gather_rows(ffn_grad)
 
     raw = dot(hidden_first, qkv_full)
     attended, *kept = attention_forward(places, starts, raw, tables)
-    branch = scatter_rows(dot(attended, out_full, LAST))
-    middle = residual_in + residual_scale * branch
-    norm_second = inverse_root(middle)
-    normed_second = middle * norm_second
-    hidden_second = gather_rows((normed_second * ffn_scale).astype(jnp.bfloat16))
+    branch = dot(attended, out_full, LAST).astype(jnp.bfloat16)
+    if square:
+        hidden_second, middle = middle_plane(branch, tokens_half, ffn_scale[None, :])
+    else:
+        middle = residual_in + residual_scale * scatter_rows(branch)
+        hidden_second = gather_rows((middle * inverse_root(middle) * ffn_scale).astype(jnp.bfloat16))
 
     gate_proj = dot(hidden_second, gate_full)
     up_proj = dot(hidden_second, up_full)
@@ -415,12 +847,12 @@
     silu_slope = sigmoid_gate * (1.0 + gate_proj * (1.0 - sigmoid_gate))
     grad_gate_proj = (grad_hidden * up_proj * silu_slope).astype(jnp.bfloat16)
     grad_up_proj = (grad_hidden * silu_gate).astype(jnp.bfloat16)
-    grad_second = scatter_rows(
+    grad_second = (
         dot(grad_gate_proj, gate_full, LAST) + dot(grad_up_proj, up_full, LAST)
-    )
-    ffn_out = scatter_rows(dot(hidden, down_full, LAST))
+    ).astype(jnp.bfloat16)
+    ffn_out = dot(hidden, down_full, LAST).astype(jnp.bfloat16)
+    ffn_out = scatter_beside(ffn_out, share) if square else scatter_rows(ffn_out)
     result = (middle + residual_scale * ffn_out).astype(jnp.bfloat16)
-    result = lax.all_gather(result, "tensor", axis=0, tiled=True)
 
     def collect(gradient):
         mine = lax.psum_scatter(
@@ -435,42 +867,63 @@
     grad_gate = collect(dot(hidden_second, grad_gate_proj, FIRST))
     grad_up = collect(dot(hidden_second, grad_up_proj, FIRST))
 
-    grad_ffn_gain = jnp.sum(grad_second * normed_second, axis=0)
-    grad_middle = grad_result + norm_backward(grad_second * ffn_scale, normed_second, norm_second)
-    attn_grad = gather_rows((residual_scale * grad_middle).astype(jnp.bfloat16))
+    if square:
+        attn_grad, grad_middle = second_plane(
+            grad_second, middle, cotangent_half, ffn_scale[None, :]
+        )
+    else:
+        root = inverse_root(middle)
+        grad_middle = grad_result + norm_backward(
+            scatter_rows(grad_second) * ffn_scale, middle * root, root
+        )
+        attn_grad = gather_rows((residual_scale * grad_middle).astype(jnp.bfloat16))
     grad_attended = dot(attn_grad, out_full).astype(jnp.bfloat16)
     back = attention_backward(places, starts, grad_attended, kept, tables)
-    grad_first = scatter_rows(dot(back, qkv_full, LAST))
+    grad_first = dot(back, qkv_full, LAST).astype(jnp.bfloat16)
+    if square:
+        grad_tokens, result = last_plane(
+            grad_first, tokens_half, grad_middle, attn_scale[None, :], result
+        )
+    else:
+        root = inverse_root(residual_in)
+        grad_tokens = grad_middle + norm_backward(
+            scatter_rows(grad_first) * attn_scale, residual_in * root, root
+        )
+        grad_tokens = lax.all_gather(grad_tokens, "tensor", axis=0, tiled=True)
+        result = lax.all_gather(result, "tensor", axis=0, tiled=True)
     grad_attn = collect(
         jnp.concatenate([dot(hidden_first, back, FIRST), dot(attn_grad, attended, FIRST)], axis=1)
     )
-    norm_first = inverse_root(residual_in)
-    normed_first = residual_in * norm_first
-    grad_attn_gain = jnp.sum(grad_first * normed_first, axis=0)
-    grad_tokens = grad_middle + norm_backward(grad_first * attn_scale, normed_first, norm_first)
-    grad_tokens = lax.all_gather(grad_tokens, "tensor", axis=0, tiled=True)
-
-    gain_grads = lax.psum(
-        jnp.stack([grad_attn_gain, grad_ffn_gain]), ("fsdp", "context", "tensor")
-    )
-    rank = lax.axis_index("fsdp") * groups + lax.axis_index("context")
-    gain_grads = lax.dynamic_slice_in_dim(gain_grads, rank * depth, depth, 1)
-
     def kv_columns(gradient):
         gradient = gradient.astype(jnp.float32).reshape(kv_count, sharing, depth, HEAD)
         return jnp.transpose(jnp.sum(gradient, axis=1), (1, 0, 2)).reshape(depth, -1)
 
+    grad_query = columns(grad_attn[:, :, :width])
+    grad_key = kv_columns(grad_attn[:, :, width : width + HEAD])
+    grad_value = kv_columns(grad_attn[:, :, width + HEAD : width + 2 * HEAD])
+    grad_gate, grad_up = columns(grad_gate), columns(grad_up)
+
+    def against(*pairs):
+        return sum(jnp.sum(weight.astype(jnp.float32) * g, axis=1) for weight, g in pairs)
+
+    gain_grads = jnp.stack(
+        [
+            against((w_query, grad_query), (w_key, grad_key), (w_value, grad_value)),
+            against((w_gate, grad_gate), (w_up, grad_up)),
+        ]
+    )
+    gain_grads += swap_cores(gain_grads) if square else lax.psum(gain_grads, "tensor") - gain_grads
     return (
         result,
         grad_tokens,
-        gain_grads[0],
-        columns(grad_attn[:, :, :width]),
-        kv_columns(grad_attn[:, :, width : width + HEAD]),
-        kv_columns(grad_attn[:, :, width + HEAD : width + 2 * HEAD]),
+        gain_grads[0] / attn_gain.astype(jnp.float32),
+        grad_query,
+        grad_key,
+        grad_value,
         columns(grad_attn[:, :, width + 2 * HEAD :]).T,
-        gain_grads[1],
-        columns(grad_gate),
-        columns(grad_up),
+        gain_grads[1] / ffn_gain.astype(jnp.float32),
+        grad_gate,
+        grad_up,
         columns(grad_down).T,
     )
 

time: 1520 us -> 994 us (0.65)
  waiting for transfers between devices: 967 us -> 157 us
  Pallas kernels: 106 us -> 446 us
  blocking collectives: 111 us -> 16.5 us
  local copies, waits for them, and re-layouts: 37.8 us -> 61.9 us
  other arithmetic: 42 us -> 64.1 us
    pallas_call x0 -> x4, Pallas kernels: none -> 339 us  [the longest x1 99 us: second_plane(): pl.pallas_call(second_kernel, out_shape=[full, jax.ShapeDtypeStruct((shar...]
    all_gather x6 -> x3, waiting for transfers between devices: 254 us -> 0.01 us  [local(): lax.all_gather(w.reshape(groups * depth, -1), 'fsdp', axis=0, tiled=True)]
    all_gather x4 -> x1, waiting for transfers between devices: 220 us -> 0.01 us  [spread(): return lax.all_gather(mine, 'fsdp', axis=0, tiled=True)]
    reduce_scatter x4 -> x0, waiting for transfers between devices: 215 us -> none  [scatter_rows(): lax.psum_scatter(partial.astype(jnp.bfloat16), PLANE, scatter_dimension=0...]
    reduce_scatter x4, waiting for transfers between devices: 273 us -> 113 us  [collect(): lax.psum_scatter(gradient.astype(jnp.bfloat16), 'fsdp', scatter_dimension...]
    all_to_all x4 -> x1, blocking collectives: 71.7 us -> 16.5 us  [spread(): mine = lax.all_to_all(weight_blocks, 'context', 0, 0)]
    psum x1 -> x0, blocking collectives: 39.3 us -> none  [local(): lax.psum(jnp.stack([grad_attn_gain, grad_ffn_gain]), ('fsdp', 'context',...]
    ppermute x0 -> x9, waiting for transfers between devices: none -> 34.4 us  [the longest x3 34.3 us: gather_beside(): got = lax.ppermute(block, 'context', context_pairs(step)) if step else block]
  transfers between devices with their start and end apart: 22 -> 21, of which waited for: 16 -> 6; matrix products, arithmetic and copies ran while one was open for 11% -> 22% of each run, Pallas kernels for 0% -> 29%
where the time goes in v2:
time: 994 us; the launch traced here: 988 us
  Pallas kernels  446 us (45%)
  matrix products  204 us (21%)
  waiting for transfers between devices  157 us (16%)
  other arithmetic  64.1 us (6%)
  local copies, waits for them, and re-layouts  61.9 us (6%)
  starting transfers between devices  23.9 us (2%)
  blocking collectives  16.5 us (2%)
  between operations  15.3 us (2%)
    dot_general x15, matrix products, dot(): lax.dot_general(left_side, right_side, dims, preferred_element_type=jnp.f...  204 us
    reduce_scatter x4, waiting for transfers between devices, collect(): lax.psum_scatter(gradient.astype(jnp.bfloat16), 'fsdp', scatter_dimension...  113 us
    pallas_call x1, Pallas kernels, second_plane(): pl.pallas_call(second_kernel, out_shape=[full, jax.ShapeDtypeStruct((shar...  99 us
    pallas_call x1, Pallas kernels, middle_plane(): pl.pallas_call(middle_kernel, out_shape=[full, jax.ShapeDtypeStruct((shar...  98.1 us
    pallas_call x1, Pallas kernels, start_plane(): pl.pallas_call(start_kernel, out_shape=[full, weight, weight, weight], in...  81.8 us
    pallas_call x1, Pallas kernels, last_plane(): pl.pallas_call(last_kernel, out_shape=[jax.ShapeDtypeStruct((2, share, wi...  60.4 us
    pallas_call x1, Pallas kernels, attention_backward(): pl.pallas_call(attention_backward_kernel, out_shape=jax.ShapeDtypeStruct(...  55.7 us
    pallas_call x1, Pallas kernels, attention_forward(): pl.pallas_call(attention_forward_kernel, out_shape=[kept] * 4 + [jax.Shap...  50.7 us
  transfers between devices with their start and end apart: 21, of which 6 were waited for; matrix products, arithmetic and copies ran while one was open for 22% of the time, Pallas kernels for 29%

profile of v2, /device:TPU:0, one launch (start us, length us, event | category | flops | bytes accessed | tf_op | source)
XLA Modules:
  0.0 988.3 jit_solution(16738594617133216829)
XLA Ops:
  15.6 16.5 %all_to_all.25 = bf16[4,128,768]{1,2,0:T(8,128)(2,1)S(1)} all-to-all(bf16[4,128,768]{1,2,0:T(8,128)(2,1)} %broadcast_dynamic-update-slice_fusion), channel_id=1, replica_groups=mesh['fsdp'=4,'context'=4,'tensor'=2] {'context'}, dimensions={0} | all-to-all | bytes 1572864 | tf_op jit(solution)/shard_map/all_to_all | solution.py:784
  45.9 81.8 %gather_tokens.1 = (bf16[4,2,320,2048]{3,2,1,0:T(8,128)(2,1)}, bf16[4,128,1024]{2,1,0:T(8,128)(2,1)}, bf16[4,128,1024]{2,1,0:T(8,128)(2,1)}, bf16[4,128,1024]{2,1,0:T(8,128)(2,1)}) custom-call(bf16[320,2048]{1,0:T(8,128)(2,1)} %constant_dynamic-slice_fusion.block.residual, bf16[4,128,1024]{2,1,0:T(8,128)(2,1)} %bitcast.172, bf16[4,128,1024]{2,1,0:T(8,128)(2,1)} %bitcast.173, ...), custom_call_target="tpu_custom_call" | custom-call | bytes 240000000 | tf_op jit(solution)/shard_map/gather_tokens/pallas_call | solution.py:534
  153.4 9.9 %collective-permute-done = bf16[320,2048]{1,0:T(8,128)(2,1)} collective-permute-done((bf16[320,2048]{1,0:T(8,128)(2,1)}, bf16[320,2048]{1,0:T(8,128)(2,1)}, u32[]{:S(2)}, u32[]{:S(2)}) %collective-permute-start) | collective-permute-done | bytes 1310752 | tf_op jit(solution)/shard_map/ppermute | solution.py:708
  165.8 24.4 %collective-permute-done.1 = bf16[320,2048]{1,0:T(8,128)(2,1)} collective-permute-done((bf16[320,2048]{1,0:T(8,128)(2,1)}, bf16[320,2048]{1,0:T(8,128)(2,1)}, u32[]{:S(2)}, u32[]{:S(2)}) %collective-permute-start.1) | collective-permute-done | bytes 1310752 | tf_op jit(solution)/shard_map/ppermute | solution.py:708
  211.6 50.7 %attention_forward.1 = (bf16[2560,256]{1,0:T(8,128)(2,1)S(1)}, bf16[2560,256]{1,0:T(8,128)(2,1)S(1)}, bf16[2560,256]{1,0:T(8,128)(2,1)S(1)}, bf16[2560,256]{1,0:T(8,128)(2,1)}, f32[4,1,2560]{2,1,0:T(1,128)S(1)}) custom-call(s32[20]{0:T(128)S(1)} %compare_select_fusion.1.to_ref, s32[20]{0:T(128)S(1)} %bitcast.156, f32[2560,384]{1,0:T(8,128)} %fusion.10.raw_ref, ...), custom_call_target="tpu_custom_call" | custom-call | flops 5368709120 | bytes 10485760 | tf_op jit(solution)/shard_map/attention_forward/pallas_call | solution.py:277
  267.9 98.1 %middle_rows.1 = (bf16[4,2,320,2048]{3,2,1,0:T(8,128)(2,1)}, f32[320,2048]{1,0:T(8,128)S(1)}) custom-call(bf16[4,2,320,2048]{3,2,1,0:T(8,128)(2,1)} %bitcast.158, bf16[320,2048]{1,0:T(8,128)(2,1)S(1)} %copy-done.2, f32[1,2048]{1,0:T(1,128)S(1)} %bitcast.154), custom_call_target="tpu_custom_call" | custom-call | bytes 300000000 | tf_op jit(solution)/shard_map/middle_rows/pallas_call | solution.py:574
  367.6 16.5 %fusion.20 = f32[2560,1024]{1,0:T(8,128)} fusion(bf16[2560,2048]{1,0:T(8,128)(2,1)} %bitcast.196, bf16[2048,1024]{1,0:T(8,128)(2,1)} %all-gather.11.cloned.1.call-done), kind=kOutput, calls=%fused_computation.90 | convolution fusion | flops 10737418240 | bytes 25165824 | tf_op jit(solution)/shard_map/dot_general | solution.py:31
  384.1 16.4 %fusion.19 = f32[2560,1024]{1,0:T(8,128)} fusion(bf16[2560,2048]{1,0:T(8,128)(2,1)} %bitcast.197, bf16[2048,1024]{1,0:T(8,128)(2,1)} %all-gather.9.cloned.1.call-done), kind=kOutput, calls=%fused_computation.89 | convolution fusion | flops 10737418240 | bytes 25165824 | tf_op jit(solution)/shard_map/dot_general | solution.py:31
  400.5 8.8 select_bitcast_fusion.1
  409.3 8.9 pad_maximum_fusion
  418.2 26.7 %multiply_convert_fusion = (bf16[2560,1024]{1,0:T(8,128)(2,1)}, bf16[2560,1024]{1,0:T(8,128)(2,1)}, bf16[2560,1024]{1,0:T(8,128)(2,1)}) fusion(f32[2560,1024]{1,0:T(8,128)} %fusion.19, f32[2560,1024]{1,0:T(8,128)} %fusion.20, bf16[2560,2048]{1,0:T(8,128)(2,1)} %bitcast.159, bf16[2048,1024]{1,0:T(8,128)(2,1)} %all-gather.5.cloned.1.call-done), kind=kOutput, calls=%fused_computation.11 | convolution fusion | flops 10776739840 | bytes 51380224 | tf_op jit(solution)/shard_map/dot_general | solution.py:31
  445.0 18.2 %fusion.21 = f32[2560,2048]{1,0:T(8,128)} fusion(bf16[2560,1024]{1,0:T(8,128)(2,1)} %get-tuple-element.79, bf16[2048,1024]{1,0:T(8,128)(2,1)} %all-gather.11.cloned.1.call-done), kind=kOutput, calls=%fused_computation.91 | convolution fusion | flops 10737418240 | bytes 30408704 | tf_op jit(solution)/shard_map/dot_general | solution.py:31
  463.1 20.0 %add_convert_fusion = bf16[2560,2048]{1,0:T(8,128)(2,1)} fusion(f32[2560,2048]{1,0:T(8,128)} %fusion.21, bf16[2560,1024]{1,0:T(8,128)(2,1)} %get-tuple-element.80, bf16[2048,1024]{1,0:T(8,128)(2,1)} %all-gather.9.cloned.1.call-done), kind=kOutput, calls=%fused_computation.3 | convolution fusion | flops 10747904000 | bytes 40894464 | tf_op jit(solution)/shard_map/dot_general | solution.py:31
  483.1 99.0 %second_rows.1 = (bf16[4,2,320,2048]{3,2,1,0:T(8,128)(2,1)}, f32[320,2048]{1,0:T(8,128)S(1)}) custom-call(bf16[4,2,320,2048]{3,2,1,0:T(8,128)(2,1)} %bitcast.166, f32[320,2048]{1,0:T(8,128)} %copy-done.4, bf16[320,2048]{1,0:T(8,128)(2,1)S(1)} %get-tuple-element.77.cotangent, f32[1,2048]{1,0:T(1,128)S(1)} %bitcast.155), custom_call_target="tpu_custom_call" | custom-call | bytes 300000000 | tf_op jit(solution)/shard_map/second_rows/pallas_call | solution.py:623
  582.2 8.9 convolution_convert_fusion.8
  595.6 55.7 %attention_backward.1 = bf16[2560,384]{1,0:T(8,128)(2,1)} custom-call(s32[20]{0:T(128)S(1)} %compare_select_fusion.1.to_ref, s32[20]{0:T(128)S(1)} %bitcast.157, bf16[2560,256]{1,0:T(8,128)(2,1)S(1)} %convolution_convert_fusion.3.grad_ref, bf16[2560,256]{1,0:T(8,128)(2,1)S(1)} %copy-done.17, bf16[2560,256]{1,0:T(8,128)(2,1)S(1)} %copy-done.19, ...), custom_call_target="tpu_custom_call" | custom-call | flops 13421772800 | bytes 10485760 | tf_op jit(solution)/shard_map/attention_backward/pallas_call | solution.py:291
  659.2 17.0 %convolution_convert_fusion.5 = bf16[2048,1024]{1,0:T(8,128)(2,1)} fusion(bf16[2560,2048]{1,0:T(8,128)(2,1)} %bitcast.198, bf16[2560,1024]{1,0:T(8,128)(2,1)} %get-tuple-element.80), kind=kOutput, calls=%fused_computation.21 | convolution fusion | flops 10739515392 | bytes 19922944 | tf_op jit(solution)/shard_map/dot_general | solution.py:31
  676.3 16.8 %convolution_convert_fusion.6 = bf16[2048,1024]{1,0:T(8,128)(2,1)} fusion(bf16[2560,2048]{1,0:T(8,128)(2,1)} %bitcast.199, bf16[2560,1024]{1,0:T(8,128)(2,1)} %get-tuple-element.79), kind=kOutput, calls=%fused_computation.22 | convolution fusion | flops 10739515392 | bytes 19922944 | tf_op jit(solution)/shard_map/dot_general | solution.py:31
  693.2 14.6 %convolution_convert_fusion = bf16[2560,2048]{1,0:T(8,128)(2,1)S(1)} fusion(bf16[2560,1024]{1,0:T(8,128)(2,1)} %get-tuple-element.78, bf16[2048,1024]{1,0:T(8,128)(2,1)} %all-gather.5.cloned.1.call-done), kind=kOutput, calls=%fused_computation.5 | convolution fusion | flops 10742661120 | bytes 19922944 | tf_op jit(solution)/shard_map/dot_general | solution.py:31
  713.9 16.8 %convolution_convert_fusion.4 = bf16[2048,1024]{1,0:T(8,128)(2,1)} fusion(bf16[2560,2048]{1,0:T(8,128)(2,1)} %bitcast.160, bf16[2560,1024]{1,0:T(8,128)(2,1)} %get-tuple-element.78), kind=kOutput, calls=%fused_computation.20 | convolution fusion | flops 10739515392 | bytes 19922944 | tf_op jit(solution)/shard_map/dot_general | solution.py:31
  760.6 29.8 %reduce-scatter.9.cloned.1.call-done = bf16[512,1024]{1,0:T(8,128)(2,1)} async-done(((bf16[2048,1024]{1,0:T(8,128)(2,1)}), bf16[512,1024]{1,0:T(8,128)(2,1)}) %reduce-scatter.9.cloned.1.call-update) | async-done | bytes 1048592 | tf_op jit(solution)/shard_map/reduce_scatter | solution.py:858
  795.9 74.2 %reduce-scatter.7.cloned.1.call-done = bf16[512,1024]{1,0:T(8,128)(2,1)} async-done(((bf16[2048,1024]{1,0:T(8,128)(2,1)}), bf16[512,1024]{1,0:T(8,128)(2,1)}) %reduce-scatter.7.cloned.1.call-update) | async-done | bytes 1048592 | tf_op jit(solution)/shard_map/reduce_scatter | solution.py:858
  879.0 60.4 %last_rows.1 = (f32[2,320,2048]{2,1,0:T(8,128)}, bf16[2,320,2048]{2,1,0:T(8,128)(2,1)S(1)}) custom-call(bf16[4,2,320,2048]{3,2,1,0:T(8,128)(2,1)} %bitcast.161, bf16[320,2048]{1,0:T(8,128)(2,1)S(1)} %copy-done.3, f32[320,2048]{1,0:T(8,128)} %copy-done.5, f32[1,2048]{1,0:T(1,128)S(1)} %bitcast.153, bf16[320,2048]{1,0:T(8,128)(2,1)S(1)} %fusion.8.result), custom_call_target="tpu_custom_call" | custom-call | bytes 210000000 | tf_op jit(solution)/shard_map/last_rows/pallas_call | solution.py:675
  958.6 9.4 all-to-all-done.4
  (201 shorter events, 173.3 us)
Async XLA Ops:
  7.2 188.1 %all-gather.7.cloned.1.call-start = ((), (), s32[]{:S(2)}) async-start(), calls=%async_computation.10 | async-start | bytes 3932160 | tf_op jit(solution)/shard_map/all_gather | solution.py:786
  33.3 334.3 %all-gather.11.cloned.1.call-start = ((), (), s32[]{:S(2)}) async-start(), calls=%async_computation.12 | async-start | bytes 5242880 | tf_op jit(solution)/shard_map/all_gather | solution.py:809
  127.7 256.3 %all-gather.9.cloned.1.call-start = ((), (), s32[]{:S(2)}) async-start(), calls=%async_computation.11 | async-start | bytes 5242880 | tf_op jit(solution)/shard_map/all_gather | solution.py:809
  128.5 289.7 %all-gather.5.cloned.1.call-start = ((), (), s32[]{:S(2)}) async-start(), calls=%async_computation.9 | async-start | bytes 5242880 | tf_op jit(solution)/shard_map/all_gather | solution.py:809
  131.4 31.9 %collective-permute-start = (bf16[320,2048]{1,0:T(8,128)(2,1)}, bf16[320,2048]{1,0:T(8,128)(2,1)}, u32[]{:S(2)}, u32[]{:S(2)}) collective-permute-start(bf16[320,2048]{1,0:T(8,128)(2,1)} %get-tuple-element.76), channel_id=1, source_target_pairs={{0,2},{2,0},{4,6},{6,4},{1,3},{3,1},{5,7},{7,5},{8,10},{10,8},{12,... | collective-permute-start | bytes 3932168 | tf_op jit(solution)/shard_map/ppermute | solution.py:708
  131.9 58.3 %collective-permute-start.1 = (bf16[320,2048]{1,0:T(8,128)(2,1)}, bf16[320,2048]{1,0:T(8,128)(2,1)}, u32[]{:S(2)}, u32[]{:S(2)}) collective-permute-start(bf16[320,2048]{1,0:T(8,128)(2,1)} %get-tuple-element.76), channel_id=1, source_target_pairs={{0,4},{2,6},{4,0},{6,2},{1,5},{3,7},{5,1},{7,3},{8,12},{10,14},{12... | collective-permute-start | bytes 3932168 | tf_op jit(solution)/shard_map/ppermute | solution.py:708
  133.4 59.3 %collective-permute-start.2 = (bf16[320,2048]{1,0:T(8,128)(2,1)}, bf16[320,2048]{1,0:T(8,128)(2,1)}, u32[]{:S(2)}, u32[]{:S(2)}) collective-permute-start(bf16[320,2048]{1,0:T(8,128)(2,1)} %get-tuple-element.76), channel_id=1, source_target_pairs={{0,6},{2,4},{4,2},{6,0},{1,7},{3,5},{5,3},{7,1},{8,14},{10,12},{12... | collective-permute-start | bytes 3932168 | tf_op jit(solution)/shard_map/ppermute | solution.py:708
  134.9 595.9 %reduce-scatter.5.cloned.1.call-start = ((), (), s32[]{:S(2)}) async-start(), calls=%async_computation.13 | async-start | bytes 3276800 | tf_op jit(solution)/shard_map/reduce_scatter | solution.py:858
  195.3 205.2 %collective-permute-start.3 = (bf16[4,320,2048]{2,1,0:T(8,128)(2,1)}, bf16[4,320,2048]{2,1,0:T(8,128)(2,1)}, u32[]{:S(2)}, u32[]{:S(2)}) collective-permute-start(bf16[4,320,2048]{2,1,0:T(8,128)(2,1)} %bitcast_dynamic-update-slice_fusion), channel_id=1, source_target_pairs={{0,1},{1,0},{2,3},{3,2},{4,5},{5,4},{6,7},{7,6},{8,9},{9,8},{10,11... | collective-permute-start | bytes 15728648 | tf_op jit(solution)/shard_map/ppermute | solution.py:700
  483.1 99.0 %copy-start.8 = (bf16[2560,256]{1,0:T(8,128)(2,1)S(1)}, bf16[2560,256]{1,0:T(8,128)(2,1)}, u32[]{:S(2)}) copy-start(bf16[2560,256]{1,0:T(8,128)(2,1)} %copy-done.7) | copy-start | bytes 3932164
  591.1 60.2 %slice-start = ((s8[10485760]{0:T(1024)(128)(4,1)}), s8[2097152]{0:T(1024)(128)(4,1)S(1)}, s32[]{:S(2)}) async-start(s8[10485760]{0:T(1024)(128)(4,1)} %bitcast.162), calls=%async_computation.17 | async-start | bytes 4194304
  659.1 131.3 %reduce-scatter.9.cloned.1.call-start = ((), (), s32[]{:S(2)}) async-start(), calls=%async_computation.15 | async-start | bytes 5242880 | tf_op jit(solution)/shard_map/reduce_scatter | solution.py:858
  676.2 193.9 %reduce-scatter.7.cloned.1.call-start = ((), (), s32[]{:S(2)}) async-start(), calls=%async_computation.14 | async-start | bytes 5242880 | tf_op jit(solution)/shard_map/reduce_scatter | solution.py:858
  693.1 256.6 %reduce-scatter.11.cloned.1.call-start = ((), (), s32[]{:S(2)}) async-start(), calls=%async_computation.16 | async-start | bytes 5242880 | tf_op jit(solution)/shard_map/reduce_scatter | solution.py:858
  713.4 23.2 %collective-permute-start.4 = (bf16[4,320,2048]{2,1,0:T(8,128)(2,1)}, bf16[4,320,2048]{2,1,0:T(8,128)(2,1)}, u32[]{:S(2)}, u32[]{:S(2)}) collective-permute-start(bf16[4,320,2048]{2,1,0:T(8,128)(2,1)} %dynamic-slice_bitcast_fusion), channel_id=1, source_target_pairs={{0,1},{1,0},{2,3},{3,2},{4,5},{5,4},{6,7},{7,6},{8,9},{9,8},{10,11... | collective-permute-start | bytes 15728648 | tf_op jit(solution)/shard_map/ppermute | solution.py:700
  732.8 26.7 %all-to-all-start.1 = ((bf16[4,128,640]{1,2,0:T(8,128)(2,1)}), bf16[4,128,640]{1,2,0:T(8,128)(2,1)S(1)}, u32[]{:S(2)}, u32[]{:S(2)}) async-start(bf16[4,128,640]{1,2,0:T(8,128)(2,1)} %copy_bitcast_fusion), calls=%async_computation.2 | async-start | bytes 1310720 | tf_op jit(solution)/shard_map/all_to_all | solution.py:861
  747.7 126.8 %collective-permute-start.5 = (bf16[320,2048]{1,0:T(8,128)(2,1)}, bf16[320,2048]{1,0:T(8,128)(2,1)}, u32[]{:S(2)}, u32[]{:S(2)}) collective-permute-start(bf16[320,2048]{1,0:T(8,128)(2,1)} %get-tuple-element.83), channel_id=1, source_target_pairs={{0,2},{2,0},{4,6},{6,4},{1,3},{3,1},{5,7},{7,5},{8,10},{10,8},{12,... | collective-permute-start | bytes 3932168 | tf_op jit(solution)/shard_map/ppermute | solution.py:725
  749.7 124.8 %collective-permute-start.6 = (bf16[320,2048]{1,0:T(8,128)(2,1)}, bf16[320,2048]{1,0:T(8,128)(2,1)}, u32[]{:S(2)}, u32[]{:S(2)}) collective-permute-start(bf16[320,2048]{1,0:T(8,128)(2,1)} %get-tuple-element.85), channel_id=1, source_target_pairs={{0,4},{2,6},{4,0},{6,2},{1,5},{3,7},{5,1},{7,3},{8,12},{10,14},{12... | collective-permute-start | bytes 3932168 | tf_op jit(solution)/shard_map/ppermute | solution.py:725
  751.2 123.3 %collective-permute-start.7 = (bf16[320,2048]{1,0:T(8,128)(2,1)}, bf16[320,2048]{1,0:T(8,128)(2,1)}, u32[]{:S(2)}, u32[]{:S(2)}) collective-permute-start(bf16[320,2048]{1,0:T(8,128)(2,1)} %get-tuple-element.84), channel_id=1, source_target_pairs={{0,6},{2,4},{4,2},{6,0},{1,7},{3,5},{5,3},{7,1},{8,14},{10,12},{12... | collective-permute-start | bytes 3932168 | tf_op jit(solution)/shard_map/ppermute | solution.py:725
  760.6 118.4 %copy-start.27 = (f32[128,1024]{1,0:T(8,128)}, f32[128,1024]{1,0:T(8,128)S(1)}, u32[]{:S(2)}) copy-start(f32[128,1024]{1,0:T(8,128)S(1)} %copy.90) | copy-start | bytes 1572868
  790.4 79.7 %all-to-all-start.3 = ((bf16[4,128,1024]{2,1,0:T(8,128)(2,1)}), bf16[4,128,1024]{2,1,0:T(8,128)(2,1)S(1)}, u32[]{:S(2)}, u32[]{:S(2)}) async-start(bf16[4,128,1024]{2,1,0:T(8,128)(2,1)} %bitcast.188), calls=%async_computation.6 | async-start | bytes 2097152 | tf_op jit(solution)/shard_map/all_to_all | solution.py:861
  870.1 79.6 %all-to-all-start.2 = ((bf16[4,128,1024]{2,1,0:T(8,128)(2,1)}), bf16[4,128,1024]{2,1,0:T(8,128)(2,1)}, u32[]{:S(2)}, u32[]{:S(2)}) async-start(bf16[4,128,1024]{2,1,0:T(8,128)(2,1)} %bitcast.184), calls=%async_computation.4 | async-start | bytes 2097152 | tf_op jit(solution)/shard_map/all_to_all | solution.py:861
  949.7 18.3 %all-to-all-start.4 = ((bf16[4,128,1024]{2,1,0:T(8,128)(2,1)}), bf16[4,128,1024]{2,1,0:T(8,128)(2,1)}, u32[]{:S(2)}, u32[]{:S(2)}) async-start(bf16[4,128,1024]{2,1,0:T(8,128)(2,1)} %bitcast.186), calls=%async_computation.8 | async-start | bytes 2097152 | tf_op jit(solution)/shard_map/all_to_all | solution.py:861
  958.5 12.8 %collective-permute-start.8 = (f32[2,128]{1,0:T(2,128)S(1)}, f32[2,128]{1,0:T(2,128)S(1)}, u32[]{:S(2)}, u32[]{:S(2)}) collective-permute-start(f32[2,128]{1,0:T(2,128)S(1)} %pad_maximum_fusion.4), channel_id=1, source_target_pairs={{0,1},{1,0},{2,3},{3,2},{4,5},{5,4},{6,7},{7,6},{8,9},{9,8},{10,11... | collective-permute-start | bytes 3080 | tf_op jit(solution)/shard_map/ppermute | solution.py:700
  (41 other events, 579.5 us)
Sparse Core Ops, SparseCore 0:
  33.4 63.2 all-gather.6
  127.9 81.1 all-gather.10
  210.6 79.3 all-gather.8
  291.4 79.2 all-gather.4
  659.3 52.5 reduce-scatter.4
  714.0 76.4 reduce-scatter.8
  792.8 77.2 reduce-scatter.6
  872.4 77.2 reduce-scatter.10

commit v3 on v2

--- a/solution.py
+++ b/solution.py
@@ -91,8 +91,28 @@
     return jnp.where(seen, scores, masked_score)
 
 
+def turned_over(target, source):
+    for first in range(0, source.shape[0], TILE):
+        block = source[first : first + TILE, :128].astype(jnp.float32)
+        target[:, first : first + TILE] = jnp.transpose(block)[:HEAD].astype(jnp.bfloat16)
+
+
+def head_pairs(width, work):
+    together = min(PAIR, width // HEAD)
+
+    def step(i, carry):
+        work([i * together + j for j in range(together)])
+        return carry
+
+    lax.fori_loop(0, width // HEAD // together, step, 0)
+
+
+PAIR = 2
+
+
 def attention_forward_kernel(
-    to_ref, start_ref, raw_ref, cos_ref, sin_ref, out_ref, q_ref, k_ref, v_ref, log_ref, held
+    to_ref, start_ref, raw_ref, cos_ref, sin_ref, out_ref, q_ref, k_ref, v_ref, log_ref,
+    held, values_ref, tile_ref,
 ):
     width = q_ref.shape[1]
     pieces = to_ref.shape[0]
@@ -123,11 +143,12 @@
         return carry
 
     lax.fori_loop(0, pieces, place, 0)
+    turned_over(values_ref, v_ref)
 
     def work(row, parts, one_segment):
         rows = pl.ds(row, TILE)
 
-        def one_head(head, carry):
+        def one_head(head):
             query = only_head(q_ref[rows, :], head)
             scores = [
                 visible_scores(k_ref[pl.ds(first, count), :], query, own, one_segment)
@@ -140,22 +161,22 @@
             total = functools.reduce(
                 jnp.add, [jnp.sum(e, axis=0, keepdims=True) for e in exponent]
             )
-            inverse = 1.0 / total
             result = functools.reduce(
                 jnp.add,
                 [
-                    dot((e * inverse).astype(jnp.bfloat16), v_ref[pl.ds(first, count), :], FIRST)
+                    dot(values_ref[:, pl.ds(first, count)], e.astype(jnp.bfloat16))
                     for e, (first, count, own) in zip(exponent, parts)
                 ],
             )
             log_ref[head, :, rows] = largest + jnp.log(total)
-            before = held[rows, :]
-            held[rows, :] = jnp.where(
-                lanes(before) // HEAD == head, result.astype(jnp.bfloat16), before
-            )
-            return carry
-
-        lax.fori_loop(0, width // HEAD, one_head, 0)
+            tile_ref[pl.ds(pl.multiple_of(head * HEAD, HEAD), HEAD), :] = result * (1.0 / total)
+
+        def heads(together):
+            for head in together:
+                one_head(head)
+
+        head_pairs(width, heads)
+        held[rows, :] = jnp.transpose(tile_ref[...]).astype(jnp.bfloat16)
 
     query_tiles(work)
 
@@ -178,12 +199,9 @@
     log_ref,
     cos_ref,
     sin_ref,
-    out_ref,
-    og_ref,
-    dq_ref,
-    dk_ref,
-    dv_ref,
+    *rest,
 ):
+    out_ref, og_ref, dq_ref, dk_ref, dv_ref, keys_ref, tile_ref = rest[-7:]
     width = q_ref.shape[1]
     pieces = to_ref.shape[0]
     piece = grad_ref.shape[0] // pieces
@@ -195,38 +213,54 @@
         return carry
 
     lax.fori_loop(0, pieces, place, 0)
+    turned_over(keys_ref, k_ref)
     dk_ref[...] = jnp.zeros_like(dk_ref)
     dv_ref[...] = jnp.zeros_like(dv_ref)
 
     def work(row, parts, one_segment):
         rows = pl.ds(row, TILE)
-        dq_ref[rows, :] = jnp.zeros((TILE, width), jnp.float32)
-
-        def one_head(head, carry):
-            query = only_head(q_ref[rows, :], head)
-            out_grad = only_head(og_ref[rows, :], head)
-            log_total = log_ref[head, :, rows]
-            weights, products = [], []
-            for first, count, own in parts:
+
+        def heads(together):
+            queries, out_grads, all_weights, all_grads = [], [], [], []
+            for head in together:
+                query = only_head(q_ref[rows, :], head)
+                out_grad = only_head(og_ref[rows, :], head)
+                log_total = log_ref[head, :, rows]
+                weights, products = [], []
+                for first, count, own in parts:
+                    keys = pl.ds(first, count)
+                    scores = visible_scores(k_ref[keys, :], query, own, one_segment)
+                    weights.append(jnp.exp(scores - log_total))
+                    products.append(dot(v_ref[keys, :], out_grad, LAST))
+                inner = functools.reduce(
+                    jnp.add,
+                    [jnp.sum(w * d, axis=0, keepdims=True) for w, d in zip(weights, products)],
+                )
+                grads = [
+                    (w * (d - inner)).astype(jnp.bfloat16) for w, d in zip(weights, products)
+                ]
+                queries.append(query)
+                out_grads.append(out_grad)
+                all_weights.append([w.astype(jnp.bfloat16) for w in weights])
+                all_grads.append(grads)
+                tile_ref[pl.ds(pl.multiple_of(head * HEAD, HEAD), HEAD), :] = functools.reduce(
+                    jnp.add,
+                    [
+                        dot(keys_ref[:, pl.ds(first, count)], g)
+                        for (first, count, own), g in zip(parts, grads)
+                    ],
+                )
+            query = jnp.concatenate(queries, axis=0)
+            out_grad = jnp.concatenate(out_grads, axis=0)
+            for i, (first, count, own) in enumerate(parts):
                 keys = pl.ds(first, count)
-                scores = visible_scores(k_ref[keys, :], query, own, one_segment)
-                weights.append(jnp.exp(scores - log_total))
-                products.append(dot(v_ref[keys, :], out_grad, LAST))
-            inner = functools.reduce(
-                jnp.add,
-                [jnp.sum(w * d, axis=0, keepdims=True) for w, d in zip(weights, products)],
-            )
-            query_grad = jnp.zeros((TILE, width), jnp.float32)
-            for (first, count, own), w, d in zip(parts, weights, products):
-                keys = pl.ds(first, count)
-                score_grad = (w * (d - inner)).astype(jnp.bfloat16)
-                dv_ref[keys, :] += dot(w.astype(jnp.bfloat16), out_grad)
-                dk_ref[keys, :] += dot(score_grad, query)
-                query_grad += dot(score_grad, k_ref[keys, :], FIRST)
-            dq_ref[rows, :] += only_head(query_grad, head)
-            return carry
-
-        lax.fori_loop(0, width // HEAD, one_head, 0)
+                weights = jnp.concatenate([w[i] for w in all_weights], axis=1)
+                grads = jnp.concatenate([g[i] for g in all_grads], axis=1)
+                dv_ref[keys, :] += dot(weights, out_grad)
+                dk_ref[keys, :] += dot(grads, query)
+
+        head_pairs(width, heads)
+        dq_ref[rows, :] = jnp.transpose(tile_ref[...])
 
     query_tiles(work)
 
@@ -279,30 +313,36 @@
         out_shape=[kept] * 4 + [jax.ShapeDtypeStruct((width // HEAD, 1, rows), jnp.float32)],
         in_specs=[SMEM, SMEM, VMEM, VMEM, VMEM],
         out_specs=[VMEM] * 5,
-        scratch_shapes=[pltpu.VMEM((rows, width), jnp.bfloat16)],
+        scratch_shapes=[
+            pltpu.VMEM((rows, width), jnp.bfloat16),
+            pltpu.VMEM((HEAD, rows), jnp.bfloat16),
+            pltpu.VMEM((width, TILE), jnp.float32),
+        ],
         compiler_params=pltpu.CompilerParams(vmem_limit_bytes=VMEM_LIMIT),
         cost_estimate=attention_cost(width, 4),
         name="attention_forward",
     )(places, starts, raw, *tables)
 
 
-def attention_backward(places, starts, out_grad, kept, tables):
+def attention_backward(places, starts, out_grad, kept, tables, early):
     rows, width = out_grad.shape
     return pl.pallas_call(
         attention_backward_kernel,
         out_shape=jax.ShapeDtypeStruct((rows, width + 2 * HEAD), jnp.bfloat16),
-        in_specs=[SMEM, SMEM] + [VMEM] * 7,
+        in_specs=[SMEM, SMEM] + [VMEM] * 7 + [ANY] * len(early),
         out_specs=VMEM,
         scratch_shapes=[
             pltpu.VMEM((rows, width), jnp.bfloat16),
             pltpu.VMEM((rows, width), jnp.float32),
             pltpu.VMEM((rows, width), jnp.float32),
             pltpu.VMEM((rows, width), jnp.float32),
+            pltpu.VMEM((HEAD, rows), jnp.bfloat16),
+            pltpu.VMEM((width, TILE), jnp.float32),
         ],
         compiler_params=pltpu.CompilerParams(vmem_limit_bytes=VMEM_LIMIT),
         cost_estimate=attention_cost(width, 10),
         name="attention_backward",
-    )(places, starts, out_grad, *kept, *tables)
+    )(places, starts, out_grad, *kept, *tables, *early)
 
 
 MESH = pl.DeviceIdType.MESH
@@ -503,21 +543,34 @@
 
 
 def start_kernel(
-    block, gate, up, down, out, gate_out, up_out, down_out, sent, landed, local
+    block, gate, up, down, cotangent, out, gate_out, up_out, down_out, scaled, sent, landed, local
 ):
     p = Plane(sent, landed, diagonal=True)
     gather = Gather(p, block, out)
+    columns = gate_out.shape[2]
+
+    def part(weight, rank):
+        return weight.at[:, pl.ds(pl.multiple_of(rank * columns, 128), columns)]
+
     mine = [pltpu.make_async_copy(block, out.at[p.rank, p.core], local.at[0])]
     for k in range(CHUNKS):
         gather.start(k)
     moves = []
     for i, (source, target) in enumerate(((gate, gate_out), (up, up_out), (down, down_out))):
-        mine.append(pltpu.make_async_copy(source.at[p.rank], target.at[p.rank], local.at[i + 1]))
+        mine.append(
+            pltpu.make_async_copy(part(source, p.rank), target.at[p.rank], local.at[i + 1])
+        )
         for partner, rank in ((p.x, p.at_x), (p.y, p.at_y), (p.both, p.at_both)):
-            number = p.send(source.at[rank], target.at[p.rank], partner)
+            number = p.send(part(source, rank), target.at[p.rank], partner)
             moves.append((number, target.at[rank]))
     for started in mine:
         started.start()
+
+    def scale(rows):
+        value = residual_scale * cotangent[rows, :].astype(jnp.float32)
+        scaled[rows, :] = value.astype(jnp.bfloat16)
+
+    slabs(0, scaled.shape[0], scale)
     gather.forward()
     gather.finish()
     for number, target in moves:
@@ -527,28 +580,63 @@
         started.wait()
 
 
-def start_plane(block, gate, up, down):
+def start_plane(block, gate, up, down, cotangent):
     share, width = block.shape
+    depth, units = gate.shape
     full = jax.ShapeDtypeStruct((4, 2, share, width), block.dtype)
-    weight = jax.ShapeDtypeStruct(gate.shape, gate.dtype)
-    full, *weights = pl.pallas_call(
+    weight = jax.ShapeDtypeStruct((4, depth, units // 4), gate.dtype)
+    full, *rest = pl.pallas_call(
         start_kernel,
-        out_shape=[full, weight, weight, weight],
-        in_specs=[ANY] * 4,
-        out_specs=[ANY] * 4,
+        out_shape=[full, weight, weight, weight, jax.ShapeDtypeStruct(cotangent.shape, jnp.bfloat16)],
+        in_specs=[VMEM, ANY, ANY, ANY, VMEM],
+        out_specs=[ANY] * 4 + [VMEM],
         scratch_shapes=wires(GATHER_COPIES + 9) + [pltpu.SemaphoreType.DMA((4,))],
-        compiler_params=pltpu.CompilerParams(collective_id=1, has_side_effects=True),
+        compiler_params=pltpu.CompilerParams(
+            collective_id=1, has_side_effects=True, vmem_limit_bytes=VMEM_LIMIT
+        ),
         cost_estimate=lasting(80),
         name="gather_tokens",
-    )(block, gate, up, down)
-    return full.reshape(8 * share, width), weights
+    )(block, gate, up, down, cotangent)
+    return full.reshape(8 * share, width), rest[:3], rest[3]
 
 
 def middle_kernel(
-    partial, residual, gain, out, middle, sent, landed, own_copy, hidden, *scratch
+    partial,
+    residual,
+    gain,
+    beside,
+    from_x,
+    from_y,
+    from_both,
+    out,
+    middle,
+    beside_out,
+    sent,
+    landed,
+    local,
+    hidden,
+    held_beside,
+    held_blocks,
+    *scratch,
 ):
     p = Plane(sent, landed)
+    blocks = ((from_x, p.at_x), (from_y, p.at_y), (from_both, p.at_both))
+    loads = [pltpu.make_async_copy(beside, held_beside, local.at[0])]
+    for i, (block, rank) in enumerate(blocks):
+        loads.append(pltpu.make_async_copy(block, held_blocks.at[i], local.at[i + 1]))
+    for started in loads:
+        started.start()
     total = Scatter(p, partial, *scratch)
+    kept, across = [], []
+    loads[0].wait()
+    kept.append(pltpu.make_async_copy(held_beside, beside_out.at[p.rank], local.at[0]))
+    kept[0].start()
+    for i, (block, rank) in enumerate(blocks):
+        loads[i + 1].wait()
+        place = beside_out.at[rank, p.core]
+        kept.append(pltpu.make_async_copy(held_blocks.at[i], place, local.at[i + 1]))
+        kept[i + 1].start()
+        across.append(p.send(held_blocks.at[i], place, p.sibling))
     share = hidden.shape[0]
     gather = Gather(p, hidden, out)
 
@@ -560,41 +648,73 @@
     for k in range(CHUNKS):
         slabs(k * (share // CHUNKS), share // CHUNKS, work)
         gather.start(k)
-    mine = pltpu.make_async_copy(hidden, out.at[p.rank, p.core], own_copy)
-    mine.start()
+    kept.append(pltpu.make_async_copy(hidden, out.at[p.rank, p.core], local.at[4]))
+    kept[4].start()
     gather.forward()
     gather.finish()
+    for number, rank in zip(across, (p.at_x, p.at_y, p.at_both)):
+        p.arrive(number, beside_out.at[rank, 1 - p.core])
     p.finish()
-    mine.wait()
-
-
-def middle_plane(partial, residual, gain):
+    for started in kept:
+        started.wait()
+
+
+def middle_plane(partial, residual, gain, beside, blocks):
     share, width = residual.shape
     full = jax.ShapeDtypeStruct((4, 2, share, width), jnp.bfloat16)
-    out, middle = pl.pallas_call(
+    out, middle, beside_out = pl.pallas_call(
         middle_kernel,
-        out_shape=[full, jax.ShapeDtypeStruct((share, width), jnp.float32)],
-        in_specs=[ANY, VMEM, VMEM],
-        out_specs=[ANY, VMEM],
-        scratch_shapes=wires(GATHER_COPIES + SCATTER_COPIES)
-        + [pltpu.SemaphoreType.DMA, pltpu.VMEM((share, width), jnp.bfloat16)]
+        out_shape=[full, jax.ShapeDtypeStruct((share, width), jnp.float32), full],
+        in_specs=[ANY, VMEM, VMEM] + [ANY] * 4,
+        out_specs=[ANY, VMEM, ANY],
+        scratch_shapes=wires(GATHER_COPIES + SCATTER_COPIES + 3)
+        + [
+            pltpu.SemaphoreType.DMA((5,)),
+            pltpu.VMEM((share, width), jnp.bfloat16),
+            pltpu.VMEM((2, share, width), jnp.bfloat16),
+            pltpu.VMEM((3, share, width), jnp.bfloat16),
+        ]
         + scatter_scratch(share, width),
         compiler_params=pltpu.CompilerParams(
             collective_id=2, has_side_effects=True, vmem_limit_bytes=VMEM_LIMIT
         ),
         cost_estimate=lasting(100),
         name="middle_rows",
-    )(partial.reshape(full.shape), residual, gain)
-    return out.reshape(8 * share, width), middle
+    )(partial.reshape(full.shape), residual, gain, beside.reshape(2, share, width), *blocks)
+    return out.reshape(8 * share, width), middle, beside_out.reshape(8 * share, width)
 
 
 def second_kernel(
-    partial, middle, cotangent, gain, out, grad_middle, sent, landed, own_copy, hidden, *scratch
+    partial,
+    other_partial,
+    middle,
+    cotangent,
+    gain,
+    early_first,
+    early_second,
+    out,
+    grad_middle,
+    pairs,
+    sent,
+    landed,
+    local,
+    hidden,
+    held,
+    theirs,
+    *scratch,
 ):
     p = Plane(sent, landed)
     total = Scatter(p, partial, *scratch)
     share = hidden.shape[0]
     gather = Gather(p, hidden, out)
+    order = (p.rank, p.at_x, p.at_y, p.at_both)
+    kept, across = [], []
+    for i, rank in enumerate(order):
+        across.append(p.send(other_partial.at[rank, 1 - p.core], theirs.at[i], p.sibling))
+        kept.append(
+            pltpu.make_async_copy(other_partial.at[rank, p.core], held.at[i], local.at[i])
+        )
+        kept[i].start()
 
     def work(rows):
         value = middle[rows, :]
@@ -609,43 +729,88 @@
     for k in range(CHUNKS):
         slabs(k * (share // CHUNKS), share // CHUNKS, work)
         gather.start(k)
-    mine = pltpu.make_async_copy(hidden, out.at[p.rank, p.core], own_copy)
+    mine = pltpu.make_async_copy(hidden, out.at[p.rank, p.core], local.at[4])
     mine.start()
+    for i in range(4):
+        p.arrive(across[i], theirs.at[i])
+        kept[i].wait()
+        add_rows(held.at[i], theirs.at[i], 0, share)
+    whole = pltpu.make_async_copy(held, pairs, local.at[5])
+    whole.start()
     gather.forward()
     gather.finish()
     p.finish()
     mine.wait()
-
-
-def second_plane(partial, middle, cotangent, gain):
+    whole.wait()
+
+
+def second_plane(partial, other_partial, middle, cotangent, gain, early):
     share, width = middle.shape
     full = jax.ShapeDtypeStruct((4, 2, share, width), jnp.bfloat16)
-    out, grad_middle = pl.pallas_call(
+    quarter = jax.ShapeDtypeStruct((4, share, width), jnp.bfloat16)
+    out, grad_middle, pairs = pl.pallas_call(
         second_kernel,
-        out_shape=[full, jax.ShapeDtypeStruct((share, width), jnp.float32)],
-        in_specs=[ANY, VMEM, VMEM, VMEM],
-        out_specs=[ANY, VMEM],
-        scratch_shapes=wires(GATHER_COPIES + SCATTER_COPIES)
-        + [pltpu.SemaphoreType.DMA, pltpu.VMEM((share, width), jnp.bfloat16)]
+        out_shape=[full, jax.ShapeDtypeStruct((share, width), jnp.float32), quarter],
+        in_specs=[ANY, ANY, VMEM, VMEM, VMEM, ANY, ANY],
+        out_specs=[ANY, VMEM, ANY],
+        scratch_shapes=wires(GATHER_COPIES + SCATTER_COPIES + 4)
+        + [
+            pltpu.SemaphoreType.DMA((6,)),
+            pltpu.VMEM((share, width), jnp.bfloat16),
+            pltpu.VMEM(quarter.shape, jnp.bfloat16),
+            pltpu.VMEM(quarter.shape, jnp.bfloat16),
+        ]
         + scatter_scratch(share, width),
         compiler_params=pltpu.CompilerParams(
             collective_id=3, has_side_effects=True, vmem_limit_bytes=VMEM_LIMIT
         ),
         cost_estimate=lasting(100),
         name="second_rows",
-    )(partial.reshape(full.shape), middle, cotangent, gain)
-    return out.reshape(8 * share, width), grad_middle
+    )(
+        partial.reshape(full.shape),
+        other_partial.reshape(full.shape),
+        middle,
+        cotangent,
+        gain,
+        *early,
+    )
+    return out.reshape(8 * share, width), grad_middle, pairs
 
 
 def last_kernel(
-    partial, residual, grad_middle, gain, result, out, result_out, sent, landed, local_copy, held, *scratch
+    partial,
+    residual,
+    grad_middle,
+    gain,
+    middle,
+    ffn_own,
+    ffn_x,
+    ffn_y,
+    ffn_both,
+    out,
+    result_out,
+    done,
+    sent,
+    landed,
+    local,
+    held,
+    result,
+    *scratch,
 ):
     p = Plane(sent, landed)
-    kept = [pltpu.make_async_copy(result, result_out.at[p.core], local_copy.at[0])]
+    done[...] = jnp.zeros_like(done)
+    total = Scatter(p, partial, *scratch)
+    share = held.shape[0]
+
+    def finish_result(rows):
+        parts = (ffn_own, ffn_x, ffn_y, ffn_both)
+        ffn = sum(part[rows, :].astype(jnp.float32) for part in parts)
+        result[rows, :] = (middle[rows, :] + residual_scale * ffn).astype(jnp.bfloat16)
+
+    slabs(0, share, finish_result)
+    kept = [pltpu.make_async_copy(result, result_out.at[p.core], local.at[0])]
     kept[0].start()
     given = p.send(result, result_out.at[p.core], p.sibling)
-    total = Scatter(p, partial, *scratch)
-    share = held.shape[0]
 
     def work(rows):
         value = residual[rows, :].astype(jnp.float32)
@@ -660,7 +825,7 @@
         cut = chunk(k, share)
         slabs(k * (share // CHUNKS), share // CHUNKS, work)
         across.append(p.send(held.at[cut], out.at[p.core, cut], p.sibling))
-    kept.append(pltpu.make_async_copy(held, out.at[p.core], local_copy.at[1]))
+    kept.append(pltpu.make_async_copy(held, out.at[p.core], local.at[1]))
     kept[1].start()
     p.arrive(given, result_out.at[1 - p.core])
     for k in range(CHUNKS):
@@ -670,26 +835,56 @@
         started.wait()
 
 
-def last_plane(partial, residual, grad_middle, gain, result):
+def last_plane(partial, residual, grad_middle, gain, middle, ffn_parts):
     share, width = residual.shape
-    out, result_out = pl.pallas_call(
+    out, result_out, done = pl.pallas_call(
         last_kernel,
         out_shape=[
             jax.ShapeDtypeStruct((2, share, width), jnp.float32),
             jax.ShapeDtypeStruct((2, share, width), jnp.bfloat16),
+            jax.ShapeDtypeStruct((8, 128), jnp.float32),
         ],
-        in_specs=[ANY, VMEM, VMEM, VMEM, ANY],
-        out_specs=[ANY, ANY],
+        in_specs=[ANY] + [VMEM] * 8,
+        out_specs=[ANY, ANY, VMEM],
         scratch_shapes=wires(CHUNKS + 1 + SCATTER_COPIES)
-        + [pltpu.SemaphoreType.DMA((2,)), pltpu.VMEM((share, width), jnp.float32)]
+        + [
+            pltpu.SemaphoreType.DMA((2,)),
+            pltpu.VMEM((share, width), jnp.float32),
+            pltpu.VMEM((share, width), jnp.bfloat16),
+        ]
         + scatter_scratch(share, width),
         compiler_params=pltpu.CompilerParams(
             collective_id=4, has_side_effects=True, vmem_limit_bytes=VMEM_LIMIT
         ),
         cost_estimate=lasting(70),
         name="last_rows",
-    )(partial.reshape(4, 2, share, width), residual, grad_middle, gain, result)
-    return out.reshape(2 * share, width), result_out.reshape(2 * share, width)
+    )(partial.reshape(4, 2, share, width), residual, grad_middle, gain, middle, *ffn_parts)
+    return out.reshape(2 * share, width), result_out.reshape(2 * share, width), done
+
+
+def exchange_kernel(blocks, *rest):
+    out, sent, landed = rest[-3:]
+    p = Plane(sent, landed, diagonal=True)
+    moves = []
+    for partner, rank in ((p.both, p.at_both), (p.x, p.at_x), (p.y, p.at_y)):
+        moves.append((p.send(blocks.at[rank], out.at[p.rank], partner), out.at[rank]))
+    out[p.rank] = blocks[p.rank]
+    for number, target in moves:
+        p.arrive(number, target)
+    p.finish()
+
+
+def exchange(blocks, early):
+    return pl.pallas_call(
+        exchange_kernel,
+        out_shape=jax.ShapeDtypeStruct(blocks.shape, blocks.dtype),
+        in_specs=[VMEM] + [ANY] * len(early),
+        out_specs=VMEM,
+        scratch_shapes=wires(3),
+        compiler_params=pltpu.CompilerParams(collective_id=5, has_side_effects=True),
+        cost_estimate=lasting(8),
+        name="exchange_blocks",
+    )(blocks, *early)
 
 
 def context_pairs(step):
@@ -700,30 +895,123 @@
     return lax.ppermute(values, "tensor", [(0, 1), (1, 0)])
 
 
-def gather_beside(block):
-    rank, core = lax.axis_index("context"), lax.axis_index("tensor")
-    share, width = block.shape
-    mine = jnp.zeros((4, share, width), block.dtype)
-    for step in range(4):
-        got = lax.ppermute(block, "context", context_pairs(step)) if step else block
-        mine = lax.dynamic_update_slice(mine, got[None], (rank ^ step, 0, 0))
-    theirs = swap_cores(mine)
-    first = jnp.where(core == 0, mine, theirs)
-    second = jnp.where(core == 0, theirs, mine)
-    return jnp.stack([first, second], axis=1).reshape(8 * share, width)
-
-
-def scatter_beside(partial, share):
-    rank, core = lax.axis_index("context"), lax.axis_index("tensor")
-    blocks = partial.reshape(4, 2, share, -1)
-    keep = lax.dynamic_index_in_dim(blocks, core, 1, False)
-    give = lax.dynamic_index_in_dim(blocks, 1 - core, 1, False)
-    both = (keep.astype(jnp.float32) + swap_cores(give).astype(jnp.float32)).astype(jnp.bfloat16)
-    total = lax.dynamic_index_in_dim(both, rank, 0, False).astype(jnp.float32)
-    for step in range(1, 4):
-        block = lax.dynamic_index_in_dim(both, rank ^ step, 0, False)
-        total += lax.ppermute(block, "context", context_pairs(step)).astype(jnp.float32)
-    return total
+def ffn_first_kernel(hidden, gate_w, up_w, m, gate, up):
+    for j in range(gate_w.shape[1] // 256):
+        cut = slice(j * 256, j * 256 + 256)
+        gate_part = dot(hidden[...], gate_w[:, cut])
+        up_part = dot(hidden[...], up_w[:, cut])
+        gate[:, cut] = gate_part.astype(jnp.bfloat16)
+        up[:, cut] = up_part.astype(jnp.bfloat16)
+        sigmoid = 1.0 / (1.0 + jnp.exp(-gate_part))
+        m[:, cut] = (gate_part * sigmoid * up_part).astype(jnp.bfloat16)
+
+
+def ffn_second_kernel(grad, gate, up, m, gate_w, up_w, down_w, early, slopes, forward, back):
+    units = gate_w.shape[1]
+    for j in range(units // 256):
+        cut = slice(j * 256, j * 256 + 256)
+        grad_part = dot(grad[...], down_w[:, cut])
+        gate_part = gate[:, cut].astype(jnp.float32)
+        up_part = up[:, cut].astype(jnp.float32)
+        sigmoid = 1.0 / (1.0 + jnp.exp(-gate_part))
+        slope = sigmoid * (1.0 + gate_part * (1.0 - sigmoid))
+        slopes[:, cut] = (grad_part * up_part * slope).astype(jnp.bfloat16)
+        slopes[:, units + j * 256 : units + j * 256 + 256] = (
+            grad_part * gate_part * sigmoid
+        ).astype(jnp.bfloat16)
+    for j in range(gate_w.shape[0] // 512):
+        cut = slice(j * 512, j * 512 + 512)
+        forward[:, cut] = dot(m[...], down_w[cut, :], LAST).astype(jnp.bfloat16)
+        back[:, cut] = (
+            dot(slopes[:, :units], gate_w[cut, :], LAST)
+            + dot(slopes[:, units:], up_w[cut, :], LAST)
+        ).astype(jnp.bfloat16)
+
+
+def first_rows_kernel(values, gain, weight, hidden, raw):
+    value = values[...].astype(jnp.float32)
+    normed = (value * row_root(value) * gain[...]).astype(jnp.bfloat16)
+    hidden[...] = normed
+    raw[...] = dot(normed, weight[...])
+
+
+def first_rows(values, gain, weight):
+    count, width = values.shape
+    columns = weight.shape[1]
+    return pl.pallas_call(
+        first_rows_kernel,
+        grid=(count // ROW_TILE,),
+        in_specs=[
+            pl.BlockSpec((ROW_TILE, width), lambda i: (i, 0)),
+            pl.BlockSpec((1, width), lambda i: (0, 0)),
+            pl.BlockSpec((width, columns), lambda i: (0, 0)),
+        ],
+        out_specs=[
+            pl.BlockSpec((ROW_TILE, width), lambda i: (i, 0)),
+            pl.BlockSpec((ROW_TILE, columns), lambda i: (i, 0)),
+        ],
+        out_shape=[
+            jax.ShapeDtypeStruct((count, width), jnp.bfloat16),
+            jax.ShapeDtypeStruct((count, columns), jnp.float32),
+        ],
+        compiler_params=pltpu.CompilerParams(vmem_limit_bytes=VMEM_LIMIT),
+        cost_estimate=lasting(12),
+        name="first_rows",
+    )(values, gain, weight)
+
+
+def attention_weights_kernel(hidden, back, grad, attended, *early_and_out):
+    out = early_and_out[-1]
+    columns = back.shape[1]
+    out[:, :columns] = dot(hidden[...], back[...], FIRST).astype(jnp.bfloat16)
+    out[:, columns:] = dot(grad[...], attended[...], FIRST).astype(jnp.bfloat16)
+
+
+def attention_weights(hidden, back, grad, attended, early):
+    count, width = hidden.shape
+    first, second = back.shape[1], attended.shape[1]
+    tall = pl.BlockSpec((count, 512), lambda i: (0, i))
+    return pl.pallas_call(
+        attention_weights_kernel,
+        grid=(width // 512,),
+        in_specs=[
+            tall,
+            pl.BlockSpec((count, first), lambda i: (0, 0)),
+            tall,
+            pl.BlockSpec((count, second), lambda i: (0, 0)),
+        ]
+        + [ANY] * len(early),
+        out_specs=pl.BlockSpec((512, first + second), lambda i: (i, 0)),
+        out_shape=jax.ShapeDtypeStruct((width, first + second), jnp.bfloat16),
+        compiler_params=pltpu.CompilerParams(vmem_limit_bytes=VMEM_LIMIT),
+        cost_estimate=lasting(12),
+        name="attention_weights",
+    )(hidden, back, grad, attended, *early)
+
+
+ROW_TILE = 256
+
+
+def row_tiles(kernel, name, rows, weights, extra, widths):
+    count = rows[0].shape[0]
+
+    def tile(width):
+        return pl.BlockSpec((ROW_TILE, width), lambda i: (i, 0))
+
+    whole = [
+        pl.BlockSpec(w.shape, lambda i: (0, 0), pipeline_mode=pl.Buffered(1)) for w in weights
+    ]
+    flops = 2 * count * sum(w.size for w in weights)
+    return pl.pallas_call(
+        kernel,
+        grid=(count // ROW_TILE,),
+        in_specs=[tile(r.shape[1]) for r in rows] + whole + [ANY] * len(extra),
+        out_specs=[tile(width) for width in widths],
+        out_shape=[jax.ShapeDtypeStruct((count, width), jnp.bfloat16) for width in widths],
+        compiler_params=pltpu.CompilerParams(vmem_limit_bytes=56 * 1024 * 1024),
+        cost_estimate=pl.CostEstimate(flops=flops, bytes_accessed=flops // 400, transcendentals=0),
+        name=name,
+    )(*rows, *weights, *extra)
 
 
 def norm_backward(gradient, normed, inv_root):
@@ -798,13 +1086,17 @@
     gains_full = packed[:, 2 * width + 2 * HEAD :].astype(jnp.float32)
     attn_scale, ffn_scale = gains_full[:, 0], gains_full[:, 1]
     square = groups == 4 and cores == 2
-    ffn_blocks = blocks(w_gate), blocks(w_up), blocks(w_down.T)
     tokens_half, cotangent_half = my_rows(tokens), my_rows(cotangent)
     if square:
-        inputs_full, ffn_blocks = start_plane(tokens_half, *ffn_blocks)
+        inputs_full, ffn_blocks, ffn_grad = start_plane(
+            tokens_half, w_gate, w_up, w_down.T, cotangent
+        )
     else:
         inputs_full = gather_rows(tokens_half)
-        ffn_blocks = [lax.all_to_all(w, "context", 0, 0) for w in ffn_blocks]
+        ffn_grad = (residual_scale * cotangent.astype(jnp.float32)).astype(jnp.bfloat16)
+        ffn_blocks = [
+            lax.all_to_all(blocks(w), "context", 0, 0) for w in (w_gate, w_up, w_down.T)
+        ]
     gate_full, up_full, down_full = (
         lax.all_gather(w.reshape(groups * depth, -1), "fsdp", axis=0, tiled=True)
         for w in ffn_blocks
@@ -822,67 +1114,95 @@
     )
     tables = rope_tables()
 
-    inputs_full = inputs_full.astype(jnp.float32)
-    hidden_first = (inputs_full * inverse_root(inputs_full) * attn_scale).astype(jnp.bfloat16)
     residual_in = tokens_half.astype(jnp.float32)
     grad_result = cotangent_half.astype(jnp.float32)
-    ffn_grad = (residual_scale * grad_result).astype(jnp.bfloat16)
-    ffn_grad = gather_beside(ffn_grad) if square else gather_rows(ffn_grad)
-
-    raw = dot(hidden_first, qkv_full)
+    my_ffn_grad = my_rows(ffn_grad)
+
+    hidden_first, raw = first_rows(inputs_full, attn_scale[None, :], qkv_full)
     attended, *kept = attention_forward(places, starts, raw, tables)
     branch = dot(attended, out_full, LAST).astype(jnp.bfloat16)
     if square:
-        hidden_second, middle = middle_plane(branch, tokens_half, ffn_scale[None, :])
+        ffn_grad_blocks = [
+            lax.ppermute(my_ffn_grad, "context", context_pairs(step)) for step in (1, 2, 3)
+        ]
+        hidden_second, middle, ffn_grad = middle_plane(
+            branch, tokens_half, ffn_scale[None, :], ffn_grad, ffn_grad_blocks
+        )
     else:
+        ffn_grad = gather_rows(my_ffn_grad)
         middle = residual_in + residual_scale * scatter_rows(branch)
         hidden_second = gather_rows((middle * inverse_root(middle) * ffn_scale).astype(jnp.bfloat16))
 
-    gate_proj = dot(hidden_second, gate_full)
-    up_proj = dot(hidden_second, up_full)
-    sigmoid_gate = jax.nn.sigmoid(gate_proj)
-    silu_gate = gate_proj * sigmoid_gate
-    hidden = (silu_gate * up_proj).astype(jnp.bfloat16)
-    grad_hidden = dot(ffn_grad, down_full)
-    silu_slope = sigmoid_gate * (1.0 + gate_proj * (1.0 - sigmoid_gate))
-    grad_gate_proj = (grad_hidden * up_proj * silu_slope).astype(jnp.bfloat16)
-    grad_up_proj = (grad_hidden * silu_gate).astype(jnp.bfloat16)
-    grad_second = (
-        dot(grad_gate_proj, gate_full, LAST) + dot(grad_up_proj, up_full, LAST)
-    ).astype(jnp.bfloat16)
-    ffn_out = dot(hidden, down_full, LAST).astype(jnp.bfloat16)
-    ffn_out = scatter_beside(ffn_out, share) if square else scatter_rows(ffn_out)
-    result = (middle + residual_scale * ffn_out).astype(jnp.bfloat16)
-
-    def collect(gradient):
-        mine = lax.psum_scatter(
-            gradient.astype(jnp.bfloat16), "fsdp", scatter_dimension=0, tiled=True
-        )
-        return lax.all_to_all(mine.reshape(groups, depth, -1), "context", 0, 0)
+    units = gate_full.shape[1]
+    hidden, gate_proj, up_proj = row_tiles(
+        ffn_first_kernel,
+        "ffn_first",
+        [hidden_second],
+        [gate_full, up_full],
+        [],
+        [units, units, units],
+    )
+    grad_down = dot(ffn_grad, hidden, FIRST).astype(jnp.bfloat16)
+    slopes, ffn_out, grad_second = row_tiles(
+        ffn_second_kernel,
+        "ffn_second",
+        [ffn_grad, gate_proj, up_proj, hidden],
+        [gate_full, up_full, down_full],
+        [grad_down],
+        [2 * units, gate_full.shape[0], gate_full.shape[0]],
+    )
+    grad_gate_up = dot(hidden_second, slopes, FIRST).astype(jnp.bfloat16)
+
+    def sum_groups(gradient):
+        return lax.psum_scatter(gradient, "fsdp", scatter_dimension=0, tiled=True)
+
+    def hand_back(gradient):
+        return lax.all_to_all(gradient.reshape(groups, depth, -1), "context", 0, 0)
 
     def columns(gradient):
         return jnp.transpose(gradient, (1, 0, 2)).reshape(depth, -1).astype(jnp.float32)
 
-    grad_down = collect(dot(ffn_grad, hidden, FIRST))
-    grad_gate = collect(dot(hidden_second, grad_gate_proj, FIRST))
-    grad_up = collect(dot(hidden_second, grad_up_proj, FIRST))
-
     if square:
-        attn_grad, grad_middle = second_plane(
-            grad_second, middle, cotangent_half, ffn_scale[None, :]
+        attn_grad, grad_middle, ffn_pairs = second_plane(
+            grad_second,
+            ffn_out,
+            middle,
+            cotangent_half,
+            ffn_scale[None, :],
+            [grad_down, grad_gate_up],
         )
+        ffn_parts = [ffn_pairs[0]] + [
+            lax.ppermute(ffn_pairs[step], "context", context_pairs(step)) for step in (1, 2, 3)
+        ]
     else:
         root = inverse_root(middle)
         grad_middle = grad_result + norm_backward(
             scatter_rows(grad_second) * ffn_scale, middle * root, root
         )
         attn_grad = gather_rows((residual_scale * grad_middle).astype(jnp.bfloat16))
+        ffn_parts = []
     grad_attended = dot(attn_grad, out_full).astype(jnp.bfloat16)
-    back = attention_backward(places, starts, grad_attended, kept, tables)
+    grad_down = sum_groups(grad_down)
+    grad_gate_up = sum_groups(grad_gate_up)
+    back = attention_backward(places, starts, grad_attended, kept, tables, [grad_down])
+    grad_down = hand_back(grad_down)
+    grad_attn = attention_weights(
+        hidden_first, back, attn_grad, attended, [grad_gate_up, grad_down, *ffn_parts[1:]]
+    )
+    grad_attn = sum_groups(grad_attn)
+    grad_gate_up = hand_back(grad_gate_up)
     grad_first = dot(back, qkv_full, LAST).astype(jnp.bfloat16)
     if square:
-        grad_tokens, result = last_plane(
-            grad_first, tokens_half, grad_middle, attn_scale[None, :], result
+        grad_tokens, result, done = last_plane(
+            grad_first,
+            tokens_half,
+            grad_middle,
+            attn_scale[None, :],
+            middle,
+            ffn_parts,
+        )
+        grad_attn = exchange(
+            grad_attn.reshape(groups, depth, -1), [done, grad_gate_up]
         )
     else:
         root = inverse_root(residual_in)
@@ -890,10 +1210,9 @@
             scatter_rows(grad_first) * attn_scale, residual_in * root, root
         )
         grad_tokens = lax.all_gather(grad_tokens, "tensor", axis=0, tiled=True)
+        result = (middle + residual_scale * scatter_rows(ffn_out)).astype(jnp.bfloat16)
+        grad_attn = hand_back(grad_attn)
         result = lax.all_gather(result, "tensor", axis=0, tiled=True)
-    grad_attn = collect(
-        jnp.concatenate([dot(hidden_first, back, FIRST), dot(attn_grad, attended, FIRST)], axis=1)
-    )
     def kv_columns(gradient):
         gradient = gradient.astype(jnp.float32).reshape(kv_count, sharing, depth, HEAD)
         return jnp.transpose(jnp.sum(gradient, axis=1), (1, 0, 2)).reshape(depth, -1)
@@ -901,7 +1220,7 @@
     grad_query = columns(grad_attn[:, :, :width])
     grad_key = kv_columns(grad_attn[:, :, width : width + HEAD])
     grad_value = kv_columns(grad_attn[:, :, width + HEAD : width + 2 * HEAD])
-    grad_gate, grad_up = columns(grad_gate), columns(grad_up)
+    grad_gate, grad_up = columns(grad_gate_up[:, :, :units]), columns(grad_gate_up[:, :, units:])
 
     def against(*pairs):
         return sum(jnp.sum(weight.astype(jnp.float32) * g, axis=1) for weight, g in pairs)

time: 994 us -> 792 us (0.80)
  matrix products: 204 us -> 67 us
  waiting for transfers between devices: 157 us -> 29.1 us
  Pallas kernels: 446 us -> 559 us
  other arithmetic: 64.1 us -> 18.8 us
    dot_general x15 -> x5, matrix products: 204 us -> 67 us  [dot(): lax.dot_general(left_side, right_side, dims, preferred_element_type=jnp.f...]
    pallas_call x1 -> x6, Pallas kernels: 81.8 us -> 210 us  [the longest x1 85.2 us: start_plane(): pl.pallas_call(start_kernel, out_shape=[full, weight, weight, weight, jax...]
    reduce_scatter x4 -> x3, waiting for transfers between devices: 113 us -> 0.02 us  [sum_groups(): return lax.psum_scatter(gradient, 'fsdp', scatter_dimension=0, tiled=True)]
    ppermute x6, waiting for transfers between devices: 34.4 us -> 0.02 us  [the longest x3 0.01 us: local(): lax.ppermute(my_ffn_grad, 'context', context_pairs(step))]
    all_gather x3, waiting for transfers between devices: 0.01 us -> 26.5 us  [local(): lax.all_gather(w.reshape(groups * depth, -1), 'fsdp', axis=0, tiled=True)]
    another operation x2 -> x0, other arithmetic: 17.7 us -> none  [gather_beside(): return jnp.stack([first, second], axis=1).reshape(8 * share, width)]
    convert_element_type x4 -> x1, other arithmetic: 20.1 us -> 4.02 us  [columns(): jnp.transpose(gradient, (1, 0, 2)).reshape(depth, -1).astype(jnp.float32)]
    pallas_call x1, Pallas kernels: 50.7 us -> 37 us  [attention_forward(): pl.pallas_call(attention_forward_kernel, out_shape=[kept] * 4 + [jax.Shap...]
  transfers between devices with their start and end apart: 21 -> 16, of which waited for: 6 -> 2; matrix products, arithmetic and copies ran while one was open for 22% -> 15% of each run, Pallas kernels for 29% -> 68%
where the time goes in v3:
time: 792 us; the launch traced here: 786 us
  Pallas kernels  559 us (71%)
  matrix products  67 us (8%)
  local copies, waits for them, and re-layouts  65.1 us (8%)
  waiting for transfers between devices  29.1 us (4%)
  other arithmetic  18.8 us (2%)
  blocking collectives  16.4 us (2%)
  starting transfers between devices  15.5 us (2%)
  between operations  14.9 us (2%)
    pallas_call x1, Pallas kernels, second_plane(): pl.pallas_call(second_kernel, out_shape=[full, jax.ShapeDtypeStruct((shar...  99.7 us
    pallas_call x1, Pallas kernels, middle_plane(): pl.pallas_call(middle_kernel, out_shape=[full, jax.ShapeDtypeStruct((shar...  98.7 us
    pallas_call x1, Pallas kernels, start_plane(): pl.pallas_call(start_kernel, out_shape=[full, weight, weight, weight, jax...  85.2 us
    pallas_call x2, Pallas kernels, row_tiles(): pl.pallas_call(kernel, grid=(count // ROW_TILE,), in_specs=[tile(r.shape[...  85 us
    dot_general x5, matrix products, dot(): lax.dot_general(left_side, right_side, dims, preferred_element_type=jnp.f...  67 us
    pallas_call x1, Pallas kernels, last_plane(): pl.pallas_call(last_kernel, out_shape=[jax.ShapeDtypeStruct((2, share, wi...  60.5 us
    pallas_call x1, Pallas kernels, attention_backward(): pl.pallas_call(attention_backward_kernel, out_shape=jax.ShapeDtypeStruct(...  52.5 us
    pallas_call x1, Pallas kernels, attention_forward(): pl.pallas_call(attention_forward_kernel, out_shape=[kept] * 4 + [jax.Shap...  37 us
  transfers between devices with their start and end apart: 16, of which 2 were waited for; matrix products, arithmetic and copies ran while one was open for 15% of the time, Pallas kernels for 68%

profile of v3, /device:TPU:0, one launch (start us, length us, event | category | flops | bytes accessed | tf_op | source)
XLA Modules:
  0.0 785.5 jit_solution(9256646199952408290)
XLA Ops:
  17.2 16.4 %all_to_all.15 = bf16[4,128,768]{2,1,0:T(8,128)(2,1)} all-to-all(bf16[4,128,768]{2,1,0:T(8,128)(2,1)S(1)} %concatenate.9), channel_id=1, replica_groups=mesh['fsdp'=4,'context'=4,'tensor'=2] {'context'}, dimensions={0} | all-to-all | bytes 1572864 | tf_op jit(solution)/shard_map/all_to_all | solution.py:1072
  37.9 85.2 %gather_tokens.1 = (bf16[4,2,320,2048]{3,2,1,0:T(8,128)(2,1)}, bf16[4,128,1024]{2,1,0:T(8,128)(2,1)}, bf16[4,128,1024]{2,1,0:T(8,128)(2,1)}, bf16[4,128,1024]{2,1,0:T(8,128)(2,1)}, bf16[640,2048]{1,0:T(8,128)(2,1)}) custom-call(bf16[320,2048]{1,0:T(8,128)(2,1)} %constant_dynamic-slice_fusion.2.block.residual, bf16[128,4096]{1,0:T(8,128)(2,1)S(1)} %copy-done.8, ...), custom_call_target="tpu_custom_call" | custom-call | bytes 240000000 | tf_op jit(solution)/shard_map/gather_tokens/pallas_call | solution.py:588
  136.1 13.1 %first_rows.1 = (bf16[2560,2048]{1,0:T(8,128)(2,1)}, f32[2560,384]{1,0:T(8,128)S(1)}) custom-call(bf16[2560,2048]{1,0:T(8,128)(2,1)} %bitcast.111, f32[1,2048]{1,0:T(1,128)S(1)} %bitcast.100, bf16[2048,384]{1,0:T(8,128)(2,1)S(1)} %slice.70.weight), custom_call_target="tpu_custom_call" | custom-call | bytes 36000000 | tf_op jit(solution)/shard_map/first_rows/pallas_call | solution.py:941
  151.1 37.0 %attention_forward.1 = (bf16[2560,256]{1,0:T(8,128)(2,1)S(1)}, bf16[2560,256]{1,0:T(8,128)(2,1)S(1)}, bf16[2560,256]{1,0:T(8,128)(2,1)S(1)}, bf16[2560,256]{1,0:T(8,128)(2,1)}, f32[4,1,2560]{2,1,0:T(1,128)S(1)}) custom-call(s32[20]{0:T(128)S(1)} %compare_select_fusion.1.to_ref, s32[20]{0:T(128)S(1)} %bitcast.104, f32[2560,384]{1,0:T(8,128)} %copy-done.16, ...), custom_call_target="tpu_custom_call" | custom-call | flops 5368709120 | bytes 10485760 | tf_op jit(solution)/shard_map/attention_forward/pallas_call | solution.py:311
  188.2 5.6 convolution_convert_fusion.1
  193.8 98.7 %middle_rows.1 = (bf16[4,2,320,2048]{3,2,1,0:T(8,128)(2,1)}, f32[320,2048]{1,0:T(8,128)}, bf16[4,2,320,2048]{3,2,1,0:T(8,128)(2,1)}) custom-call(bf16[4,2,320,2048]{3,2,1,0:T(8,128)(2,1)} %bitcast.106, bf16[320,2048]{1,0:T(8,128)(2,1)S(1)} %copy-done.2, f32[1,2048]{1,0:T(1,128)S(1)} %bitcast.102, bf16[2,320,2048]{2,1,0:T(8,128)(2,1)} %bitcast.116, ...), custom_call_target="tpu_custom_call" | custom-call | bytes 300000000 | tf_op jit(solution)/shard_map/middle_rows/pallas_call | solution.py:665
  292.6 29.7 %ffn_first.1 = (bf16[2560,1024]{1,0:T(8,128)(2,1)}, bf16[2560,1024]{1,0:T(8,128)(2,1)}, bf16[2560,1024]{1,0:T(8,128)(2,1)}) custom-call(bf16[2560,2048]{1,0:T(8,128)(2,1)} %bitcast.135, bf16[2048,1024]{1,0:T(8,128)(2,1)} %all-gather.7.cloned.1.call-done.gate_w, bf16[2048,1024]{1,0:T(8,128)(2,1)} %all-gather.9.cloned.1.call-done.up_w), custom_call_target="tpu_custom_call" | custom-call | flops 21474836480 | bytes 53687092 | tf_op jit(solution)/shard_map/ffn_first/pallas_call | solution.py:1005
  322.3 17.2 %convolution_convert_fusion.4.early.early_first = bf16[2048,1024]{1,0:T(8,128)(2,1)} fusion(bf16[2560,2048]{1,0:T(8,128)(2,1)} %bitcast.137, bf16[2560,1024]{1,0:T(8,128)(2,1)} %get-tuple-element.48.m), kind=kOutput, calls=%fused_computation.4 | convolution fusion | flops 10739515392 | bytes 19922944 | tf_op jit(solution)/shard_map/dot_general | solution.py:31
  339.6 26.5 %all-gather.11.cloned.1.call-done.down_w = bf16[2048,1024]{1,0:T(8,128)(2,1)} async-done(((bf16[512,1024]{1,0:T(8,128)(2,1)}), bf16[2048,1024]{1,0:T(8,128)(2,1)}) %all-gather.11.cloned.1.call-update) | async-done | bytes 4194320 | tf_op jit(solution)/shard_map/all_gather | solution.py:1101
  366.1 55.3 %ffn_second.1 = (bf16[2560,2048]{1,0:T(8,128)(2,1)}, bf16[2560,2048]{1,0:T(8,128)(2,1)}, bf16[2560,2048]{1,0:T(8,128)(2,1)}) custom-call(bf16[2560,2048]{1,0:T(8,128)(2,1)} %bitcast.138, bf16[2560,1024]{1,0:T(8,128)(2,1)} %get-tuple-element.46.gate, bf16[2560,1024]{1,0:T(8,128)(2,1)} %get-tuple-element.47.up, bf16[2560,1024]{1,0:T(8,128)(2,1)} %get-tuple-element.48.m, ...), custom_call_target="tpu_custom_call" | custom-call | flops 32212254720 | bytes 80530640 | tf_op jit(solution)/shard_map/ffn_second/pallas_call | solution.py:1005
  421.4 28.9 %convolution_convert_fusion.2.early_second = bf16[2048,2048]{1,0:T(8,128)(2,1)} fusion(bf16[2560,2048]{1,0:T(8,128)(2,1)} %bitcast.136, bf16[2560,2048]{1,0:T(8,128)(2,1)} %get-tuple-element.53), kind=kOutput, calls=%fused_computation.2 | convolution fusion | flops 21479030784 | bytes 29360128 | tf_op jit(solution)/shard_map/dot_general | solution.py:31
  451.7 99.7 %second_rows.1 = (bf16[4,2,320,2048]{3,2,1,0:T(8,128)(2,1)}, f32[320,2048]{1,0:T(8,128)S(1)}, bf16[4,320,2048]{2,1,0:T(8,128)(2,1)}) custom-call(bf16[4,2,320,2048]{3,2,1,0:T(8,128)(2,1)} %bitcast.110, bf16[4,2,320,2048]{3,2,1,0:T(8,128)(2,1)} %bitcast.109, f32[320,2048]{1,0:T(8,128)} %get-tuple-element.52.middle, ...), custom_call_target="tpu_custom_call" | custom-call | bytes 300000000 | tf_op jit(solution)/shard_map/second_rows/pallas_call | solution.py:751
  551.4 6.3 slice_bitcast_fusion
  561.2 5.3 convolution_convert_fusion.3.grad_ref
  566.5 3.5 all-to-all-start.1
  575.1 52.5 %attention_backward.1.back = bf16[2560,384]{1,0:T(8,128)(2,1)} custom-call(s32[20]{0:T(128)S(1)} %compare_select_fusion.1.to_ref, s32[20]{0:T(128)S(1)} %bitcast.105, bf16[2560,256]{1,0:T(8,128)(2,1)S(1)} %copy-done.18, bf16[2560,256]{1,0:T(8,128)(2,1)S(1)} %copy-done.20, bf16[2560,256]{1,0:T(8,128)(2,1)} %copy-done.21, ...), custom_call_target="tpu_custom_call" | custom-call | flops 13421772800 | bytes 10485760 | tf_op jit(solution)/shard_map/attention_backward/pallas_call | solution.py:329
  630.7 13.9 %attention_weights.1 = bf16[2048,640]{1,0:T(8,128)(2,1)} custom-call(bf16[2560,2048]{1,0:T(8,128)(2,1)} %get-tuple-element.63.hidden, bf16[2560,384]{1,0:T(8,128)(2,1)} %attention_backward.1.back, bf16[2560,2048]{1,0:T(8,128)(2,1)} %bitcast.112, bf16[2560,256]{1,0:T(8,128)(2,1)S(1)} %copy-done.4, ...), custom_call_target="tpu_custom_call" | custom-call | bytes 36000000 | tf_op jit(solution)/shard_map/attention_weights/pallas_call | solution.py:974
  644.6 4.6 all-to-all-start.2
  653.9 10.1 %convolution_convert_fusion = bf16[2560,2048]{1,0:T(8,128)(2,1)} fusion(bf16[2560,384]{1,0:T(8,128)(2,1)} %attention_backward.1.back, bf16[2048,768]{1,0:T(8,128)(2,1)} %all-gather.5.cloned.1.call-done), kind=kOutput, calls=%fused_computation | convolution fusion | flops 4031774720 | bytes 14024704 | tf_op jit(solution)/shard_map/dot_general | solution.py:31
  664.0 60.5 %last_rows.1 = (f32[2,320,2048]{2,1,0:T(8,128)}, bf16[2,320,2048]{2,1,0:T(8,128)(2,1)}, f32[8,128]{1,0:T(8,128)S(1)}) custom-call(bf16[4,2,320,2048]{3,2,1,0:T(8,128)(2,1)} %bitcast.114, bf16[320,2048]{1,0:T(8,128)(2,1)S(1)} %copy-done.2, f32[320,2048]{1,0:T(8,128)} %copy-done.9, f32[1,2048]{1,0:T(1,128)S(1)} %bitcast.101, ...), custom_call_target="tpu_custom_call" | custom-call | bytes 210000000 | tf_op jit(solution)/shard_map/last_rows/pallas_call | solution.py:840
  725.1 4.0 convert_bitcast_fusion.1
  737.9 13.1 %exchange_blocks.1 = bf16[4,128,640]{2,1,0:T(8,128)(2,1)} custom-call(bf16[4,128,640]{2,1,0:T(8,128)(2,1)} %bitcast.128, f32[8,128]{1,0:T(8,128)} %copy-done.15, bf16[4,128,2048]{2,1,0:T(8,128)(2,1)} %all-to-all-done.2.rest_1_), custom_call_target="tpu_custom_call" | custom-call | bytes 24000000 | tf_op jit(solution)/shard_map/exchange_blocks/pallas_call | solution.py:878
  769.3 3.6 copy.87
  772.8 5.6 copy.88
  (157 shorter events, 74.3 us)
Async XLA Ops:
  7.2 28.7 %copy-start = (bf16[640,2048]{1,0:T(8,128)(2,1)S(1)}, bf16[640,2048]{1,0:T(8,128)(2,1)}, u32[]{:S(2)}) copy-start(bf16[640,2048]{1,0:T(8,128)(2,1)} %param.14) | copy-start | bytes 7864324
  7.2 126.4 %all-gather.5.cloned.1.call-start = ((), (), s32[]{:S(2)}) async-start(), calls=%async_computation.6 | async-start | bytes 3932160 | tf_op jit(solution)/shard_map/all_gather | solution.py:1074
  33.6 259.0 %all-gather.7.cloned.1.call-start = ((), (), s32[]{:S(2)}) async-start(), calls=%async_computation.7 | async-start | bytes 5242880 | tf_op jit(solution)/shard_map/all_gather | solution.py:1101
  123.2 169.4 %all-gather.9.cloned.1.call-start = ((), (), s32[]{:S(2)}) async-start(), calls=%async_computation.8 | async-start | bytes 5242880 | tf_op jit(solution)/shard_map/all_gather | solution.py:1101
  123.9 242.2 %all-gather.11.cloned.1.call-start = ((), (), s32[]{:S(2)}) async-start(), calls=%async_computation.9 | async-start | bytes 5242880 | tf_op jit(solution)/shard_map/all_gather | solution.py:1101
  124.0 8.5 %copy-start.17 = (s32[1,20]{1,0:T(1,128)S(1)}, s32[1,20]{1,0:T(1,128)}, u32[]{:S(2)}) copy-start(s32[1,20]{1,0:T(1,128)} %param.26) | copy-start | bytes 244
  124.0 8.5 %copy-start.34 = (s32[1,20]{1,0:T(1,128)S(1)}, s32[1,20]{1,0:T(1,128)}, u32[]{:S(2)}) copy-start(s32[1,20]{1,0:T(1,128)} %param.25) | copy-start | bytes 244
  126.5 67.2 %collective-permute-start = (bf16[320,2048]{1,0:T(8,128)(2,1)}, bf16[320,2048]{1,0:T(8,128)(2,1)S(1)}, u32[]{:S(2)}, u32[]{:S(2)}) collective-permute-start(bf16[320,2048]{1,0:T(8,128)(2,1)} %constant_dynamic-slice_fusion.1), channel_id=1, source_target_pairs={{0,2},{2,0},{4,6},{6,4},{1,3},{3,1},{5,7},{7,5},{8,10},{10,8},{12,... | collective-permute-start | bytes 3932168 | tf_op jit(solution)/shard_map/ppermute | solution.py:1126
  127.1 66.7 %collective-permute-start.1 = (bf16[320,2048]{1,0:T(8,128)(2,1)}, bf16[320,2048]{1,0:T(8,128)(2,1)}, u32[]{:S(2)}, u32[]{:S(2)}) collective-permute-start(bf16[320,2048]{1,0:T(8,128)(2,1)} %constant_dynamic-slice_fusion.1), channel_id=1, source_target_pairs={{0,4},{2,6},{4,0},{6,2},{1,5},{3,7},{5,1},{7,3},{8,12},{10,14},{12... | collective-permute-start | bytes 3932168 | tf_op jit(solution)/shard_map/ppermute | solution.py:1126
  128.6 65.2 %collective-permute-start.2 = (bf16[320,2048]{1,0:T(8,128)(2,1)}, bf16[320,2048]{1,0:T(8,128)(2,1)}, u32[]{:S(2)}, u32[]{:S(2)}) collective-permute-start(bf16[320,2048]{1,0:T(8,128)(2,1)} %constant_dynamic-slice_fusion.1), channel_id=1, source_target_pairs={{0,6},{2,4},{4,2},{6,0},{1,7},{3,5},{5,3},{7,1},{8,14},{10,12},{12... | collective-permute-start | bytes 3932168 | tf_op jit(solution)/shard_map/ppermute | solution.py:1126
  130.0 436.5 %reduce-scatter.4.cloned.1.call-start = ((), (), s32[]{:S(2)}) async-start(), calls=%async_computation.10 | async-start | bytes 5242880 | tf_op jit(solution)/shard_map/reduce_scatter | solution.py:1157
  133.6 17.5 %copy-start.11 = (f32[1280,128]{1,0:T(8,128)}, f32[1280,128]{1,0:T(8,128)S(1)}, u32[]{:S(2)}) copy-start(f32[1280,128]{1,0:T(8,128)S(1)} %get-tuple-element.105.sin_ref) | copy-start | bytes 1966084
  135.9 13.2 %copy-start.13 = (f32[2048]{0:T(1024)}, f32[2048]{0:T(1024)S(1)}, u32[]{:S(2)}) copy-start(f32[2048]{0:T(1024)S(1)} %get-tuple-element.88) | copy-start | bytes 24580
  339.6 289.8 %reduce-scatter.6.cloned.1.call-start = ((), (), s32[]{:S(2)}) async-start(), calls=%async_computation.11 | async-start | bytes 10485760 | tf_op jit(solution)/shard_map/reduce_scatter | solution.py:1157
  551.4 9.8 %copy-start.24 = (bf16[4,2,320,2048]{3,2,1,0:T(8,128)(2,1)S(1)}, bf16[4,2,320,2048]{3,2,1,0:T(8,128)(2,1)}, u32[]{:S(2)}) copy-start(bf16[4,2,320,2048]{3,2,1,0:T(8,128)(2,1)} %get-tuple-element.54) | copy-start | bytes 31457284
  557.7 69.9 %collective-permute-start.3 = (bf16[320,2048]{1,0:T(8,128)(2,1)}, bf16[320,2048]{1,0:T(8,128)(2,1)}, u32[]{:S(2)}, u32[]{:S(2)}) collective-permute-start(bf16[320,2048]{1,0:T(8,128)(2,1)} %get-tuple-element.91), channel_id=1, source_target_pairs={{0,2},{2,0},{4,6},{6,4},{1,3},{3,1},{5,7},{7,5},{8,10},{10,8},{12,... | collective-permute-start | bytes 3932168 | tf_op jit(solution)/shard_map/ppermute | solution.py:1175
  559.0 68.6 %collective-permute-start.4 = (bf16[320,2048]{1,0:T(8,128)(2,1)}, bf16[320,2048]{1,0:T(8,128)(2,1)}, u32[]{:S(2)}, u32[]{:S(2)}) collective-permute-start(bf16[320,2048]{1,0:T(8,128)(2,1)} %get-tuple-element.90), channel_id=1, source_target_pairs={{0,4},{2,6},{4,0},{6,2},{1,5},{3,7},{5,1},{7,3},{8,12},{10,14},{12... | collective-permute-start | bytes 3932168 | tf_op jit(solution)/shard_map/ppermute | solution.py:1175
  559.8 67.8 %collective-permute-start.5 = (bf16[320,2048]{1,0:T(8,128)(2,1)}, bf16[320,2048]{1,0:T(8,128)(2,1)}, u32[]{:S(2)}, u32[]{:S(2)}) collective-permute-start(bf16[320,2048]{1,0:T(8,128)(2,1)} %get-tuple-element.89), channel_id=1, source_target_pairs={{0,6},{2,4},{4,2},{6,0},{1,7},{3,5},{5,3},{7,1},{8,14},{10,12},{12... | collective-permute-start | bytes 3932168 | tf_op jit(solution)/shard_map/ppermute | solution.py:1175
  566.5 62.9 %all-to-all-start.1 = ((bf16[4,128,1024]{2,1,0:T(8,128)(2,1)}), bf16[4,128,1024]{2,1,0:T(8,128)(2,1)S(1)}, u32[]{:S(2)}, u32[]{:S(2)}) async-start(bf16[4,128,1024]{2,1,0:T(8,128)(2,1)} %bitcast.99), calls=%async_computation.3 | async-start | bytes 2097152 | tf_op jit(solution)/shard_map/all_to_all | solution.py:1160
  570.0 167.8 %reduce-scatter.8.cloned.1.call-start = ((), (), s32[]{:S(2)}) async-start(), calls=%async_computation.12 | async-start | bytes 3276800 | tf_op jit(solution)/shard_map/reduce_scatter | solution.py:1157
  644.6 80.5 %all-to-all-start.2 = ((bf16[4,128,2048]{2,1,0:T(8,128)(2,1)}), bf16[4,128,2048]{2,1,0:T(8,128)(2,1)}, u32[]{:S(2)}, u32[]{:S(2)}) async-start(bf16[4,128,2048]{2,1,0:T(8,128)(2,1)} %bitcast.115), calls=%async_computation.5 | async-start | bytes 4194304 | tf_op jit(solution)/shard_map/all_to_all | solution.py:1160
  653.9 10.1 %copy-start.5 = (bf16[320,2048]{1,0:T(8,128)(2,1)S(1)}, bf16[320,2048]{1,0:T(8,128)(2,1)}, u32[]{:S(2)}) copy-start(bf16[320,2048]{1,0:T(8,128)(2,1)} %get-tuple-element.92.ffn_own) | copy-start | bytes 3932164
  653.9 10.1 %copy-start.14 = (f32[2048]{0:T(1024)S(1)}, f32[2048]{0:T(1024)}, u32[]{:S(2)}) copy-start(f32[2048]{0:T(1024)} %copy-done.13) | copy-start | bytes 24580
  755.8 12.9 %collective-permute-start.6 = (f32[2,128]{1,0:T(2,128)S(1)}, f32[2,128]{1,0:T(2,128)S(1)}, u32[]{:S(2)}, u32[]{:S(2)}) collective-permute-start(f32[2,128]{1,0:T(2,128)S(1)} %pad_maximum_fusion.2), channel_id=1, source_target_pairs={{0,1},{1,0},{2,3},{3,2},{4,5},{5,4},{6,7},{7,6},{8,9},{9,8},{10,11... | collective-permute-start | bytes 3080 | tf_op jit(solution)/shard_map/ppermute | solution.py:895
  (27 other events, 92.3 us)
Sparse Core Ops, SparseCore 0:
  33.7 63.2 all-gather.4
  123.3 81.1 all-gather.6
  206.0 79.2 all-gather.8
  286.8 79.2 all-gather.10
  368.3 75.2 reduce-scatter.3
  450.4 142.9 reduce-scatter.5
  644.7 49.8 reduce-scatter.7

commit v4 on v3

--- a/solution.py
+++ b/solution.py
@@ -358,7 +358,7 @@
 
 
 class Plane:
-    def __init__(self, sent, landed, diagonal=False):
+    def __init__(self, sent, landed, diagonal=False, entered=False):
         self.sent, self.landed = sent, landed
         self.copies = []
         self.rank = lax.axis_index("context")
@@ -370,6 +370,8 @@
         self.y = {"context": self.at_y}
         self.both = {"context": self.at_both}
         self.sibling = {"tensor": 1 - self.core}
+        if entered:
+            return
         barrier = pltpu.get_barrier_semaphore()
         partners = [self.x, self.y, self.sibling] + ([self.both] if diagonal else [])
         for partner in partners:
@@ -462,32 +464,39 @@
 
 class Scatter:
     def __init__(self, plane, partial, held, other, near_x, near_y, far_x, far_y, local):
-        p = plane
+        p = self.plane = plane
         rows = near_x.shape[0]
         half = rows // 2
-        top, low = pl.ds(0, half), pl.ds(half, half)
+        halves = top, low = pl.ds(0, half), pl.ds(half, half)
         order = (p.at_both, p.at_x, p.at_y, p.rank)
-        across, kept = [], []
-        for i, rank in enumerate(order):
-            across.append(p.send(partial.at[rank, 1 - p.core], other.at[i], p.sibling))
-            kept.append(pltpu.make_async_copy(partial.at[rank, p.core], held.at[i], local.at[i]))
+        across, kept = {}, []
+        for i, h in ((0, 0), (0, 1), (1, 0), (2, 0), (1, 1), (2, 1), (3, 0), (3, 1)):
+            source = partial.at[order[i], 1 - p.core, halves[h]]
+            across[i, h] = p.send(source, other.at[i, halves[h]], p.sibling)
+        for i in range(4):
+            kept.append(
+                pltpu.make_async_copy(partial.at[order[i], p.core], held.at[i], local.at[i])
+            )
             kept[i].start()
 
-        def pair(i):
-            p.arrive(across[i], other.at[i])
-            kept[i].wait()
-            add_rows(held.at[i], other.at[i], 0, rows)
-
-        pair(0)
+        def pair(i, h):
+            p.arrive(across[i, h], other.at[i, halves[h]])
+            add_rows(held.at[i], other.at[i], h * half, half)
+
+        kept[0].wait()
+        pair(0, 0)
         first = p.send(held.at[0, top], far_x, p.x)
+        pair(0, 1)
         second = p.send(held.at[0, low], far_y, p.y)
-        pair(1)
+        kept[1].wait()
+        pair(1, 0)
         third = p.send(held.at[1, top], near_x.at[top], p.x)
-        pair(2)
-        fourth = p.send(held.at[2, low], near_y.at[low], p.y)
+        kept[2].wait()
+        pair(2, 0)
         p.arrive(first, far_x)
         add_rows(held.at[2], far_x, 0, half)
-        fifth = p.send(held.at[2, top], near_y.at[top], p.y)
+        fourth = p.send(held.at[2, top], near_y.at[top], p.y)
+        pair(1, 1)
         p.arrive(second, far_y)
 
         def step(i, carry):
@@ -498,19 +507,26 @@
             return carry
 
         lax.fori_loop(0, half // SLAB, step, 0)
-        sixth = p.send(held.at[1, low], near_x.at[low], p.x)
-        pair(3)
-        p.arrive(third, near_x.at[top])
-        p.arrive(fourth, near_y.at[low])
-        p.arrive(fifth, near_y.at[top])
-        p.arrive(sixth, near_x.at[low])
+        fifth = p.send(held.at[1, low], near_x.at[low], p.x)
+        pair(2, 1)
+        sixth = p.send(held.at[2, low], near_y.at[low], p.y)
+        kept[3].wait()
+        pair(3, 0)
+        pair(3, 1)
+        self.halves = halves
+        self.from_x, self.from_y = (third, fifth), (fourth, sixth)
         self.parts = (held.at[3], near_x, near_y)
+
+    def ready(self, h):
+        _, near_x, near_y = self.parts
+        self.plane.arrive(self.from_x[h], near_x.at[self.halves[h]])
+        self.plane.arrive(self.from_y[h], near_y.at[self.halves[h]])
 
     def rows(self, rows):
         return sum(part[rows, :].astype(jnp.float32) for part in self.parts)
 
 
-SCATTER_COPIES = 4 + 6
+SCATTER_COPIES = 8 + 6
 
 
 def scatter_scratch(share, width):
@@ -542,62 +558,73 @@
     lax.fori_loop(0, count // SLAB, step, 0)
 
 
-def start_kernel(
-    block, gate, up, down, cotangent, out, gate_out, up_out, down_out, scaled, sent, landed, local
-):
+class Exchange:
+    def __init__(self, plane, source, target, local):
+        p = plane
+        columns = target.shape[2]
+
+        def part(rank):
+            return source.at[:, pl.ds(pl.multiple_of(rank * columns, 128), columns)]
+
+        self.plane, self.target, self.moves = p, target, []
+        self.mine = pltpu.make_async_copy(part(p.rank), target.at[p.rank], local)
+        self.mine.start()
+        for partner, rank in ((p.both, p.at_both), (p.x, p.at_x), (p.y, p.at_y)):
+            self.moves.append((p.send(part(rank), target.at[p.rank], partner), rank))
+
+    def finish(self):
+        for number, rank in self.moves:
+            self.plane.arrive(number, self.target.at[rank])
+        self.mine.wait()
+
+
+def start_kernel(block, gate, cotangent, out, gate_out, scaled, my_scaled, sent, landed, local):
     p = Plane(sent, landed, diagonal=True)
     gather = Gather(p, block, out)
-    columns = gate_out.shape[2]
-
-    def part(weight, rank):
-        return weight.at[:, pl.ds(pl.multiple_of(rank * columns, 128), columns)]
-
-    mine = [pltpu.make_async_copy(block, out.at[p.rank, p.core], local.at[0])]
+    mine = pltpu.make_async_copy(block, out.at[p.rank, p.core], local.at[0])
     for k in range(CHUNKS):
         gather.start(k)
-    moves = []
-    for i, (source, target) in enumerate(((gate, gate_out), (up, up_out), (down, down_out))):
-        mine.append(
-            pltpu.make_async_copy(part(source, p.rank), target.at[p.rank], local.at[i + 1])
-        )
-        for partner, rank in ((p.x, p.at_x), (p.y, p.at_y), (p.both, p.at_both)):
-            number = p.send(part(source, rank), target.at[p.rank], partner)
-            moves.append((number, target.at[rank]))
-    for started in mine:
-        started.start()
+    exchange = Exchange(p, gate, gate_out, local.at[1])
+    mine.start()
+    share = block.shape[0]
 
     def scale(rows):
         value = residual_scale * cotangent[rows, :].astype(jnp.float32)
         scaled[rows, :] = value.astype(jnp.bfloat16)
 
+    def keep(rows):
+        from_rows = pl.ds(pl.multiple_of(p.core * share + rows.start, SLAB), SLAB)
+        my_scaled[rows, :] = scaled[from_rows, :]
+
     slabs(0, scaled.shape[0], scale)
+    slabs(0, share, keep)
     gather.forward()
     gather.finish()
-    for number, target in moves:
-        p.arrive(number, target)
+    exchange.finish()
     p.finish()
-    for started in mine:
-        started.wait()
-
-
-def start_plane(block, gate, up, down, cotangent):
+    mine.wait()
+
+
+def start_plane(block, gate, cotangent):
     share, width = block.shape
     depth, units = gate.shape
-    full = jax.ShapeDtypeStruct((4, 2, share, width), block.dtype)
-    weight = jax.ShapeDtypeStruct((4, depth, units // 4), gate.dtype)
-    full, *rest = pl.pallas_call(
+    return pl.pallas_call(
         start_kernel,
-        out_shape=[full, weight, weight, weight, jax.ShapeDtypeStruct(cotangent.shape, jnp.bfloat16)],
-        in_specs=[VMEM, ANY, ANY, ANY, VMEM],
-        out_specs=[ANY] * 4 + [VMEM],
-        scratch_shapes=wires(GATHER_COPIES + 9) + [pltpu.SemaphoreType.DMA((4,))],
+        out_shape=[
+            jax.ShapeDtypeStruct((4, 2, share, width), block.dtype),
+            jax.ShapeDtypeStruct((4, depth, units // 4), gate.dtype),
+            jax.ShapeDtypeStruct(cotangent.shape, jnp.bfloat16),
+            jax.ShapeDtypeStruct(block.shape, jnp.bfloat16),
+        ],
+        in_specs=[VMEM, ANY, VMEM],
+        out_specs=[ANY, ANY, VMEM, VMEM],
+        scratch_shapes=wires(GATHER_COPIES + 3) + [pltpu.SemaphoreType.DMA((2,))],
         compiler_params=pltpu.CompilerParams(
             collective_id=1, has_side_effects=True, vmem_limit_bytes=VMEM_LIMIT
         ),
-        cost_estimate=lasting(80),
+        cost_estimate=lasting(60),
         name="gather_tokens",
-    )(block, gate, up, down, cotangent)
-    return full.reshape(8 * share, width), rest[:3], rest[3]
+    )(block, gate, cotangent)
 
 
 def middle_kernel(
@@ -646,6 +673,8 @@
         hidden[rows, :] = (value * row_root(value) * gain[...]).astype(jnp.bfloat16)
 
     for k in range(CHUNKS):
+        if k % (CHUNKS // 2) == 0:
+            total.ready(k // (CHUNKS // 2))
         slabs(k * (share // CHUNKS), share // CHUNKS, work)
         gather.start(k)
     kept.append(pltpu.make_async_copy(hidden, out.at[p.rank, p.core], local.at[4]))
@@ -694,7 +723,10 @@
     early_second,
     out,
     grad_middle,
-    pairs,
+    pair_own,
+    pair_x,
+    pair_y,
+    pair_both,
     sent,
     landed,
     local,
@@ -727,6 +759,8 @@
         hidden[rows, :] = (residual_scale * gradient).astype(jnp.bfloat16)
 
     for k in range(CHUNKS):
+        if k % (CHUNKS // 2) == 0:
+            total.ready(k // (CHUNKS // 2))
         slabs(k * (share // CHUNKS), share // CHUNKS, work)
         gather.start(k)
     mine = pltpu.make_async_copy(hidden, out.at[p.rank, p.core], local.at[4])
@@ -735,27 +769,30 @@
         p.arrive(across[i], theirs.at[i])
         kept[i].wait()
         add_rows(held.at[i], theirs.at[i], 0, share)
-    whole = pltpu.make_async_copy(held, pairs, local.at[5])
-    whole.start()
+        target = (pair_own, pair_x, pair_y, pair_both)[i]
+        kept[i] = pltpu.make_async_copy(held.at[i], target, local.at[i])
+        kept[i].start()
     gather.forward()
     gather.finish()
     p.finish()
     mine.wait()
-    whole.wait()
+    for started in kept:
+        started.wait()
 
 
 def second_plane(partial, other_partial, middle, cotangent, gain, early):
     share, width = middle.shape
     full = jax.ShapeDtypeStruct((4, 2, share, width), jnp.bfloat16)
     quarter = jax.ShapeDtypeStruct((4, share, width), jnp.bfloat16)
-    out, grad_middle, pairs = pl.pallas_call(
+    out, grad_middle, *pairs = pl.pallas_call(
         second_kernel,
-        out_shape=[full, jax.ShapeDtypeStruct((share, width), jnp.float32), quarter],
+        out_shape=[full, jax.ShapeDtypeStruct((share, width), jnp.float32)]
+        + [jax.ShapeDtypeStruct((share, width), jnp.bfloat16)] * 4,
         in_specs=[ANY, ANY, VMEM, VMEM, VMEM, ANY, ANY],
-        out_specs=[ANY, VMEM, ANY],
+        out_specs=[ANY, VMEM] + [ANY] * 4,
         scratch_shapes=wires(GATHER_COPIES + SCATTER_COPIES + 4)
         + [
-            pltpu.SemaphoreType.DMA((6,)),
+            pltpu.SemaphoreType.DMA((5,)),
             pltpu.VMEM((share, width), jnp.bfloat16),
             pltpu.VMEM(quarter.shape, jnp.bfloat16),
             pltpu.VMEM(quarter.shape, jnp.bfloat16),
@@ -777,6 +814,14 @@
     return out.reshape(8 * share, width), grad_middle, pairs
 
 
+def lane_sums(pairs):
+    total = 0.0
+    for a, b in pairs:
+        product = a.astype(jnp.float32) * b.astype(jnp.float32)
+        total += jnp.sum(product, axis=1, keepdims=True)
+    return jnp.broadcast_to(total, (total.shape[0], 128))
+
+
 def last_kernel(
     partial,
     residual,
@@ -787,18 +832,21 @@
     ffn_x,
     ffn_y,
     ffn_both,
+    grads,
+    gate,
+    up,
     out,
     result_out,
-    done,
+    gain_out,
     sent,
     landed,
     local,
     held,
     result,
+    sums,
     *scratch,
 ):
     p = Plane(sent, landed)
-    done[...] = jnp.zeros_like(done)
     total = Scatter(p, partial, *scratch)
     share = held.shape[0]
 
@@ -811,6 +859,18 @@
     kept = [pltpu.make_async_copy(result, result_out.at[p.core], local.at[0])]
     kept[0].start()
     given = p.send(result, result_out.at[p.core], p.sibling)
+    units = gate.shape[1] // 4
+
+    def gain_rows(rows):
+        pairs = []
+        for c in range(4):
+            columns = slice(c * units, c * units + units)
+            pairs.append((grads[c, rows, :units], gate[rows, columns]))
+            pairs.append((grads[c, rows, units:], up[rows, columns]))
+        sums[0, rows, :] = lane_sums(pairs)
+
+    slabs(0, gate.shape[0], gain_rows)
+    swapped = p.send(sums.at[0], sums.at[1], p.sibling)
 
     def work(rows):
         value = residual[rows, :].astype(jnp.float32)
@@ -823,10 +883,14 @@
     across = []
     for k in range(CHUNKS):
         cut = chunk(k, share)
+        if k % (CHUNKS // 2) == 0:
+            total.ready(k // (CHUNKS // 2))
         slabs(k * (share // CHUNKS), share // CHUNKS, work)
         across.append(p.send(held.at[cut], out.at[p.core, cut], p.sibling))
     kept.append(pltpu.make_async_copy(held, out.at[p.core], local.at[1]))
     kept[1].start()
+    p.arrive(swapped, sums.at[1])
+    gain_out[...] = sums[0] + sums[1]
     p.arrive(given, result_out.at[1 - p.core])
     for k in range(CHUNKS):
         p.arrive(across[k], out.at[1 - p.core, chunk(k, share)])
@@ -835,22 +899,23 @@
         started.wait()
 
 
-def last_plane(partial, residual, grad_middle, gain, middle, ffn_parts):
+def last_plane(partial, residual, grad_middle, gain, middle, ffn_parts, grads, gate, up):
     share, width = residual.shape
-    out, result_out, done = pl.pallas_call(
+    out, result_out, gain_out = pl.pallas_call(
         last_kernel,
         out_shape=[
             jax.ShapeDtypeStruct((2, share, width), jnp.float32),
             jax.ShapeDtypeStruct((2, share, width), jnp.bfloat16),
-            jax.ShapeDtypeStruct((8, 128), jnp.float32),
+            jax.ShapeDtypeStruct((gate.shape[0], 128), jnp.float32),
         ],
-        in_specs=[ANY] + [VMEM] * 8,
+        in_specs=[ANY] + [VMEM] * 11,
         out_specs=[ANY, ANY, VMEM],
-        scratch_shapes=wires(CHUNKS + 1 + SCATTER_COPIES)
+        scratch_shapes=wires(CHUNKS + 2 + SCATTER_COPIES)
         + [
             pltpu.SemaphoreType.DMA((2,)),
             pltpu.VMEM((share, width), jnp.float32),
             pltpu.VMEM((share, width), jnp.bfloat16),
+            pltpu.VMEM((2, gate.shape[0], 128), jnp.float32),
         ]
         + scatter_scratch(share, width),
         compiler_params=pltpu.CompilerParams(
@@ -858,12 +923,25 @@
         ),
         cost_estimate=lasting(70),
         name="last_rows",
-    )(partial.reshape(4, 2, share, width), residual, grad_middle, gain, middle, *ffn_parts)
-    return out.reshape(2 * share, width), result_out.reshape(2 * share, width), done
-
-
-def exchange_kernel(blocks, *rest):
-    out, sent, landed = rest[-3:]
+    )(
+        partial.reshape(4, 2, share, width),
+        residual,
+        grad_middle,
+        gain,
+        middle,
+        *ffn_parts,
+        grads,
+        gate,
+        up,
+    )
+    return out.reshape(2 * share, width), result_out.reshape(2 * share, width), gain_out
+
+
+def qkv_columns(blocks):
+    return blocks.shape[2] // 2 + HEAD
+
+
+def exchange_kernel(blocks, weights, early, out, gain_out, sent, landed, sums):
     p = Plane(sent, landed, diagonal=True)
     moves = []
     for partner, rank in ((p.both, p.at_both), (p.x, p.at_x), (p.y, p.at_y)):
@@ -871,28 +949,118 @@
     out[p.rank] = blocks[p.rank]
     for number, target in moves:
         p.arrive(number, target)
+    columns = qkv_columns(blocks)
+
+    def gain_rows(rows):
+        pairs = [(out[c, rows, :columns], weights[c, rows, :columns]) for c in range(4)]
+        sums[0, rows, :] = lane_sums(pairs)
+
+    slabs(0, blocks.shape[1], gain_rows)
+    swapped = p.send(sums.at[0], sums.at[1], p.sibling)
+    p.arrive(swapped, sums.at[1])
+    gain_out[...] = sums[0] + sums[1]
     p.finish()
 
 
-def exchange(blocks, early):
+def exchange(blocks, weights, early):
+    depth = blocks.shape[1]
     return pl.pallas_call(
         exchange_kernel,
-        out_shape=jax.ShapeDtypeStruct(blocks.shape, blocks.dtype),
-        in_specs=[VMEM] + [ANY] * len(early),
-        out_specs=VMEM,
-        scratch_shapes=wires(3),
+        out_shape=[
+            jax.ShapeDtypeStruct(blocks.shape, blocks.dtype),
+            jax.ShapeDtypeStruct((depth, 128), jnp.float32),
+        ],
+        in_specs=[VMEM, VMEM, ANY],
+        out_specs=[VMEM, VMEM],
+        scratch_shapes=wires(4) + [pltpu.VMEM((2, depth, 128), jnp.float32)],
         compiler_params=pltpu.CompilerParams(collective_id=5, has_side_effects=True),
         cost_estimate=lasting(8),
         name="exchange_blocks",
-    )(blocks, *early)
+    )(blocks, weights, early)
+
+
+def finish_kernel(
+    attn, down, gate_up, tokens, result, attn_sums, ffn_sums, gains,
+    query_out, pair_out, out_out, gate_out, up_out, down_out, tokens_out, result_out, gain_out,
+):
+    width = query_out.shape[1]
+    units = gate_out.shape[1]
+    query_out[...] = attn[0, :, :width].astype(jnp.float32)
+    pair_out[...] = attn[0, :, width : width + 128].astype(jnp.float32)
+    out_out[...] = jnp.transpose(attn[0, :, width + 128 :].astype(jnp.float32))
+    gate_out[...] = gate_up[0, :, :units].astype(jnp.float32)
+    up_out[...] = gate_up[0, :, units:].astype(jnp.float32)
+    down_out[...] = jnp.transpose(down[0].astype(jnp.float32))
+    tokens_out[...] = tokens[...]
+    result_out[...] = result[...]
+    gain_out[0:1, :] = jnp.transpose(attn_sums[...])[0:1] / gains[0:1, :]
+    gain_out[1:2, :] = jnp.transpose(ffn_sums[...])[0:1] / gains[1:2, :]
+
+
+def finish(attn, down, gate_up, tokens, result, attn_sums, ffn_sums, gains):
+    groups, depth, units = down.shape
+    width = attn.shape[2] // 2 - HEAD
+    rows, columns = tokens.shape
+    part = rows // groups
+
+    def block(c, *shape):
+        return pl.BlockSpec((1, *shape), lambda i: (i, 0, 0))
+
+    def wide(count):
+        return pl.BlockSpec((depth, count), lambda i: (0, i))
+
+    def tall(count, other):
+        return pl.BlockSpec((count, other), lambda i: (i, 0))
+
+    def whole(array):
+        return pl.BlockSpec(array.shape, lambda i: (0, 0))
+
+    def f32(*shape):
+        return jax.ShapeDtypeStruct(shape, jnp.float32)
+
+    return pl.pallas_call(
+        finish_kernel,
+        grid=(groups,),
+        in_specs=[
+            block(0, depth, attn.shape[2]),
+            block(0, depth, units),
+            block(0, depth, 2 * units),
+            tall(part, columns),
+            tall(part, columns),
+            whole(attn_sums),
+            whole(ffn_sums),
+            whole(gains),
+        ],
+        out_specs=[
+            wide(width),
+            wide(128),
+            tall(width, depth),
+            wide(units),
+            wide(units),
+            tall(units, depth),
+            tall(part, columns),
+            tall(part, columns),
+            pl.BlockSpec((2, 128), lambda i: (0, 0)),
+        ],
+        out_shape=[
+            f32(depth, groups * width),
+            f32(depth, groups * 128),
+            f32(groups * width, depth),
+            f32(depth, groups * units),
+            f32(depth, groups * units),
+            f32(groups * units, depth),
+            f32(rows, columns),
+            jax.ShapeDtypeStruct(result.shape, result.dtype),
+            f32(2, 128),
+        ],
+        compiler_params=pltpu.CompilerParams(vmem_limit_bytes=VMEM_LIMIT),
+        cost_estimate=lasting(12),
+        name="finish",
+    )(attn, down, gate_up, tokens, result, attn_sums, ffn_sums, gains)
 
 
 def context_pairs(step):
     return [(i, i ^ step) for i in range(4)]
-
-
-def swap_cores(values):
-    return lax.ppermute(values, "tensor", [(0, 1), (1, 0)])
 
 
 def ffn_first_kernel(hidden, gate_w, up_w, m, gate, up):
@@ -928,16 +1096,44 @@
         ).astype(jnp.bfloat16)
 
 
-def first_rows_kernel(values, gain, weight, hidden, raw):
+def first_rows_kernel(
+    values, gain, weight, up, down, hidden, raw, up_out, down_out, sent, landed, local
+):
+    step, last = pl.program_id(0), pl.num_programs(0) - 1
+
+    def exchanges(act):
+        for i, (source, target) in enumerate(((up, up_out), (down, down_out))):
+            act(i, source, target)
+
+    @pl.when(step == 0)
+    def start():
+        p = Plane(sent, landed, diagonal=True)
+        exchanges(lambda i, source, target: Exchange(p, source, target, local.at[i]))
+
     value = values[...].astype(jnp.float32)
     normed = (value * row_root(value) * gain[...]).astype(jnp.bfloat16)
     hidden[...] = normed
     raw[...] = dot(normed, weight[...])
 
-
-def first_rows(values, gain, weight):
+    @pl.when(step == last)
+    def finish():
+        p = Plane(sent, landed, entered=True)
+        columns = up_out.shape[2]
+        for i, (source, target) in enumerate(((up, up_out), (down, down_out))):
+            part = source.at[:, pl.ds(0, columns)]
+            for j, rank in enumerate((p.at_both, p.at_x, p.at_y)):
+                move = p.copy(3 * i + j, part, target.at[rank], p.x)
+                move.wait_recv()
+                move.wait_send()
+            own = source.at[:, pl.ds(pl.multiple_of(p.rank * columns, 128), columns)]
+            pltpu.make_async_copy(own, target.at[p.rank], local.at[i]).wait()
+
+
+def first_rows(values, gain, weight, up, down):
     count, width = values.shape
     columns = weight.shape[1]
+    depth, units = up.shape
+    moved = jax.ShapeDtypeStruct((4, depth, units // 4), up.dtype)
     return pl.pallas_call(
         first_rows_kernel,
         grid=(count // ROW_TILE,),
@@ -945,19 +1141,28 @@
             pl.BlockSpec((ROW_TILE, width), lambda i: (i, 0)),
             pl.BlockSpec((1, width), lambda i: (0, 0)),
             pl.BlockSpec((width, columns), lambda i: (0, 0)),
+            ANY,
+            ANY,
         ],
         out_specs=[
             pl.BlockSpec((ROW_TILE, width), lambda i: (i, 0)),
             pl.BlockSpec((ROW_TILE, columns), lambda i: (i, 0)),
+            ANY,
+            ANY,
         ],
         out_shape=[
             jax.ShapeDtypeStruct((count, width), jnp.bfloat16),
             jax.ShapeDtypeStruct((count, columns), jnp.float32),
+            moved,
+            moved,
         ],
-        compiler_params=pltpu.CompilerParams(vmem_limit_bytes=VMEM_LIMIT),
-        cost_estimate=lasting(12),
+        scratch_shapes=wires(6) + [pltpu.SemaphoreType.DMA((2,))],
+        compiler_params=pltpu.CompilerParams(
+            collective_id=6, has_side_effects=True, vmem_limit_bytes=VMEM_LIMIT
+        ),
+        cost_estimate=lasting(25),
         name="first_rows",
-    )(values, gain, weight)
+    )(values, gain, weight, up, down)
 
 
 def attention_weights_kernel(hidden, back, grad, attended, *early_and_out):
@@ -1075,11 +1280,10 @@
 
     gains = jnp.stack([attn_gain, ffn_gain], axis=1)
     gains = jnp.broadcast_to(jnp.pad(gains, ((0, 0), (0, 126))), (groups, depth, 128))
-    packed = spread(
-        jnp.concatenate(
-            [blocks(w_query), kv_blocks(w_key), kv_blocks(w_value), blocks(w_out.T), gains], axis=2
-        )
+    my_packed = jnp.concatenate(
+        [blocks(w_query), kv_blocks(w_key), kv_blocks(w_value), blocks(w_out.T), gains], axis=2
     )
+    packed = spread(my_packed)
     width = w_query.shape[1] // groups
     qkv_full = packed[:, : width + 2 * HEAD]
     out_full = packed[:, width + 2 * HEAD : 2 * width + 2 * HEAD]
@@ -1087,20 +1291,36 @@
     attn_scale, ffn_scale = gains_full[:, 0], gains_full[:, 1]
     square = groups == 4 and cores == 2
     tokens_half, cotangent_half = my_rows(tokens), my_rows(cotangent)
+    tables = rope_tables()
+
+    def over_groups(blocks_here):
+        return lax.all_gather(
+            blocks_here.reshape(groups * depth, -1), "fsdp", axis=0, tiled=True
+        )
+
+    down_turned = w_down.T
     if square:
-        inputs_full, ffn_blocks, ffn_grad = start_plane(
-            tokens_half, w_gate, w_up, w_down.T, cotangent
+        inputs_full, gate_blocks, ffn_grad, my_ffn_grad = start_plane(
+            tokens_half, w_gate, cotangent
         )
+        gate_full = over_groups(gate_blocks)
+        hidden_first, raw, up_blocks, down_blocks = first_rows(
+            inputs_full.reshape(-1, inputs_full.shape[3]),
+            attn_scale[None, :],
+            qkv_full,
+            w_up,
+            down_turned,
+        )
+        up_full, down_full = over_groups(up_blocks), over_groups(down_blocks)
     else:
-        inputs_full = gather_rows(tokens_half)
-        ffn_grad = (residual_scale * cotangent.astype(jnp.float32)).astype(jnp.bfloat16)
-        ffn_blocks = [
-            lax.all_to_all(blocks(w), "context", 0, 0) for w in (w_gate, w_up, w_down.T)
-        ]
-    gate_full, up_full, down_full = (
-        lax.all_gather(w.reshape(groups * depth, -1), "fsdp", axis=0, tiled=True)
-        for w in ffn_blocks
-    )
+        gate_full, up_full, down_full = (
+            spread(blocks(w)) for w in (w_gate, w_up, down_turned)
+        )
+        inputs_full = gather_rows(tokens_half).astype(jnp.float32)
+        hidden_first = inputs_full * inverse_root(inputs_full) * attn_scale
+        hidden_first = hidden_first.astype(jnp.bfloat16)
+        raw = dot(hidden_first, qkv_full)
+        my_ffn_grad = (residual_scale * cotangent_half.astype(jnp.float32)).astype(jnp.bfloat16)
 
     segment, starts = piece_segment[0] % 13, piece_start[0]
     places = jnp.where(
@@ -1112,13 +1332,10 @@
             starts + (segment - 1 - BRANCHES) * SEG + (BRANCHES - 1) * SEG,
         ),
     )
-    tables = rope_tables()
 
     residual_in = tokens_half.astype(jnp.float32)
     grad_result = cotangent_half.astype(jnp.float32)
-    my_ffn_grad = my_rows(ffn_grad)
-
-    hidden_first, raw = first_rows(inputs_full, attn_scale[None, :], qkv_full)
+
     attended, *kept = attention_forward(places, starts, raw, tables)
     branch = dot(attended, out_full, LAST).astype(jnp.bfloat16)
     if square:
@@ -1193,16 +1410,37 @@
     grad_gate_up = hand_back(grad_gate_up)
     grad_first = dot(back, qkv_full, LAST).astype(jnp.bfloat16)
     if square:
-        grad_tokens, result, done = last_plane(
+        grad_tokens, result, ffn_sums = last_plane(
             grad_first,
             tokens_half,
             grad_middle,
             attn_scale[None, :],
             middle,
             ffn_parts,
+            grad_gate_up,
+            w_gate,
+            w_up,
         )
-        grad_attn = exchange(
-            grad_attn.reshape(groups, depth, -1), [done, grad_gate_up]
+        grad_attn, attn_sums = exchange(
+            grad_attn.reshape(groups, depth, -1), my_packed, ffn_sums
+        )
+        my_gains = jnp.stack([attn_gain, ffn_gain]).astype(jnp.float32)
+        query, pair, out, gate, up, down, grad_tokens, result, gain_grads = finish(
+            grad_attn, grad_down, grad_gate_up, grad_tokens, result, attn_sums, ffn_sums, my_gains
+        )
+        key, value = jnp.moveaxis(pair.reshape(depth, groups, 2, HEAD), 2, 0)
+        return (
+            result,
+            grad_tokens,
+            gain_grads[0],
+            query,
+            key.reshape(depth, -1),
+            value.reshape(depth, -1),
+            out,
+            gain_grads[1],
+            gate,
+            up,
+            down,
         )
     else:
         root = inverse_root(residual_in)
@@ -1231,7 +1469,7 @@
             against((w_gate, grad_gate), (w_up, grad_up)),
         ]
     )
-    gain_grads += swap_cores(gain_grads) if square else lax.psum(gain_grads, "tensor") - gain_grads
+    gain_grads = lax.psum(gain_grads, "tensor")
     return (
         result,
         grad_tokens,

time: 792 us -> 756 us (0.955)
  local copies, waits for them, and re-layouts: 65.1 us -> 39 us
  other arithmetic: 18.8 us -> 5.27 us
    all_gather x3, waiting for transfers between devices: 26.5 us -> 7.62 us  [over_groups(): lax.all_gather(blocks_here.reshape(groups * depth, -1), 'fsdp', axis=0, t...]
    pallas_call x1, Pallas kernels: 13.1 us -> 28.8 us  [first_rows(): pl.pallas_call(first_rows_kernel, grid=(count // ROW_TILE,), in_specs=[pl...]
    pallas_call x2 -> x3, Pallas kernels: 98.4 us -> 85.5 us  [the longest x1 62.2 us: start_plane(): pl.pallas_call(start_kernel, out_shape=[jax.ShapeDtypeStruct((4, 2, share...]
    all_to_all x2, waiting for transfers between devices: 1.77 us -> 14 us  [hand_back(): return lax.all_to_all(gradient.reshape(groups, depth, -1), 'context', 0, 0)]
    unnamed x84 -> x79, local copies, waits for them, and re-layouts: 36.1 us -> 27.6 us
  transfers between devices with their start and end apart: 16 -> 15, of which waited for: 2 -> 3; matrix products, arithmetic and copies ran while one was open for 15% -> 11% of each run, Pallas kernels for 68% -> 69%
where the time goes in v4:
time: 756 us; the launch traced here: 749 us
  Pallas kernels  556 us (74%)
  matrix products  72.4 us (10%)
  local copies, waits for them, and re-layouts  39 us (5%)
  waiting for transfers between devices  29.5 us (4%)
  blocking collectives  16.4 us (2%)
  starting transfers between devices  15.2 us (2%)
  between operations  14.8 us (2%)
    pallas_call x1, Pallas kernels, second_plane(): pl.pallas_call(second_kernel, out_shape=[full, jax.ShapeDtypeStruct((shar...  99.6 us
    pallas_call x1, Pallas kernels, middle_plane(): pl.pallas_call(middle_kernel, out_shape=[full, jax.ShapeDtypeStruct((shar...  95.8 us
    pallas_call x2, Pallas kernels, row_tiles(): pl.pallas_call(kernel, grid=(count // ROW_TILE,), in_specs=[tile(r.shape[...  84.4 us
    dot_general x5, matrix products, dot(): lax.dot_general(left_side, right_side, dims, preferred_element_type=jnp.f...  72.4 us
    pallas_call x1, Pallas kernels, start_plane(): pl.pallas_call(start_kernel, out_shape=[jax.ShapeDtypeStruct((4, 2, share...  62.2 us
    pallas_call x1, Pallas kernels, last_plane(): pl.pallas_call(last_kernel, out_shape=[jax.ShapeDtypeStruct((2, share, wi...  58.9 us
    pallas_call x1, Pallas kernels, attention_backward(): pl.pallas_call(attention_backward_kernel, out_shape=jax.ShapeDtypeStruct(...  52.5 us
    pallas_call x1, Pallas kernels, attention_forward(): pl.pallas_call(attention_forward_kernel, out_shape=[kept] * 4 + [jax.Shap...  37 us
  transfers between devices with their start and end apart: 15, of which 3 were waited for; matrix products, arithmetic and copies ran while one was open for 11% of the time, Pallas kernels for 69%

profile of v4, /device:TPU:0, one launch (start us, length us, event | category | flops | bytes accessed | tf_op | source)
XLA Modules:
  0.0 748.9 jit_solution(15244890893658826484)
XLA Ops:
  16.8 16.4 %all_to_all.15 = bf16[4,128,768]{2,1,0:T(8,128)(2,1)} all-to-all(bf16[4,128,768]{2,1,0:T(8,128)(2,1)S(1)} %concatenate.9.weights), channel_id=1, replica_groups=mesh['fsdp'=4,'context'=4,'tensor'=2] {'context'}, dimensions={0} | all-to-all | bytes 1572864 | tf_op jit(solution)/shard_map/all_to_all | solution.py:1277
  34.6 62.2 %gather_tokens.1 = (bf16[4,2,320,2048]{3,2,1,0:T(8,128)(2,1)}, bf16[4,128,1024]{2,1,0:T(8,128)(2,1)}, bf16[640,2048]{1,0:T(8,128)(2,1)}, bf16[320,2048]{1,0:T(8,128)(2,1)S(1)}) custom-call(bf16[320,2048]{1,0:T(8,128)(2,1)S(1)} %constant_dynamic-slice_fusion.1.block.residual, bf16[128,4096]{1,0:T(8,128)(2,1)S(1)} %copy-done.10, bf16[640,2048]{1,0:T(8,128)(2,1)} %cotangent.1), custom_call_target="tpu_custom_call" | custom-call | bytes 180000000 | tf_op jit(solution)/shard_map/gather_tokens/pallas_call | solution.py:611
  103.3 28.8 %first_rows.1 = (bf16[2560,2048]{1,0:T(8,128)(2,1)}, f32[2560,384]{1,0:T(8,128)}, bf16[4,128,1024]{2,1,0:T(8,128)(2,1)}, bf16[4,128,1024]{2,1,0:T(8,128)(2,1)}) custom-call(bf16[2560,2048]{1,0:T(8,128)(2,1)} %bitcast.70, f32[1,2048]{1,0:T(1,128)S(1)} %bitcast.59, bf16[2048,384]{1,0:T(8,128)(2,1)S(1)} %slice.30.weight, bf16[128,4096]{1,0:T(8,128)(2,1)S(1)} %copy-done.12, ...), custom_call_target="tpu_custom_call" | custom-call | bytes 75000000 | tf_op jit(solution)/shard_map/first_rows/pallas_call | solution.py:1137
  139.4 37.0 %attention_forward.1 = (bf16[2560,256]{1,0:T(8,128)(2,1)S(1)}, bf16[2560,256]{1,0:T(8,128)(2,1)S(1)}, bf16[2560,256]{1,0:T(8,128)(2,1)S(1)}, bf16[2560,256]{1,0:T(8,128)(2,1)}, f32[4,1,2560]{2,1,0:T(1,128)S(1)}) custom-call(s32[20]{0:T(128)S(1)} %compare_select_fusion.1.to_ref, s32[20]{0:T(128)S(1)} %bitcast.63, f32[2560,384]{1,0:T(8,128)} %get-tuple-element.55.raw_ref, ...), custom_call_target="tpu_custom_call" | custom-call | flops 5368709120 | bytes 10485760 | tf_op jit(solution)/shard_map/attention_forward/pallas_call | solution.py:311
  176.5 7.7 %convolution_convert_fusion.1 = bf16[2560,2048]{1,0:T(8,128)(2,1)} fusion(bf16[2560,256]{1,0:T(8,128)(2,1)S(1)} %get-tuple-element.56.attended, bf16[2048,768]{1,0:T(8,128)(2,1)} %all-gather.5.cloned.1.call-done), kind=kOutput, calls=%fused_computation.1 | convolution fusion | flops 2689597440 | bytes 12845056 | tf_op jit(solution)/shard_map/dot_general | solution.py:31
  184.2 7.7 %collective-permute-done.1.from_y = bf16[320,2048]{1,0:T(8,128)(2,1)} collective-permute-done((bf16[320,2048]{1,0:T(8,128)(2,1)}, bf16[320,2048]{1,0:T(8,128)(2,1)}, u32[]{:S(2)}, u32[]{:S(2)}) %collective-permute-start.1) | collective-permute-done | bytes 1310752 | tf_op jit(solution)/shard_map/ppermute | solution.py:1343
  191.9 95.8 %middle_rows.1 = (bf16[4,2,320,2048]{3,2,1,0:T(8,128)(2,1)}, f32[320,2048]{1,0:T(8,128)}, bf16[4,2,320,2048]{3,2,1,0:T(8,128)(2,1)}) custom-call(bf16[4,2,320,2048]{3,2,1,0:T(8,128)(2,1)} %bitcast.65, bf16[320,2048]{1,0:T(8,128)(2,1)S(1)} %copy-done.3, f32[1,2048]{1,0:T(1,128)S(1)} %bitcast.61, bf16[2,320,2048]{2,1,0:T(8,128)(2,1)} %bitcast.76, ...), custom_call_target="tpu_custom_call" | custom-call | bytes 300000000 | tf_op jit(solution)/shard_map/middle_rows/pallas_call | solution.py:694
  287.8 29.1 %ffn_first.1 = (bf16[2560,1024]{1,0:T(8,128)(2,1)}, bf16[2560,1024]{1,0:T(8,128)(2,1)}, bf16[2560,1024]{1,0:T(8,128)(2,1)}) custom-call(bf16[2560,2048]{1,0:T(8,128)(2,1)} %bitcast.93, bf16[2048,1024]{1,0:T(8,128)(2,1)} %all-gather.7.cloned.1.call-done.gate_w, bf16[2048,1024]{1,0:T(8,128)(2,1)} %all-gather.9.cloned.1.call-done.up_w), custom_call_target="tpu_custom_call" | custom-call | flops 21474836480 | bytes 53687092 | tf_op jit(solution)/shard_map/ffn_first/pallas_call | solution.py:1210
  316.9 17.3 %convolution_convert_fusion.4.early.early_first = bf16[2048,1024]{1,0:T(8,128)(2,1)} fusion(bf16[2560,2048]{1,0:T(8,128)(2,1)} %bitcast.95, bf16[2560,1024]{1,0:T(8,128)(2,1)} %get-tuple-element.65.m), kind=kOutput, calls=%fused_computation.4 | convolution fusion | flops 10739515392 | bytes 19922944 | tf_op jit(solution)/shard_map/dot_general | solution.py:31
  334.3 7.6 %all-gather.11.cloned.1.call-done.down_w = bf16[2048,1024]{1,0:T(8,128)(2,1)} async-done(((bf16[512,1024]{1,0:T(8,128)(2,1)}), bf16[2048,1024]{1,0:T(8,128)(2,1)}) %all-gather.11.cloned.1.call-update) | async-done | bytes 4194320 | tf_op jit(solution)/shard_map/all_gather | solution.py:1297
  341.8 55.3 %ffn_second.1 = (bf16[2560,2048]{1,0:T(8,128)(2,1)}, bf16[2560,2048]{1,0:T(8,128)(2,1)}, bf16[2560,2048]{1,0:T(8,128)(2,1)}) custom-call(bf16[2560,2048]{1,0:T(8,128)(2,1)} %bitcast.96, bf16[2560,1024]{1,0:T(8,128)(2,1)} %get-tuple-element.63.gate, bf16[2560,1024]{1,0:T(8,128)(2,1)} %get-tuple-element.64.up, bf16[2560,1024]{1,0:T(8,128)(2,1)} %get-tuple-element.65.m, ...), custom_call_target="tpu_custom_call" | custom-call | flops 32212254720 | bytes 80530640 | tf_op jit(solution)/shard_map/ffn_second/pallas_call | solution.py:1210
  397.1 28.9 %convolution_convert_fusion.2.early_second = bf16[2048,2048]{1,0:T(8,128)(2,1)} fusion(bf16[2560,2048]{1,0:T(8,128)(2,1)} %bitcast.94, bf16[2560,2048]{1,0:T(8,128)(2,1)} %get-tuple-element.70), kind=kOutput, calls=%fused_computation.2 | convolution fusion | flops 21479030784 | bytes 29360128 | tf_op jit(solution)/shard_map/dot_general | solution.py:31
  426.0 2.5 constant_dynamic-slice_fusion.cotangent
  428.5 99.6 %second_rows.1 = (bf16[4,2,320,2048]{3,2,1,0:T(8,128)(2,1)}, f32[320,2048]{1,0:T(8,128)}, bf16[320,2048]{1,0:T(8,128)(2,1)S(1)}, bf16[320,2048]{1,0:T(8,128)(2,1...) custom-call(bf16[4,2,320,2048]{3,2,1,0:T(8,128)(2,1)} %bitcast.67, bf16[4,2,320,2048]{3,2,1,0:T(8,128)(2,1)} %bitcast.66, ...), custom_call_target="tpu_custom_call" | custom-call | bytes 300000000 | tf_op jit(solution)/shard_map/second_rows/pallas_call | solution.py:787
  532.6 8.2 %convolution_convert_fusion.3.grad_ref = bf16[2560,256]{1,0:T(8,128)(2,1)} fusion(bf16[2560,2048]{1,0:T(8,128)(2,1)} %bitcast.68, bf16[2048,768]{1,0:T(8,128)(2,1)} %all-gather.5.cloned.1.call-done), kind=kOutput, calls=%fused_computation.3 | convolution fusion | flops 2685009920 | bytes 12845056 | tf_op jit(solution)/shard_map/dot_general | solution.py:31
  540.9 3.5 all-to-all-start.1
  549.4 52.5 %attention_backward.1.back = bf16[2560,384]{1,0:T(8,128)(2,1)} custom-call(s32[20]{0:T(128)S(1)} %compare_select_fusion.1.to_ref, s32[20]{0:T(128)S(1)} %bitcast.64, bf16[2560,256]{1,0:T(8,128)(2,1)S(1)} %copy-done.27, bf16[2560,256]{1,0:T(8,128)(2,1)S(1)} %copy-done.29, bf16[2560,256]{1,0:T(8,128)(2,1)} %copy-done.30, ...), custom_call_target="tpu_custom_call" | custom-call | flops 13421772800 | bytes 10485760 | tf_op jit(solution)/shard_map/attention_backward/pallas_call | solution.py:329
  603.7 13.9 %attention_weights.1 = bf16[2048,640]{1,0:T(8,128)(2,1)} custom-call(bf16[2560,2048]{1,0:T(8,128)(2,1)} %get-tuple-element.54.hidden, bf16[2560,384]{1,0:T(8,128)(2,1)} %attention_backward.1.back, bf16[2560,2048]{1,0:T(8,128)(2,1)} %bitcast.69, bf16[2560,256]{1,0:T(8,128)(2,1)S(1)} %copy-done.9, ...), custom_call_target="tpu_custom_call" | custom-call | bytes 36000000 | tf_op jit(solution)/shard_map/attention_weights/pallas_call | solution.py:1179
  617.6 4.1 all-to-all-start.2
  621.7 10.4 %convolution_convert_fusion = bf16[2560,2048]{1,0:T(8,128)(2,1)} fusion(bf16[2560,384]{1,0:T(8,128)(2,1)} %attention_backward.1.back, bf16[2048,768]{1,0:T(8,128)(2,1)} %all-gather.5.cloned.1.call-done), kind=kOutput, calls=%fused_computation | convolution fusion | flops 4031774720 | bytes 14024704 | tf_op jit(solution)/shard_map/dot_general | solution.py:31
  632.1 14.0 %all-to-all-done.2.grads.gate_up = bf16[4,128,2048]{2,1,0:T(8,128)(2,1)S(1)} async-done(((bf16[4,128,2048]{2,1,0:T(8,128)(2,1)}), bf16[4,128,2048]{2,1,0:T(8,128)(2,1)S(1)}, u32[]{:S(2)}, u32[]{:S(2)}) %all-to-all-start.2) | async-done | bytes 2097184 | tf_op jit(solution)/shard_map/all_to_all | solution.py:1377
  651.2 58.9 %last_rows.1 = (f32[2,320,2048]{2,1,0:T(8,128)}, bf16[2,320,2048]{2,1,0:T(8,128)(2,1)}, f32[128,128]{1,0:T(8,128)S(1)}) custom-call(bf16[4,2,320,2048]{3,2,1,0:T(8,128)(2,1)} %bitcast.71, bf16[320,2048]{1,0:T(8,128)(2,1)S(1)} %copy-done.3, f32[320,2048]{1,0:T(8,128)} %get-tuple-element.79.grad_middle, f32[1,2048]{1,0:T(1,128)S(1)} %bitcast.60, ...), custom_call_target="tpu_custom_call" | custom-call | bytes 210000000 | tf_op jit(solution)/shard_map/last_rows/pallas_call | solution.py:904
  710.7 14.0 %exchange_blocks.1 = (bf16[4,128,640]{2,1,0:T(8,128)(2,1)}, f32[128,128]{1,0:T(8,128)}) custom-call(bf16[4,128,640]{2,1,0:T(8,128)(2,1)} %bitcast.81, bf16[4,128,768]{2,1,0:T(8,128)(2,1)} %copy-done.31, f32[128,128]{1,0:T(8,128)} %copy-done.20), custom_call_target="tpu_custom_call" | custom-call | bytes 24000000 | tf_op jit(solution)/shard_map/exchange_blocks/pallas_call | solution.py:967
  730.4 9.3 %finish.1 = (f32[128,1024]{1,0:T(8,128)}, f32[128,512]{1,0:T(8,128)S(1)}, f32[1024,128]{1,0:T(8,128)}, f32[128,4096]{1,0:T(8,128)}, f32[128,4096]{1,0:T(8,128)},...) custom-call(bf16[4,128,640]{2,1,0:T(8,128)(2,1)S(1)} %copy-done.17, ...), custom_call_target="tpu_custom_call" | custom-call | bytes 36000000 | tf_op jit(solution)/shard_map/finish/pallas_call | solution.py:1021
  (132 shorter events, 49.5 us)
Async XLA Ops:
  7.2 26.1 %copy-start = (bf16[640,2048]{1,0:T(8,128)(2,1)S(1)}, bf16[640,2048]{1,0:T(8,128)(2,1)}, u32[]{:S(2)}) copy-start(bf16[640,2048]{1,0:T(8,128)(2,1)} %param.14) | copy-start | bytes 7864324
  7.2 92.4 %all-gather.5.cloned.1.call-start = ((), (), s32[]{:S(2)}) async-start(), calls=%async_computation.6 | async-start | bytes 3932160 | tf_op jit(solution)/shard_map/all_gather | solution.py:1279
  16.8 79.9 %copy-start.31 = (bf16[4,128,768]{2,1,0:T(8,128)(2,1)}, bf16[4,128,768]{2,1,0:T(8,128)(2,1)S(1)}, u32[]{:S(2)}) copy-start(bf16[4,128,768]{2,1,0:T(8,128)(2,1)S(1)} %concatenate.9.weights) | copy-start | bytes 2359300
  33.3 254.5 %all-gather.7.cloned.1.call-start = ((), (), s32[]{:S(2)}) async-start(), calls=%async_computation.7 | async-start | bytes 5242880 | tf_op jit(solution)/shard_map/all_gather | solution.py:1297
  34.6 64.4 %copy-start.32 = (bf16[4096,128]{1,0:T(8,128)(2,1)S(1)}, bf16[4096,128]{1,0:T(8,128)(2,1)}, u32[]{:S(2)}) copy-start(bf16[4096,128]{1,0:T(8,128)(2,1)} %param.24) | copy-start | bytes 3145732
  98.9 188.8 %all-gather.9.cloned.1.call-start = ((), (), s32[]{:S(2)}) async-start(), calls=%async_computation.8 | async-start | bytes 5242880 | tf_op jit(solution)/shard_map/all_gather | solution.py:1297
  103.2 28.8 %copy-start.22 = (f32[2048]{0:T(1024)}, f32[2048]{0:T(1024)S(1)}, u32[]{:S(2)}) copy-start(f32[2048]{0:T(1024)S(1)} %get-tuple-element.118) | copy-start | bytes 24580
  103.3 32.4 %copy-start.26 = (s32[1,20]{1,0:T(1,128)S(1)}, s32[1,20]{1,0:T(1,128)}, u32[]{:S(2)}) copy-start(s32[1,20]{1,0:T(1,128)} %param.26) | copy-start | bytes 244
  103.3 32.4 %copy-start.35 = (s32[1,20]{1,0:T(1,128)S(1)}, s32[1,20]{1,0:T(1,128)}, u32[]{:S(2)}) copy-start(s32[1,20]{1,0:T(1,128)} %param.25) | copy-start | bytes 244
  132.1 209.8 %all-gather.11.cloned.1.call-start = ((), (), s32[]{:S(2)}) async-start(), calls=%async_computation.9 | async-start | bytes 5242880 | tf_op jit(solution)/shard_map/all_gather | solution.py:1297
  132.1 52.1 %collective-permute-start = (bf16[320,2048]{1,0:T(8,128)(2,1)}, bf16[320,2048]{1,0:T(8,128)(2,1)S(1)}, u32[]{:S(2)}, u32[]{:S(2)}) collective-permute-start(bf16[320,2048]{1,0:T(8,128)(2,1)} %copy-done.25), channel_id=1, source_target_pairs={{0,2},{2,0},{4,6},{6,4},{1,3},{3,1},{5,7},{7,5},{8,10},{10,8},{12,... | collective-permute-start | bytes 3932168 | tf_op jit(solution)/shard_map/ppermute | solution.py:1343
  133.1 58.8 %collective-permute-start.1 = (bf16[320,2048]{1,0:T(8,128)(2,1)}, bf16[320,2048]{1,0:T(8,128)(2,1)}, u32[]{:S(2)}, u32[]{:S(2)}) collective-permute-start(bf16[320,2048]{1,0:T(8,128)(2,1)} %copy-done.25), channel_id=1, source_target_pairs={{0,4},{2,6},{4,0},{6,2},{1,5},{3,7},{5,1},{7,3},{8,12},{10,14},{12... | collective-permute-start | bytes 3932168 | tf_op jit(solution)/shard_map/ppermute | solution.py:1343
  134.1 57.8 %collective-permute-start.2 = (bf16[320,2048]{1,0:T(8,128)(2,1)}, bf16[320,2048]{1,0:T(8,128)(2,1)}, u32[]{:S(2)}, u32[]{:S(2)}) collective-permute-start(bf16[320,2048]{1,0:T(8,128)(2,1)} %copy-done.25), channel_id=1, source_target_pairs={{0,6},{2,4},{4,2},{6,0},{1,7},{3,5},{5,3},{7,1},{8,14},{10,12},{12... | collective-permute-start | bytes 3932168 | tf_op jit(solution)/shard_map/ppermute | solution.py:1343
  139.2 37.3 %copy-start.18 = (f32[1280,128]{1,0:T(8,128)}, f32[1280,128]{1,0:T(8,128)S(1)}, u32[]{:S(2)}) copy-start(f32[1280,128]{1,0:T(8,128)S(1)} %get-tuple-element.127.sin_ref) | copy-start | bytes 1966084
  139.2 401.6 %reduce-scatter.4.cloned.1.call-start = ((), (), s32[]{:S(2)}) async-start(), calls=%async_computation.10 | async-start | bytes 5242880 | tf_op jit(solution)/shard_map/reduce_scatter | solution.py:1374
  334.2 267.8 %reduce-scatter.6.cloned.1.call-start = ((), (), s32[]{:S(2)}) async-start(), calls=%async_computation.11 | async-start | bytes 10485760 | tf_op jit(solution)/shard_map/reduce_scatter | solution.py:1374
  529.1 72.8 %collective-permute-start.3 = (bf16[320,2048]{1,0:T(8,128)(2,1)}, bf16[320,2048]{1,0:T(8,128)(2,1)}, u32[]{:S(2)}, u32[]{:S(2)}) collective-permute-start(bf16[320,2048]{1,0:T(8,128)(2,1)} %get-tuple-element.76), channel_id=1, source_target_pairs={{0,2},{2,0},{4,6},{6,4},{1,3},{3,1},{5,7},{7,5},{8,10},{10,8},{12,... | collective-permute-start | bytes 3932168 | tf_op jit(solution)/shard_map/ppermute | solution.py:1392
  530.7 71.2 %collective-permute-start.4 = (bf16[320,2048]{1,0:T(8,128)(2,1)}, bf16[320,2048]{1,0:T(8,128)(2,1)}, u32[]{:S(2)}, u32[]{:S(2)}) collective-permute-start(bf16[320,2048]{1,0:T(8,128)(2,1)} %get-tuple-element.77), channel_id=1, source_target_pairs={{0,4},{2,6},{4,0},{6,2},{1,5},{3,7},{5,1},{7,3},{8,12},{10,14},{12... | collective-permute-start | bytes 3932168 | tf_op jit(solution)/shard_map/ppermute | solution.py:1392
  531.3 70.6 %collective-permute-start.5 = (bf16[320,2048]{1,0:T(8,128)(2,1)}, bf16[320,2048]{1,0:T(8,128)(2,1)}, u32[]{:S(2)}, u32[]{:S(2)}) collective-permute-start(bf16[320,2048]{1,0:T(8,128)(2,1)} %get-tuple-element.78), channel_id=1, source_target_pairs={{0,6},{2,4},{4,2},{6,0},{1,7},{3,5},{5,3},{7,1},{8,14},{10,12},{12... | collective-permute-start | bytes 3932168 | tf_op jit(solution)/shard_map/ppermute | solution.py:1392
  540.9 61.1 %all-to-all-start.1 = ((bf16[4,128,1024]{2,1,0:T(8,128)(2,1)}), bf16[4,128,1024]{2,1,0:T(8,128)(2,1)S(1)}, u32[]{:S(2)}, u32[]{:S(2)}) async-start(bf16[4,128,1024]{2,1,0:T(8,128)(2,1)} %bitcast.58), calls=%async_computation.3 | async-start | bytes 2097152 | tf_op jit(solution)/shard_map/all_to_all | solution.py:1377
  544.4 166.3 %reduce-scatter.8.cloned.1.call-start = ((), (), s32[]{:S(2)}) async-start(), calls=%async_computation.12 | async-start | bytes 3276800 | tf_op jit(solution)/shard_map/reduce_scatter | solution.py:1374
  601.9 15.6 %copy-start.6 = (bf16[4,128,1024]{2,1,0:T(8,128)(2,1)}, bf16[4,128,1024]{2,1,0:T(8,128)(2,1)S(1)}, u32[]{:S(2)}) copy-start(bf16[4,128,1024]{2,1,0:T(8,128)(2,1)S(1)} %all-to-all-done.1.early_and_out_1_.down) | copy-start | bytes 3145732
  617.6 28.5 %all-to-all-start.2 = ((bf16[4,128,2048]{2,1,0:T(8,128)(2,1)}), bf16[4,128,2048]{2,1,0:T(8,128)(2,1)S(1)}, u32[]{:S(2)}, u32[]{:S(2)}) async-start(bf16[4,128,2048]{2,1,0:T(8,128)(2,1)} %bitcast.72), calls=%async_computation.5 | async-start | bytes 4194304 | tf_op jit(solution)/shard_map/all_to_all | solution.py:1377
  621.7 25.7 %copy-start.23 = (f32[2048]{0:T(1024)S(1)}, f32[2048]{0:T(1024)}, u32[]{:S(2)}) copy-start(f32[2048]{0:T(1024)} %copy-done.22) | copy-start | bytes 24580
  (27 other events, 84.5 us)
Sparse Core Ops, SparseCore 0:
  33.4 63.2 all-gather.4
  99.0 81.0 all-gather.6
  181.8 79.2 all-gather.8
  262.5 79.2 all-gather.10
  344.0 75.2 reduce-scatter.3
  426.1 142.9 reduce-scatter.5
  617.7 51.0 reduce-scatter.7

commit v5 on v4

--- a/solution.py
+++ b/solution.py
@@ -411,7 +411,7 @@
     def __init__(self, plane, block, out):
         self.plane, self.block, self.out = plane, block, out
         self.rows = block.shape[0]
-        self.to_x, self.to_y, self.across = {}, {}, {}
+        self.to_x, self.to_y, self.across, self.onward = {}, {}, {}, {}
 
     def start(self, k):
         p, cut = self.plane, chunk(k, self.rows)
@@ -420,24 +420,30 @@
         self.to_y[k] = p.send(self.block.at[cut], target, p.y)
         self.across[0, k] = p.send(self.block.at[cut], target, p.sibling)
 
+    def forward_chunk(self, k):
+        p, out = self.plane, self.out
+        cut = chunk(k, self.rows)
+        from_x, from_y = out.at[p.at_x, p.core, cut], out.at[p.at_y, p.core, cut]
+        p.arrive(self.to_x[k], from_x)
+        if k < CHUNKS // 2:
+            self.onward[k] = p.send(from_x, from_x, p.y)
+        self.across[1, k] = p.send(from_x, from_x, p.sibling)
+        p.arrive(self.to_y[k], from_y)
+        if k >= CHUNKS // 2:
+            self.onward[k] = p.send(from_y, from_y, p.x)
+        self.across[2, k] = p.send(from_y, from_y, p.sibling)
+
+    def forward_far(self):
+        p = self.plane
+        for k in range(CHUNKS):
+            far = self.out.at[p.at_both, p.core, chunk(k, self.rows)]
+            p.arrive(self.onward[k], far)
+            self.across[3, k] = p.send(far, far, p.sibling)
+
     def forward(self):
-        p, out = self.plane, self.out
-        onward = {}
         for k in range(CHUNKS):
-            cut = chunk(k, self.rows)
-            from_x, from_y = out.at[p.at_x, p.core, cut], out.at[p.at_y, p.core, cut]
-            p.arrive(self.to_x[k], from_x)
-            if k < CHUNKS // 2:
-                onward[k] = p.send(from_x, from_x, p.y)
-            self.across[1, k] = p.send(from_x, from_x, p.sibling)
-            p.arrive(self.to_y[k], from_y)
-            if k >= CHUNKS // 2:
-                onward[k] = p.send(from_y, from_y, p.x)
-            self.across[2, k] = p.send(from_y, from_y, p.sibling)
-        for k in range(CHUNKS):
-            far = out.at[p.at_both, p.core, chunk(k, self.rows)]
-            p.arrive(onward[k], far)
-            self.across[3, k] = p.send(far, far, p.sibling)
+            self.forward_chunk(k)
+        self.forward_far()
 
     def finish(self):
         p = self.plane
@@ -713,66 +719,214 @@
     return out.reshape(8 * share, width), middle, beside_out.reshape(8 * share, width)
 
 
+UNITS = ((0, 0), (0, 1), (1, 0), (2, 0), (1, 1), (2, 1), (3, 0), (3, 1))
+
+
 def second_kernel(
-    partial,
-    other_partial,
+    slopes,
+    gate_w,
+    up_w,
     middle,
     cotangent,
     gain,
-    early_first,
-    early_second,
-    out,
+    early,
     grad_middle,
-    pair_own,
-    pair_x,
-    pair_y,
-    pair_both,
+    hidden,
     sent,
     landed,
-    local,
-    hidden,
+    loading,
+    slopes_in,
+    given,
     held,
-    theirs,
-    *scratch,
+    other,
+    near_x,
+    near_y,
+    far_x,
+    far_y,
 ):
     p = Plane(sent, landed)
-    total = Scatter(p, partial, *scratch)
-    share = hidden.shape[0]
-    gather = Gather(p, hidden, out)
-    order = (p.rank, p.at_x, p.at_y, p.at_both)
-    kept, across = [], []
-    for i, rank in enumerate(order):
-        across.append(p.send(other_partial.at[rank, 1 - p.core], theirs.at[i], p.sibling))
-        kept.append(
-            pltpu.make_async_copy(other_partial.at[rank, p.core], held.at[i], local.at[i])
-        )
-        kept[i].start()
+    share, width = near_x.shape
+    half = share // 2
+    units = gate_w.shape[1]
+    order = (p.at_both, p.at_x, p.at_y, p.rank)
+    top, low = halves = pl.ds(0, half), pl.ds(half, half)
+
+    def loads(u):
+        i, h = UNITS[u]
+        for j, core in enumerate((1 - p.core, p.core)):
+            row = (order[i] * 2 + core) * share + h * half
+            yield pltpu.make_async_copy(
+                slopes.at[pl.ds(pl.multiple_of(row, 32), half)],
+                slopes_in.at[u % 2, halves[j]],
+                loading.at[u % 2, j],
+            )
+
+    def compute(u):
+        i, h = UNITS[u]
+        slot = u % 2
+
+        def step(j, carry):
+            cut = pl.ds(pl.multiple_of(j * 1024, 1024), 1024)
+            back = dot(slopes_in[slot, :, :units], gate_w[cut, :], LAST) + dot(
+                slopes_in[slot, :, units:], up_w[cut, :], LAST
+            )
+            given[slot, :, cut] = back[:half].astype(jnp.bfloat16)
+            held[i, halves[h], cut] = back[half:].astype(jnp.bfloat16)
+            return carry
+
+        lax.fori_loop(0, width // 1024, step, 0)
+
+    moves, across = {}, {}
+
+    def settle(u):
+        i, h = UNITS[u]
+        p.arrive(across[u], other.at[i, halves[h]])
+        add_rows(held.at[i], other.at[i], h * half, half)
+        if u == 0:
+            moves["far_x"] = p.send(held.at[0, top], far_x, p.x)
+        elif u == 1:
+            moves["far_y"] = p.send(held.at[0, low], far_y, p.y)
+        elif u == 2:
+            moves["x", 0] = p.send(held.at[1, top], near_x.at[top], p.x)
+        elif u == 3:
+            p.arrive(moves["far_x"], far_x)
+            add_rows(held.at[2], far_x, 0, half)
+            moves["y", 0] = p.send(held.at[2, top], near_y.at[top], p.y)
+        elif u == 4:
+            p.arrive(moves["far_y"], far_y)
+
+            def step(k, carry):
+                rows, at = pl.ds(half + k * SLAB, SLAB), pl.ds(k * SLAB, SLAB)
+                held[1, rows, :] = (
+                    held[1, rows, :].astype(jnp.float32) + far_y[at, :].astype(jnp.float32)
+                ).astype(jnp.bfloat16)
+                return carry
+
+            lax.fori_loop(0, half // SLAB, step, 0)
+            moves["x", 1] = p.send(held.at[1, low], near_x.at[low], p.x)
+        elif u == 5:
+            moves["y", 1] = p.send(held.at[2, low], near_y.at[low], p.y)
+
+    for started in loads(0):
+        started.start()
+    for u in range(8):
+        for started in loads(u):
+            started.wait()
+        if u < 7:
+            for started in loads(u + 1):
+                started.start()
+        if u >= 2:
+            p.copies[across[u - 2]].wait_send()
+        compute(u)
+        i, h = UNITS[u]
+        across[u] = p.send(given.at[u % 2], other.at[i, halves[h]], p.sibling)
+        if u >= 1:
+            settle(u - 1)
+    settle(7)
 
     def work(rows):
         value = middle[rows, :]
         root = row_root(value)
         normed = value * root
-        slope = total.rows(rows) * gain[...]
+        total = sum(part[rows, :].astype(jnp.float32) for part in (held.at[3], near_x, near_y))
+        slope = total * gain[...]
         mean = jnp.mean(slope * normed, axis=-1, keepdims=True)
         gradient = cotangent[rows, :].astype(jnp.float32) + root * (slope - normed * mean)
         grad_middle[rows, :] = gradient
         hidden[rows, :] = (residual_scale * gradient).astype(jnp.bfloat16)
 
+    for h in range(2):
+        p.arrive(moves["x", h], near_x.at[halves[h]])
+        p.arrive(moves["y", h], near_y.at[halves[h]])
+        slabs(h * half, half, work)
+    for u in (6, 7):
+        p.copies[across[u]].wait_send()
+    for number, started in enumerate(p.copies):
+        if number not in across.values():
+            started.wait_send()
+
+
+def second_plane(slopes, gate_w, up_w, middle, cotangent, gain, early):
+    share, width = middle.shape
+    kind = jnp.bfloat16
+    half = share // 2
+    quarter = pltpu.VMEM((4, share, width), kind)
+    return pl.pallas_call(
+        second_kernel,
+        out_shape=[
+            jax.ShapeDtypeStruct((share, width), jnp.float32),
+            jax.ShapeDtypeStruct((share, width), kind),
+        ],
+        in_specs=[ANY] + [VMEM] * 5 + [ANY],
+        out_specs=[VMEM, VMEM],
+        scratch_shapes=wires(8 + 6)
+        + [
+            pltpu.SemaphoreType.DMA((2, 2)),
+            pltpu.VMEM((2, share, slopes.shape[1]), kind),
+            pltpu.VMEM((2, half, width), kind),
+            quarter,
+            quarter,
+            pltpu.VMEM((share, width), kind),
+            pltpu.VMEM((share, width), kind),
+            pltpu.VMEM((half, width), kind),
+            pltpu.VMEM((half, width), kind),
+        ],
+        compiler_params=pltpu.CompilerParams(
+            collective_id=3, has_side_effects=True, vmem_limit_bytes=VMEM_LIMIT
+        ),
+        cost_estimate=lasting(60),
+        name="second_rows",
+    )(slopes, gate_w, up_w, middle, cotangent, gain, early)
+
+
+def spread_kernel(
+    hidden, m, down_w, out, pair_own, pair_x, pair_y, pair_both,
+    sent, landed, local, loading, m_in, given, held, theirs,
+):
+    p = Plane(sent, landed)
+    share, width = hidden.shape
+    gather = Gather(p, hidden, out)
     for k in range(CHUNKS):
-        if k % (CHUNKS // 2) == 0:
-            total.ready(k // (CHUNKS // 2))
-        slabs(k * (share // CHUNKS), share // CHUNKS, work)
         gather.start(k)
     mine = pltpu.make_async_copy(hidden, out.at[p.rank, p.core], local.at[4])
     mine.start()
+    order = (p.rank, p.at_x, p.at_y, p.at_both)
+    halves = pl.ds(0, share), pl.ds(share, share)
+
+    def loads(i):
+        for j, core in enumerate((1 - p.core, p.core)):
+            yield pltpu.make_async_copy(
+                m.at[order[i], core], m_in.at[i % 2, halves[j]], loading.at[i % 2, j]
+            )
+
+    across = []
+    for started in loads(0):
+        started.start()
+    for i in range(4):
+        for started in loads(i):
+            started.wait()
+        if i < 3:
+            for started in loads(i + 1):
+                started.start()
+
+        def step(j, carry, i=i):
+            cut = pl.ds(pl.multiple_of(j * 512, 512), 512)
+            value = dot(m_in[i % 2], down_w[cut, :], LAST)
+            given[i, :, cut] = value[:share].astype(jnp.bfloat16)
+            held[i, :, cut] = value[share:].astype(jnp.bfloat16)
+            return carry
+
+        lax.fori_loop(0, width // 512, step, 0)
+        across.append(p.send(given.at[i], theirs.at[i], p.sibling))
+        gather.forward_chunk(i)
+    kept = []
     for i in range(4):
         p.arrive(across[i], theirs.at[i])
-        kept[i].wait()
         add_rows(held.at[i], theirs.at[i], 0, share)
         target = (pair_own, pair_x, pair_y, pair_both)[i]
-        kept[i] = pltpu.make_async_copy(held.at[i], target, local.at[i])
+        kept.append(pltpu.make_async_copy(held.at[i], target, local.at[i]))
         kept[i].start()
-    gather.forward()
+    gather.forward_far()
     gather.finish()
     p.finish()
     mine.wait()
@@ -780,38 +934,32 @@
         started.wait()
 
 
-def second_plane(partial, other_partial, middle, cotangent, gain, early):
-    share, width = middle.shape
+def spread_plane(hidden, m, down_w):
+    share, width = hidden.shape
+    units = m.shape[1]
     full = jax.ShapeDtypeStruct((4, 2, share, width), jnp.bfloat16)
-    quarter = jax.ShapeDtypeStruct((4, share, width), jnp.bfloat16)
-    out, grad_middle, *pairs = pl.pallas_call(
-        second_kernel,
-        out_shape=[full, jax.ShapeDtypeStruct((share, width), jnp.float32)]
-        + [jax.ShapeDtypeStruct((share, width), jnp.bfloat16)] * 4,
-        in_specs=[ANY, ANY, VMEM, VMEM, VMEM, ANY, ANY],
-        out_specs=[ANY, VMEM] + [ANY] * 4,
-        scratch_shapes=wires(GATHER_COPIES + SCATTER_COPIES + 4)
+    quarter = pltpu.VMEM((4, share, width), jnp.bfloat16)
+    out, *pairs = pl.pallas_call(
+        spread_kernel,
+        out_shape=[full] + [jax.ShapeDtypeStruct((share, width), jnp.bfloat16)] * 4,
+        in_specs=[VMEM, ANY, VMEM],
+        out_specs=[ANY] * 5,
+        scratch_shapes=wires(GATHER_COPIES + 4)
         + [
             pltpu.SemaphoreType.DMA((5,)),
-            pltpu.VMEM((share, width), jnp.bfloat16),
-            pltpu.VMEM(quarter.shape, jnp.bfloat16),
-            pltpu.VMEM(quarter.shape, jnp.bfloat16),
-        ]
-        + scatter_scratch(share, width),
+            pltpu.SemaphoreType.DMA((2, 2)),
+            pltpu.VMEM((2, 2 * share, units), jnp.bfloat16),
+            quarter,
+            quarter,
+            quarter,
+        ],
         compiler_params=pltpu.CompilerParams(
-            collective_id=3, has_side_effects=True, vmem_limit_bytes=VMEM_LIMIT
+            collective_id=7, has_side_effects=True, vmem_limit_bytes=VMEM_LIMIT
         ),
-        cost_estimate=lasting(100),
-        name="second_rows",
-    )(
-        partial.reshape(full.shape),
-        other_partial.reshape(full.shape),
-        middle,
-        cotangent,
-        gain,
-        *early,
-    )
-    return out.reshape(8 * share, width), grad_middle, pairs
+        cost_estimate=lasting(60),
+        name="spread_rows",
+    )(hidden, m.reshape(4, 2, share, units), down_w)
+    return out.reshape(8 * share, width), pairs
 
 
 def lane_sums(pairs):
@@ -1074,8 +1222,8 @@
         m[:, cut] = (gate_part * sigmoid * up_part).astype(jnp.bfloat16)
 
 
-def ffn_second_kernel(grad, gate, up, m, gate_w, up_w, down_w, early, slopes, forward, back):
-    units = gate_w.shape[1]
+def ffn_slopes_kernel(grad, gate, up, down_w, early, slopes):
+    units = down_w.shape[1]
     for j in range(units // 256):
         cut = slice(j * 256, j * 256 + 256)
         grad_part = dot(grad[...], down_w[:, cut])
@@ -1086,13 +1234,6 @@
         slopes[:, cut] = (grad_part * up_part * slope).astype(jnp.bfloat16)
         slopes[:, units + j * 256 : units + j * 256 + 256] = (
             grad_part * gate_part * sigmoid
-        ).astype(jnp.bfloat16)
-    for j in range(gate_w.shape[0] // 512):
-        cut = slice(j * 512, j * 512 + 512)
-        forward[:, cut] = dot(m[...], down_w[cut, :], LAST).astype(jnp.bfloat16)
-        back[:, cut] = (
-            dot(slopes[:, :units], gate_w[cut, :], LAST)
-            + dot(slopes[:, units:], up_w[cut, :], LAST)
         ).astype(jnp.bfloat16)
 
 
@@ -1165,33 +1306,60 @@
     )(values, gain, weight, up, down)
 
 
-def attention_weights_kernel(hidden, back, grad, attended, *early_and_out):
-    out = early_and_out[-1]
+def attention_weights_kernel(hidden, back, grad, attended, weight, moving, *rest):
+    out, rows_out, moved, sent, landed, local = rest[-6:]
+    step, last = pl.program_id(0), pl.num_programs(0) - 1
+
+    @pl.when(step == 0)
+    def start():
+        p = Plane(sent, landed, diagonal=True)
+        pltpu.make_async_copy(moving.at[p.rank], moved.at[p.rank], local).start()
+        for partner, rank in ((p.both, p.at_both), (p.x, p.at_x), (p.y, p.at_y)):
+            p.send(moving.at[rank], moved.at[p.rank], partner)
+
     columns = back.shape[1]
     out[:, :columns] = dot(hidden[...], back[...], FIRST).astype(jnp.bfloat16)
     out[:, columns:] = dot(grad[...], attended[...], FIRST).astype(jnp.bfloat16)
-
-
-def attention_weights(hidden, back, grad, attended, early):
+    rows_out[...] = dot(back[...], weight[...], LAST).astype(jnp.bfloat16)
+
+    @pl.when(step == last)
+    def finish():
+        p = Plane(sent, landed, entered=True)
+        for number, rank in enumerate((p.at_both, p.at_x, p.at_y)):
+            move = p.copy(number, moving.at[rank], moved.at[rank], p.x)
+            move.wait_recv()
+            move.wait_send()
+        pltpu.make_async_copy(moving.at[p.rank], moved.at[p.rank], local).wait()
+
+
+def attention_weights(hidden, back, grad, attended, weight, moving, early):
     count, width = hidden.shape
     first, second = back.shape[1], attended.shape[1]
-    tall = pl.BlockSpec((count, 512), lambda i: (0, i))
+    tall = pl.BlockSpec((count, 256), lambda i: (0, i))
     return pl.pallas_call(
         attention_weights_kernel,
-        grid=(width // 512,),
+        grid=(width // 256,),
         in_specs=[
             tall,
             pl.BlockSpec((count, first), lambda i: (0, 0)),
             tall,
             pl.BlockSpec((count, second), lambda i: (0, 0)),
+            pl.BlockSpec((256, first), lambda i: (i, 0)),
         ]
-        + [ANY] * len(early),
-        out_specs=pl.BlockSpec((512, first + second), lambda i: (i, 0)),
-        out_shape=jax.ShapeDtypeStruct((width, first + second), jnp.bfloat16),
-        compiler_params=pltpu.CompilerParams(vmem_limit_bytes=VMEM_LIMIT),
-        cost_estimate=lasting(12),
+        + [ANY] * (1 + len(early)),
+        out_specs=[pl.BlockSpec((256, first + second), lambda i: (i, 0)), tall, ANY],
+        out_shape=[
+            jax.ShapeDtypeStruct((width, first + second), jnp.bfloat16),
+            jax.ShapeDtypeStruct((count, width), jnp.bfloat16),
+            jax.ShapeDtypeStruct(moving.shape, moving.dtype),
+        ],
+        scratch_shapes=wires(3) + [pltpu.SemaphoreType.DMA],
+        compiler_params=pltpu.CompilerParams(
+            collective_id=8, has_side_effects=True, vmem_limit_bytes=VMEM_LIMIT
+        ),
+        cost_estimate=lasting(25),
         name="attention_weights",
-    )(hidden, back, grad, attended, *early)
+    )(hidden, back, grad, attended, weight, moving, *early)
 
 
 ROW_TILE = 256
@@ -1360,13 +1528,13 @@
         [units, units, units],
     )
     grad_down = dot(ffn_grad, hidden, FIRST).astype(jnp.bfloat16)
-    slopes, ffn_out, grad_second = row_tiles(
-        ffn_second_kernel,
-        "ffn_second",
-        [ffn_grad, gate_proj, up_proj, hidden],
-        [gate_full, up_full, down_full],
+    (slopes,) = row_tiles(
+        ffn_slopes_kernel,
+        "ffn_slopes",
+        [ffn_grad, gate_proj, up_proj],
+        [down_full],
         [grad_down],
-        [2 * units, gate_full.shape[0], gate_full.shape[0]],
+        [2 * units],
     )
     grad_gate_up = dot(hidden_second, slopes, FIRST).astype(jnp.bfloat16)
 
@@ -1380,19 +1548,18 @@
         return jnp.transpose(gradient, (1, 0, 2)).reshape(depth, -1).astype(jnp.float32)
 
     if square:
-        attn_grad, grad_middle, ffn_pairs = second_plane(
-            grad_second,
-            ffn_out,
-            middle,
-            cotangent_half,
-            ffn_scale[None, :],
-            [grad_down, grad_gate_up],
+        grad_middle, my_attn_grad = second_plane(
+            slopes, gate_full, up_full, middle, cotangent_half, ffn_scale[None, :], grad_gate_up
         )
+        attn_grad, ffn_pairs = spread_plane(my_attn_grad, hidden, down_full)
         ffn_parts = [ffn_pairs[0]] + [
             lax.ppermute(ffn_pairs[step], "context", context_pairs(step)) for step in (1, 2, 3)
         ]
     else:
         root = inverse_root(middle)
+        ffn_out = dot(hidden, down_full, LAST)
+        grad_second = dot(slopes[:, :units], gate_full, LAST)
+        grad_second += dot(slopes[:, units:], up_full, LAST)
         grad_middle = grad_result + norm_backward(
             scatter_rows(grad_second) * ffn_scale, middle * root, root
         )
@@ -1403,12 +1570,23 @@
     grad_gate_up = sum_groups(grad_gate_up)
     back = attention_backward(places, starts, grad_attended, kept, tables, [grad_down])
     grad_down = hand_back(grad_down)
-    grad_attn = attention_weights(
-        hidden_first, back, attn_grad, attended, [grad_gate_up, grad_down, *ffn_parts[1:]]
-    )
+    if square:
+        grad_attn, grad_first, grad_gate_up = attention_weights(
+            hidden_first,
+            back,
+            attn_grad,
+            attended,
+            qkv_full,
+            grad_gate_up.reshape(groups, depth, -1),
+            [grad_down, *ffn_parts[1:]],
+        )
+    else:
+        grad_attn = jnp.concatenate(
+            [dot(hidden_first, back, FIRST), dot(attn_grad, attended, FIRST)], axis=1
+        ).astype(jnp.bfloat16)
+        grad_first = dot(back, qkv_full, LAST).astype(jnp.bfloat16)
+        grad_gate_up = hand_back(grad_gate_up)
     grad_attn = sum_groups(grad_attn)
-    grad_gate_up = hand_back(grad_gate_up)
-    grad_first = dot(back, qkv_full, LAST).astype(jnp.bfloat16)
     if square:
         grad_tokens, result, ffn_sums = last_plane(
             grad_first,

time: 756 us -> 727 us (0.962)
  waiting for transfers between devices: 29.5 us -> 14.1 us
  matrix products: 72.4 us -> 61.7 us
    pallas_call x2, Pallas kernels: 84.4 us -> 51.1 us  [row_tiles(): pl.pallas_call(kernel, grid=(count // ROW_TILE,), in_specs=[tile(r.shape[...]
    pallas_call x2 -> x3, Pallas kernels: 113 us -> 144 us  [the longest x1 63.4 us: second_plane(): pl.pallas_call(second_kernel, out_shape=[jax.ShapeDtypeStruct((share, wid...]
    all_to_all x2 -> x1, waiting for transfers between devices: 14 us -> 0.01 us  [hand_back(): return lax.all_to_all(gradient.reshape(groups, depth, -1), 'context', 0, 0)]
    dot_general x5 -> x4, matrix products: 72.4 us -> 61.7 us  [dot(): lax.dot_general(left_side, right_side, dims, preferred_element_type=jnp.f...]
    unnamed x79 -> x83, local copies, waits for them, and re-layouts: 27.6 us -> 29.6 us
  transfers between devices with their start and end apart: 15 -> 14, of which waited for: 3 -> 2; matrix products, arithmetic and copies ran while one was open for 11% -> 10% of each run, Pallas kernels for 69% -> 70%
where the time goes in v5:
time: 727 us; the launch traced here: 719 us
  Pallas kernels  555 us (76%)
  matrix products  61.7 us (8%)
  local copies, waits for them, and re-layouts  40 us (6%)
  blocking collectives  16.4 us (2%)
  between operations  14.9 us (2%)
  waiting for transfers between devices  14.1 us (2%)
  starting transfers between devices  11 us (2%)
    pallas_call x1, Pallas kernels, middle_plane(): pl.pallas_call(middle_kernel, out_shape=[full, jax.ShapeDtypeStruct((shar...  95.8 us
    pallas_call x1, Pallas kernels, second_plane(): pl.pallas_call(second_kernel, out_shape=[jax.ShapeDtypeStruct((share, wid...  63.4 us
    pallas_call x1, Pallas kernels, start_plane(): pl.pallas_call(start_kernel, out_shape=[jax.ShapeDtypeStruct((4, 2, share...  62.3 us
    dot_general x4, matrix products, dot(): lax.dot_general(left_side, right_side, dims, preferred_element_type=jnp.f...  61.7 us
    pallas_call x1, Pallas kernels, last_plane(): pl.pallas_call(last_kernel, out_shape=[jax.ShapeDtypeStruct((2, share, wi...  59.5 us
    pallas_call x1, Pallas kernels, attention_backward(): pl.pallas_call(attention_backward_kernel, out_shape=jax.ShapeDtypeStruct(...  52.7 us
    pallas_call x2, Pallas kernels, row_tiles(): pl.pallas_call(kernel, grid=(count // ROW_TILE,), in_specs=[tile(r.shape[...  51.1 us
    pallas_call x1, Pallas kernels, spread_plane(): pl.pallas_call(spread_kernel, out_shape=[full] + [jax.ShapeDtypeStruct((s...  50 us
  transfers between devices with their start and end apart: 14, of which 2 were waited for; matrix products, arithmetic and copies ran while one was open for 10% of the time, Pallas kernels for 70%

profile of v5, /device:TPU:0, one launch (start us, length us, event | category | flops | bytes accessed | tf_op | source)
XLA Modules:
  0.0 718.7 jit_solution(11098900855966847808)
XLA Ops:
  12.8 1.8 copy.44
  16.8 16.4 %all_to_all.10 = bf16[4,128,768]{2,1,0:T(8,128)(2,1)} all-to-all(bf16[4,128,768]{2,1,0:T(8,128)(2,1)S(1)} %concatenate.9.weights), channel_id=1, replica_groups=mesh['fsdp'=4,'context'=4,'tensor'=2] {'context'}, dimensions={0} | all-to-all | bytes 1572864 | tf_op jit(solution)/shard_map/all_to_all | solution.py:1445
  34.6 62.3 %gather_tokens.1 = (bf16[4,2,320,2048]{3,2,1,0:T(8,128)(2,1)}, bf16[4,128,1024]{2,1,0:T(8,128)(2,1)}, bf16[640,2048]{1,0:T(8,128)(2,1)}, bf16[320,2048]{1,0:T(8,128)(2,1)S(1)}) custom-call(bf16[320,2048]{1,0:T(8,128)(2,1)S(1)} %constant_dynamic-slice_fusion.1.block.residual, bf16[128,4096]{1,0:T(8,128)(2,1)S(1)} %copy-done.10, bf16[640,2048]{1,0:T(8,128)(2,1)} %cotangent.1), custom_call_target="tpu_custom_call" | custom-call | bytes 180000000 | tf_op jit(solution)/shard_map/gather_tokens/pallas_call | solution.py:617
  100.4 1.7 slice.30.weight
  104.6 28.8 %first_rows.1 = (bf16[2560,2048]{1,0:T(8,128)(2,1)}, f32[2560,384]{1,0:T(8,128)}, bf16[4,128,1024]{2,1,0:T(8,128)(2,1)S(1)}, bf16[4,128,1024]{2,1,0:T(8,128)(2,1)}) custom-call(bf16[2560,2048]{1,0:T(8,128)(2,1)} %bitcast.68, f32[1,2048]{1,0:T(1,128)S(1)} %bitcast.58, bf16[2048,384]{1,0:T(8,128)(2,1)S(1)} %slice.30.weight, bf16[128,4096]{1,0:T(8,128)(2,1)S(1)} %copy-done.12, ...), custom_call_target="tpu_custom_call" | custom-call | bytes 75000000 | tf_op jit(solution)/shard_map/first_rows/pallas_call | solution.py:1278
  138.1 2.4 fusion.2
  141.8 37.1 %attention_forward.1 = (bf16[2560,256]{1,0:T(8,128)(2,1)S(1)}, bf16[2560,256]{1,0:T(8,128)(2,1)S(1)}, bf16[2560,256]{1,0:T(8,128)(2,1)S(1)}, bf16[2560,256]{1,0:T(8,128)(2,1)}, f32[4,1,2560]{2,1,0:T(1,128)S(1)}) custom-call(s32[20]{0:T(128)S(1)} %compare_select_fusion.1.to_ref, s32[20]{0:T(128)S(1)} %bitcast.62, f32[2560,384]{1,0:T(8,128)} %get-tuple-element.56.raw_ref, ...), custom_call_target="tpu_custom_call" | custom-call | flops 5368709120 | bytes 10485760 | tf_op jit(solution)/shard_map/attention_forward/pallas_call | solution.py:311
  178.9 7.7 %convolution_convert_fusion = bf16[2560,2048]{1,0:T(8,128)(2,1)} fusion(bf16[2560,256]{1,0:T(8,128)(2,1)S(1)} %get-tuple-element.57.attended, bf16[2048,768]{1,0:T(8,128)(2,1)} %all-gather.5.cloned.1.call-done), kind=kOutput, calls=%fused_computation | convolution fusion | flops 2689597440 | bytes 12845056 | tf_op jit(solution)/shard_map/dot_general | solution.py:31
  186.6 7.7 %collective-permute-done.1.from_y = bf16[320,2048]{1,0:T(8,128)(2,1)} collective-permute-done((bf16[320,2048]{1,0:T(8,128)(2,1)}, bf16[320,2048]{1,0:T(8,128)(2,1)}, u32[]{:S(2)}, u32[]{:S(2)}) %collective-permute-start.1) | collective-permute-done | bytes 1310752 | tf_op jit(solution)/shard_map/ppermute | solution.py:1511
  194.3 95.8 %middle_rows.1 = (bf16[4,2,320,2048]{3,2,1,0:T(8,128)(2,1)}, f32[320,2048]{1,0:T(8,128)}, bf16[4,2,320,2048]{3,2,1,0:T(8,128)(2,1)}) custom-call(bf16[4,2,320,2048]{3,2,1,0:T(8,128)(2,1)} %bitcast.64, bf16[320,2048]{1,0:T(8,128)(2,1)S(1)} %copy-done.3, f32[1,2048]{1,0:T(1,128)S(1)} %bitcast.60, bf16[2,320,2048]{2,1,0:T(8,128)(2,1)} %bitcast.75, ...), custom_call_target="tpu_custom_call" | custom-call | bytes 300000000 | tf_op jit(solution)/shard_map/middle_rows/pallas_call | solution.py:700
  290.1 29.2 %ffn_first.1 = (bf16[2560,1024]{1,0:T(8,128)(2,1)}, bf16[2560,1024]{1,0:T(8,128)(2,1)}, bf16[2560,1024]{1,0:T(8,128)(2,1)}) custom-call(bf16[2560,2048]{1,0:T(8,128)(2,1)} %bitcast.93, bf16[2048,1024]{1,0:T(8,128)(2,1)} %all-gather.7.cloned.1.call-done.gate_w, bf16[2048,1024]{1,0:T(8,128)(2,1)} %all-gather.9.cloned.1.call-done.up_w), custom_call_target="tpu_custom_call" | custom-call | flops 21474836480 | bytes 53687092 | tf_op jit(solution)/shard_map/ffn_first/pallas_call | solution.py:1378
  319.3 16.9 %convolution_convert_fusion.3.early = bf16[2048,1024]{1,0:T(8,128)(2,1)} fusion(bf16[2560,2048]{1,0:T(8,128)(2,1)} %bitcast.69, bf16[2560,1024]{1,0:T(8,128)(2,1)} %get-tuple-element.67), kind=kOutput, calls=%fused_computation.3 | convolution fusion | flops 10739515392 | bytes 19922944 | tf_op jit(solution)/shard_map/dot_general | solution.py:31
  336.3 6.2 all-gather.11.cloned.1.call-done.down_w
  342.5 21.9 %ffn_slopes.1.slopes = bf16[2560,2048]{1,0:T(8,128)(2,1)} custom-call(bf16[2560,2048]{1,0:T(8,128)(2,1)} %bitcast.70, bf16[2560,1024]{1,0:T(8,128)(2,1)} %get-tuple-element.64.gate, bf16[2560,1024]{1,0:T(8,128)(2,1)} %get-tuple-element.65.up, bf16[2048,1024]{1,0:T(8,128)(2,1)} %all-gather.11.cloned.1.call-done.down_w, ...), custom_call_target="tpu_custom_call" | custom-call | flops 10737418240 | bytes 26843544 | tf_op jit(solution)/shard_map/ffn_slopes/pallas_call | solution.py:1378
  364.4 28.8 %convolution_convert_fusion.1.early = bf16[2048,2048]{1,0:T(8,128)(2,1)} fusion(bf16[2560,2048]{1,0:T(8,128)(2,1)} %bitcast.94, bf16[2560,2048]{1,0:T(8,128)(2,1)} %ffn_slopes.1.slopes), kind=kOutput, calls=%fused_computation.1 | convolution fusion | flops 21479030784 | bytes 29360128 | tf_op jit(solution)/shard_map/dot_general | solution.py:31
  394.7 63.4 %second_rows.1 = (f32[320,2048]{1,0:T(8,128)S(1)}, bf16[320,2048]{1,0:T(8,128)(2,1)S(1)}) custom-call(bf16[2560,2048]{1,0:T(8,128)(2,1)} %ffn_slopes.1.slopes, bf16[2048,1024]{1,0:T(8,128)(2,1)} %all-gather.7.cloned.1.call-done.gate_w, bf16[2048,1024]{1,0:T(8,128)(2,1)} %all-gather.9.cloned.1.call-done.up_w, f32[320,2048]{1,0:T(8,128)} %get-tuple-element.68.middle, ...), custom_call_target="tpu_custom_call" | custom-call | bytes 180000000 | tf_op jit(solution)/shard_map/second_rows/pallas_call | solution.py:854
  460.7 50.0 %spread_rows.1 = (bf16[4,2,320,2048]{3,2,1,0:T(8,128)(2,1)}, bf16[320,2048]{1,0:T(8,128)(2,1)S(1)}, bf16[320,2048]{1,0:T(8,128)(2,1)}, bf16[320,2048]{1,0:T(8,128)(2,1)}, bf16[320,2048]{1,0:T(8,128)(2,1)}) custom-call(bf16[320,2048]{1,0:T(8,128)(2,1)} %copy-done.18, bf16[4,2,320,1024]{3,2,1,0:T(8,128)(2,1)} %bitcast.71, ...), custom_call_target="tpu_custom_call" | custom-call | bytes 180000000 | tf_op jit(solution)/shard_map/spread_rows/pallas_call | solution.py:942
  515.2 8.2 %convolution_convert_fusion.2.grad_ref = bf16[2560,256]{1,0:T(8,128)(2,1)} fusion(bf16[2560,2048]{1,0:T(8,128)(2,1)} %bitcast.65, bf16[2048,768]{1,0:T(8,128)(2,1)} %all-gather.5.cloned.1.call-done), kind=kOutput, calls=%fused_computation.2 | convolution fusion | flops 2685009920 | bytes 12845056 | tf_op jit(solution)/shard_map/dot_general | solution.py:31
  523.5 3.5 all-to-all-start.1
  532.0 52.7 %attention_backward.1.back = bf16[2560,384]{1,0:T(8,128)(2,1)} custom-call(s32[20]{0:T(128)S(1)} %compare_select_fusion.1.to_ref, s32[20]{0:T(128)S(1)} %bitcast.63, bf16[2560,256]{1,0:T(8,128)(2,1)S(1)} %copy-done.29, bf16[2560,256]{1,0:T(8,128)(2,1)S(1)} %copy-done.31, bf16[2560,256]{1,0:T(8,128)(2,1)} %copy-done.32, ...), custom_call_target="tpu_custom_call" | custom-call | flops 13421772800 | bytes 10485760 | tf_op jit(solution)/shard_map/attention_backward/pallas_call | solution.py:329
  586.5 31.0 %attention_weights.1 = (bf16[2048,640]{1,0:T(8,128)(2,1)}, bf16[2560,2048]{1,0:T(8,128)(2,1)}, bf16[4,128,2048]{2,1,0:T(8,128)(2,1)}) custom-call(bf16[2560,2048]{1,0:T(8,128)(2,1)} %get-tuple-element.55.hidden, bf16[2560,384]{1,0:T(8,128)(2,1)} %attention_backward.1.back, bf16[2560,2048]{1,0:T(8,128)(2,1)} %bitcast.66, bf16[2560,256]{1,0:T(8,128)(2,1)S(1)} %copy-done.9, ...), custom_call_target="tpu_custom_call" | custom-call | bytes 75000000 | tf_op jit(solution)/shard_map/attention_weights/pallas_call | solution.py:1339
  620.4 59.5 %last_rows.1 = (f32[2,320,2048]{2,1,0:T(8,128)}, bf16[2,320,2048]{2,1,0:T(8,128)(2,1)}, f32[128,128]{1,0:T(8,128)S(1)}) custom-call(bf16[4,2,320,2048]{3,2,1,0:T(8,128)(2,1)} %bitcast.67, bf16[320,2048]{1,0:T(8,128)(2,1)S(1)} %copy-done.3, f32[320,2048]{1,0:T(8,128)} %copy-done.15, f32[1,2048]{1,0:T(1,128)S(1)} %bitcast.59, ...), custom_call_target="tpu_custom_call" | custom-call | bytes 210000000 | tf_op jit(solution)/shard_map/last_rows/pallas_call | solution.py:1052
  680.5 14.0 %exchange_blocks.1 = (bf16[4,128,640]{2,1,0:T(8,128)(2,1)}, f32[128,128]{1,0:T(8,128)}) custom-call(bf16[4,128,640]{2,1,0:T(8,128)(2,1)} %bitcast.81, bf16[4,128,768]{2,1,0:T(8,128)(2,1)} %copy-done.33, f32[128,128]{1,0:T(8,128)} %copy-done.24), custom_call_target="tpu_custom_call" | custom-call | bytes 24000000 | tf_op jit(solution)/shard_map/exchange_blocks/pallas_call | solution.py:1115
  700.1 9.3 %finish.1 = (f32[128,1024]{1,0:T(8,128)}, f32[128,512]{1,0:T(8,128)S(1)}, f32[1024,128]{1,0:T(8,128)}, f32[128,4096]{1,0:T(8,128)}, f32[128,4096]{1,0:T(8,128)},...) custom-call(bf16[4,128,640]{2,1,0:T(8,128)(2,1)S(1)} %copy-done.21, ...), custom_call_target="tpu_custom_call" | custom-call | bytes 36000000 | tf_op jit(solution)/shard_map/finish/pallas_call | solution.py:1169
  (134 shorter events, 47.5 us)
Async XLA Ops:
  7.2 26.1 %copy-start = (bf16[640,2048]{1,0:T(8,128)(2,1)S(1)}, bf16[640,2048]{1,0:T(8,128)(2,1)}, u32[]{:S(2)}) copy-start(bf16[640,2048]{1,0:T(8,128)(2,1)} %param.14) | copy-start | bytes 7864324
  7.2 93.2 %all-gather.5.cloned.1.call-start = ((), (), s32[]{:S(2)}) async-start(), calls=%async_computation.5 | async-start | bytes 3932160 | tf_op jit(solution)/shard_map/all_gather | solution.py:1447
  16.8 80.0 %copy-start.33 = (bf16[4,128,768]{2,1,0:T(8,128)(2,1)}, bf16[4,128,768]{2,1,0:T(8,128)(2,1)S(1)}, u32[]{:S(2)}) copy-start(bf16[4,128,768]{2,1,0:T(8,128)(2,1)S(1)} %concatenate.9.weights) | copy-start | bytes 2359300
  33.3 256.8 %all-gather.7.cloned.1.call-start = ((), (), s32[]{:S(2)}) async-start(), calls=%async_computation.6 | async-start | bytes 5242880 | tf_op jit(solution)/shard_map/all_gather | solution.py:1465
  34.6 64.5 %copy-start.34 = (bf16[4096,128]{1,0:T(8,128)(2,1)S(1)}, bf16[4096,128]{1,0:T(8,128)(2,1)}, u32[]{:S(2)}) copy-start(bf16[4096,128]{1,0:T(8,128)(2,1)} %param.24) | copy-start | bytes 3145732
  99.0 191.1 %all-gather.9.cloned.1.call-start = ((), (), s32[]{:S(2)}) async-start(), calls=%async_computation.7 | async-start | bytes 5242880 | tf_op jit(solution)/shard_map/all_gather | solution.py:1465
  102.1 31.3 %copy-start.4 = (bf16[2048,384]{1,0:T(8,128)(2,1)}, bf16[2048,384]{1,0:T(8,128)(2,1)S(1)}, u32[]{:S(2)}) copy-start(bf16[2048,384]{1,0:T(8,128)(2,1)S(1)} %slice.30.weight) | copy-start | bytes 4718596
  104.6 33.5 %copy-start.28 = (s32[1,20]{1,0:T(1,128)S(1)}, s32[1,20]{1,0:T(1,128)}, u32[]{:S(2)}) copy-start(s32[1,20]{1,0:T(1,128)} %param.26) | copy-start | bytes 244
  104.6 33.5 %copy-start.37 = (s32[1,20]{1,0:T(1,128)S(1)}, s32[1,20]{1,0:T(1,128)}, u32[]{:S(2)}) copy-start(s32[1,20]{1,0:T(1,128)} %param.25) | copy-start | bytes 244
  134.4 208.1 %all-gather.11.cloned.1.call-start = ((), (), s32[]{:S(2)}) async-start(), calls=%async_computation.8 | async-start | bytes 5242880 | tf_op jit(solution)/shard_map/all_gather | solution.py:1465
  134.5 52.1 %collective-permute-start = (bf16[320,2048]{1,0:T(8,128)(2,1)}, bf16[320,2048]{1,0:T(8,128)(2,1)S(1)}, u32[]{:S(2)}, u32[]{:S(2)}) collective-permute-start(bf16[320,2048]{1,0:T(8,128)(2,1)} %copy-done.27), channel_id=1, source_target_pairs={{0,2},{2,0},{4,6},{6,4},{1,3},{3,1},{5,7},{7,5},{8,10},{10,8},{12,... | collective-permute-start | bytes 3932168 | tf_op jit(solution)/shard_map/ppermute | solution.py:1511
  135.5 58.8 %collective-permute-start.1 = (bf16[320,2048]{1,0:T(8,128)(2,1)}, bf16[320,2048]{1,0:T(8,128)(2,1)}, u32[]{:S(2)}, u32[]{:S(2)}) collective-permute-start(bf16[320,2048]{1,0:T(8,128)(2,1)} %copy-done.27), channel_id=1, source_target_pairs={{0,4},{2,6},{4,0},{6,2},{1,5},{3,7},{5,1},{7,3},{8,12},{10,14},{12... | collective-permute-start | bytes 3932168 | tf_op jit(solution)/shard_map/ppermute | solution.py:1511
  136.5 57.8 %collective-permute-start.2 = (bf16[320,2048]{1,0:T(8,128)(2,1)}, bf16[320,2048]{1,0:T(8,128)(2,1)}, u32[]{:S(2)}, u32[]{:S(2)}) collective-permute-start(bf16[320,2048]{1,0:T(8,128)(2,1)} %copy-done.27), channel_id=1, source_target_pairs={{0,6},{2,4},{4,2},{6,0},{1,7},{3,5},{5,3},{7,1},{8,14},{10,12},{12... | collective-permute-start | bytes 3932168 | tf_op jit(solution)/shard_map/ppermute | solution.py:1511
  141.5 37.3 %copy-start.22 = (f32[1280,128]{1,0:T(8,128)}, f32[1280,128]{1,0:T(8,128)S(1)}, u32[]{:S(2)}) copy-start(f32[1280,128]{1,0:T(8,128)S(1)} %get-tuple-element.129.sin_ref) | copy-start | bytes 1966084
  141.6 381.9 %reduce-scatter.4.cloned.1.call-start = ((), (), s32[]{:S(2)}) async-start(), calls=%async_computation.9 | async-start | bytes 5242880 | tf_op jit(solution)/shard_map/reduce_scatter | solution.py:1542
  336.2 248.6 %reduce-scatter.6.cloned.1.call-start = ((), (), s32[]{:S(2)}) async-start(), calls=%async_computation.10 | async-start | bytes 10485760 | tf_op jit(solution)/shard_map/reduce_scatter | solution.py:1542
  511.7 73.1 %collective-permute-start.3 = (bf16[320,2048]{1,0:T(8,128)(2,1)}, bf16[320,2048]{1,0:T(8,128)(2,1)}, u32[]{:S(2)}, u32[]{:S(2)}) collective-permute-start(bf16[320,2048]{1,0:T(8,128)(2,1)} %get-tuple-element.75), channel_id=1, source_target_pairs={{0,2},{2,0},{4,6},{6,4},{1,3},{3,1},{5,7},{7,5},{8,10},{10,8},{12,... | collective-permute-start | bytes 3932168 | tf_op jit(solution)/shard_map/ppermute | solution.py:1556
  513.2 71.6 %collective-permute-start.4 = (bf16[320,2048]{1,0:T(8,128)(2,1)}, bf16[320,2048]{1,0:T(8,128)(2,1)}, u32[]{:S(2)}, u32[]{:S(2)}) collective-permute-start(bf16[320,2048]{1,0:T(8,128)(2,1)} %get-tuple-element.76), channel_id=1, source_target_pairs={{0,4},{2,6},{4,0},{6,2},{1,5},{3,7},{5,1},{7,3},{8,12},{10,14},{12... | collective-permute-start | bytes 3932168 | tf_op jit(solution)/shard_map/ppermute | solution.py:1556
  514.1 70.7 %collective-permute-start.5 = (bf16[320,2048]{1,0:T(8,128)(2,1)}, bf16[320,2048]{1,0:T(8,128)(2,1)}, u32[]{:S(2)}, u32[]{:S(2)}) collective-permute-start(bf16[320,2048]{1,0:T(8,128)(2,1)} %get-tuple-element.77), channel_id=1, source_target_pairs={{0,6},{2,4},{4,2},{6,0},{1,7},{3,5},{5,3},{7,1},{8,14},{10,12},{12... | collective-permute-start | bytes 3932168 | tf_op jit(solution)/shard_map/ppermute | solution.py:1556
  523.5 61.3 %all-to-all-start.1 = ((bf16[4,128,1024]{2,1,0:T(8,128)(2,1)}), bf16[4,128,1024]{2,1,0:T(8,128)(2,1)S(1)}, u32[]{:S(2)}, u32[]{:S(2)}) async-start(bf16[4,128,1024]{2,1,0:T(8,128)(2,1)} %bitcast.56), calls=%async_computation.3 | async-start | bytes 2097152 | tf_op jit(solution)/shard_map/all_to_all | solution.py:1545
  527.0 153.5 %reduce-scatter.8.cloned.1.call-start = ((), (), s32[]{:S(2)}) async-start(), calls=%async_computation.11 | async-start | bytes 3276800 | tf_op jit(solution)/shard_map/reduce_scatter | solution.py:1542
  584.8 32.7 %copy-start.5 = (bf16[4,128,1024]{2,1,0:T(8,128)(2,1)}, bf16[4,128,1024]{2,1,0:T(8,128)(2,1)S(1)}, u32[]{:S(2)}) copy-start(bf16[4,128,1024]{2,1,0:T(8,128)(2,1)S(1)} %all-to-all-done.1.rest_0_.down) | copy-start | bytes 3145732
  586.5 31.0 %copy-start.35 = (bf16[128]{0:T(256)(128)(2,1)S(1)}, bf16[128]{0:T(256)(128)(2,1)}, u32[]{:S(2)}) copy-start(bf16[128]{0:T(256)(128)(2,1)} %param.21) | copy-start | bytes 772
  586.5 31.1 %copy-start.36 = (bf16[128]{0:T(256)(128)(2,1)S(1)}, bf16[128]{0:T(256)(128)(2,1)}, u32[]{:S(2)}) copy-start(bf16[128]{0:T(256)(128)(2,1)} %param.16) | copy-start | bytes 772
  (28 other events, 83.3 us)
Sparse Core Ops, SparseCore 0:
  33.4 63.2 all-gather.4
  99.1 81.0 all-gather.6
  182.4 79.2 all-gather.8
  263.2 79.2 all-gather.10
  344.6 75.2 reduce-scatter.3
  422.3 144.9 reduce-scatter.5
  617.7 50.0 reduce-scatter.7

commit v6 on v5

--- a/solution.py
+++ b/solution.py
@@ -2,6 +2,7 @@
 
 import jax
 import jax.numpy as jnp
+import numpy as np
 from jax import lax
 from jax.experimental import pallas as pl
 from jax.experimental.pallas import tpu as pltpu
@@ -32,13 +33,14 @@
 
 
 def rope_tables():
-    frequency = rope_base ** (-(jnp.arange(HEAD // 2).astype(jnp.float32) * 2.0) / HEAD)
-    angles = jnp.arange(DEPTH).astype(jnp.float32)[:, None] * frequency[None, :]
-    sine = jnp.sin(angles)
-    cosine = jnp.cos(angles)
+    steps = np.arange(HEAD // 2, dtype=np.float32)
+    frequency = np.float32(rope_base) ** (-(steps * np.float32(2)) / np.float32(HEAD))
+    angles = np.arange(DEPTH, dtype=np.float32)[:, None] * frequency.astype(np.float32)
+    angles = angles.astype(np.float64)
+    cosine, sine = np.cos(angles).astype(np.float32), np.sin(angles).astype(np.float32)
     return (
-        jnp.concatenate([cosine] * 4, axis=-1),
-        jnp.concatenate([-sine, sine, -sine, sine], axis=-1),
+        jnp.asarray(np.concatenate([cosine] * 4, axis=-1)),
+        jnp.asarray(np.concatenate([-sine, sine, -sine, sine], axis=-1)),
     )
 
 
@@ -565,72 +567,155 @@
 
 
 class Exchange:
-    def __init__(self, plane, source, target, local):
+    def __init__(self, plane, source, target, local, first=0, columns=None):
         p = plane
-        columns = target.shape[2]
+        columns = columns or target.shape[2]
 
         def part(rank):
             return source.at[:, pl.ds(pl.multiple_of(rank * columns, 128), columns)]
 
-        self.plane, self.target, self.moves = p, target, []
-        self.mine = pltpu.make_async_copy(part(p.rank), target.at[p.rank], local)
+        def place(rank):
+            return target.at[rank, :, pl.ds(first, columns)]
+
+        self.plane, self.place, self.moves = p, place, []
+        self.mine = pltpu.make_async_copy(part(p.rank), place(p.rank), local)
         self.mine.start()
         for partner, rank in ((p.both, p.at_both), (p.x, p.at_x), (p.y, p.at_y)):
-            self.moves.append((p.send(part(rank), target.at[p.rank], partner), rank))
+            self.moves.append((p.send(part(rank), place(p.rank), partner), rank))
 
     def finish(self):
         for number, rank in self.moves:
-            self.plane.arrive(number, self.target.at[rank])
+            self.plane.arrive(number, self.place(rank))
         self.mine.wait()
 
 
-def start_kernel(block, gate, cotangent, out, gate_out, scaled, my_scaled, sent, landed, local):
+def first_kernel(query, pair, out_turned, gains, packed, gains_out, sent, landed, local, far_sent, far_landed):
+    groups = lax.axis_size("fsdp")
+    group, rank = lax.axis_index("fsdp"), lax.axis_index("context")
+    depth = gains.shape[1]
+    others = [(i, j) for i in range(groups) for j in range(4) if i or j]
+
+    def device(i, j):
+        return {"fsdp": lax.rem(group + i, groups), "context": lax.rem(rank + j, 4)}
+
+    def place(f, c):
+        return gains_out.at[:, pl.ds(pl.multiple_of((f * 4 + c) * depth, 128), depth)]
+
+    barrier = pltpu.get_barrier_semaphore()
+    for i, j in others:
+        pl.semaphore_signal(barrier, inc=1, device_id=device(i, j), device_id_type=MESH)
+    pl.semaphore_wait(barrier, len(others))
+    p = Plane(sent, landed, entered=True)
+    width = query.shape[1] // 4
+    exchanges = [
+        Exchange(p, query, packed, local.at[0], 0, width),
+        Exchange(p, pair, packed, local.at[1], width, 128),
+        Exchange(p, out_turned, packed, local.at[2], width + 128, width),
+    ]
+    far = []
+    for n, (i, j) in enumerate(others):
+        far.append(
+            pltpu.make_async_remote_copy(
+                src_ref=gains,
+                dst_ref=place(group, rank),
+                send_sem=far_sent.at[n],
+                recv_sem=far_landed.at[n],
+                device_id=device(i, j),
+                device_id_type=MESH,
+            )
+        )
+        far[n].start()
+    gains_out[:, pl.ds(pl.multiple_of((group * 4 + rank) * depth, 128), depth)] = gains[...]
+    for started in far:
+        started.wait()
+    for exchange in exchanges:
+        exchange.finish()
+    p.finish()
+
+
+def first_exchange(query, pair, out_turned, gains):
+    depth, columns = query.shape
+    groups = lax.axis_size("fsdp")
+    far = groups * 4 - 1
+    return pl.pallas_call(
+        first_kernel,
+        out_shape=[
+            jax.ShapeDtypeStruct((4, depth, columns // 2 + 128), query.dtype),
+            jax.ShapeDtypeStruct((8, groups * 4 * depth), jnp.float32),
+        ],
+        in_specs=[ANY, ANY, ANY, VMEM],
+        out_specs=[ANY, VMEM],
+        scratch_shapes=wires(9) + [pltpu.SemaphoreType.DMA((3,))] + wires(far),
+        compiler_params=pltpu.CompilerParams(collective_id=9, has_side_effects=True),
+        cost_estimate=lasting(10),
+        name="first_exchange",
+    )(query, pair, out_turned, gains)
+
+
+def start_kernel(
+    block, up, cotangent, early, out, up_out, scaled, sent, landed, local
+):
     p = Plane(sent, landed, diagonal=True)
     gather = Gather(p, block, out)
     mine = pltpu.make_async_copy(block, out.at[p.rank, p.core], local.at[0])
     for k in range(CHUNKS):
         gather.start(k)
-    exchange = Exchange(p, gate, gate_out, local.at[1])
+    exchanges = [Exchange(p, up, up_out, local.at[1])]
     mine.start()
-    share = block.shape[0]
 
     def scale(rows):
         value = residual_scale * cotangent[rows, :].astype(jnp.float32)
         scaled[rows, :] = value.astype(jnp.bfloat16)
 
-    def keep(rows):
-        from_rows = pl.ds(pl.multiple_of(p.core * share + rows.start, SLAB), SLAB)
-        my_scaled[rows, :] = scaled[from_rows, :]
-
     slabs(0, scaled.shape[0], scale)
-    slabs(0, share, keep)
     gather.forward()
     gather.finish()
-    exchange.finish()
+    for exchange in exchanges:
+        exchange.finish()
     p.finish()
     mine.wait()
 
 
-def start_plane(block, gate, cotangent):
+def start_plane(block, up, cotangent, early):
     share, width = block.shape
-    depth, units = gate.shape
+    depth, units = up.shape
     return pl.pallas_call(
         start_kernel,
         out_shape=[
             jax.ShapeDtypeStruct((4, 2, share, width), block.dtype),
-            jax.ShapeDtypeStruct((4, depth, units // 4), gate.dtype),
+            jax.ShapeDtypeStruct((4, depth, units // 4), up.dtype),
             jax.ShapeDtypeStruct(cotangent.shape, jnp.bfloat16),
-            jax.ShapeDtypeStruct(block.shape, jnp.bfloat16),
         ],
-        in_specs=[VMEM, ANY, VMEM],
-        out_specs=[ANY, ANY, VMEM, VMEM],
+        in_specs=[VMEM, ANY, VMEM, ANY],
+        out_specs=[ANY, ANY, VMEM],
         scratch_shapes=wires(GATHER_COPIES + 3) + [pltpu.SemaphoreType.DMA((2,))],
         compiler_params=pltpu.CompilerParams(
             collective_id=1, has_side_effects=True, vmem_limit_bytes=VMEM_LIMIT
         ),
         cost_estimate=lasting(60),
         name="gather_tokens",
-    )(block, gate, cotangent)
+    )(block, up, cotangent, early)
+
+
+def columns_kernel(weight, early, out, sent, landed, local):
+    p = Plane(sent, landed, diagonal=True)
+    exchange = Exchange(p, weight, out, local)
+    exchange.finish()
+    p.finish()
+
+
+def exchange_columns(weight, early):
+    depth, units = weight.shape
+    return pl.pallas_call(
+        columns_kernel,
+        out_shape=jax.ShapeDtypeStruct((4, depth, units // 4), weight.dtype),
+        in_specs=[ANY, ANY],
+        out_specs=ANY,
+        scratch_shapes=wires(3) + [pltpu.SemaphoreType.DMA],
+        compiler_params=pltpu.CompilerParams(collective_id=10, has_side_effects=True),
+        cost_estimate=lasting(15),
+        name="exchange_columns",
+    )(weight, early)
 
 
 def middle_kernel(
@@ -676,7 +761,7 @@
     def work(rows):
         value = residual[rows, :].astype(jnp.float32) + residual_scale * total.rows(rows)
         middle[rows, :] = value
-        hidden[rows, :] = (value * row_root(value) * gain[...]).astype(jnp.bfloat16)
+        hidden[rows, :] = (value * row_root(value) * gain[1:2, :]).astype(jnp.bfloat16)
 
     for k in range(CHUNKS):
         if k % (CHUNKS // 2) == 0:
@@ -719,11 +804,65 @@
     return out.reshape(8 * share, width), middle, beside_out.reshape(8 * share, width)
 
 
+class WeightTiles:
+    def __init__(self, rows, slopes, target, rows_in, tile_out, wires_in):
+        self.rows, self.slopes, self.target = rows, slopes, target
+        self.rows_in, self.tile_out, self.wires = rows_in, tile_out, wires_in
+        self.count = rows.shape[1] // TILE
+        self.load(0, 0).start()
+
+    def load(self, d, slot):
+        columns = pl.ds(pl.multiple_of(d * TILE, TILE), TILE)
+        return pltpu.make_async_copy(
+            self.rows.at[:, columns], self.rows_in.at[slot], self.wires.at[0, slot]
+        )
+
+    def store(self, d, slot):
+        columns = pl.ds(pl.multiple_of(d * TILE, TILE), TILE)
+        return pltpu.make_async_copy(
+            self.tile_out.at[slot], self.target.at[columns], self.wires.at[1, slot]
+        )
+
+    def run(self, first, last):
+        def step(d, carry):
+            slot = lax.rem(d, 2)
+            self.load(d, slot).wait()
+
+            @pl.when(d < self.count - 1)
+            def _():
+                self.load(d + 1, 1 - slot).start()
+
+            @pl.when(d >= 2)
+            def _():
+                self.store(d - 2, slot).wait()
+
+            self.tile_out[slot] = dot(self.rows_in[slot], self.slopes[...], FIRST).astype(
+                jnp.bfloat16
+            )
+            self.store(d, slot).start()
+            return carry
+
+        lax.fori_loop(first, last, step, 0)
+
+    def finish(self):
+        for d in (self.count - 2, self.count - 1):
+            self.store(d, d % 2).wait()
+
+
+def tile_scratch(count, units):
+    return [
+        pltpu.SemaphoreType.DMA((2, 2)),
+        pltpu.VMEM((2, count, TILE), jnp.bfloat16),
+        pltpu.VMEM((2, TILE, units), jnp.bfloat16),
+    ]
+
+
 UNITS = ((0, 0), (0, 1), (1, 0), (2, 0), (1, 1), (2, 1), (3, 0), (3, 1))
 
 
 def second_kernel(
     slopes,
+    normed_rows,
     gate_w,
     up_w,
     middle,
@@ -732,10 +871,15 @@
     early,
     grad_middle,
     hidden,
+    weight_grads,
     sent,
     landed,
     loading,
-    slopes_in,
+    tile_wires,
+    rows_in,
+    tile_out,
+    gate_in,
+    up_in,
     given,
     held,
     other,
@@ -747,35 +891,40 @@
     p = Plane(sent, landed)
     share, width = near_x.shape
     half = share // 2
-    units = gate_w.shape[1]
     order = (p.at_both, p.at_x, p.at_y, p.rank)
     top, low = halves = pl.ds(0, half), pl.ds(half, half)
 
+    def places(u):
+        i, h = UNITS[u]
+        for core in (1 - p.core, p.core):
+            row = (order[i] * 2 + core) * share + h * half
+            yield pl.ds(pl.multiple_of(row, 32), half)
+
+    units = gate_in.shape[1]
+
     def loads(u):
-        i, h = UNITS[u]
-        for j, core in enumerate((1 - p.core, p.core)):
-            row = (order[i] * 2 + core) * share + h * half
-            yield pltpu.make_async_copy(
-                slopes.at[pl.ds(pl.multiple_of(row, 32), half)],
-                slopes_in.at[u % 2, halves[j]],
-                loading.at[u % 2, j],
-            )
+        for j, rows in enumerate(places(u)):
+            for n, target in enumerate((gate_in, up_in)):
+                yield pltpu.make_async_copy(
+                    slopes.at[rows, pl.ds(n * units, units)],
+                    target.at[rows],
+                    loading.at[u, 2 * j + n],
+                )
 
     def compute(u):
         i, h = UNITS[u]
         slot = u % 2
-
-        def step(j, carry):
-            cut = pl.ds(pl.multiple_of(j * 1024, 1024), 1024)
-            back = dot(slopes_in[slot, :, :units], gate_w[cut, :], LAST) + dot(
-                slopes_in[slot, :, units:], up_w[cut, :], LAST
-            )
+        gate_rows = jnp.concatenate([gate_in[rows, :] for rows in places(u)], axis=0)
+        up_rows = jnp.concatenate([up_in[rows, :] for rows in places(u)], axis=0)
+        for j in range(width // 1024):
+            cut = slice(j * 1024, j * 1024 + 1024)
+            back = dot(gate_rows, gate_w[cut, :], LAST) + dot(up_rows, up_w[cut, :], LAST)
             given[slot, :, cut] = back[:half].astype(jnp.bfloat16)
             held[i, halves[h], cut] = back[half:].astype(jnp.bfloat16)
-            return carry
-
-        lax.fori_loop(0, width // 1024, step, 0)
-
+
+    tiles = WeightTiles(normed_rows, gate_in, weight_grads, rows_in, tile_out, tile_wires)
+
+    moves, across = {}, {}
     moves, across = {}, {}
 
     def settle(u):
@@ -807,29 +956,51 @@
         elif u == 5:
             moves["y", 1] = p.send(held.at[2, low], near_y.at[low], p.y)
 
-    for started in loads(0):
-        started.start()
     for u in range(8):
         for started in loads(u):
-            started.wait()
-        if u < 7:
-            for started in loads(u + 1):
-                started.start()
+            started.start()
+
+    def unit(u):
         if u >= 2:
             p.copies[across[u - 2]].wait_send()
         compute(u)
         i, h = UNITS[u]
         across[u] = p.send(given.at[u % 2], other.at[i, halves[h]], p.sibling)
-        if u >= 1:
-            settle(u - 1)
+
+    def wait_loads(units_here):
+        for u in units_here:
+            for started in loads(u):
+                started.wait()
+
+    wait_loads((0,))
+    unit(0)
+    wait_loads((1,))
+    unit(1)
+    settle(0)
+    wait_loads((2, 3))
+    unit(2)
+    settle(1)
+    unit(3)
+    settle(2)
+    wait_loads((4, 5, 6, 7))
+    unit(4)
+    tiles.run(0, 2)
+    settle(3)
+    unit(5)
+    settle(4)
+    unit(6)
+    settle(5)
+    unit(7)
+    settle(6)
     settle(7)
+    tiles.run(2, tiles.count)
 
     def work(rows):
         value = middle[rows, :]
         root = row_root(value)
         normed = value * root
         total = sum(part[rows, :].astype(jnp.float32) for part in (held.at[3], near_x, near_y))
-        slope = total * gain[...]
+        slope = total * gain[1:2, :]
         mean = jnp.mean(slope * normed, axis=-1, keepdims=True)
         gradient = cotangent[rows, :].astype(jnp.float32) + root * (slope - normed * mean)
         grad_middle[rows, :] = gradient
@@ -841,13 +1012,15 @@
         slabs(h * half, half, work)
     for u in (6, 7):
         p.copies[across[u]].wait_send()
+    tiles.finish()
     for number, started in enumerate(p.copies):
         if number not in across.values():
             started.wait_send()
 
 
-def second_plane(slopes, gate_w, up_w, middle, cotangent, gain, early):
+def second_plane(slopes, normed_rows, gate_w, up_w, middle, cotangent, gain, early):
     share, width = middle.shape
+    count, units = slopes.shape[0], slopes.shape[1] // 2
     kind = jnp.bfloat16
     half = share // 2
     quarter = pltpu.VMEM((4, share, width), kind)
@@ -856,13 +1029,16 @@
         out_shape=[
             jax.ShapeDtypeStruct((share, width), jnp.float32),
             jax.ShapeDtypeStruct((share, width), kind),
+            jax.ShapeDtypeStruct((width, units), kind),
         ],
-        in_specs=[ANY] + [VMEM] * 5 + [ANY],
-        out_specs=[VMEM, VMEM],
+        in_specs=[ANY, ANY] + [VMEM] * 5 + [ANY],
+        out_specs=[VMEM, VMEM, ANY],
         scratch_shapes=wires(8 + 6)
+        + [pltpu.SemaphoreType.DMA((8, 4))]
+        + tile_scratch(count, units)
         + [
-            pltpu.SemaphoreType.DMA((2, 2)),
-            pltpu.VMEM((2, share, slopes.shape[1]), kind),
+            pltpu.VMEM((count, units), kind),
+            pltpu.VMEM((count, units), kind),
             pltpu.VMEM((2, half, width), kind),
             quarter,
             quarter,
@@ -872,16 +1048,17 @@
             pltpu.VMEM((half, width), kind),
         ],
         compiler_params=pltpu.CompilerParams(
-            collective_id=3, has_side_effects=True, vmem_limit_bytes=VMEM_LIMIT
+            collective_id=3, has_side_effects=True, vmem_limit_bytes=60 * 1024 * 1024
         ),
         cost_estimate=lasting(60),
         name="second_rows",
-    )(slopes, gate_w, up_w, middle, cotangent, gain, early)
+    )(slopes, normed_rows, gate_w, up_w, middle, cotangent, gain, early)
 
 
 def spread_kernel(
-    hidden, m, down_w, out, pair_own, pair_x, pair_y, pair_both,
-    sent, landed, local, loading, m_in, given, held, theirs,
+    hidden, m, down_w, normed_rows, slopes, early, out, pair_own, pair_x, pair_y, pair_both,
+    weight_grads, sent, landed, local, loading, tile_wires, rows_in, tile_out, up_in,
+    m_in, given, held, theirs,
 ):
     p = Plane(sent, landed)
     share, width = hidden.shape
@@ -900,8 +1077,12 @@
             )
 
     across = []
+    units = up_in.shape[1]
+    up_load = pltpu.make_async_copy(slopes.at[:, pl.ds(units, units)], up_in, local.at[5])
+    up_load.start()
     for started in loads(0):
         started.start()
+    tiles = WeightTiles(normed_rows, up_in, weight_grads, rows_in, tile_out, tile_wires)
     for i in range(4):
         for started in loads(i):
             started.wait()
@@ -918,7 +1099,10 @@
 
         lax.fori_loop(0, width // 512, step, 0)
         across.append(p.send(given.at[i], theirs.at[i], p.sibling))
+        if i == 0:
+            up_load.wait()
         gather.forward_chunk(i)
+        tiles.run(i, i + 1)
     kept = []
     for i in range(4):
         p.arrive(across[i], theirs.at[i])
@@ -927,6 +1111,8 @@
         kept.append(pltpu.make_async_copy(held.at[i], target, local.at[i]))
         kept[i].start()
     gather.forward_far()
+    tiles.run(4, tiles.count)
+    tiles.finish()
     gather.finish()
     p.finish()
     mine.wait()
@@ -934,32 +1120,38 @@
         started.wait()
 
 
-def spread_plane(hidden, m, down_w):
+def spread_plane(hidden, m, down_w, normed_rows, slopes, early):
     share, width = hidden.shape
     units = m.shape[1]
     full = jax.ShapeDtypeStruct((4, 2, share, width), jnp.bfloat16)
     quarter = pltpu.VMEM((4, share, width), jnp.bfloat16)
-    out, *pairs = pl.pallas_call(
+    out, *pairs, weight_grads = pl.pallas_call(
         spread_kernel,
-        out_shape=[full] + [jax.ShapeDtypeStruct((share, width), jnp.bfloat16)] * 4,
-        in_specs=[VMEM, ANY, VMEM],
-        out_specs=[ANY] * 5,
+        out_shape=[full]
+        + [jax.ShapeDtypeStruct((share, width), jnp.bfloat16)] * 4
+        + [jax.ShapeDtypeStruct((width, units), jnp.bfloat16)],
+        in_specs=[VMEM, ANY, VMEM, ANY, ANY, ANY],
+        out_specs=[ANY] * 6,
         scratch_shapes=wires(GATHER_COPIES + 4)
         + [
-            pltpu.SemaphoreType.DMA((5,)),
+            pltpu.SemaphoreType.DMA((6,)),
             pltpu.SemaphoreType.DMA((2, 2)),
+        ]
+        + tile_scratch(8 * share, units)
+        + [
+            pltpu.VMEM((8 * share, units), jnp.bfloat16),
             pltpu.VMEM((2, 2 * share, units), jnp.bfloat16),
             quarter,
             quarter,
             quarter,
         ],
         compiler_params=pltpu.CompilerParams(
-            collective_id=7, has_side_effects=True, vmem_limit_bytes=VMEM_LIMIT
+            collective_id=7, has_side_effects=True, vmem_limit_bytes=60 * 1024 * 1024
         ),
         cost_estimate=lasting(60),
         name="spread_rows",
-    )(hidden, m.reshape(4, 2, share, units), down_w)
-    return out.reshape(8 * share, width), pairs
+    )(hidden, m.reshape(4, 2, share, units), down_w, normed_rows, slopes, early)
+    return out.reshape(8 * share, width), pairs, weight_grads
 
 
 def lane_sums(pairs):
@@ -980,11 +1172,13 @@
     ffn_x,
     ffn_y,
     ffn_both,
-    grads,
+    ups,
+    gates,
     gate,
     up,
     out,
     result_out,
+    up_out,
     gain_out,
     sent,
     landed,
@@ -994,7 +1188,11 @@
     sums,
     *scratch,
 ):
-    p = Plane(sent, landed)
+    p = Plane(sent, landed, diagonal=True)
+    moves = []
+    for partner, rank in ((p.both, p.at_both), (p.x, p.at_x), (p.y, p.at_y)):
+        moves.append((p.send(ups.at[rank], up_out.at[p.rank], partner), up_out.at[rank]))
+    up_out[p.rank] = ups[p.rank]
     total = Scatter(p, partial, *scratch)
     share = held.shape[0]
 
@@ -1013,10 +1211,12 @@
         pairs = []
         for c in range(4):
             columns = slice(c * units, c * units + units)
-            pairs.append((grads[c, rows, :units], gate[rows, columns]))
-            pairs.append((grads[c, rows, units:], up[rows, columns]))
+            pairs.append((gates[c, rows, :], gate[rows, columns]))
+            pairs.append((up_out[c, rows, :], up[rows, columns]))
         sums[0, rows, :] = lane_sums(pairs)
 
+    for number, target in moves:
+        p.arrive(number, target)
     slabs(0, gate.shape[0], gain_rows)
     swapped = p.send(sums.at[0], sums.at[1], p.sibling)
 
@@ -1024,7 +1224,7 @@
         value = residual[rows, :].astype(jnp.float32)
         root = row_root(value)
         normed = value * root
-        slope = total.rows(rows) * gain[...]
+        slope = total.rows(rows) * gain[0:1, :]
         mean = jnp.mean(slope * normed, axis=-1, keepdims=True)
         held[rows, :] = grad_middle[rows, :] + root * (slope - normed * mean)
 
@@ -1047,18 +1247,21 @@
         started.wait()
 
 
-def last_plane(partial, residual, grad_middle, gain, middle, ffn_parts, grads, gate, up):
+def last_plane(
+    partial, residual, grad_middle, gain, middle, ffn_parts, ups, gates, gate, up
+):
     share, width = residual.shape
-    out, result_out, gain_out = pl.pallas_call(
+    out, result_out, up_out, gain_out = pl.pallas_call(
         last_kernel,
         out_shape=[
             jax.ShapeDtypeStruct((2, share, width), jnp.float32),
             jax.ShapeDtypeStruct((2, share, width), jnp.bfloat16),
+            jax.ShapeDtypeStruct(ups.shape, ups.dtype),
             jax.ShapeDtypeStruct((gate.shape[0], 128), jnp.float32),
         ],
-        in_specs=[ANY] + [VMEM] * 11,
-        out_specs=[ANY, ANY, VMEM],
-        scratch_shapes=wires(CHUNKS + 2 + SCATTER_COPIES)
+        in_specs=[ANY] + [VMEM] * 12,
+        out_specs=[ANY, ANY, VMEM, VMEM],
+        scratch_shapes=wires(CHUNKS + 5 + SCATTER_COPIES)
         + [
             pltpu.SemaphoreType.DMA((2,)),
             pltpu.VMEM((share, width), jnp.float32),
@@ -1078,80 +1281,85 @@
         gain,
         middle,
         *ffn_parts,
-        grads,
+        ups,
+        gates,
         gate,
         up,
     )
-    return out.reshape(2 * share, width), result_out.reshape(2 * share, width), gain_out
-
-
-def qkv_columns(blocks):
-    return blocks.shape[2] // 2 + HEAD
-
-
-def exchange_kernel(blocks, weights, early, out, gain_out, sent, landed, sums):
+    return (
+        out.reshape(2 * share, width),
+        result_out.reshape(2 * share, width),
+        up_out,
+        gain_out,
+    )
+
+
+def exchange_kernel(blocks, query, pair, other_sums, out, gain_out, sent, landed, sums):
     p = Plane(sent, landed, diagonal=True)
     moves = []
     for partner, rank in ((p.both, p.at_both), (p.x, p.at_x), (p.y, p.at_y)):
         moves.append((p.send(blocks.at[rank], out.at[p.rank], partner), out.at[rank]))
     out[p.rank] = blocks[p.rank]
+    width = query.shape[1] // 4
+
+    def attention_rows(rows):
+        pairs = []
+        for c in range(4):
+            pairs.append((out[c, rows, :width], query[rows, c * width : c * width + width]))
+            pairs.append((out[c, rows, width : width + 128], pair[rows, c * 128 : c * 128 + 128]))
+        sums[0, rows, :] = lane_sums(pairs)
+
     for number, target in moves:
         p.arrive(number, target)
-    columns = qkv_columns(blocks)
-
-    def gain_rows(rows):
-        pairs = [(out[c, rows, :columns], weights[c, rows, :columns]) for c in range(4)]
-        sums[0, rows, :] = lane_sums(pairs)
-
-    slabs(0, blocks.shape[1], gain_rows)
+    slabs(0, blocks.shape[1], attention_rows)
     swapped = p.send(sums.at[0], sums.at[1], p.sibling)
     p.arrive(swapped, sums.at[1])
-    gain_out[...] = sums[0] + sums[1]
+    gain_out[0] = sums[0] + sums[1]
+    gain_out[1] = other_sums[...]
     p.finish()
 
 
-def exchange(blocks, weights, early):
+def exchange(blocks, query, pair, other_sums):
     depth = blocks.shape[1]
     return pl.pallas_call(
         exchange_kernel,
         out_shape=[
             jax.ShapeDtypeStruct(blocks.shape, blocks.dtype),
-            jax.ShapeDtypeStruct((depth, 128), jnp.float32),
+            jax.ShapeDtypeStruct((2, depth, 128), jnp.float32),
         ],
-        in_specs=[VMEM, VMEM, ANY],
-        out_specs=[VMEM, VMEM],
+        in_specs=[VMEM] * 4,
+        out_specs=[VMEM] * 2,
         scratch_shapes=wires(4) + [pltpu.VMEM((2, depth, 128), jnp.float32)],
         compiler_params=pltpu.CompilerParams(collective_id=5, has_side_effects=True),
         cost_estimate=lasting(8),
         name="exchange_blocks",
-    )(blocks, weights, early)
+    )(blocks, query, pair, other_sums)
 
 
 def finish_kernel(
-    attn, down, gate_up, tokens, result, attn_sums, ffn_sums, gains,
+    attn, down, gate, up, tokens, result, sums, gains,
     query_out, pair_out, out_out, gate_out, up_out, down_out, tokens_out, result_out, gain_out,
 ):
     width = query_out.shape[1]
-    units = gate_out.shape[1]
     query_out[...] = attn[0, :, :width].astype(jnp.float32)
     pair_out[...] = attn[0, :, width : width + 128].astype(jnp.float32)
     out_out[...] = jnp.transpose(attn[0, :, width + 128 :].astype(jnp.float32))
-    gate_out[...] = gate_up[0, :, :units].astype(jnp.float32)
-    up_out[...] = gate_up[0, :, units:].astype(jnp.float32)
+    gate_out[...] = gate[0].astype(jnp.float32)
+    up_out[...] = up[0].astype(jnp.float32)
     down_out[...] = jnp.transpose(down[0].astype(jnp.float32))
     tokens_out[...] = tokens[...]
     result_out[...] = result[...]
-    gain_out[0:1, :] = jnp.transpose(attn_sums[...])[0:1] / gains[0:1, :]
-    gain_out[1:2, :] = jnp.transpose(ffn_sums[...])[0:1] / gains[1:2, :]
-
-
-def finish(attn, down, gate_up, tokens, result, attn_sums, ffn_sums, gains):
+    for i in range(2):
+        gain_out[i : i + 1, :] = jnp.transpose(sums[i])[0:1] / gains[i : i + 1, :]
+
+
+def finish(attn, down, gate, up, tokens, result, sums, gains):
     groups, depth, units = down.shape
     width = attn.shape[2] // 2 - HEAD
     rows, columns = tokens.shape
     part = rows // groups
 
-    def block(c, *shape):
+    def block(*shape):
         return pl.BlockSpec((1, *shape), lambda i: (i, 0, 0))
 
     def wide(count):
@@ -1159,9 +1367,6 @@
 
     def tall(count, other):
         return pl.BlockSpec((count, other), lambda i: (i, 0))
-
-    def whole(array):
-        return pl.BlockSpec(array.shape, lambda i: (0, 0))
 
     def f32(*shape):
         return jax.ShapeDtypeStruct(shape, jnp.float32)
@@ -1170,14 +1375,14 @@
         finish_kernel,
         grid=(groups,),
         in_specs=[
-            block(0, depth, attn.shape[2]),
-            block(0, depth, units),
-            block(0, depth, 2 * units),
+            block(depth, attn.shape[2]),
+            block(depth, units),
+            block(depth, units),
+            block(depth, units),
             tall(part, columns),
             tall(part, columns),
-            whole(attn_sums),
-            whole(ffn_sums),
-            whole(gains),
+            pl.BlockSpec(sums.shape, lambda i: (0, 0, 0)),
+            pl.BlockSpec(gains.shape, lambda i: (0, 0)),
         ],
         out_specs=[
             wide(width),
@@ -1204,7 +1409,7 @@
         compiler_params=pltpu.CompilerParams(vmem_limit_bytes=VMEM_LIMIT),
         cost_estimate=lasting(12),
         name="finish",
-    )(attn, down, gate_up, tokens, result, attn_sums, ffn_sums, gains)
+    )(attn, down, gate, up, tokens, result, sums, gains)
 
 
 def context_pairs(step):
@@ -1212,7 +1417,8 @@
 
 
 def ffn_first_kernel(hidden, gate_w, up_w, m, gate, up):
-    for j in range(gate_w.shape[1] // 256):
+    units = m.shape[1]
+    for j in range(units // 256):
         cut = slice(j * 256, j * 256 + 256)
         gate_part = dot(hidden[...], gate_w[:, cut])
         up_part = dot(hidden[...], up_w[:, cut])
@@ -1238,72 +1444,67 @@
 
 
 def first_rows_kernel(
-    values, gain, weight, up, down, hidden, raw, up_out, down_out, sent, landed, local
+    values, gains, weight, cotangent, down, hidden, raw, scaled, down_out, sent, landed, local
 ):
     step, last = pl.program_id(0), pl.num_programs(0) - 1
 
-    def exchanges(act):
-        for i, (source, target) in enumerate(((up, up_out), (down, down_out))):
-            act(i, source, target)
-
     @pl.when(step == 0)
     def start():
-        p = Plane(sent, landed, diagonal=True)
-        exchanges(lambda i, source, target: Exchange(p, source, target, local.at[i]))
-
+        Exchange(Plane(sent, landed, diagonal=True), down, down_out, local)
+
+    scaled[...] = (residual_scale * cotangent[...].astype(jnp.float32)).astype(jnp.bfloat16)
     value = values[...].astype(jnp.float32)
-    normed = (value * row_root(value) * gain[...]).astype(jnp.bfloat16)
+    normed = (value * row_root(value) * gains[0:1, :]).astype(jnp.bfloat16)
     hidden[...] = normed
     raw[...] = dot(normed, weight[...])
 
     @pl.when(step == last)
     def finish():
         p = Plane(sent, landed, entered=True)
-        columns = up_out.shape[2]
-        for i, (source, target) in enumerate(((up, up_out), (down, down_out))):
-            part = source.at[:, pl.ds(0, columns)]
-            for j, rank in enumerate((p.at_both, p.at_x, p.at_y)):
-                move = p.copy(3 * i + j, part, target.at[rank], p.x)
-                move.wait_recv()
-                move.wait_send()
-            own = source.at[:, pl.ds(pl.multiple_of(p.rank * columns, 128), columns)]
-            pltpu.make_async_copy(own, target.at[p.rank], local.at[i]).wait()
-
-
-def first_rows(values, gain, weight, up, down):
+        columns = down_out.shape[2]
+        part = down.at[:, pl.ds(0, columns)]
+        for j, rank in enumerate((p.at_both, p.at_x, p.at_y)):
+            move = p.copy(j, part, down_out.at[rank], p.x)
+            move.wait_recv()
+            move.wait_send()
+        own = down.at[:, pl.ds(pl.multiple_of(p.rank * columns, 128), columns)]
+        pltpu.make_async_copy(own, down_out.at[p.rank], local).wait()
+
+
+def first_rows(values, gains, packed, columns, cotangent, down):
     count, width = values.shape
-    columns = weight.shape[1]
-    depth, units = up.shape
-    moved = jax.ShapeDtypeStruct((4, depth, units // 4), up.dtype)
+    depth, units = down.shape
+    steps = count // ROW_TILE
+    part = pl.BlockSpec((cotangent.shape[0] // steps, width), lambda i: (i, 0))
     return pl.pallas_call(
         first_rows_kernel,
-        grid=(count // ROW_TILE,),
+        grid=(steps,),
         in_specs=[
             pl.BlockSpec((ROW_TILE, width), lambda i: (i, 0)),
-            pl.BlockSpec((1, width), lambda i: (0, 0)),
+            pl.BlockSpec((8, width), lambda i: (0, 0)),
             pl.BlockSpec((width, columns), lambda i: (0, 0)),
-            ANY,
+            part,
             ANY,
         ],
         out_specs=[
             pl.BlockSpec((ROW_TILE, width), lambda i: (i, 0)),
             pl.BlockSpec((ROW_TILE, columns), lambda i: (i, 0)),
-            ANY,
+            part,
             ANY,
         ],
         out_shape=[
             jax.ShapeDtypeStruct((count, width), jnp.bfloat16),
             jax.ShapeDtypeStruct((count, columns), jnp.float32),
-            moved,
-            moved,
+            jax.ShapeDtypeStruct(cotangent.shape, jnp.bfloat16),
+            jax.ShapeDtypeStruct((4, depth, units // 4), down.dtype),
         ],
-        scratch_shapes=wires(6) + [pltpu.SemaphoreType.DMA((2,))],
+        scratch_shapes=wires(3) + [pltpu.SemaphoreType.DMA],
         compiler_params=pltpu.CompilerParams(
             collective_id=6, has_side_effects=True, vmem_limit_bytes=VMEM_LIMIT
         ),
         cost_estimate=lasting(25),
         name="first_rows",
-    )(values, gain, weight, up, down)
+    )(values, gains, packed, cotangent, down)
 
 
 def attention_weights_kernel(hidden, back, grad, attended, weight, moving, *rest):
@@ -1446,49 +1647,66 @@
         mine = mine.reshape(groups * depth, -1)
         return lax.all_gather(mine, "fsdp", axis=0, tiled=True)
 
-    gains = jnp.stack([attn_gain, ffn_gain], axis=1)
-    gains = jnp.broadcast_to(jnp.pad(gains, ((0, 0), (0, 126))), (groups, depth, 128))
-    my_packed = jnp.concatenate(
-        [blocks(w_query), kv_blocks(w_key), kv_blocks(w_value), blocks(w_out.T), gains], axis=2
-    )
-    packed = spread(my_packed)
+    square = groups == 4 and cores == 2
     width = w_query.shape[1] // groups
-    qkv_full = packed[:, : width + 2 * HEAD]
-    out_full = packed[:, width + 2 * HEAD : 2 * width + 2 * HEAD]
-    gains_full = packed[:, 2 * width + 2 * HEAD :].astype(jnp.float32)
-    attn_scale, ffn_scale = gains_full[:, 0], gains_full[:, 1]
-    square = groups == 4 and cores == 2
+    columns_qkv = width + 2 * HEAD
+    out_turned, down_turned = w_out.T, w_down.T
     tokens_half, cotangent_half = my_rows(tokens), my_rows(cotangent)
-    tables = rope_tables()
 
     def over_groups(blocks_here):
         return lax.all_gather(
             blocks_here.reshape(groups * depth, -1), "fsdp", axis=0, tiled=True
         )
 
-    down_turned = w_down.T
     if square:
-        inputs_full, gate_blocks, ffn_grad, my_ffn_grad = start_plane(
-            tokens_half, w_gate, cotangent
+        gains = jnp.pad(jnp.stack([attn_gain, ffn_gain]).astype(jnp.float32), ((0, 6), (0, 0)))
+        w_pair = jnp.stack(
+            [w_key.reshape(depth, groups, HEAD), w_value.reshape(depth, groups, HEAD)], axis=2
+        ).reshape(depth, -1)
+        packed, gain_rows = first_exchange(w_query, w_pair, out_turned, gains)
+        packed = over_groups(packed)
+        gate_blocks = exchange_columns(w_gate, gain_rows)
+        inputs_full, up_blocks, ffn_grad = start_plane(
+            tokens_half, w_up, cotangent, gate_blocks
         )
-        gate_full = over_groups(gate_blocks)
-        hidden_first, raw, up_blocks, down_blocks = first_rows(
+        gate_full, up_full = over_groups(gate_blocks), over_groups(up_blocks)
+        hidden_first, raw, my_ffn_grad, down_blocks = first_rows(
             inputs_full.reshape(-1, inputs_full.shape[3]),
-            attn_scale[None, :],
-            qkv_full,
-            w_up,
+            gain_rows,
+            packed,
+            columns_qkv,
+            cotangent_half,
             down_turned,
         )
-        up_full, down_full = over_groups(up_blocks), over_groups(down_blocks)
+        down_full = over_groups(down_blocks)
+        out_full = packed[:, columns_qkv:]
     else:
-        gate_full, up_full, down_full = (
-            spread(blocks(w)) for w in (w_gate, w_up, down_turned)
+        gains = jnp.stack([attn_gain, ffn_gain], axis=1)
+        gains = jnp.broadcast_to(jnp.pad(gains, ((0, 0), (0, 126))), (groups, depth, 128))
+        packed = spread(
+            jnp.concatenate(
+                [
+                    blocks(w_query),
+                    kv_blocks(w_key),
+                    kv_blocks(w_value),
+                    blocks(out_turned),
+                    gains,
+                ],
+                axis=2,
+            )
         )
+        qkv_full = packed[:, :columns_qkv]
+        out_full = packed[:, columns_qkv : columns_qkv + width]
+        gains_full = packed[:, columns_qkv + width :].astype(jnp.float32)
+        attn_scale, ffn_scale = gains_full[:, 0], gains_full[:, 1]
+        gate_full, up_full = spread(blocks(w_gate)), spread(blocks(w_up))
+        down_full = spread(blocks(down_turned))
         inputs_full = gather_rows(tokens_half).astype(jnp.float32)
         hidden_first = inputs_full * inverse_root(inputs_full) * attn_scale
         hidden_first = hidden_first.astype(jnp.bfloat16)
         raw = dot(hidden_first, qkv_full)
         my_ffn_grad = (residual_scale * cotangent_half.astype(jnp.float32)).astype(jnp.bfloat16)
+    tables = rope_tables()
 
     segment, starts = piece_segment[0] % 13, piece_start[0]
     places = jnp.where(
@@ -1511,14 +1729,14 @@
             lax.ppermute(my_ffn_grad, "context", context_pairs(step)) for step in (1, 2, 3)
         ]
         hidden_second, middle, ffn_grad = middle_plane(
-            branch, tokens_half, ffn_scale[None, :], ffn_grad, ffn_grad_blocks
+            branch, tokens_half, gain_rows, ffn_grad, ffn_grad_blocks
         )
     else:
         ffn_grad = gather_rows(my_ffn_grad)
         middle = residual_in + residual_scale * scatter_rows(branch)
         hidden_second = gather_rows((middle * inverse_root(middle) * ffn_scale).astype(jnp.bfloat16))
 
-    units = gate_full.shape[1]
+    units = down_full.shape[1]
     hidden, gate_proj, up_proj = row_tiles(
         ffn_first_kernel,
         "ffn_first",
@@ -1536,8 +1754,6 @@
         [grad_down],
         [2 * units],
     )
-    grad_gate_up = dot(hidden_second, slopes, FIRST).astype(jnp.bfloat16)
-
     def sum_groups(gradient):
         return lax.psum_scatter(gradient, "fsdp", scatter_dimension=0, tiled=True)
 
@@ -1548,16 +1764,27 @@
         return jnp.transpose(gradient, (1, 0, 2)).reshape(depth, -1).astype(jnp.float32)
 
     if square:
-        grad_middle, my_attn_grad = second_plane(
-            slopes, gate_full, up_full, middle, cotangent_half, ffn_scale[None, :], grad_gate_up
+        grad_middle, my_attn_grad, grad_gate = second_plane(
+            slopes,
+            hidden_second,
+            gate_full,
+            up_full,
+            middle,
+            cotangent_half,
+            gain_rows,
+            grad_down,
         )
-        attn_grad, ffn_pairs = spread_plane(my_attn_grad, hidden, down_full)
+        attn_grad, ffn_pairs, grad_up = spread_plane(
+            my_attn_grad, hidden, down_full, hidden_second, slopes, grad_gate
+        )
         ffn_parts = [ffn_pairs[0]] + [
             lax.ppermute(ffn_pairs[step], "context", context_pairs(step)) for step in (1, 2, 3)
         ]
     else:
         root = inverse_root(middle)
         ffn_out = dot(hidden, down_full, LAST)
+        grad_gate = dot(hidden_second, slopes[:, :units], FIRST).astype(jnp.bfloat16)
+        grad_up = dot(hidden_second, slopes[:, units:], FIRST).astype(jnp.bfloat16)
         grad_second = dot(slopes[:, :units], gate_full, LAST)
         grad_second += dot(slopes[:, units:], up_full, LAST)
         grad_middle = grad_result + norm_backward(
@@ -1567,17 +1794,17 @@
         ffn_parts = []
     grad_attended = dot(attn_grad, out_full).astype(jnp.bfloat16)
     grad_down = sum_groups(grad_down)
-    grad_gate_up = sum_groups(grad_gate_up)
+    grad_gate, grad_up = sum_groups(grad_gate), sum_groups(grad_up)
     back = attention_backward(places, starts, grad_attended, kept, tables, [grad_down])
     grad_down = hand_back(grad_down)
     if square:
-        grad_attn, grad_first, grad_gate_up = attention_weights(
+        grad_attn, grad_first, grad_gate = attention_weights(
             hidden_first,
             back,
             attn_grad,
             attended,
-            qkv_full,
-            grad_gate_up.reshape(groups, depth, -1),
+            packed,
+            grad_gate.reshape(groups, depth, -1),
             [grad_down, *ffn_parts[1:]],
         )
     else:
@@ -1585,26 +1812,27 @@
             [dot(hidden_first, back, FIRST), dot(attn_grad, attended, FIRST)], axis=1
         ).astype(jnp.bfloat16)
         grad_first = dot(back, qkv_full, LAST).astype(jnp.bfloat16)
-        grad_gate_up = hand_back(grad_gate_up)
+        grad_gate, grad_up = hand_back(grad_gate), hand_back(grad_up)
     grad_attn = sum_groups(grad_attn)
     if square:
-        grad_tokens, result, ffn_sums = last_plane(
+        grad_tokens, result, grad_up, ffn_sums = last_plane(
             grad_first,
             tokens_half,
             grad_middle,
-            attn_scale[None, :],
+            gain_rows,
             middle,
             ffn_parts,
-            grad_gate_up,
+            grad_up.reshape(groups, depth, -1),
+            grad_gate,
             w_gate,
             w_up,
         )
-        grad_attn, attn_sums = exchange(
-            grad_attn.reshape(groups, depth, -1), my_packed, ffn_sums
+        grad_attn, sums = exchange(
+            grad_attn.reshape(groups, depth, -1), w_query, w_pair, ffn_sums
         )
         my_gains = jnp.stack([attn_gain, ffn_gain]).astype(jnp.float32)
         query, pair, out, gate, up, down, grad_tokens, result, gain_grads = finish(
-            grad_attn, grad_down, grad_gate_up, grad_tokens, result, attn_sums, ffn_sums, my_gains
+            grad_attn, grad_down, grad_gate, grad_up, grad_tokens, result, sums, my_gains
         )
         key, value = jnp.moveaxis(pair.reshape(depth, groups, 2, HEAD), 2, 0)
         return (
@@ -1636,7 +1864,7 @@
     grad_query = columns(grad_attn[:, :, :width])
     grad_key = kv_columns(grad_attn[:, :, width : width + HEAD])
     grad_value = kv_columns(grad_attn[:, :, width + HEAD : width + 2 * HEAD])
-    grad_gate, grad_up = columns(grad_gate_up[:, :, :units]), columns(grad_gate_up[:, :, units:])
+    grad_gate, grad_up = columns(grad_gate), columns(grad_up)
 
     def against(*pairs):
         return sum(jnp.sum(weight.astype(jnp.float32) * g, axis=1) for weight, g in pairs)

time: 727 us -> 696 us (0.957)
  Pallas kernels: 555 us -> 586 us
  matrix products: 61.7 us -> 32.8 us
  blocking collectives: 16.4 us -> 0 us
    dot_general x4 -> x3, matrix products: 61.7 us -> 32.8 us  [dot(): lax.dot_general(left_side, right_side, dims, preferred_element_type=jnp.f...]
    pallas_call x2 -> x4, Pallas kernels: 38.1 us -> 60.4 us  [the longest x1 18.3 us: first_rows(): pl.pallas_call(first_rows_kernel, grid=(steps,), in_specs=[pl.BlockSpec((...]
    all_to_all x1 -> x0, blocking collectives: 16.4 us -> none  [spread(): mine = lax.all_to_all(weight_blocks, 'context', 0, 0)]
    unnamed x83 -> x74, local copies, waits for them, and re-layouts: 29.6 us -> 30.2 us
  transfers between devices with their start and end apart: 14 -> 15, of which waited for: 2 -> 1; matrix products, arithmetic and copies ran while one was open for 10% -> 5% of each run, Pallas kernels for 70% -> 79%
where the time goes in v6:
time: 696 us; the launch traced here: 690 us
  Pallas kernels  586 us (84%)
  local copies, waits for them, and re-layouts  33.9 us (5%)
  matrix products  32.8 us (5%)
  between operations  14.8 us (2%)
  starting transfers between devices  11.8 us (2%)
  waiting for transfers between devices  10.2 us (1%)
    pallas_call x1, Pallas kernels, middle_plane(): pl.pallas_call(middle_kernel, out_shape=[full, jax.ShapeDtypeStruct((shar...  96.6 us
    pallas_call x1, Pallas kernels, second_plane(): pl.pallas_call(second_kernel, out_shape=[jax.ShapeDtypeStruct((share, wid...  65.2 us
    pallas_call x1, Pallas kernels, last_plane(): pl.pallas_call(last_kernel, out_shape=[jax.ShapeDtypeStruct((2, share, wi...  64.2 us
    pallas_call x1, Pallas kernels, start_plane(): pl.pallas_call(start_kernel, out_shape=[jax.ShapeDtypeStruct((4, 2, share...  63.1 us
    pallas_call x1, Pallas kernels, spread_plane(): pl.pallas_call(spread_kernel, out_shape=[full] + [jax.ShapeDtypeStruct((s...  55.3 us
    pallas_call x1, Pallas kernels, attention_backward(): pl.pallas_call(attention_backward_kernel, out_shape=jax.ShapeDtypeStruct(...  52.5 us
    pallas_call x2, Pallas kernels, row_tiles(): pl.pallas_call(kernel, grid=(count // ROW_TILE,), in_specs=[tile(r.shape[...  50.4 us
    pallas_call x1, Pallas kernels, attention_forward(): pl.pallas_call(attention_forward_kernel, out_shape=[kept] * 4 + [jax.Shap...  36.8 us
  transfers between devices with their start and end apart: 15, of which 1 were waited for; matrix products, arithmetic and copies ran while one was open for 5% of the time, Pallas kernels for 79%

profile of v6, /device:TPU:0, one launch (start us, length us, event | category | flops | bytes accessed | tf_op | source)
XLA Modules:
  0.0 690.3 jit_solution(8351158408212163347)
XLA Ops:
  10.1 1.8 copy.33
  13.2 17.6 %first_exchange.1 = (bf16[4,128,640]{2,1,0:T(8,128)(2,1)}, f32[8,2048]{1,0:T(8,128)}) custom-call(bf16[128,1024]{1,0:T(8,128)(2,1)} %query.3, bf16[128,512]{1,0:T(8,128)(2,1)} %copy.34.pair, bf16[128,1024]{1,0:T(8,128)(2,1)} %bitcast.66, f32[8,128]{1,0:T(8,128)} %pad.4.gains), custom_call_target="tpu_custom_call" | custom-call | bytes 30000000 | tf_op jit(solution)/shard_map/first_exchange/pallas_call | solution.py:640
  30.9 15.2 %exchange_columns.1.early = bf16[4,128,1024]{2,1,0:T(8,128)(2,1)} custom-call(bf16[128,4096]{1,0:T(8,128)(2,1)} %gate.1, f32[8,2048]{1,0:T(8,128)} %get-tuple-element.58.early.gains.gain), custom_call_target="tpu_custom_call" | custom-call | bytes 45000000 | tf_op jit(solution)/shard_map/exchange_columns/pallas_call | solution.py:709
  47.7 63.1 %gather_tokens.1 = (bf16[4,2,320,2048]{3,2,1,0:T(8,128)(2,1)}, bf16[4,128,1024]{2,1,0:T(8,128)(2,1)}, bf16[640,2048]{1,0:T(8,128)(2,1)}) custom-call(bf16[320,2048]{1,0:T(8,128)(2,1)S(1)} %constant_dynamic-slice_fusion.1.block.residual, bf16[128,4096]{1,0:T(8,128)(2,1)S(1)} %copy-done.12, bf16[640,2048]{1,0:T(8,128)(2,1)} %cotangent.1, ...), custom_call_target="tpu_custom_call" | custom-call | bytes 180000000 | tf_op jit(solution)/shard_map/gather_tokens/pallas_call | solution.py:682
  111.0 1.5 copy.35
  114.0 18.3 %first_rows.1 = (bf16[2560,2048]{1,0:T(8,128)(2,1)}, f32[2560,384]{1,0:T(8,128)}, bf16[320,2048]{1,0:T(8,128)(2,1)}, bf16[4,128,1024]{2,1,0:T(8,128)(2,1)S(1)}) custom-call(bf16[2560,2048]{1,0:T(8,128)(2,1)} %bitcast.59, f32[8,2048]{1,0:T(8,128)S(1)} %copy-done.14, bf16[2048,640]{1,0:T(8,128)(2,1)} %all-gather.5.cloned.1.call-done.weight, ...), custom_call_target="tpu_custom_call" | custom-call | bytes 75000000 | tf_op jit(solution)/shard_map/first_rows/pallas_call | solution.py:1479
  133.5 1.7 collective-permute-start.2
  138.4 36.8 %attention_forward.1 = (bf16[2560,256]{1,0:T(8,128)(2,1)S(1)}, bf16[2560,256]{1,0:T(8,128)(2,1)S(1)}, bf16[2560,256]{1,0:T(8,128)(2,1)S(1)}, bf16[2560,256]{1,0:T(8,128)(2,1)}, f32[4,1,2560]{2,1,0:T(1,128)S(1)}) custom-call(s32[20]{0:T(128)S(1)} %compare_select_fusion.1.to_ref, s32[20]{0:T(128)S(1)} %bitcast.50, f32[2560,384]{1,0:T(8,128)} %get-tuple-element.62.raw_ref, ...), custom_call_target="tpu_custom_call" | custom-call | flops 5368709120 | bytes 10485760 | tf_op jit(solution)/shard_map/attention_forward/pallas_call | solution.py:313
  176.3 7.2 %convolution_convert_fusion = bf16[2560,2048]{1,0:T(8,128)(2,1)} fusion(bf16[2560,256]{1,0:T(8,128)(2,1)S(1)} %get-tuple-element.63.attended, bf16[2048,640]{1,0:T(8,128)(2,1)} %all-gather.5.cloned.1.call-done.weight), kind=kOutput, calls=%fused_computation | convolution fusion | flops 2689597440 | bytes 12845056 | tf_op jit(solution)/shard_map/dot_general | solution.py:32
  183.5 10.0 %collective-permute-done.1.from_y = bf16[320,2048]{1,0:T(8,128)(2,1)} collective-permute-done((bf16[320,2048]{1,0:T(8,128)(2,1)}, bf16[320,2048]{1,0:T(8,128)(2,1)}, u32[]{:S(2)}, u32[]{:S(2)}) %collective-permute-start.1) | collective-permute-done | bytes 1310752 | tf_op jit(solution)/shard_map/ppermute | solution.py:1729
  193.5 96.6 %middle_rows.1 = (bf16[4,2,320,2048]{3,2,1,0:T(8,128)(2,1)}, f32[320,2048]{1,0:T(8,128)}, bf16[4,2,320,2048]{3,2,1,0:T(8,128)(2,1)}) custom-call(bf16[4,2,320,2048]{3,2,1,0:T(8,128)(2,1)} %bitcast.52, bf16[320,2048]{1,0:T(8,128)(2,1)S(1)} %copy-done.3, f32[8,2048]{1,0:T(8,128)S(1)} %copy-done.14, bf16[2,320,2048]{2,1,0:T(8,128)(2,1)} %bitcast.64, ...), custom_call_target="tpu_custom_call" | custom-call | bytes 300000000 | tf_op jit(solution)/shard_map/middle_rows/pallas_call | solution.py:785
  290.2 29.1 %ffn_first.1 = (bf16[2560,1024]{1,0:T(8,128)(2,1)}, bf16[2560,1024]{1,0:T(8,128)(2,1)}, bf16[2560,1024]{1,0:T(8,128)(2,1)}) custom-call(bf16[2560,2048]{1,0:T(8,128)(2,1)} %bitcast.53, bf16[2048,1024]{1,0:T(8,128)(2,1)} %all-gather.7.cloned.1.call-done.gate_w, bf16[2048,1024]{1,0:T(8,128)(2,1)} %all-gather.9.cloned.1.call-done.up_w), custom_call_target="tpu_custom_call" | custom-call | flops 21474836480 | bytes 53687092 | tf_op jit(solution)/shard_map/ffn_first/pallas_call | solution.py:1579
  319.3 17.4 %convolution_convert_fusion.2.early = bf16[2048,1024]{1,0:T(8,128)(2,1)} fusion(bf16[2560,2048]{1,0:T(8,128)(2,1)} %bitcast.60, bf16[2560,1024]{1,0:T(8,128)(2,1)} %get-tuple-element.72), kind=kOutput, calls=%fused_computation.2 | convolution fusion | flops 10739515392 | bytes 19922944 | tf_op jit(solution)/shard_map/dot_general | solution.py:32
  336.8 21.3 %ffn_slopes.1.slopes = bf16[2560,2048]{1,0:T(8,128)(2,1)} custom-call(bf16[2560,2048]{1,0:T(8,128)(2,1)} %bitcast.61, bf16[2560,1024]{1,0:T(8,128)(2,1)} %get-tuple-element.69.gate, bf16[2560,1024]{1,0:T(8,128)(2,1)} %get-tuple-element.70.up, bf16[2048,1024]{1,0:T(8,128)(2,1)} %all-gather.11.cloned.1.call-done.down_w, ...), custom_call_target="tpu_custom_call" | custom-call | flops 10737418240 | bytes 26843544 | tf_op jit(solution)/shard_map/ffn_slopes/pallas_call | solution.py:1579
  358.1 65.2 %second_rows.1 = (f32[320,2048]{1,0:T(8,128)}, bf16[320,2048]{1,0:T(8,128)(2,1)}, bf16[2048,1024]{1,0:T(8,128)(2,1)}) custom-call(bf16[2560,2048]{1,0:T(8,128)(2,1)} %ffn_slopes.1.slopes, bf16[2560,2048]{1,0:T(8,128)(2,1)} %bitcast.54, bf16[2048,1024]{1,0:T(8,128)(2,1)} %all-gather.7.cloned.1.call-done.gate_w, ...), custom_call_target="tpu_custom_call" | custom-call | bytes 180000000 | tf_op jit(solution)/shard_map/second_rows/pallas_call | solution.py:1027
  423.6 55.3 %spread_rows.1 = (bf16[4,2,320,2048]{3,2,1,0:T(8,128)(2,1)}, bf16[320,2048]{1,0:T(8,128)(2,1)}, bf16[320,2048]{1,0:T(8,128)(2,1)}, bf16[320,2048]{1,0:T(8,128)(2...) custom-call(bf16[320,2048]{1,0:T(8,128)(2,1)} %get-tuple-element.74.hidden, ...), custom_call_target="tpu_custom_call" | custom-call | bytes 180000000 | tf_op jit(solution)/shard_map/spread_rows/pallas_call | solution.py:1128
  482.5 8.2 %convolution_convert_fusion.1.grad_ref = bf16[2560,256]{1,0:T(8,128)(2,1)} fusion(bf16[2560,2048]{1,0:T(8,128)(2,1)} %bitcast.57, bf16[2048,640]{1,0:T(8,128)(2,1)} %all-gather.5.cloned.1.call-done.weight), kind=kOutput, calls=%fused_computation.1 | convolution fusion | flops 2685009920 | bytes 12845056 | tf_op jit(solution)/shard_map/dot_general | solution.py:32
  490.7 3.5 all-to-all-start
  499.6 52.5 %attention_backward.1.back = bf16[2560,384]{1,0:T(8,128)(2,1)} custom-call(s32[20]{0:T(128)S(1)} %compare_select_fusion.1.to_ref, s32[20]{0:T(128)S(1)} %bitcast.51, bf16[2560,256]{1,0:T(8,128)(2,1)S(1)} %copy-done.29, bf16[2560,256]{1,0:T(8,128)(2,1)S(1)} %copy-done.31, bf16[2560,256]{1,0:T(8,128)(2,1)} %copy-done.32, ...), custom_call_target="tpu_custom_call" | custom-call | flops 13421772800 | bytes 10485760 | tf_op jit(solution)/shard_map/attention_backward/pallas_call | solution.py:331
  552.2 1.6 copy-done.17
  553.8 24.6 %attention_weights.1 = (bf16[2048,640]{1,0:T(8,128)(2,1)}, bf16[2560,2048]{1,0:T(8,128)(2,1)}, bf16[4,128,1024]{2,1,0:T(8,128)(2,1)S(1)}) custom-call(bf16[2560,2048]{1,0:T(8,128)(2,1)} %get-tuple-element.61.hidden, bf16[2560,384]{1,0:T(8,128)(2,1)} %attention_backward.1.back, bf16[2560,2048]{1,0:T(8,128)(2,1)} %bitcast.58, ...), custom_call_target="tpu_custom_call" | custom-call | bytes 75000000 | tf_op jit(solution)/shard_map/attention_weights/pallas_call | solution.py:1540
  583.4 64.2 %last_rows.1 = (f32[2,320,2048]{2,1,0:T(8,128)}, bf16[2,320,2048]{2,1,0:T(8,128)(2,1)}, bf16[4,128,1024]{2,1,0:T(8,128)(2,1)S(1)}, f32[128,128]{1,0:T(8,128)S(1)}) custom-call(bf16[4,2,320,2048]{3,2,1,0:T(8,128)(2,1)} %bitcast.56, bf16[320,2048]{1,0:T(8,128)(2,1)} %copy-done.2, f32[320,2048]{1,0:T(8,128)} %get-tuple-element.86.grad_middle, ...), custom_call_target="tpu_custom_call" | custom-call | bytes 210000000 | tf_op jit(solution)/shard_map/last_rows/pallas_call | solution.py:1254
  649.2 16.9 %exchange_blocks.1 = (bf16[4,128,640]{2,1,0:T(8,128)(2,1)}, f32[2,128,128]{2,1,0:T(8,128)}) custom-call(bf16[4,128,640]{2,1,0:T(8,128)(2,1)} %bitcast.69, bf16[128,1024]{1,0:T(8,128)(2,1)} %query.3, bf16[128,512]{1,0:T(8,128)(2,1)} %copy.34.pair, f32[128,128]{1,0:T(8,128)} %copy-done.24), custom_call_target="tpu_custom_call" | custom-call | bytes 24000000 | tf_op jit(solution)/shard_map/exchange_blocks/pallas_call | solution.py:1324
  671.8 9.3 %finish.1 = (f32[128,1024]{1,0:T(8,128)}, f32[128,512]{1,0:T(8,128)S(1)}, f32[1024,128]{1,0:T(8,128)}, f32[128,4096]{1,0:T(8,128)}, f32[128,4096]{1,0:T(8,128)},...) custom-call(bf16[4,128,640]{2,1,0:T(8,128)(2,1)S(1)} %copy-done.22, ...), custom_call_target="tpu_custom_call" | custom-call | bytes 36000000 | tf_op jit(solution)/shard_map/finish/pallas_call | solution.py:1374
  (117 shorter events, 36.5 us)
Async XLA Ops:
  7.2 39.0 %copy-start = (bf16[640,2048]{1,0:T(8,128)(2,1)S(1)}, bf16[640,2048]{1,0:T(8,128)(2,1)}, u32[]{:S(2)}) copy-start(bf16[640,2048]{1,0:T(8,128)(2,1)} %param.16) | copy-start | bytes 7864324
  7.2 106.8 %all-gather.5.cloned.1.call-start = ((), (), s32[]{:S(2)}) async-start(), calls=%async_computation.5 | async-start | bytes 3276800 | tf_op jit(solution)/shard_map/all_gather | solution.py:1657
  30.8 259.3 %all-gather.7.cloned.1.call-start = ((), (), s32[]{:S(2)}) async-start(), calls=%async_computation.6 | async-start | bytes 5242880 | tf_op jit(solution)/shard_map/all_gather | solution.py:1657
  46.1 244.1 %all-gather.9.cloned.1.call-start = ((), (), s32[]{:S(2)}) async-start(), calls=%async_computation.7 | async-start | bytes 5242880 | tf_op jit(solution)/shard_map/all_gather | solution.py:1657
  47.7 63.2 %copy-start.2 = (bf16[320,2048]{1,0:T(8,128)(2,1)}, bf16[320,2048]{1,0:T(8,128)(2,1)S(1)}, u32[]{:S(2)}) copy-start(bf16[320,2048]{1,0:T(8,128)(2,1)S(1)} %constant_dynamic-slice_fusion.1.block.residual) | copy-start | bytes 3932164
  110.9 3.1 copy-start.14
  110.9 225.9 %all-gather.11.cloned.1.call-start = ((), (), s32[]{:S(2)}) async-start(), calls=%async_computation.8 | async-start | bytes 5242880 | tf_op jit(solution)/shard_map/all_gather | solution.py:1657
  114.0 18.4 %copy-start.4 = (bf16[320,2048]{1,0:T(8,128)(2,1)}, bf16[320,2048]{1,0:T(8,128)(2,1)S(1)}, u32[]{:S(2)}) copy-start(bf16[320,2048]{1,0:T(8,128)(2,1)S(1)} %constant_dynamic-slice_fusion.cotangent) | copy-start | bytes 3932164
  114.0 23.3 %copy-start.26 = (f32[1280,128]{1,0:T(8,128)S(1)}, f32[1280,128]{1,0:T(8,128)}, u32[]{:S(2)}) copy-start(f32[1280,128]{1,0:T(8,128)} %constant.41.clone.sin_ref) | copy-start | bytes 1966084
  133.5 50.1 %collective-permute-start.2 = (bf16[320,2048]{1,0:T(8,128)(2,1)}, bf16[320,2048]{1,0:T(8,128)(2,1)}, u32[]{:S(2)}, u32[]{:S(2)}) collective-permute-start(bf16[320,2048]{1,0:T(8,128)(2,1)} %get-tuple-element.65), channel_id=1, source_target_pairs={{0,6},{2,4},{4,2},{6,0},{1,7},{3,5},{5,3},{7,1},{8,14},{10,12},{12... | collective-permute-start | bytes 3932168 | tf_op jit(solution)/shard_map/ppermute | solution.py:1729
  135.2 58.3 %collective-permute-start.1 = (bf16[320,2048]{1,0:T(8,128)(2,1)}, bf16[320,2048]{1,0:T(8,128)(2,1)}, u32[]{:S(2)}, u32[]{:S(2)}) collective-permute-start(bf16[320,2048]{1,0:T(8,128)(2,1)} %get-tuple-element.65), channel_id=1, source_target_pairs={{0,4},{2,6},{4,0},{6,2},{1,5},{3,7},{5,1},{7,3},{8,12},{10,14},{12... | collective-permute-start | bytes 3932168 | tf_op jit(solution)/shard_map/ppermute | solution.py:1729
  136.3 57.2 %collective-permute-start = (bf16[320,2048]{1,0:T(8,128)(2,1)}, bf16[320,2048]{1,0:T(8,128)(2,1)}, u32[]{:S(2)}, u32[]{:S(2)}) collective-permute-start(bf16[320,2048]{1,0:T(8,128)(2,1)} %get-tuple-element.65), channel_id=1, source_target_pairs={{0,2},{2,0},{4,6},{6,4},{1,3},{3,1},{5,7},{7,5},{8,10},{10,8},{12,... | collective-permute-start | bytes 3932168 | tf_op jit(solution)/shard_map/ppermute | solution.py:1729
  137.0 353.7 %reduce-scatter.5.cloned.1.call-start = ((), (), s32[]{:S(2)}) async-start(), calls=%async_computation.9 | async-start | bytes 5242880 | tf_op jit(solution)/shard_map/reduce_scatter | solution.py:1758
  176.3 7.2 %copy-start.32 = (bf16[2560,256]{1,0:T(8,128)(2,1)}, bf16[2560,256]{1,0:T(8,128)(2,1)S(1)}, u32[]{:S(2)}) copy-start(bf16[2560,256]{1,0:T(8,128)(2,1)S(1)} %get-tuple-element.78.k_ref) | copy-start | bytes 3932164
  176.3 17.2 %copy-start.3 = (bf16[320,2048]{1,0:T(8,128)(2,1)S(1)}, bf16[320,2048]{1,0:T(8,128)(2,1)}, u32[]{:S(2)}) copy-start(bf16[320,2048]{1,0:T(8,128)(2,1)} %copy-done.2) | copy-start | bytes 3932164
  336.8 215.4 %reduce-scatter.7.cloned.1.call-start = ((), (), s32[]{:S(2)}) async-start(), calls=%async_computation.10 | async-start | bytes 5242880 | tf_op jit(solution)/shard_map/reduce_scatter | solution.py:1758
  423.4 156.0 %reduce-scatter.11.cloned.1.call-start = ((), (), s32[]{:S(2)}) async-start(), calls=%async_computation.12 | async-start | bytes 5242880 | tf_op jit(solution)/shard_map/reduce_scatter | solution.py:1758
  479.0 73.1 %collective-permute-start.3 = (bf16[320,2048]{1,0:T(8,128)(2,1)}, bf16[320,2048]{1,0:T(8,128)(2,1)}, u32[]{:S(2)}, u32[]{:S(2)}) collective-permute-start(bf16[320,2048]{1,0:T(8,128)(2,1)} %get-tuple-element.81), channel_id=1, source_target_pairs={{0,2},{2,0},{4,6},{6,4},{1,3},{3,1},{5,7},{7,5},{8,10},{10,8},{12,... | collective-permute-start | bytes 3932168 | tf_op jit(solution)/shard_map/ppermute | solution.py:1781
  480.0 72.1 %collective-permute-start.4 = (bf16[320,2048]{1,0:T(8,128)(2,1)}, bf16[320,2048]{1,0:T(8,128)(2,1)}, u32[]{:S(2)}, u32[]{:S(2)}) collective-permute-start(bf16[320,2048]{1,0:T(8,128)(2,1)} %get-tuple-element.82), channel_id=1, source_target_pairs={{0,4},{2,6},{4,0},{6,2},{1,5},{3,7},{5,1},{7,3},{8,12},{10,14},{12... | collective-permute-start | bytes 3932168 | tf_op jit(solution)/shard_map/ppermute | solution.py:1781
  481.1 71.0 %collective-permute-start.5 = (bf16[320,2048]{1,0:T(8,128)(2,1)}, bf16[320,2048]{1,0:T(8,128)(2,1)}, u32[]{:S(2)}, u32[]{:S(2)}) collective-permute-start(bf16[320,2048]{1,0:T(8,128)(2,1)} %get-tuple-element.83), channel_id=1, source_target_pairs={{0,6},{2,4},{4,2},{6,0},{1,7},{3,5},{5,3},{7,1},{8,14},{10,12},{12... | collective-permute-start | bytes 3932168 | tf_op jit(solution)/shard_map/ppermute | solution.py:1781
  490.7 61.4 %all-to-all-start = ((bf16[4,128,1024]{2,1,0:T(8,128)(2,1)}), bf16[4,128,1024]{2,1,0:T(8,128)(2,1)S(1)}, u32[]{:S(2)}, u32[]{:S(2)}) async-start(bf16[4,128,1024]{2,1,0:T(8,128)(2,1)} %bitcast.48), calls=%async_computation.2 | async-start | bytes 2097152 | tf_op jit(solution)/shard_map/all_to_all | solution.py:1761
  494.2 155.0 %reduce-scatter.9.cloned.1.call-start = ((), (), s32[]{:S(2)}) async-start(), calls=%async_computation.11 | async-start | bytes 3276800 | tf_op jit(solution)/shard_map/reduce_scatter | solution.py:1758
  552.1 26.3 %copy-start.5 = (bf16[4,128,1024]{2,1,0:T(8,128)(2,1)}, bf16[4,128,1024]{2,1,0:T(8,128)(2,1)S(1)}, u32[]{:S(2)}) copy-start(bf16[4,128,1024]{2,1,0:T(8,128)(2,1)S(1)} %all-to-all-done.rest_0_.down) | copy-start | bytes 3145732
  671.8 11.5 %copy-start.1 = (bf16[640,2048]{1,0:T(8,128)(2,1)S(1)}, bf16[640,2048]{1,0:T(8,128)(2,1)}, u32[]{:S(2)}) copy-start(bf16[640,2048]{1,0:T(8,128)(2,1)} %param.16) | copy-start | bytes 7864324
  (25 other events, 30.5 us)
Sparse Core Ops, SparseCore 0:
  30.9 52.9 all-gather.4
  85.5 79.5 all-gather.6
  166.7 79.3 all-gather.8
  247.5 79.2 all-gather.10
  336.9 74.5 reduce-scatter.4
  423.5 74.6 reduce-scatter.6
  500.5 77.2 reduce-scatter.10
  580.2 52.6 reduce-scatter.8

commit v7 on v6

--- a/solution.py
+++ b/solution.py
@@ -296,7 +296,7 @@
 
 SMEM = pl.BlockSpec(memory_space=pltpu.SMEM)
 VMEM = pl.BlockSpec(memory_space=pltpu.VMEM)
-VMEM_LIMIT = 48 * 1024 * 1024
+VMEM_LIMIT = 60 * 1024 * 1024
 
 
 def attention_cost(width, products):
@@ -471,40 +471,48 @@
 
 
 class Scatter:
-    def __init__(self, plane, partial, held, other, near_x, near_y, far_x, far_y, local):
+    def __init__(
+        self, plane, rows_in, weights, columns, given, held, other, near_x, near_y, far_x, far_y
+    ):
         p = self.plane = plane
         rows = near_x.shape[0]
         half = rows // 2
         halves = top, low = pl.ds(0, half), pl.ds(half, half)
         order = (p.at_both, p.at_x, p.at_y, p.rank)
-        across, kept = {}, []
-        for i, h in ((0, 0), (0, 1), (1, 0), (2, 0), (1, 1), (2, 1), (3, 0), (3, 1)):
-            source = partial.at[order[i], 1 - p.core, halves[h]]
-            across[i, h] = p.send(source, other.at[i, halves[h]], p.sibling)
-        for i in range(4):
-            kept.append(
-                pltpu.make_async_copy(partial.at[order[i], p.core], held.at[i], local.at[i])
-            )
-            kept[i].start()
+        across = {}
+
+        def make(i, h):
+            for core, target in ((1 - p.core, given), (p.core, held)):
+                value = dot(rows_in[order[i], core, halves[h], :], weights[:, columns], LAST)
+                target[i, halves[h], :] = value.astype(jnp.bfloat16)
+                if target is given:
+                    source = given.at[i, halves[h]]
+                    across[i, h] = p.send(source, other.at[i, halves[h]], p.sibling)
 
         def pair(i, h):
             p.arrive(across[i, h], other.at[i, halves[h]])
             add_rows(held.at[i], other.at[i], h * half, half)
 
-        kept[0].wait()
+        make(0, 0)
+        make(0, 1)
         pair(0, 0)
         first = p.send(held.at[0, top], far_x, p.x)
+        make(1, 0)
         pair(0, 1)
         second = p.send(held.at[0, low], far_y, p.y)
-        kept[1].wait()
+        make(2, 0)
         pair(1, 0)
         third = p.send(held.at[1, top], near_x.at[top], p.x)
-        kept[2].wait()
+        make(1, 1)
+        make(2, 1)
+        make(3, 0)
+        make(3, 1)
         pair(2, 0)
+        pair(1, 1)
+        pair(2, 1)
         p.arrive(first, far_x)
         add_rows(held.at[2], far_x, 0, half)
         fourth = p.send(held.at[2, top], near_y.at[top], p.y)
-        pair(1, 1)
         p.arrive(second, far_y)
 
         def step(i, carry):
@@ -516,9 +524,7 @@
 
         lax.fori_loop(0, half // SLAB, step, 0)
         fifth = p.send(held.at[1, low], near_x.at[low], p.x)
-        pair(2, 1)
         sixth = p.send(held.at[2, low], near_y.at[low], p.y)
-        kept[3].wait()
         pair(3, 0)
         pair(3, 1)
         self.halves = halves
@@ -540,13 +546,13 @@
 def scatter_scratch(share, width):
     kind = jnp.bfloat16
     return [
+        pltpu.VMEM((4, share, width), kind),
         pltpu.VMEM((4, share, width), kind),
         pltpu.VMEM((4, share, width), kind),
         pltpu.VMEM((share, width), kind),
         pltpu.VMEM((share, width), kind),
         pltpu.VMEM((share // 2, width), kind),
         pltpu.VMEM((share // 2, width), kind),
-        pltpu.SemaphoreType.DMA((4,)),
     ]
 
 
@@ -652,87 +658,96 @@
     )(query, pair, out_turned, gains)
 
 
-def start_kernel(
-    block, up, cotangent, early, out, up_out, scaled, sent, landed, local
-):
-    p = Plane(sent, landed, diagonal=True)
+def start_kernel(block, cotangent, early, out, scaled, my_scaled, sent, landed, local):
+    p = Plane(sent, landed)
     gather = Gather(p, block, out)
-    mine = pltpu.make_async_copy(block, out.at[p.rank, p.core], local.at[0])
+    mine = pltpu.make_async_copy(block, out.at[p.rank, p.core], local)
     for k in range(CHUNKS):
         gather.start(k)
-    exchanges = [Exchange(p, up, up_out, local.at[1])]
     mine.start()
+    share = block.shape[0]
 
     def scale(rows):
         value = residual_scale * cotangent[rows, :].astype(jnp.float32)
         scaled[rows, :] = value.astype(jnp.bfloat16)
 
+    def keep(rows):
+        from_rows = pl.ds(pl.multiple_of(p.core * share + rows.start, SLAB), SLAB)
+        my_scaled[rows, :] = scaled[from_rows, :]
+
     slabs(0, scaled.shape[0], scale)
+    slabs(0, share, keep)
     gather.forward()
     gather.finish()
-    for exchange in exchanges:
-        exchange.finish()
     p.finish()
     mine.wait()
 
 
-def start_plane(block, up, cotangent, early):
+def start_plane(block, cotangent, early):
     share, width = block.shape
-    depth, units = up.shape
     return pl.pallas_call(
         start_kernel,
         out_shape=[
             jax.ShapeDtypeStruct((4, 2, share, width), block.dtype),
-            jax.ShapeDtypeStruct((4, depth, units // 4), up.dtype),
             jax.ShapeDtypeStruct(cotangent.shape, jnp.bfloat16),
+            jax.ShapeDtypeStruct(block.shape, jnp.bfloat16),
         ],
-        in_specs=[VMEM, ANY, VMEM, ANY],
-        out_specs=[ANY, ANY, VMEM],
-        scratch_shapes=wires(GATHER_COPIES + 3) + [pltpu.SemaphoreType.DMA((2,))],
+        in_specs=[VMEM, VMEM, ANY],
+        out_specs=[ANY, VMEM, VMEM],
+        scratch_shapes=wires(GATHER_COPIES) + [pltpu.SemaphoreType.DMA],
         compiler_params=pltpu.CompilerParams(
             collective_id=1, has_side_effects=True, vmem_limit_bytes=VMEM_LIMIT
         ),
         cost_estimate=lasting(60),
         name="gather_tokens",
-    )(block, up, cotangent, early)
-
-
-def columns_kernel(weight, early, out, sent, landed, local):
+    )(block, cotangent, early)
+
+
+def columns_kernel(gate, up, down, early, both_out, down_out, sent, landed, local):
     p = Plane(sent, landed, diagonal=True)
-    exchange = Exchange(p, weight, out, local)
-    exchange.finish()
+    units = down_out.shape[2]
+    exchanges = [
+        Exchange(p, gate, both_out, local.at[0], 0, units),
+        Exchange(p, up, both_out, local.at[1], units, units),
+        Exchange(p, down, down_out, local.at[2]),
+    ]
+    for exchange in exchanges:
+        exchange.finish()
     p.finish()
 
 
-def exchange_columns(weight, early):
-    depth, units = weight.shape
+def exchange_columns(gate, up, down, early):
+    depth, units = gate.shape
     return pl.pallas_call(
         columns_kernel,
-        out_shape=jax.ShapeDtypeStruct((4, depth, units // 4), weight.dtype),
-        in_specs=[ANY, ANY],
-        out_specs=ANY,
-        scratch_shapes=wires(3) + [pltpu.SemaphoreType.DMA],
+        out_shape=[
+            jax.ShapeDtypeStruct((4, depth, units // 2), gate.dtype),
+            jax.ShapeDtypeStruct((4, depth, units // 4), gate.dtype),
+        ],
+        in_specs=[ANY] * 4,
+        out_specs=[ANY] * 2,
+        scratch_shapes=wires(9) + [pltpu.SemaphoreType.DMA((3,))],
         compiler_params=pltpu.CompilerParams(collective_id=10, has_side_effects=True),
-        cost_estimate=lasting(15),
+        cost_estimate=lasting(30),
         name="exchange_columns",
-    )(weight, early)
+    )(gate, up, down, early)
 
 
 def middle_kernel(
-    partial,
+    attended,
+    weights,
     residual,
     gain,
     beside,
     from_x,
     from_y,
     from_both,
-    out,
+    hidden,
     middle,
     beside_out,
     sent,
     landed,
     local,
-    hidden,
     held_beside,
     held_blocks,
     *scratch,
@@ -744,7 +759,9 @@
         loads.append(pltpu.make_async_copy(block, held_blocks.at[i], local.at[i + 1]))
     for started in loads:
         started.start()
-    total = Scatter(p, partial, *scratch)
+    width = attended.shape[3]
+    columns = slice(weights.shape[1] - width, weights.shape[1])
+    total = Scatter(p, attended, weights, columns, *scratch)
     kept, across = [], []
     loads[0].wait()
     kept.append(pltpu.make_async_copy(held_beside, beside_out.at[p.rank], local.at[0]))
@@ -756,22 +773,15 @@
         kept[i + 1].start()
         across.append(p.send(held_blocks.at[i], place, p.sibling))
     share = hidden.shape[0]
-    gather = Gather(p, hidden, out)
 
     def work(rows):
         value = residual[rows, :].astype(jnp.float32) + residual_scale * total.rows(rows)
         middle[rows, :] = value
         hidden[rows, :] = (value * row_root(value) * gain[1:2, :]).astype(jnp.bfloat16)
 
-    for k in range(CHUNKS):
-        if k % (CHUNKS // 2) == 0:
-            total.ready(k // (CHUNKS // 2))
-        slabs(k * (share // CHUNKS), share // CHUNKS, work)
-        gather.start(k)
-    kept.append(pltpu.make_async_copy(hidden, out.at[p.rank, p.core], local.at[4]))
-    kept[4].start()
-    gather.forward()
-    gather.finish()
+    for h in range(2):
+        total.ready(h)
+        slabs(h * (share // 2), share // 2, work)
     for number, rank in zip(across, (p.at_x, p.at_y, p.at_both)):
         p.arrive(number, beside_out.at[rank, 1 - p.core])
     p.finish()
@@ -779,18 +789,21 @@
         started.wait()
 
 
-def middle_plane(partial, residual, gain, beside, blocks):
+def middle_plane(attended, weights, residual, gain, beside, blocks):
     share, width = residual.shape
     full = jax.ShapeDtypeStruct((4, 2, share, width), jnp.bfloat16)
-    out, middle, beside_out = pl.pallas_call(
+    hidden, middle, beside_out = pl.pallas_call(
         middle_kernel,
-        out_shape=[full, jax.ShapeDtypeStruct((share, width), jnp.float32), full],
-        in_specs=[ANY, VMEM, VMEM] + [ANY] * 4,
-        out_specs=[ANY, VMEM, ANY],
-        scratch_shapes=wires(GATHER_COPIES + SCATTER_COPIES + 3)
+        out_shape=[
+            jax.ShapeDtypeStruct((share, width), jnp.bfloat16),
+            jax.ShapeDtypeStruct((share, width), jnp.float32),
+            full,
+        ],
+        in_specs=[VMEM] * 4 + [ANY] * 4,
+        out_specs=[VMEM, VMEM, ANY],
+        scratch_shapes=wires(SCATTER_COPIES + 3)
         + [
-            pltpu.SemaphoreType.DMA((5,)),
-            pltpu.VMEM((share, width), jnp.bfloat16),
+            pltpu.SemaphoreType.DMA((4,)),
             pltpu.VMEM((2, share, width), jnp.bfloat16),
             pltpu.VMEM((3, share, width), jnp.bfloat16),
         ]
@@ -798,10 +811,152 @@
         compiler_params=pltpu.CompilerParams(
             collective_id=2, has_side_effects=True, vmem_limit_bytes=VMEM_LIMIT
         ),
-        cost_estimate=lasting(100),
+        cost_estimate=lasting(55),
         name="middle_rows",
-    )(partial.reshape(full.shape), residual, gain, beside.reshape(2, share, width), *blocks)
-    return out.reshape(8 * share, width), middle, beside_out.reshape(8 * share, width)
+    )(
+        attended.reshape(4, 2, share, -1),
+        weights,
+        residual,
+        gain,
+        beside.reshape(2, share, width),
+        *blocks,
+    )
+    return hidden, middle, beside_out.reshape(8 * share, width)
+
+
+def ffn_rows_kernel(
+    block,
+    weights_in,
+    out,
+    m,
+    gate,
+    up,
+    sent,
+    landed,
+    local,
+    loading,
+    storing,
+    weights,
+    rows_in,
+    m_held,
+    gate_held,
+    up_held,
+):
+    p = Plane(sent, landed)
+    gather = Gather(p, block, out)
+    for k in range(CHUNKS):
+        gather.start(k)
+    weights_load = pltpu.make_async_copy(weights_in, weights, local.at[0])
+    weights_load.start()
+    mine = pltpu.make_async_copy(block, out.at[p.rank, p.core], local.at[1])
+    mine.start()
+    units = m.shape[3]
+    stores = []
+
+    def load(n, rank, core):
+        return pltpu.make_async_copy(out.at[rank, core], rows_in.at[n % 2], loading.at[n % 2])
+
+    def compute(n, rank, core, source):
+        slot = n % 2
+        if n >= 2:
+            for started in stores[n - 2]:
+                started.wait()
+
+        def step(j, carry):
+            cut = pl.ds(pl.multiple_of(j * 256, 256), 256)
+            beyond = pl.ds(pl.multiple_of(units + j * 256, 256), 256)
+            gate_part = dot(source[...], weights[:, cut])
+            up_part = dot(source[...], weights[:, beyond])
+            gate_held[slot, :, cut] = gate_part.astype(jnp.bfloat16)
+            up_held[slot, :, cut] = up_part.astype(jnp.bfloat16)
+            sigmoid = 1.0 / (1.0 + jnp.exp(-gate_part))
+            m_held[slot, :, cut] = (gate_part * sigmoid * up_part).astype(jnp.bfloat16)
+            return carry
+
+        lax.fori_loop(0, units // 256, step, 0)
+        stores.append(
+            [
+                pltpu.make_async_copy(held.at[slot], target.at[rank, core], storing.at[slot, i])
+                for i, (held, target) in enumerate(((m_held, m), (gate_held, gate), (up_held, up)))
+            ]
+        )
+        for started in stores[n]:
+            started.start()
+
+    def from_sibling(i, rank):
+        for k in range(CHUNKS):
+            p.arrive(
+                gather.across[i, k], out.at[rank, 1 - p.core, chunk(k, gather.rows)]
+            )
+
+    weights_load.wait()
+    compute(0, p.rank, p.core, block)
+    gather.forward_chunk(0)
+    from_sibling(0, p.rank)
+    load(1, p.rank, 1 - p.core).start()
+    load(1, p.rank, 1 - p.core).wait()
+    compute(1, p.rank, 1 - p.core, rows_in.at[1])
+    for k in range(1, CHUNKS):
+        gather.forward_chunk(k)
+    load(2, p.at_x, p.core).start()
+    load(3, p.at_y, p.core).start()
+    load(2, p.at_x, p.core).wait()
+    compute(2, p.at_x, p.core, rows_in.at[0])
+    from_sibling(1, p.at_x)
+    load(4, p.at_x, 1 - p.core).start()
+    load(3, p.at_y, p.core).wait()
+    compute(3, p.at_y, p.core, rows_in.at[1])
+    from_sibling(2, p.at_y)
+    load(5, p.at_y, 1 - p.core).start()
+    load(4, p.at_x, 1 - p.core).wait()
+    compute(4, p.at_x, 1 - p.core, rows_in.at[0])
+    gather.forward_far()
+    load(6, p.at_both, p.core).start()
+    load(5, p.at_y, 1 - p.core).wait()
+    compute(5, p.at_y, 1 - p.core, rows_in.at[1])
+    from_sibling(3, p.at_both)
+    load(7, p.at_both, 1 - p.core).start()
+    load(6, p.at_both, p.core).wait()
+    compute(6, p.at_both, p.core, rows_in.at[0])
+    load(7, p.at_both, 1 - p.core).wait()
+    compute(7, p.at_both, 1 - p.core, rows_in.at[1])
+    p.finish()
+    mine.wait()
+    for n in (6, 7):
+        for started in stores[n]:
+            started.wait()
+
+
+def ffn_rows(block, weights):
+    share, width = block.shape
+    units = weights.shape[1] // 2
+    kind = jnp.bfloat16
+    full = jax.ShapeDtypeStruct((4, 2, share, width), kind)
+    part = jax.ShapeDtypeStruct((4, 2, share, units), kind)
+    held = pltpu.VMEM((2, share, units), kind)
+    outs = pl.pallas_call(
+        ffn_rows_kernel,
+        out_shape=[full, part, part, part],
+        in_specs=[VMEM, ANY],
+        out_specs=[ANY] * 4,
+        scratch_shapes=wires(GATHER_COPIES)
+        + [
+            pltpu.SemaphoreType.DMA((2,)),
+            pltpu.SemaphoreType.DMA((2,)),
+            pltpu.SemaphoreType.DMA((2, 3)),
+            pltpu.VMEM(weights.shape, kind),
+            pltpu.VMEM((2, share, width), kind),
+            held,
+            held,
+            held,
+        ],
+        compiler_params=pltpu.CompilerParams(
+            collective_id=11, has_side_effects=True, vmem_limit_bytes=VMEM_LIMIT
+        ),
+        cost_estimate=lasting(60),
+        name="ffn_rows",
+    )(block, weights)
+    return [array.reshape(8 * share, -1) for array in outs]
 
 
 class WeightTiles:
@@ -863,8 +1018,7 @@
 def second_kernel(
     slopes,
     normed_rows,
-    gate_w,
-    up_w,
+    weights,
     middle,
     cotangent,
     gain,
@@ -918,7 +1072,9 @@
         up_rows = jnp.concatenate([up_in[rows, :] for rows in places(u)], axis=0)
         for j in range(width // 1024):
             cut = slice(j * 1024, j * 1024 + 1024)
-            back = dot(gate_rows, gate_w[cut, :], LAST) + dot(up_rows, up_w[cut, :], LAST)
+            back = dot(gate_rows, weights[cut, :units], LAST) + dot(
+                up_rows, weights[cut, units:], LAST
+            )
             given[slot, :, cut] = back[:half].astype(jnp.bfloat16)
             held[i, halves[h], cut] = back[half:].astype(jnp.bfloat16)
 
@@ -1018,7 +1174,7 @@
             started.wait_send()
 
 
-def second_plane(slopes, normed_rows, gate_w, up_w, middle, cotangent, gain, early):
+def second_plane(slopes, normed_rows, weights, middle, cotangent, gain, early):
     share, width = middle.shape
     count, units = slopes.shape[0], slopes.shape[1] // 2
     kind = jnp.bfloat16
@@ -1031,7 +1187,7 @@
             jax.ShapeDtypeStruct((share, width), kind),
             jax.ShapeDtypeStruct((width, units), kind),
         ],
-        in_specs=[ANY, ANY] + [VMEM] * 5 + [ANY],
+        in_specs=[ANY, ANY] + [VMEM] * 4 + [ANY],
         out_specs=[VMEM, VMEM, ANY],
         scratch_shapes=wires(8 + 6)
         + [pltpu.SemaphoreType.DMA((8, 4))]
@@ -1052,7 +1208,7 @@
         ),
         cost_estimate=lasting(60),
         name="second_rows",
-    )(slopes, normed_rows, gate_w, up_w, middle, cotangent, gain, early)
+    )(slopes, normed_rows, weights, middle, cotangent, gain, early)
 
 
 def spread_kernel(
@@ -1162,38 +1318,32 @@
     return jnp.broadcast_to(total, (total.shape[0], 128))
 
 
+LATER = 10
+
+
 def last_kernel(
-    partial,
-    residual,
-    grad_middle,
+    back,
+    weights,
     gain,
-    middle,
-    ffn_own,
-    ffn_x,
-    ffn_y,
-    ffn_both,
     ups,
-    gates,
-    gate,
-    up,
-    out,
-    result_out,
-    up_out,
-    gain_out,
-    sent,
-    landed,
-    local,
-    held,
-    result,
-    sums,
-    *scratch,
+    *rest,
 ):
+    later, rest = rest[:LATER], rest[LATER:]
+    out, result_out, up_out, gain_out, sent, landed, local, loading, held, result, sums = rest[:11]
+    landing, scratch = rest[11 : 11 + LATER], rest[11 + LATER :]
+    loads = [
+        pltpu.make_async_copy(source, target, loading.at[i])
+        for i, (source, target) in enumerate(zip(later, landing))
+    ]
+    for started in loads:
+        started.start()
+    middle, ffn_own, ffn_x, ffn_y, ffn_both, gates, gate, up, residual, grad_middle = landing
     p = Plane(sent, landed, diagonal=True)
     moves = []
     for partner, rank in ((p.both, p.at_both), (p.x, p.at_x), (p.y, p.at_y)):
         moves.append((p.send(ups.at[rank], up_out.at[p.rank], partner), up_out.at[rank]))
     up_out[p.rank] = ups[p.rank]
-    total = Scatter(p, partial, *scratch)
+    total = Scatter(p, back, weights, slice(0, back.shape[3]), *scratch)
     share = held.shape[0]
 
     def finish_result(rows):
@@ -1201,6 +1351,8 @@
         ffn = sum(part[rows, :].astype(jnp.float32) for part in parts)
         result[rows, :] = (middle[rows, :] + residual_scale * ffn).astype(jnp.bfloat16)
 
+    for started in loads:
+        started.wait()
     slabs(0, share, finish_result)
     kept = [pltpu.make_async_copy(result, result_out.at[p.core], local.at[0])]
     kept[0].start()
@@ -1248,9 +1400,10 @@
 
 
 def last_plane(
-    partial, residual, grad_middle, gain, middle, ffn_parts, ups, gates, gate, up
+    back, weights, residual, grad_middle, gain, middle, ffn_parts, ups, gates, gate, up
 ):
     share, width = residual.shape
+    later = [middle, *ffn_parts, gates, gate, up, residual, grad_middle]
     out, result_out, up_out, gain_out = pl.pallas_call(
         last_kernel,
         out_shape=[
@@ -1259,15 +1412,17 @@
             jax.ShapeDtypeStruct(ups.shape, ups.dtype),
             jax.ShapeDtypeStruct((gate.shape[0], 128), jnp.float32),
         ],
-        in_specs=[ANY] + [VMEM] * 12,
+        in_specs=[VMEM] * 4 + [ANY] * LATER,
         out_specs=[ANY, ANY, VMEM, VMEM],
         scratch_shapes=wires(CHUNKS + 5 + SCATTER_COPIES)
         + [
             pltpu.SemaphoreType.DMA((2,)),
+            pltpu.SemaphoreType.DMA((LATER,)),
             pltpu.VMEM((share, width), jnp.float32),
             pltpu.VMEM((share, width), jnp.bfloat16),
             pltpu.VMEM((2, gate.shape[0], 128), jnp.float32),
         ]
+        + [pltpu.VMEM(array.shape, array.dtype) for array in later]
         + scatter_scratch(share, width),
         compiler_params=pltpu.CompilerParams(
             collective_id=4, has_side_effects=True, vmem_limit_bytes=VMEM_LIMIT
@@ -1275,16 +1430,11 @@
         cost_estimate=lasting(70),
         name="last_rows",
     )(
-        partial.reshape(4, 2, share, width),
-        residual,
-        grad_middle,
+        back.reshape(4, 2, share, -1),
+        weights,
         gain,
-        middle,
-        *ffn_parts,
         ups,
-        gates,
-        gate,
-        up,
+        *later,
     )
     return (
         out.reshape(2 * share, width),
@@ -1416,12 +1566,12 @@
     return [(i, i ^ step) for i in range(4)]
 
 
-def ffn_first_kernel(hidden, gate_w, up_w, m, gate, up):
+def ffn_first_kernel(hidden, weights, m, gate, up):
     units = m.shape[1]
     for j in range(units // 256):
         cut = slice(j * 256, j * 256 + 256)
-        gate_part = dot(hidden[...], gate_w[:, cut])
-        up_part = dot(hidden[...], up_w[:, cut])
+        gate_part = dot(hidden[...], weights[:, cut])
+        up_part = dot(hidden[...], weights[:, units + j * 256 : units + j * 256 + 256])
         gate[:, cut] = gate_part.astype(jnp.bfloat16)
         up[:, cut] = up_part.astype(jnp.bfloat16)
         sigmoid = 1.0 / (1.0 + jnp.exp(-gate_part))
@@ -1443,72 +1593,39 @@
         ).astype(jnp.bfloat16)
 
 
-def first_rows_kernel(
-    values, gains, weight, cotangent, down, hidden, raw, scaled, down_out, sent, landed, local
-):
-    step, last = pl.program_id(0), pl.num_programs(0) - 1
-
-    @pl.when(step == 0)
-    def start():
-        Exchange(Plane(sent, landed, diagonal=True), down, down_out, local)
-
-    scaled[...] = (residual_scale * cotangent[...].astype(jnp.float32)).astype(jnp.bfloat16)
+def first_rows_kernel(values, gains, weight, hidden, raw):
     value = values[...].astype(jnp.float32)
     normed = (value * row_root(value) * gains[0:1, :]).astype(jnp.bfloat16)
     hidden[...] = normed
     raw[...] = dot(normed, weight[...])
 
-    @pl.when(step == last)
-    def finish():
-        p = Plane(sent, landed, entered=True)
-        columns = down_out.shape[2]
-        part = down.at[:, pl.ds(0, columns)]
-        for j, rank in enumerate((p.at_both, p.at_x, p.at_y)):
-            move = p.copy(j, part, down_out.at[rank], p.x)
-            move.wait_recv()
-            move.wait_send()
-        own = down.at[:, pl.ds(pl.multiple_of(p.rank * columns, 128), columns)]
-        pltpu.make_async_copy(own, down_out.at[p.rank], local).wait()
-
-
-def first_rows(values, gains, packed, columns, cotangent, down):
+
+def first_rows(values, gains, packed, columns):
     count, width = values.shape
-    depth, units = down.shape
-    steps = count // ROW_TILE
-    part = pl.BlockSpec((cotangent.shape[0] // steps, width), lambda i: (i, 0))
     return pl.pallas_call(
         first_rows_kernel,
-        grid=(steps,),
+        grid=(count // ROW_TILE,),
         in_specs=[
             pl.BlockSpec((ROW_TILE, width), lambda i: (i, 0)),
             pl.BlockSpec((8, width), lambda i: (0, 0)),
             pl.BlockSpec((width, columns), lambda i: (0, 0)),
-            part,
-            ANY,
         ],
         out_specs=[
             pl.BlockSpec((ROW_TILE, width), lambda i: (i, 0)),
             pl.BlockSpec((ROW_TILE, columns), lambda i: (i, 0)),
-            part,
-            ANY,
         ],
         out_shape=[
             jax.ShapeDtypeStruct((count, width), jnp.bfloat16),
             jax.ShapeDtypeStruct((count, columns), jnp.float32),
-            jax.ShapeDtypeStruct(cotangent.shape, jnp.bfloat16),
-            jax.ShapeDtypeStruct((4, depth, units // 4), down.dtype),
         ],
-        scratch_shapes=wires(3) + [pltpu.SemaphoreType.DMA],
-        compiler_params=pltpu.CompilerParams(
-            collective_id=6, has_side_effects=True, vmem_limit_bytes=VMEM_LIMIT
-        ),
-        cost_estimate=lasting(25),
+        compiler_params=pltpu.CompilerParams(vmem_limit_bytes=VMEM_LIMIT),
+        cost_estimate=lasting(4),
         name="first_rows",
-    )(values, gains, packed, cotangent, down)
-
-
-def attention_weights_kernel(hidden, back, grad, attended, weight, moving, *rest):
-    out, rows_out, moved, sent, landed, local = rest[-6:]
+    )(values, gains, packed)
+
+
+def attention_weights_kernel(hidden, back, grad, attended, moving, *rest):
+    out, moved, sent, landed, local = rest[-5:]
     step, last = pl.program_id(0), pl.num_programs(0) - 1
 
     @pl.when(step == 0)
@@ -1521,7 +1638,6 @@
     columns = back.shape[1]
     out[:, :columns] = dot(hidden[...], back[...], FIRST).astype(jnp.bfloat16)
     out[:, columns:] = dot(grad[...], attended[...], FIRST).astype(jnp.bfloat16)
-    rows_out[...] = dot(back[...], weight[...], LAST).astype(jnp.bfloat16)
 
     @pl.when(step == last)
     def finish():
@@ -1533,7 +1649,7 @@
         pltpu.make_async_copy(moving.at[p.rank], moved.at[p.rank], local).wait()
 
 
-def attention_weights(hidden, back, grad, attended, weight, moving, early):
+def attention_weights(hidden, back, grad, attended, moving, early):
     count, width = hidden.shape
     first, second = back.shape[1], attended.shape[1]
     tall = pl.BlockSpec((count, 256), lambda i: (0, i))
@@ -1545,13 +1661,11 @@
             pl.BlockSpec((count, first), lambda i: (0, 0)),
             tall,
             pl.BlockSpec((count, second), lambda i: (0, 0)),
-            pl.BlockSpec((256, first), lambda i: (i, 0)),
         ]
         + [ANY] * (1 + len(early)),
-        out_specs=[pl.BlockSpec((256, first + second), lambda i: (i, 0)), tall, ANY],
+        out_specs=[pl.BlockSpec((256, first + second), lambda i: (i, 0)), ANY],
         out_shape=[
             jax.ShapeDtypeStruct((width, first + second), jnp.bfloat16),
-            jax.ShapeDtypeStruct((count, width), jnp.bfloat16),
             jax.ShapeDtypeStruct(moving.shape, moving.dtype),
         ],
         scratch_shapes=wires(3) + [pltpu.SemaphoreType.DMA],
@@ -1560,7 +1674,7 @@
         ),
         cost_estimate=lasting(25),
         name="attention_weights",
-    )(hidden, back, grad, attended, weight, moving, *early)
+    )(hidden, back, grad, attended, moving, *early)
 
 
 ROW_TILE = 256
@@ -1665,20 +1779,12 @@
         ).reshape(depth, -1)
         packed, gain_rows = first_exchange(w_query, w_pair, out_turned, gains)
         packed = over_groups(packed)
-        gate_blocks = exchange_columns(w_gate, gain_rows)
-        inputs_full, up_blocks, ffn_grad = start_plane(
-            tokens_half, w_up, cotangent, gate_blocks
+        both_blocks, down_blocks = exchange_columns(w_gate, w_up, down_turned, gain_rows)
+        inputs_full, ffn_grad, my_ffn_grad = start_plane(tokens_half, cotangent, down_blocks)
+        both_full, down_full = over_groups(both_blocks), over_groups(down_blocks)
+        hidden_first, raw = first_rows(
+            inputs_full.reshape(-1, inputs_full.shape[3]), gain_rows, packed, columns_qkv
         )
-        gate_full, up_full = over_groups(gate_blocks), over_groups(up_blocks)
-        hidden_first, raw, my_ffn_grad, down_blocks = first_rows(
-            inputs_full.reshape(-1, inputs_full.shape[3]),
-            gain_rows,
-            packed,
-            columns_qkv,
-            cotangent_half,
-            down_turned,
-        )
-        down_full = over_groups(down_blocks)
         out_full = packed[:, columns_qkv:]
     else:
         gains = jnp.stack([attn_gain, ffn_gain], axis=1)
@@ -1699,7 +1805,7 @@
         out_full = packed[:, columns_qkv : columns_qkv + width]
         gains_full = packed[:, columns_qkv + width :].astype(jnp.float32)
         attn_scale, ffn_scale = gains_full[:, 0], gains_full[:, 1]
-        gate_full, up_full = spread(blocks(w_gate)), spread(blocks(w_up))
+        both_full = spread(jnp.concatenate([blocks(w_gate), blocks(w_up)], axis=2))
         down_full = spread(blocks(down_turned))
         inputs_full = gather_rows(tokens_half).astype(jnp.float32)
         hidden_first = inputs_full * inverse_root(inputs_full) * attn_scale
@@ -1723,28 +1829,30 @@
     grad_result = cotangent_half.astype(jnp.float32)
 
     attended, *kept = attention_forward(places, starts, raw, tables)
-    branch = dot(attended, out_full, LAST).astype(jnp.bfloat16)
     if square:
         ffn_grad_blocks = [
             lax.ppermute(my_ffn_grad, "context", context_pairs(step)) for step in (1, 2, 3)
         ]
-        hidden_second, middle, ffn_grad = middle_plane(
-            branch, tokens_half, gain_rows, ffn_grad, ffn_grad_blocks
+        hidden_block, middle, ffn_grad = middle_plane(
+            attended, packed, tokens_half, gain_rows, ffn_grad, ffn_grad_blocks
         )
     else:
         ffn_grad = gather_rows(my_ffn_grad)
-        middle = residual_in + residual_scale * scatter_rows(branch)
+        middle = residual_in + residual_scale * scatter_rows(dot(attended, out_full, LAST))
         hidden_second = gather_rows((middle * inverse_root(middle) * ffn_scale).astype(jnp.bfloat16))
 
     units = down_full.shape[1]
-    hidden, gate_proj, up_proj = row_tiles(
-        ffn_first_kernel,
-        "ffn_first",
-        [hidden_second],
-        [gate_full, up_full],
-        [],
-        [units, units, units],
-    )
+    if square:
+        hidden_second, hidden, gate_proj, up_proj = ffn_rows(hidden_block, both_full)
+    else:
+        hidden, gate_proj, up_proj = row_tiles(
+            ffn_first_kernel,
+            "ffn_first",
+            [hidden_second],
+            [both_full],
+            [],
+            [units, units, units],
+        )
     grad_down = dot(ffn_grad, hidden, FIRST).astype(jnp.bfloat16)
     (slopes,) = row_tiles(
         ffn_slopes_kernel,
@@ -1767,8 +1875,7 @@
         grad_middle, my_attn_grad, grad_gate = second_plane(
             slopes,
             hidden_second,
-            gate_full,
-            up_full,
+            both_full,
             middle,
             cotangent_half,
             gain_rows,
@@ -1785,8 +1892,7 @@
         ffn_out = dot(hidden, down_full, LAST)
         grad_gate = dot(hidden_second, slopes[:, :units], FIRST).astype(jnp.bfloat16)
         grad_up = dot(hidden_second, slopes[:, units:], FIRST).astype(jnp.bfloat16)
-        grad_second = dot(slopes[:, :units], gate_full, LAST)
-        grad_second += dot(slopes[:, units:], up_full, LAST)
+        grad_second = dot(slopes, both_full, LAST)
         grad_middle = grad_result + norm_backward(
             scatter_rows(grad_second) * ffn_scale, middle * root, root
         )
@@ -1798,12 +1904,11 @@
     back = attention_backward(places, starts, grad_attended, kept, tables, [grad_down])
     grad_down = hand_back(grad_down)
     if square:
-        grad_attn, grad_first, grad_gate = attention_weights(
+        grad_attn, grad_gate = attention_weights(
             hidden_first,
             back,
             attn_grad,
             attended,
-            packed,
             grad_gate.reshape(groups, depth, -1),
             [grad_down, *ffn_parts[1:]],
         )
@@ -1816,7 +1921,8 @@
     grad_attn = sum_groups(grad_attn)
     if square:
         grad_tokens, result, grad_up, ffn_sums = last_plane(
-            grad_first,
+            back,
+            packed,
             tokens_half,
             grad_middle,
             gain_rows,

time: 696 us -> 674 us (0.968)
  local copies, waits for them, and re-layouts: 33.9 us -> 17.5 us
  matrix products: 32.8 us -> 25 us
  Pallas kernels: 586 us -> 579 us
    pallas_call x3 -> x4, Pallas kernels: 130 us -> 167 us  [the longest x1 58.9 us: ffn_rows(): pl.pallas_call(ffn_rows_kernel, out_shape=[full, part, part, part], in_sp...]
    pallas_call x2 -> x1, Pallas kernels: 50.4 us -> 22.2 us  [row_tiles(): pl.pallas_call(kernel, grid=(count // ROW_TILE,), in_specs=[tile(r.shape[...]
    unnamed x74 -> x26, local copies, waits for them, and re-layouts: 30.2 us -> 11.3 us
    pallas_call x1, Pallas kernels: 63.1 us -> 51.7 us  [start_plane(): pl.pallas_call(start_kernel, out_shape=[jax.ShapeDtypeStruct((4, 2, share...]
    reduce_scatter x4, waiting for transfers between devices: 0.05 us -> 9.25 us  [sum_groups(): return lax.psum_scatter(gradient, 'fsdp', scatter_dimension=0, tiled=True)]
    dot_general x3 -> x2, matrix products: 32.8 us -> 25 us  [dot(): lax.dot_general(left_side, right_side, dims, preferred_element_type=jnp.f...]
  transfers between devices with their start and end apart: 15 -> 14, of which waited for: 1 -> 4; matrix products, arithmetic and copies ran while one was open for 5% -> 5% of each run, Pallas kernels for 79% -> 81%
where the time goes in v7:
time: 674 us; the launch traced here: 664 us
  Pallas kernels  579 us (86%)
  matrix products  25 us (4%)
  local copies, waits for them, and re-layouts  17.5 us (3%)
  between operations  14.8 us (2%)
  waiting for transfers between devices  14.6 us (2%)
  starting transfers between devices  11.3 us (2%)
    pallas_call x1, Pallas kernels, last_plane(): pl.pallas_call(last_kernel, out_shape=[jax.ShapeDtypeStruct((2, share, wi...  66.4 us
    pallas_call x1, Pallas kernels, second_plane(): pl.pallas_call(second_kernel, out_shape=[jax.ShapeDtypeStruct((share, wid...  64.4 us
    pallas_call x1, Pallas kernels, ffn_rows(): pl.pallas_call(ffn_rows_kernel, out_shape=[full, part, part, part], in_sp...  58.9 us
    pallas_call x1, Pallas kernels, middle_plane(): pl.pallas_call(middle_kernel, out_shape=[jax.ShapeDtypeStruct((share, wid...  56.3 us
    pallas_call x1, Pallas kernels, spread_plane(): pl.pallas_call(spread_kernel, out_shape=[full] + [jax.ShapeDtypeStruct((s...  54.9 us
    pallas_call x1, Pallas kernels, attention_backward(): pl.pallas_call(attention_backward_kernel, out_shape=jax.ShapeDtypeStruct(...  53.6 us
    pallas_call x1, Pallas kernels, start_plane(): pl.pallas_call(start_kernel, out_shape=[jax.ShapeDtypeStruct((4, 2, share...  51.7 us
    pallas_call x1, Pallas kernels, attention_forward(): pl.pallas_call(attention_forward_kernel, out_shape=[kept] * 4 + [jax.Shap...  38.5 us
  transfers between devices with their start and end apart: 14, of which 4 were waited for; matrix products, arithmetic and copies ran while one was open for 5% of the time, Pallas kernels for 81%

profile of v7, /device:TPU:0, one launch (start us, length us, event | category | flops | bytes accessed | tf_op | source)
XLA Modules:
  0.0 663.5 jit_solution(7844558069851980637)
XLA Ops:
  10.1 1.8 copy.34
  13.2 17.6 %first_exchange.1 = (bf16[4,128,640]{2,1,0:T(8,128)(2,1)}, f32[8,2048]{1,0:T(8,128)}) custom-call(bf16[128,1024]{1,0:T(8,128)(2,1)} %query.3, bf16[128,512]{1,0:T(8,128)(2,1)} %copy.35.pair, bf16[128,1024]{1,0:T(8,128)(2,1)} %bitcast.65, f32[8,128]{1,0:T(8,128)} %pad.4.gains), custom_call_target="tpu_custom_call" | custom-call | bytes 30000000 | tf_op jit(solution)/shard_map/first_exchange/pallas_call | solution.py:646
  30.9 2.3 copy.30
  33.2 37.8 %exchange_columns.1 = (bf16[4,128,2048]{2,1,0:T(8,128)(2,1)}, bf16[4,128,1024]{2,1,0:T(8,128)(2,1)}) custom-call(bf16[128,4096]{1,0:T(8,128)(2,1)} %rest_6_.1, bf16[128,4096]{1,0:T(8,128)(2,1)} %rest_7_.1, bf16[128,4096]{1,0:T(8,128)(2,1)} %bitcast.59, f32[8,2048]{1,0:T(8,128)} %get-tuple-element.58.early.gains.gain), custom_call_target="tpu_custom_call" | custom-call | bytes 90000000 | tf_op jit(solution)/shard_map/exchange_columns/pallas_call | solution.py:721
  73.0 51.7 %gather_tokens.1 = (bf16[4,2,320,2048]{3,2,1,0:T(8,128)(2,1)}, bf16[640,2048]{1,0:T(8,128)(2,1)}, bf16[320,2048]{1,0:T(8,128)(2,1)}) custom-call(bf16[320,2048]{1,0:T(8,128)(2,1)} %constant_dynamic-slice_fusion.1.block.residual.rest_8_, bf16[640,2048]{1,0:T(8,128)(2,1)} %cotangent.1, bf16[4,128,1024]{2,1,0:T(8,128)(2,1)} %get-tuple-element.59.early), custom_call_target="tpu_custom_call" | custom-call | bytes 180000000 | tf_op jit(solution)/shard_map/gather_tokens/pallas_call | solution.py:688
  126.9 1.5 collective-permute-start.2
  128.9 14.2 %first_rows.1 = (bf16[2560,2048]{1,0:T(8,128)(2,1)}, f32[2560,384]{1,0:T(8,128)}) custom-call(bf16[2560,2048]{1,0:T(8,128)(2,1)} %bitcast.49, f32[8,2048]{1,0:T(8,128)} %get-tuple-element.58.early.gains.gain, bf16[2048,640]{1,0:T(8,128)(2,1)} %all-gather.4.cloned.1.call-done.weight.weights), custom_call_target="tpu_custom_call" | custom-call | bytes 12000000 | tf_op jit(solution)/shard_map/first_rows/pallas_call | solution.py:1605
  143.0 38.5 %attention_forward.1 = (bf16[2560,256]{1,0:T(8,128)(2,1)}, bf16[2560,256]{1,0:T(8,128)(2,1)}, bf16[2560,256]{1,0:T(8,128)(2,1)}, bf16[2560,256]{1,0:T(8,128)(2,1)}, f32[4,1,2560]{2,1,0:T(1,128)}) custom-call(s32[20]{0:T(128)} %compare_select_fusion.1.to_ref, s32[20]{0:T(128)} %bitcast.77, f32[2560,384]{1,0:T(8,128)} %get-tuple-element.63.raw_ref, ...), custom_call_target="tpu_custom_call" | custom-call | flops 5368709120 | bytes 10485760 | tf_op jit(solution)/shard_map/attention_forward/pallas_call | solution.py:313
  181.5 3.4 collective-permute-done.1.from_y
  186.0 56.3 %middle_rows.1 = (bf16[320,2048]{1,0:T(8,128)(2,1)}, f32[320,2048]{1,0:T(8,128)}, bf16[4,2,320,2048]{3,2,1,0:T(8,128)(2,1)}) custom-call(bf16[4,2,320,256]{3,2,1,0:T(8,128)(2,1)} %bitcast.57, bf16[2048,640]{1,0:T(8,128)(2,1)} %all-gather.4.cloned.1.call-done.weight.weights, bf16[320,2048]{1,0:T(8,128)(2,1)} %constant_dynamic-slice_fusion.1.block.residual.rest_8_, ...), custom_call_target="tpu_custom_call" | custom-call | bytes 165000000 | tf_op jit(solution)/shard_map/middle_rows/pallas_call | solution.py:795
  242.4 58.9 %ffn_rows.1 = (bf16[4,2,320,2048]{3,2,1,0:T(8,128)(2,1)}, bf16[4,2,320,1024]{3,2,1,0:T(8,128)(2,1)}, bf16[4,2,320,1024]{3,2,1,0:T(8,128)(2,1)}, bf16[4,2,320,1024]{3,2,1,0:T(8,128)(2,1)}) custom-call(bf16[320,2048]{1,0:T(8,128)(2,1)} %get-tuple-element.68.block, bf16[2048,2048]{1,0:T(8,128)(2,1)} %all-gather.6.cloned.1.call-done.weights_in.weights), custom_call_target="tpu_custom_call" | custom-call | bytes 180000000 | tf_op jit(solution)/shard_map/ffn_rows/pallas_call | solution.py:937
  301.3 16.8 %bitcast_convert_fusion.early = bf16[2048,1024]{1,0:T(8,128)(2,1)} fusion(bf16[4,2,320,2048]{3,2,1,0:T(8,128)(2,1)} %get-tuple-element.67, bf16[4,2,320,1024]{3,2,1,0:T(8,128)(2,1)} %get-tuple-element.72.m), kind=kOutput, calls=%fused_computation | convolution fusion | flops 10739515392 | bytes 19922944 | tf_op jit(solution)/shard_map/dot_general | solution.py:32
  318.1 1.7 copy-done.3
  321.0 22.2 %ffn_slopes.1.slopes = bf16[2560,2048]{1,0:T(8,128)(2,1)} custom-call(bf16[2560,2048]{1,0:T(8,128)(2,1)} %bitcast.52, bf16[2560,1024]{1,0:T(8,128)(2,1)} %bitcast.54, bf16[2560,1024]{1,0:T(8,128)(2,1)} %bitcast.55, bf16[2048,1024]{1,0:T(8,128)(2,1)} %all-gather.8.cloned.1.call-done.down_w, bf16[2048,1024]{1,0:T(8,128)(2,1)} %bitcast_convert_fusion.early), custom_call_target="tpu_custom_call" | custom-call | flops 10737418240 | bytes 26843544 | tf_op jit(solution)/shard_map/ffn_slopes/pallas_call | solution.py:1693
  343.2 64.4 %second_rows.1 = (f32[320,2048]{1,0:T(8,128)}, bf16[320,2048]{1,0:T(8,128)(2,1)}, bf16[2048,1024]{1,0:T(8,128)(2,1)}) custom-call(bf16[2560,2048]{1,0:T(8,128)(2,1)} %ffn_slopes.1.slopes, bf16[2560,2048]{1,0:T(8,128)(2,1)} %bitcast.47, bf16[2048,2048]{1,0:T(8,128)(2,1)} %all-gather.6.cloned.1.call-done.weights_in.weights, ...), custom_call_target="tpu_custom_call" | custom-call | bytes 180000000 | tf_op jit(solution)/shard_map/second_rows/pallas_call | solution.py:1183
  407.9 54.9 %spread_rows.1 = (bf16[4,2,320,2048]{3,2,1,0:T(8,128)(2,1)}, bf16[320,2048]{1,0:T(8,128)(2,1)}, bf16[320,2048]{1,0:T(8,128)(2,1)}, bf16[320,2048]{1,0:T(8,128)(2...) custom-call(bf16[320,2048]{1,0:T(8,128)(2,1)} %get-tuple-element.75.hidden, ...), custom_call_target="tpu_custom_call" | custom-call | bytes 180000000 | tf_op jit(solution)/shard_map/spread_rows/pallas_call | solution.py:1284
  466.4 8.2 %convolution_convert_fusion.grad_ref = bf16[2560,256]{1,0:T(8,128)(2,1)} fusion(bf16[2560,2048]{1,0:T(8,128)(2,1)} %bitcast.50, bf16[2048,640]{1,0:T(8,128)(2,1)} %all-gather.4.cloned.1.call-done.weight.weights), kind=kOutput, calls=%fused_computation.1 | convolution fusion | flops 2685009920 | bytes 12845056 | tf_op jit(solution)/shard_map/dot_general | solution.py:32
  474.6 3.5 all-to-all-start
  478.4 53.6 %attention_backward.1.back = bf16[2560,384]{1,0:T(8,128)(2,1)} custom-call(s32[20]{0:T(128)} %compare_select_fusion.1.to_ref, s32[20]{0:T(128)} %bitcast.78, bf16[2560,256]{1,0:T(8,128)(2,1)} %convolution_convert_fusion.grad_ref, bf16[2560,256]{1,0:T(8,128)(2,1)} %get-tuple-element.78.q_ref, bf16[2560,256]{1,0:T(8,128)(2,1)} %get-tuple-element.79.k_ref, ...), custom_call_target="tpu_custom_call" | custom-call | flops 13421772800 | bytes 10485760 | tf_op jit(solution)/shard_map/attention_backward/pallas_call | solution.py:331
  534.1 18.0 %attention_weights.1 = (bf16[2048,640]{1,0:T(8,128)(2,1)}, bf16[4,128,1024]{2,1,0:T(8,128)(2,1)}) custom-call(bf16[2560,2048]{1,0:T(8,128)(2,1)} %get-tuple-element.62.hidden, bf16[2560,384]{1,0:T(8,128)(2,1)} %attention_backward.1.back, bf16[2560,2048]{1,0:T(8,128)(2,1)} %bitcast.51, bf16[2560,256]{1,0:T(8,128)(2,1)} %get-tuple-element.64.attended, ...), custom_call_target="tpu_custom_call" | custom-call | bytes 75000000 | tf_op jit(solution)/shard_map/attention_weights/pallas_call | solution.py:1656
  552.1 9.2 %reduce-scatter.11.cloned.1.call-done = bf16[512,1024]{1,0:T(8,128)(2,1)} async-done(((bf16[2048,1024]{1,0:T(8,128)(2,1)}), bf16[512,1024]{1,0:T(8,128)(2,1)}) %reduce-scatter.11.cloned.1.call-update) | async-done | bytes 1048592 | tf_op jit(solution)/shard_map/reduce_scatter | solution.py:1866
  561.4 66.4 %last_rows.1 = (f32[2,320,2048]{2,1,0:T(8,128)}, bf16[2,320,2048]{2,1,0:T(8,128)(2,1)}, bf16[4,128,1024]{2,1,0:T(8,128)(2,1)}, f32[128,128]{1,0:T(8,128)}) custom-call(bf16[4,2,320,384]{3,2,1,0:T(8,128)(2,1)} %bitcast.53, bf16[2048,640]{1,0:T(8,128)(2,1)} %all-gather.4.cloned.1.call-done.weight.weights, f32[8,2048]{1,0:T(8,128)} %get-tuple-element.58.early.gains.gain, ...), custom_call_target="tpu_custom_call" | custom-call | bytes 210000000 | tf_op jit(solution)/shard_map/last_rows/pallas_call | solution.py:1407
  627.8 14.2 %exchange_blocks.1 = (bf16[4,128,640]{2,1,0:T(8,128)(2,1)}, f32[2,128,128]{2,1,0:T(8,128)}) custom-call(bf16[4,128,640]{2,1,0:T(8,128)(2,1)} %bitcast.69, bf16[128,1024]{1,0:T(8,128)(2,1)} %query.3, bf16[128,512]{1,0:T(8,128)(2,1)} %copy.35.pair, f32[128,128]{1,0:T(8,128)} %get-tuple-element.90.other_sums), custom_call_target="tpu_custom_call" | custom-call | bytes 24000000 | tf_op jit(solution)/shard_map/exchange_blocks/pallas_call | solution.py:1474
  642.0 10.3 %finish.1 = (f32[128,1024]{1,0:T(8,128)}, f32[128,512]{1,0:T(8,128)}, f32[1024,128]{1,0:T(8,128)}, f32[128,4096]{1,0:T(8,128)}, f32[128,4096]{1,0:T(8,128)}, /*i...) custom-call(bf16[4,128,640]{2,1,0:T(8,128)(2,1)} %get-tuple-element.91.attn, ...), custom_call_target="tpu_custom_call" | custom-call | bytes 36000000 | tf_op jit(solution)/shard_map/finish/pallas_call | solution.py:1524
  (65 shorter events, 21.3 us)
Async XLA Ops:
  7.2 64.6 %copy-start = (bf16[640,2048]{1,0:T(8,128)(2,1)S(1)}, bf16[640,2048]{1,0:T(8,128)(2,1)}, u32[]{:S(2)}) copy-start(bf16[640,2048]{1,0:T(8,128)(2,1)} %param.16) | copy-start | bytes 7864324
  7.2 121.7 %all-gather.4.cloned.1.call-start = ((), (), s32[]{:S(2)}) async-start(), calls=%async_computation.5 | async-start | bytes 3276800 | tf_op jit(solution)/shard_map/all_gather | solution.py:1771
  12.6 58.4 %copy-start.7 = (f32[2,128]{1,0:T(2,128)}, f32[2,128]{1,0:T(2,128)S(1)}, u32[]{:S(2)}) copy-start(f32[2,128]{1,0:T(2,128)S(1)} %maximum_convert_fusion.gains) | copy-start | bytes 3076
  30.8 211.5 %all-gather.6.cloned.1.call-start = ((), (), s32[]{:S(2)}) async-start(), calls=%async_computation.6 | async-start | bytes 10485760 | tf_op jit(solution)/shard_map/all_gather | solution.py:1771
  71.0 250.0 %all-gather.8.cloned.1.call-start = ((), (), s32[]{:S(2)}) async-start(), calls=%async_computation.7 | async-start | bytes 5242880 | tf_op jit(solution)/shard_map/all_gather | solution.py:1771
  71.8 402.8 %reduce-scatter.5.cloned.1.call-start = ((), (), s32[]{:S(2)}) async-start(), calls=%async_computation.8 | async-start | bytes 5242880 | tf_op jit(solution)/shard_map/reduce_scatter | solution.py:1866
  73.0 55.3 %copy-start.8 = (s32[1,20]{1,0:T(1,128)S(1)}, s32[1,20]{1,0:T(1,128)}, u32[]{:S(2)}) copy-start(s32[1,20]{1,0:T(1,128)} %param.27) | copy-start | bytes 244
  73.0 55.3 %copy-start.9 = (s32[1,20]{1,0:T(1,128)S(1)}, s32[1,20]{1,0:T(1,128)}, u32[]{:S(2)}) copy-start(s32[1,20]{1,0:T(1,128)} %param.28) | copy-start | bytes 244
  124.8 56.8 %collective-permute-start = (bf16[320,2048]{1,0:T(8,128)(2,1)}, bf16[320,2048]{1,0:T(8,128)(2,1)S(1)}, u32[]{:S(2)}, u32[]{:S(2)}) collective-permute-start(bf16[320,2048]{1,0:T(8,128)(2,1)} %get-tuple-element.66), channel_id=1, source_target_pairs={{0,2},{2,0},{4,6},{6,4},{1,3},{3,1},{5,7},{7,5},{8,10},{10,8},{12,... | collective-permute-start | bytes 3932168 | tf_op jit(solution)/shard_map/ppermute | solution.py:1834
  125.8 59.1 %collective-permute-start.1 = (bf16[320,2048]{1,0:T(8,128)(2,1)}, bf16[320,2048]{1,0:T(8,128)(2,1)S(1)}, u32[]{:S(2)}, u32[]{:S(2)}) collective-permute-start(bf16[320,2048]{1,0:T(8,128)(2,1)} %get-tuple-element.66), channel_id=1, source_target_pairs={{0,4},{2,6},{4,0},{6,2},{1,5},{3,7},{5,1},{7,3},{8,12},{10,14},{12... | collective-permute-start | bytes 3932168 | tf_op jit(solution)/shard_map/ppermute | solution.py:1834
  126.9 58.1 %collective-permute-start.2 = (bf16[320,2048]{1,0:T(8,128)(2,1)}, bf16[320,2048]{1,0:T(8,128)(2,1)}, u32[]{:S(2)}, u32[]{:S(2)}) collective-permute-start(bf16[320,2048]{1,0:T(8,128)(2,1)} %get-tuple-element.66), channel_id=1, source_target_pairs={{0,6},{2,4},{4,2},{6,0},{1,7},{3,5},{5,3},{7,1},{8,14},{10,12},{12... | collective-permute-start | bytes 3932168 | tf_op jit(solution)/shard_map/ppermute | solution.py:1834
  181.5 3.5 copy-start.5
  184.9 1.1 copy-start.6
  318.1 1.7 copy-start.3
  318.1 213.9 %reduce-scatter.7.cloned.1.call-start = ((), (), s32[]{:S(2)}) async-start(), calls=%async_computation.9 | async-start | bytes 5242880 | tf_op jit(solution)/shard_map/reduce_scatter | solution.py:1866
  407.7 153.7 %reduce-scatter.11.cloned.1.call-start = ((), (), s32[]{:S(2)}) async-start(), calls=%async_computation.11 | async-start | bytes 5242880 | tf_op jit(solution)/shard_map/reduce_scatter | solution.py:1866
  462.9 69.1 %collective-permute-start.3 = (bf16[320,2048]{1,0:T(8,128)(2,1)}, bf16[320,2048]{1,0:T(8,128)(2,1)S(1)}, u32[]{:S(2)}, u32[]{:S(2)}) collective-permute-start(bf16[320,2048]{1,0:T(8,128)(2,1)} %get-tuple-element.82), channel_id=1, source_target_pairs={{0,2},{2,0},{4,6},{6,4},{1,3},{3,1},{5,7},{7,5},{8,10},{10,8},{12,... | collective-permute-start | bytes 3932168 | tf_op jit(solution)/shard_map/ppermute | solution.py:1888
  464.1 67.9 %collective-permute-start.4 = (bf16[320,2048]{1,0:T(8,128)(2,1)}, bf16[320,2048]{1,0:T(8,128)(2,1)}, u32[]{:S(2)}, u32[]{:S(2)}) collective-permute-start(bf16[320,2048]{1,0:T(8,128)(2,1)} %get-tuple-element.83), channel_id=1, source_target_pairs={{0,4},{2,6},{4,0},{6,2},{1,5},{3,7},{5,1},{7,3},{8,12},{10,14},{12... | collective-permute-start | bytes 3932168 | tf_op jit(solution)/shard_map/ppermute | solution.py:1888
  465.0 67.0 %collective-permute-start.5 = (bf16[320,2048]{1,0:T(8,128)(2,1)}, bf16[320,2048]{1,0:T(8,128)(2,1)}, u32[]{:S(2)}, u32[]{:S(2)}) collective-permute-start(bf16[320,2048]{1,0:T(8,128)(2,1)} %get-tuple-element.84), channel_id=1, source_target_pairs={{0,6},{2,4},{4,2},{6,0},{1,7},{3,5},{5,3},{7,1},{8,14},{10,12},{12... | collective-permute-start | bytes 3932168 | tf_op jit(solution)/shard_map/ppermute | solution.py:1888
  474.6 58.5 %all-to-all-start = ((bf16[4,128,1024]{2,1,0:T(8,128)(2,1)}), bf16[4,128,1024]{2,1,0:T(8,128)(2,1)S(1)}, u32[]{:S(2)}, u32[]{:S(2)}) async-start(bf16[4,128,1024]{2,1,0:T(8,128)(2,1)} %bitcast.64), calls=%async_computation.2 | async-start | bytes 2097152 | tf_op jit(solution)/shard_map/all_to_all | solution.py:1869
  478.1 149.7 %reduce-scatter.9.cloned.1.call-start = ((), (), s32[]{:S(2)}) async-start(), calls=%async_computation.10 | async-start | bytes 3276800 | tf_op jit(solution)/shard_map/reduce_scatter | solution.py:1866
  532.0 1.2 copy-start.4
  533.1 1.0 copy-start.2
  642.0 14.2 %copy-start.1 = (bf16[640,2048]{1,0:T(8,128)(2,1)S(1)}, bf16[640,2048]{1,0:T(8,128)(2,1)}, u32[]{:S(2)}) copy-start(bf16[640,2048]{1,0:T(8,128)(2,1)} %param.16) | copy-start | bytes 7864324
Sparse Core Ops, SparseCore 0:
  31.0 52.9 all-gather.3
  85.6 148.3 all-gather.5
  235.6 79.0 all-gather.7
  318.2 74.4 reduce-scatter.4
  407.8 74.0 reduce-scatter.6
  484.0 77.2 reduce-scatter.10
  563.8 52.5 reduce-scatter.8

commit v8 on v7

--- a/solution.py
+++ b/solution.py
@@ -649,7 +649,7 @@
             jax.ShapeDtypeStruct((4, depth, columns // 2 + 128), query.dtype),
             jax.ShapeDtypeStruct((8, groups * 4 * depth), jnp.float32),
         ],
-        in_specs=[ANY, ANY, ANY, VMEM],
+        in_specs=[VMEM] * 4,
         out_specs=[ANY, VMEM],
         scratch_shapes=wires(9) + [pltpu.SemaphoreType.DMA((3,))] + wires(far),
         compiler_params=pltpu.CompilerParams(collective_id=9, has_side_effects=True),
@@ -658,14 +658,15 @@
     )(query, pair, out_turned, gains)
 
 
-def start_kernel(block, cotangent, early, out, scaled, my_scaled, sent, landed, local):
+def start_kernel(tokens, cotangent, early, out, scaled, my_scaled, sent, landed, local):
     p = Plane(sent, landed)
+    share = my_scaled.shape[0]
+    block = tokens.at[pl.ds(pl.multiple_of(p.core * share, SLAB), share)]
     gather = Gather(p, block, out)
     mine = pltpu.make_async_copy(block, out.at[p.rank, p.core], local)
     for k in range(CHUNKS):
         gather.start(k)
     mine.start()
-    share = block.shape[0]
 
     def scale(rows):
         value = residual_scale * cotangent[rows, :].astype(jnp.float32)
@@ -683,14 +684,14 @@
     mine.wait()
 
 
-def start_plane(block, cotangent, early):
-    share, width = block.shape
+def start_plane(tokens, cotangent, early):
+    share, width = tokens.shape[0] // 2, tokens.shape[1]
     return pl.pallas_call(
         start_kernel,
         out_shape=[
-            jax.ShapeDtypeStruct((4, 2, share, width), block.dtype),
+            jax.ShapeDtypeStruct((4, 2, share, width), tokens.dtype),
             jax.ShapeDtypeStruct(cotangent.shape, jnp.bfloat16),
-            jax.ShapeDtypeStruct(block.shape, jnp.bfloat16),
+            jax.ShapeDtypeStruct((share, width), jnp.bfloat16),
         ],
         in_specs=[VMEM, VMEM, ANY],
         out_specs=[ANY, VMEM, VMEM],
@@ -700,7 +701,7 @@
         ),
         cost_estimate=lasting(60),
         name="gather_tokens",
-    )(block, cotangent, early)
+    )(tokens, cotangent, early)
 
 
 def columns_kernel(gate, up, down, early, both_out, down_out, sent, landed, local):
@@ -724,7 +725,7 @@
             jax.ShapeDtypeStruct((4, depth, units // 2), gate.dtype),
             jax.ShapeDtypeStruct((4, depth, units // 4), gate.dtype),
         ],
-        in_specs=[ANY] * 4,
+        in_specs=[VMEM] * 3 + [ANY],
         out_specs=[ANY] * 2,
         scratch_shapes=wires(9) + [pltpu.SemaphoreType.DMA((3,))],
         compiler_params=pltpu.CompilerParams(collective_id=10, has_side_effects=True),
@@ -736,8 +737,8 @@
 def middle_kernel(
     attended,
     weights,
-    residual,
     gain,
+    tokens,
     beside,
     from_x,
     from_y,
@@ -748,6 +749,7 @@
     sent,
     landed,
     local,
+    residual,
     held_beside,
     held_blocks,
     *scratch,
@@ -757,6 +759,9 @@
     loads = [pltpu.make_async_copy(beside, held_beside, local.at[0])]
     for i, (block, rank) in enumerate(blocks):
         loads.append(pltpu.make_async_copy(block, held_blocks.at[i], local.at[i + 1]))
+    share = hidden.shape[0]
+    first = pl.ds(pl.multiple_of(p.core * share, SLAB), share)
+    loads.append(pltpu.make_async_copy(tokens.at[first], residual, local.at[4]))
     for started in loads:
         started.start()
     width = attended.shape[3]
@@ -772,7 +777,7 @@
         kept.append(pltpu.make_async_copy(held_blocks.at[i], place, local.at[i + 1]))
         kept[i + 1].start()
         across.append(p.send(held_blocks.at[i], place, p.sibling))
-    share = hidden.shape[0]
+    loads[4].wait()
 
     def work(rows):
         value = residual[rows, :].astype(jnp.float32) + residual_scale * total.rows(rows)
@@ -789,8 +794,8 @@
         started.wait()
 
 
-def middle_plane(attended, weights, residual, gain, beside, blocks):
-    share, width = residual.shape
+def middle_plane(attended, weights, tokens, gain, beside, blocks):
+    share, width = blocks[0].shape
     full = jax.ShapeDtypeStruct((4, 2, share, width), jnp.bfloat16)
     hidden, middle, beside_out = pl.pallas_call(
         middle_kernel,
@@ -799,11 +804,12 @@
             jax.ShapeDtypeStruct((share, width), jnp.float32),
             full,
         ],
-        in_specs=[VMEM] * 4 + [ANY] * 4,
+        in_specs=[VMEM] * 3 + [ANY] * 5,
         out_specs=[VMEM, VMEM, ANY],
         scratch_shapes=wires(SCATTER_COPIES + 3)
         + [
-            pltpu.SemaphoreType.DMA((4,)),
+            pltpu.SemaphoreType.DMA((5,)),
+            pltpu.VMEM((share, width), jnp.bfloat16),
             pltpu.VMEM((2, share, width), jnp.bfloat16),
             pltpu.VMEM((3, share, width), jnp.bfloat16),
         ]
@@ -816,8 +822,8 @@
     )(
         attended.reshape(4, 2, share, -1),
         weights,
-        residual,
         gain,
+        tokens,
         beside.reshape(2, share, width),
         *blocks,
     )
@@ -1018,9 +1024,9 @@
 def second_kernel(
     slopes,
     normed_rows,
-    weights,
-    middle,
-    cotangent,
+    weights_in,
+    middle_in,
+    cotangent_in,
     gain,
     early,
     grad_middle,
@@ -1029,6 +1035,10 @@
     sent,
     landed,
     loading,
+    beside,
+    weights,
+    middle,
+    cotangent,
     tile_wires,
     rows_in,
     tile_out,
@@ -1042,8 +1052,15 @@
     far_x,
     far_y,
 ):
+    share, width = near_x.shape
+    cuts = [slice(j * 512, j * 512 + 512) for j in range(width // 512)]
+    weight_loads = [
+        pltpu.make_async_copy(weights_in.at[cut], weights.at[cut], beside.at[2 + j])
+        for j, cut in enumerate(cuts)
+    ]
+    for started in weight_loads:
+        started.start()
     p = Plane(sent, landed)
-    share, width = near_x.shape
     half = share // 2
     order = (p.at_both, p.at_x, p.at_y, p.rank)
     top, low = halves = pl.ds(0, half), pl.ds(half, half)
@@ -1070,14 +1087,20 @@
         slot = u % 2
         gate_rows = jnp.concatenate([gate_in[rows, :] for rows in places(u)], axis=0)
         up_rows = jnp.concatenate([up_in[rows, :] for rows in places(u)], axis=0)
-        for j in range(width // 1024):
-            cut = slice(j * 1024, j * 1024 + 1024)
+        for j, cut in enumerate(cuts):
+            if u == 0:
+                weight_loads[j].wait()
             back = dot(gate_rows, weights[cut, :units], LAST) + dot(
                 up_rows, weights[cut, units:], LAST
             )
             given[slot, :, cut] = back[:half].astype(jnp.bfloat16)
             held[i, halves[h], cut] = back[half:].astype(jnp.bfloat16)
 
+    first = pl.ds(pl.multiple_of(p.core * share, SLAB), share)
+    row_loads = [
+        pltpu.make_async_copy(middle_in, middle, beside.at[0]),
+        pltpu.make_async_copy(cotangent_in.at[first], cotangent, beside.at[1]),
+    ]
     tiles = WeightTiles(normed_rows, gate_in, weight_grads, rows_in, tile_out, tile_wires)
 
     moves, across = {}, {}
@@ -1128,6 +1151,8 @@
             for started in loads(u):
                 started.wait()
 
+    for started in row_loads:
+        started.start()
     wait_loads((0,))
     unit(0)
     wait_loads((1,))
@@ -1162,6 +1187,8 @@
         grad_middle[rows, :] = gradient
         hidden[rows, :] = (residual_scale * gradient).astype(jnp.bfloat16)
 
+    for started in row_loads:
+        started.wait()
     for h in range(2):
         p.arrive(moves["x", h], near_x.at[halves[h]])
         p.arrive(moves["y", h], near_y.at[halves[h]])
@@ -1187,10 +1214,16 @@
             jax.ShapeDtypeStruct((share, width), kind),
             jax.ShapeDtypeStruct((width, units), kind),
         ],
-        in_specs=[ANY, ANY] + [VMEM] * 4 + [ANY],
+        in_specs=[ANY] * 5 + [VMEM, ANY],
         out_specs=[VMEM, VMEM, ANY],
         scratch_shapes=wires(8 + 6)
-        + [pltpu.SemaphoreType.DMA((8, 4))]
+        + [
+            pltpu.SemaphoreType.DMA((8, 4)),
+            pltpu.SemaphoreType.DMA((2 + width // 512,)),
+            pltpu.VMEM(weights.shape, kind),
+            pltpu.VMEM((share, width), jnp.float32),
+            pltpu.VMEM((share, width), kind),
+        ]
         + tile_scratch(count, units)
         + [
             pltpu.VMEM((count, units), kind),
@@ -1212,9 +1245,9 @@
 
 
 def spread_kernel(
-    hidden, m, down_w, normed_rows, slopes, early, out, pair_own, pair_x, pair_y, pair_both,
+    hidden, m, down_in, normed_rows, slopes, early, out, pair_own, pair_x, pair_y, pair_both,
     weight_grads, sent, landed, local, loading, tile_wires, rows_in, tile_out, up_in,
-    m_in, given, held, theirs,
+    m_in, given, held, theirs, down_w,
 ):
     p = Plane(sent, landed)
     share, width = hidden.shape
@@ -1235,9 +1268,12 @@
     across = []
     units = up_in.shape[1]
     up_load = pltpu.make_async_copy(slopes.at[:, pl.ds(units, units)], up_in, local.at[5])
+    down_load = pltpu.make_async_copy(down_in, down_w, local.at[6])
+    down_load.start()
     up_load.start()
     for started in loads(0):
         started.start()
+    down_load.wait()
     tiles = WeightTiles(normed_rows, up_in, weight_grads, rows_in, tile_out, tile_wires)
     for i in range(4):
         for started in loads(i):
@@ -1286,11 +1322,11 @@
         out_shape=[full]
         + [jax.ShapeDtypeStruct((share, width), jnp.bfloat16)] * 4
         + [jax.ShapeDtypeStruct((width, units), jnp.bfloat16)],
-        in_specs=[VMEM, ANY, VMEM, ANY, ANY, ANY],
+        in_specs=[VMEM] + [ANY] * 5,
         out_specs=[ANY] * 6,
         scratch_shapes=wires(GATHER_COPIES + 4)
         + [
-            pltpu.SemaphoreType.DMA((6,)),
+            pltpu.SemaphoreType.DMA((7,)),
             pltpu.SemaphoreType.DMA((2, 2)),
         ]
         + tile_scratch(8 * share, units)
@@ -1300,6 +1336,7 @@
             quarter,
             quarter,
             quarter,
+            pltpu.VMEM(down_w.shape, jnp.bfloat16),
         ],
         compiler_params=pltpu.CompilerParams(
             collective_id=7, has_side_effects=True, vmem_limit_bytes=60 * 1024 * 1024
@@ -1326,11 +1363,15 @@
     weights,
     gain,
     ups,
+    early,
     *rest,
 ):
     later, rest = rest[:LATER], rest[LATER:]
     out, result_out, up_out, gain_out, sent, landed, local, loading, held, result, sums = rest[:11]
     landing, scratch = rest[11 : 11 + LATER], rest[11 + LATER :]
+    share = landing[8].shape[0]
+    first = pl.ds(pl.multiple_of(lax.axis_index("tensor") * share, SLAB), share)
+    later = [*later[:8], later[8].at[first], later[9]]
     loads = [
         pltpu.make_async_copy(source, target, loading.at[i])
         for i, (source, target) in enumerate(zip(later, landing))
@@ -1339,11 +1380,11 @@
         started.start()
     middle, ffn_own, ffn_x, ffn_y, ffn_both, gates, gate, up, residual, grad_middle = landing
     p = Plane(sent, landed, diagonal=True)
+    total = Scatter(p, back, weights, slice(0, back.shape[3]), *scratch)
     moves = []
     for partner, rank in ((p.both, p.at_both), (p.x, p.at_x), (p.y, p.at_y)):
         moves.append((p.send(ups.at[rank], up_out.at[p.rank], partner), up_out.at[rank]))
     up_out[p.rank] = ups[p.rank]
-    total = Scatter(p, back, weights, slice(0, back.shape[3]), *scratch)
     share = held.shape[0]
 
     def finish_result(rows):
@@ -1359,18 +1400,17 @@
     given = p.send(result, result_out.at[p.core], p.sibling)
     units = gate.shape[1] // 4
 
-    def gain_rows(rows):
-        pairs = []
-        for c in range(4):
-            columns = slice(c * units, c * units + units)
-            pairs.append((gates[c, rows, :], gate[rows, columns]))
-            pairs.append((up_out[c, rows, :], up[rows, columns]))
-        sums[0, rows, :] = lane_sums(pairs)
-
-    for number, target in moves:
-        p.arrive(number, target)
-    slabs(0, gate.shape[0], gain_rows)
-    swapped = p.send(sums.at[0], sums.at[1], p.sibling)
+    def gate_rows(rows):
+        sums[0, rows, :] = lane_sums(
+            [(gates[c, rows, :], gate[rows, c * units : c * units + units]) for c in range(4)]
+        )
+
+    def up_rows(rows):
+        sums[0, rows, :] += lane_sums(
+            [(up_out[c, rows, :], up[rows, c * units : c * units + units]) for c in range(4)]
+        )
+
+    slabs(0, gate.shape[0], gate_rows)
 
     def work(rows):
         value = residual[rows, :].astype(jnp.float32)
@@ -1389,6 +1429,10 @@
         across.append(p.send(held.at[cut], out.at[p.core, cut], p.sibling))
     kept.append(pltpu.make_async_copy(held, out.at[p.core], local.at[1]))
     kept[1].start()
+    for number, target in moves:
+        p.arrive(number, target)
+    slabs(0, gate.shape[0], up_rows)
+    swapped = p.send(sums.at[0], sums.at[1], p.sibling)
     p.arrive(swapped, sums.at[1])
     gain_out[...] = sums[0] + sums[1]
     p.arrive(given, result_out.at[1 - p.core])
@@ -1400,10 +1444,10 @@
 
 
 def last_plane(
-    back, weights, residual, grad_middle, gain, middle, ffn_parts, ups, gates, gate, up
+    back, weights, tokens, grad_middle, gain, middle, ffn_parts, ups, gates, gate, up, early
 ):
-    share, width = residual.shape
-    later = [middle, *ffn_parts, gates, gate, up, residual, grad_middle]
+    share, width = grad_middle.shape
+    later = [middle, *ffn_parts, gates, gate, up, tokens, grad_middle]
     out, result_out, up_out, gain_out = pl.pallas_call(
         last_kernel,
         out_shape=[
@@ -1412,7 +1456,7 @@
             jax.ShapeDtypeStruct(ups.shape, ups.dtype),
             jax.ShapeDtypeStruct((gate.shape[0], 128), jnp.float32),
         ],
-        in_specs=[VMEM] * 4 + [ANY] * LATER,
+        in_specs=[VMEM] * 4 + [ANY] * (1 + LATER),
         out_specs=[ANY, ANY, VMEM, VMEM],
         scratch_shapes=wires(CHUNKS + 5 + SCATTER_COPIES)
         + [
@@ -1422,7 +1466,8 @@
             pltpu.VMEM((share, width), jnp.bfloat16),
             pltpu.VMEM((2, gate.shape[0], 128), jnp.float32),
         ]
-        + [pltpu.VMEM(array.shape, array.dtype) for array in later]
+        + [pltpu.VMEM(array.shape, array.dtype) for array in later[:8]]
+        + [pltpu.VMEM((share, width), tokens.dtype), pltpu.VMEM((share, width), jnp.float32)]
         + scatter_scratch(share, width),
         compiler_params=pltpu.CompilerParams(
             collective_id=4, has_side_effects=True, vmem_limit_bytes=VMEM_LIMIT
@@ -1434,6 +1479,7 @@
         weights,
         gain,
         ups,
+        early,
         *later,
     )
     return (
@@ -1486,25 +1532,56 @@
     )(blocks, query, pair, other_sums)
 
 
+def finish_first_kernel(down, gate, down_out, gate_out):
+    down_out[...] = jnp.transpose(down[0].astype(jnp.float32))
+    gate_out[...] = gate[0].astype(jnp.float32)
+
+
+def finish_first(down, gate):
+    groups, depth, units = down.shape
+    block = pl.BlockSpec((1, depth, units), lambda i: (i, 0, 0))
+    return pl.pallas_call(
+        finish_first_kernel,
+        grid=(groups,),
+        in_specs=[block, block],
+        out_specs=[
+            pl.BlockSpec((units, depth), lambda i: (i, 0)),
+            pl.BlockSpec((depth, units), lambda i: (0, i)),
+        ],
+        out_shape=[
+            jax.ShapeDtypeStruct((groups * units, depth), jnp.float32),
+            jax.ShapeDtypeStruct((depth, groups * units), jnp.float32),
+        ],
+        compiler_params=pltpu.CompilerParams(vmem_limit_bytes=VMEM_LIMIT),
+        cost_estimate=lasting(5),
+        name="finish_first",
+    )(down, gate)
+
+
 def finish_kernel(
-    attn, down, gate, up, tokens, result, sums, gains,
-    query_out, pair_out, out_out, gate_out, up_out, down_out, tokens_out, result_out, gain_out,
+    attn, up, tokens, result, sums, gains,
+    query_out, key_out, value_out, out_out, up_out, tokens_out, result_out, gain_out,
 ):
     width = query_out.shape[1]
     query_out[...] = attn[0, :, :width].astype(jnp.float32)
-    pair_out[...] = attn[0, :, width : width + 128].astype(jnp.float32)
+    for c in range(key_out.shape[1] // HEAD):
+
+        @pl.when(pl.program_id(0) == c)
+        def _(c=c):
+            cut = slice(c * HEAD, c * HEAD + HEAD)
+            key_out[:, cut] = attn[0, :, width : width + HEAD].astype(jnp.float32)
+            value_out[:, cut] = attn[0, :, width + HEAD : width + 2 * HEAD].astype(jnp.float32)
+
     out_out[...] = jnp.transpose(attn[0, :, width + 128 :].astype(jnp.float32))
-    gate_out[...] = gate[0].astype(jnp.float32)
     up_out[...] = up[0].astype(jnp.float32)
-    down_out[...] = jnp.transpose(down[0].astype(jnp.float32))
     tokens_out[...] = tokens[...]
     result_out[...] = result[...]
     for i in range(2):
         gain_out[i : i + 1, :] = jnp.transpose(sums[i])[0:1] / gains[i : i + 1, :]
 
 
-def finish(attn, down, gate, up, tokens, result, sums, gains):
-    groups, depth, units = down.shape
+def finish(attn, up, tokens, result, sums, gains):
+    groups, depth, units = up.shape
     width = attn.shape[2] // 2 - HEAD
     rows, columns = tokens.shape
     part = rows // groups
@@ -1526,8 +1603,6 @@
         grid=(groups,),
         in_specs=[
             block(depth, attn.shape[2]),
-            block(depth, units),
-            block(depth, units),
             block(depth, units),
             tall(part, columns),
             tall(part, columns),
@@ -1536,22 +1611,20 @@
         ],
         out_specs=[
             wide(width),
-            wide(128),
+            pl.BlockSpec((depth, groups * HEAD), lambda i: (0, 0)),
+            pl.BlockSpec((depth, groups * HEAD), lambda i: (0, 0)),
             tall(width, depth),
             wide(units),
-            wide(units),
-            tall(units, depth),
             tall(part, columns),
             tall(part, columns),
             pl.BlockSpec((2, 128), lambda i: (0, 0)),
         ],
         out_shape=[
             f32(depth, groups * width),
-            f32(depth, groups * 128),
+            f32(depth, groups * HEAD),
+            f32(depth, groups * HEAD),
             f32(groups * width, depth),
             f32(depth, groups * units),
-            f32(depth, groups * units),
-            f32(groups * units, depth),
             f32(rows, columns),
             jax.ShapeDtypeStruct(result.shape, result.dtype),
             f32(2, 128),
@@ -1559,7 +1632,7 @@
         compiler_params=pltpu.CompilerParams(vmem_limit_bytes=VMEM_LIMIT),
         cost_estimate=lasting(12),
         name="finish",
-    )(attn, down, gate, up, tokens, result, sums, gains)
+    )(attn, up, tokens, result, sums, gains)
 
 
 def context_pairs(step):
@@ -1780,7 +1853,7 @@
         packed, gain_rows = first_exchange(w_query, w_pair, out_turned, gains)
         packed = over_groups(packed)
         both_blocks, down_blocks = exchange_columns(w_gate, w_up, down_turned, gain_rows)
-        inputs_full, ffn_grad, my_ffn_grad = start_plane(tokens_half, cotangent, down_blocks)
+        inputs_full, ffn_grad, my_ffn_grad = start_plane(tokens, cotangent, down_blocks)
         both_full, down_full = over_groups(both_blocks), over_groups(down_blocks)
         hidden_first, raw = first_rows(
             inputs_full.reshape(-1, inputs_full.shape[3]), gain_rows, packed, columns_qkv
@@ -1834,7 +1907,7 @@
             lax.ppermute(my_ffn_grad, "context", context_pairs(step)) for step in (1, 2, 3)
         ]
         hidden_block, middle, ffn_grad = middle_plane(
-            attended, packed, tokens_half, gain_rows, ffn_grad, ffn_grad_blocks
+            attended, packed, tokens, gain_rows, ffn_grad, ffn_grad_blocks
         )
     else:
         ffn_grad = gather_rows(my_ffn_grad)
@@ -1877,7 +1950,7 @@
             hidden_second,
             both_full,
             middle,
-            cotangent_half,
+            cotangent,
             gain_rows,
             grad_down,
         )
@@ -1920,10 +1993,11 @@
         grad_gate, grad_up = hand_back(grad_gate), hand_back(grad_up)
     grad_attn = sum_groups(grad_attn)
     if square:
+        down, gate = finish_first(grad_down, grad_gate)
         grad_tokens, result, grad_up, ffn_sums = last_plane(
             back,
             packed,
-            tokens_half,
+            tokens,
             grad_middle,
             gain_rows,
             middle,
@@ -1932,22 +2006,22 @@
             grad_gate,
             w_gate,
             w_up,
+            down,
         )
         grad_attn, sums = exchange(
             grad_attn.reshape(groups, depth, -1), w_query, w_pair, ffn_sums
         )
         my_gains = jnp.stack([attn_gain, ffn_gain]).astype(jnp.float32)
-        query, pair, out, gate, up, down, grad_tokens, result, gain_grads = finish(
-            grad_attn, grad_down, grad_gate, grad_up, grad_tokens, result, sums, my_gains
+        query, key, value, out, up, grad_tokens, result, gain_grads = finish(
+            grad_attn, grad_up, grad_tokens, result, sums, my_gains
         )
-        key, value = jnp.moveaxis(pair.reshape(depth, groups, 2, HEAD), 2, 0)
         return (
             result,
             grad_tokens,
             gain_grads[0],
             query,
-            key.reshape(depth, -1),
-            value.reshape(depth, -1),
+            key,
+            value,
             out,
             gain_grads[1],
             gate,

time: 674 us -> 667 us (0.990)
  local copies, waits for them, and re-layouts: 17.5 us -> 9.77 us
  transfers between devices with their start and end apart: 14 -> 14, of which waited for: 4 -> 3; matrix products, arithmetic and copies ran while one was open for 5% -> 4% of each run, Pallas kernels for 81% -> 83%
where the time goes in v8:
time: 667 us; the launch traced here: 656 us
  Pallas kernels  582 us (87%)
  matrix products  25 us (4%)
  between operations  14.8 us (2%)
  waiting for transfers between devices  11.6 us (2%)
  starting transfers between devices  11.3 us (2%)
  local copies, waits for them, and re-layouts  9.77 us (1%)
    pallas_call x1, Pallas kernels, last_plane(): pl.pallas_call(last_kernel, out_shape=[jax.ShapeDtypeStruct((2, share, wi...  67.6 us
    pallas_call x1, Pallas kernels, second_plane(): pl.pallas_call(second_kernel, out_shape=[jax.ShapeDtypeStruct((share, wid...  63.2 us
    pallas_call x1, Pallas kernels, ffn_rows(): pl.pallas_call(ffn_rows_kernel, out_shape=[full, part, part, part], in_sp...  58.7 us
    pallas_call x1, Pallas kernels, middle_plane(): pl.pallas_call(middle_kernel, out_shape=[jax.ShapeDtypeStruct((share, wid...  56 us
    pallas_call x1, Pallas kernels, spread_plane(): pl.pallas_call(spread_kernel, out_shape=[full] + [jax.ShapeDtypeStruct((s...  53.8 us
    pallas_call x1, Pallas kernels, attention_backward(): pl.pallas_call(attention_backward_kernel, out_shape=jax.ShapeDtypeStruct(...  53.6 us
    pallas_call x1, Pallas kernels, start_plane(): pl.pallas_call(start_kernel, out_shape=[jax.ShapeDtypeStruct((4, 2, share...  52.1 us
    pallas_call x1, Pallas kernels, exchange_columns(): pl.pallas_call(columns_kernel, out_shape=[jax.ShapeDtypeStruct((4, depth,...  39.5 us
  transfers between devices with their start and end apart: 14, of which 3 were waited for; matrix products, arithmetic and copies ran while one was open for 4% of the time, Pallas kernels for 83%

profile of v8, /device:TPU:0, one launch (start us, length us, event | category | flops | bytes accessed | tf_op | source)
XLA Modules:
  0.0 655.7 jit_solution(3408082847587614314)
XLA Ops:
  10.0 1.8 copy.34
  13.1 17.9 %first_exchange.1 = (bf16[4,128,640]{2,1,0:T(8,128)(2,1)}, f32[8,2048]{1,0:T(8,128)}) custom-call(bf16[128,1024]{1,0:T(8,128)(2,1)} %query.3, bf16[128,512]{1,0:T(8,128)(2,1)} %copy.35.pair, bf16[128,1024]{1,0:T(8,128)(2,1)} %bitcast.60, f32[8,128]{1,0:T(8,128)} %pad.4.gains), custom_call_target="tpu_custom_call" | custom-call | bytes 30000000 | tf_op jit(solution)/shard_map/first_exchange/pallas_call | solution.py:646
  32.4 39.5 %exchange_columns.1 = (bf16[4,128,2048]{2,1,0:T(8,128)(2,1)}, bf16[4,128,1024]{2,1,0:T(8,128)(2,1)}) custom-call(bf16[128,4096]{1,0:T(8,128)(2,1)} %rest_6_.1, bf16[128,4096]{1,0:T(8,128)(2,1)} %rest_7_.1, bf16[128,4096]{1,0:T(8,128)(2,1)} %bitcast.53, f32[8,2048]{1,0:T(8,128)} %get-tuple-element.59.early.gains.gain), custom_call_target="tpu_custom_call" | custom-call | bytes 90000000 | tf_op jit(solution)/shard_map/exchange_columns/pallas_call | solution.py:722
  72.7 52.1 %gather_tokens.1 = (bf16[4,2,320,2048]{3,2,1,0:T(8,128)(2,1)}, bf16[640,2048]{1,0:T(8,128)(2,1)}, bf16[320,2048]{1,0:T(8,128)(2,1)}) custom-call(bf16[640,2048]{1,0:T(8,128)(2,1)} %rest_8_.1, bf16[640,2048]{1,0:T(8,128)(2,1)} %cotangent_in.1, bf16[4,128,1024]{2,1,0:T(8,128)(2,1)} %get-tuple-element.60.early), custom_call_target="tpu_custom_call" | custom-call | bytes 180000000 | tf_op jit(solution)/shard_map/gather_tokens/pallas_call | solution.py:689
  124.8 1.5 collective-permute-start.2
  128.9 14.2 %first_rows.1 = (bf16[2560,2048]{1,0:T(8,128)(2,1)}, f32[2560,384]{1,0:T(8,128)}) custom-call(bf16[2560,2048]{1,0:T(8,128)(2,1)} %bitcast.44, f32[8,2048]{1,0:T(8,128)} %get-tuple-element.59.early.gains.gain, bf16[2048,640]{1,0:T(8,128)(2,1)} %all-gather.4.cloned.1.call-done.weight.weights), custom_call_target="tpu_custom_call" | custom-call | bytes 12000000 | tf_op jit(solution)/shard_map/first_rows/pallas_call | solution.py:1678
  143.1 38.5 %attention_forward.1 = (bf16[2560,256]{1,0:T(8,128)(2,1)}, bf16[2560,256]{1,0:T(8,128)(2,1)}, bf16[2560,256]{1,0:T(8,128)(2,1)}, bf16[2560,256]{1,0:T(8,128)(2,1)}, f32[4,1,2560]{2,1,0:T(1,128)}) custom-call(s32[20]{0:T(128)} %compare_select_fusion.1.to_ref, s32[20]{0:T(128)} %bitcast.69, f32[2560,384]{1,0:T(8,128)} %get-tuple-element.64.raw_ref, ...), custom_call_target="tpu_custom_call" | custom-call | flops 5368709120 | bytes 10485760 | tf_op jit(solution)/shard_map/attention_forward/pallas_call | solution.py:313
  181.6 3.6 collective-permute-done.1.from_y
  186.2 56.0 %middle_rows.1 = (bf16[320,2048]{1,0:T(8,128)(2,1)}, f32[320,2048]{1,0:T(8,128)}, bf16[4,2,320,2048]{3,2,1,0:T(8,128)(2,1)}) custom-call(bf16[4,2,320,256]{3,2,1,0:T(8,128)(2,1)} %bitcast.52, bf16[2048,640]{1,0:T(8,128)(2,1)} %all-gather.4.cloned.1.call-done.weight.weights, f32[8,2048]{1,0:T(8,128)} %get-tuple-element.59.early.gains.gain, ...), custom_call_target="tpu_custom_call" | custom-call | bytes 165000000 | tf_op jit(solution)/shard_map/middle_rows/pallas_call | solution.py:800
  242.3 58.7 %ffn_rows.1 = (bf16[4,2,320,2048]{3,2,1,0:T(8,128)(2,1)}, bf16[4,2,320,1024]{3,2,1,0:T(8,128)(2,1)}, bf16[4,2,320,1024]{3,2,1,0:T(8,128)(2,1)}, bf16[4,2,320,1024]{3,2,1,0:T(8,128)(2,1)}) custom-call(bf16[320,2048]{1,0:T(8,128)(2,1)} %get-tuple-element.69.block, bf16[2048,2048]{1,0:T(8,128)(2,1)} %all-gather.6.cloned.1.call-done.weights_in), custom_call_target="tpu_custom_call" | custom-call | bytes 180000000 | tf_op jit(solution)/shard_map/ffn_rows/pallas_call | solution.py:943
  301.0 16.8 %bitcast_convert_fusion.early = bf16[2048,1024]{1,0:T(8,128)(2,1)} fusion(bf16[4,2,320,2048]{3,2,1,0:T(8,128)(2,1)} %get-tuple-element.68, bf16[4,2,320,1024]{3,2,1,0:T(8,128)(2,1)} %get-tuple-element.73.m), kind=kOutput, calls=%fused_computation | convolution fusion | flops 10739515392 | bytes 19922944 | tf_op jit(solution)/shard_map/dot_general | solution.py:32
  317.9 21.6 %ffn_slopes.1.slopes = bf16[2560,2048]{1,0:T(8,128)(2,1)} custom-call(bf16[2560,2048]{1,0:T(8,128)(2,1)} %bitcast.47, bf16[2560,1024]{1,0:T(8,128)(2,1)} %bitcast.49, bf16[2560,1024]{1,0:T(8,128)(2,1)} %bitcast.50, bf16[2048,1024]{1,0:T(8,128)(2,1)} %all-gather.8.cloned.1.call-done.down_w.down_in, bf16[2048,1024]{1,0:T(8,128)(2,1)} %bitcast_convert_fusion.early), custom_call_target="tpu_custom_call" | custom-call | flops 10737418240 | bytes 26843544 | tf_op jit(solution)/shard_map/ffn_slopes/pallas_call | solution.py:1766
  339.5 63.2 %second_rows.1 = (f32[320,2048]{1,0:T(8,128)}, bf16[320,2048]{1,0:T(8,128)(2,1)}, bf16[2048,1024]{1,0:T(8,128)(2,1)}) custom-call(bf16[2560,2048]{1,0:T(8,128)(2,1)} %ffn_slopes.1.slopes, bf16[2560,2048]{1,0:T(8,128)(2,1)} %bitcast.42, bf16[2048,2048]{1,0:T(8,128)(2,1)} %all-gather.6.cloned.1.call-done.weights_in, ...), custom_call_target="tpu_custom_call" | custom-call | bytes 180000000 | tf_op jit(solution)/shard_map/second_rows/pallas_call | solution.py:1210
  403.0 53.8 %spread_rows.1 = (bf16[4,2,320,2048]{3,2,1,0:T(8,128)(2,1)}, bf16[320,2048]{1,0:T(8,128)(2,1)}, bf16[320,2048]{1,0:T(8,128)(2,1)}, bf16[320,2048]{1,0:T(8,128)(2...) custom-call(bf16[320,2048]{1,0:T(8,128)(2,1)} %get-tuple-element.76.hidden, ...), custom_call_target="tpu_custom_call" | custom-call | bytes 180000000 | tf_op jit(solution)/shard_map/spread_rows/pallas_call | solution.py:1320
  458.9 1.5 collective-permute-start.5
  460.3 8.2 %convolution_convert_fusion.grad_ref = bf16[2560,256]{1,0:T(8,128)(2,1)} fusion(bf16[2560,2048]{1,0:T(8,128)(2,1)} %bitcast.45, bf16[2048,640]{1,0:T(8,128)(2,1)} %all-gather.4.cloned.1.call-done.weight.weights), kind=kOutput, calls=%fused_computation.1 | convolution fusion | flops 2685009920 | bytes 12845056 | tf_op jit(solution)/shard_map/dot_general | solution.py:32
  468.5 3.5 all-to-all-start
  472.3 53.6 %attention_backward.1.back = bf16[2560,384]{1,0:T(8,128)(2,1)} custom-call(s32[20]{0:T(128)} %compare_select_fusion.1.to_ref, s32[20]{0:T(128)} %bitcast.70, bf16[2560,256]{1,0:T(8,128)(2,1)} %convolution_convert_fusion.grad_ref, bf16[2560,256]{1,0:T(8,128)(2,1)} %get-tuple-element.79.q_ref, bf16[2560,256]{1,0:T(8,128)(2,1)} %get-tuple-element.80.k_ref, ...), custom_call_target="tpu_custom_call" | custom-call | flops 13421772800 | bytes 10485760 | tf_op jit(solution)/shard_map/attention_backward/pallas_call | solution.py:331
  527.9 17.9 %attention_weights.1 = (bf16[2048,640]{1,0:T(8,128)(2,1)}, bf16[4,128,1024]{2,1,0:T(8,128)(2,1)}) custom-call(bf16[2560,2048]{1,0:T(8,128)(2,1)} %get-tuple-element.63.hidden, bf16[2560,384]{1,0:T(8,128)(2,1)} %attention_backward.1.back, bf16[2560,2048]{1,0:T(8,128)(2,1)} %bitcast.46, bf16[2560,256]{1,0:T(8,128)(2,1)} %get-tuple-element.65.attended, ...), custom_call_target="tpu_custom_call" | custom-call | bytes 75000000 | tf_op jit(solution)/shard_map/attention_weights/pallas_call | solution.py:1729
  545.9 4.5 finish_first.1
  550.4 6.1 reduce-scatter.11.cloned.1.call-done
  556.4 67.6 %last_rows.1 = (f32[2,320,2048]{2,1,0:T(8,128)}, bf16[2,320,2048]{2,1,0:T(8,128)(2,1)}, bf16[4,128,1024]{2,1,0:T(8,128)(2,1)}, f32[128,128]{1,0:T(8,128)}) custom-call(bf16[4,2,320,384]{3,2,1,0:T(8,128)(2,1)} %bitcast.48, bf16[2048,640]{1,0:T(8,128)(2,1)} %all-gather.4.cloned.1.call-done.weight.weights, f32[8,2048]{1,0:T(8,128)} %get-tuple-element.59.early.gains.gain, ...), custom_call_target="tpu_custom_call" | custom-call | bytes 210000000 | tf_op jit(solution)/shard_map/last_rows/pallas_call | solution.py:1451
  624.1 14.9 %exchange_blocks.1 = (bf16[4,128,640]{2,1,0:T(8,128)(2,1)}, f32[2,128,128]{2,1,0:T(8,128)}) custom-call(bf16[4,128,640]{2,1,0:T(8,128)(2,1)} %bitcast.63, bf16[128,1024]{1,0:T(8,128)(2,1)} %query.3, bf16[128,512]{1,0:T(8,128)(2,1)} %copy.35.pair, f32[128,128]{1,0:T(8,128)} %get-tuple-element.92.other_sums), custom_call_target="tpu_custom_call" | custom-call | bytes 24000000 | tf_op jit(solution)/shard_map/exchange_blocks/pallas_call | solution.py:1520
  638.9 8.2 %finish.1 = (f32[128,1024]{1,0:T(8,128)}, f32[128,256]{1,0:T(8,128)}, f32[128,256]{1,0:T(8,128)}, f32[1024,128]{1,0:T(8,128)}, f32[128,4096]{1,0:T(8,128)}, /*in...) custom-call(bf16[4,128,640]{2,1,0:T(8,128)(2,1)} %get-tuple-element.93.attn, ...), custom_call_target="tpu_custom_call" | custom-call | bytes 36000000 | tf_op jit(solution)/shard_map/finish/pallas_call | solution.py:1601
  (56 shorter events, 15.9 us)
Async XLA Ops:
  7.2 23.9 %copy-start.4 = (bf16[4096,128]{1,0:T(8,128)(2,1)S(1)}, bf16[4096,128]{1,0:T(8,128)(2,1)}, u32[]{:S(2)}) copy-start(bf16[4096,128]{1,0:T(8,128)(2,1)} %param.26) | copy-start | bytes 3145732
  7.2 121.7 %all-gather.4.cloned.1.call-start = ((), (), s32[]{:S(2)}) async-start(), calls=%async_computation.5 | async-start | bytes 3276800 | tf_op jit(solution)/shard_map/all_gather | solution.py:1844
  12.5 59.4 %copy-start.5 = (f32[2,128]{1,0:T(2,128)}, f32[2,128]{1,0:T(2,128)S(1)}, u32[]{:S(2)}) copy-start(f32[2,128]{1,0:T(2,128)S(1)} %maximum_convert_fusion.gains) | copy-start | bytes 3076
  31.0 211.2 %all-gather.6.cloned.1.call-start = ((), (), s32[]{:S(2)}) async-start(), calls=%async_computation.6 | async-start | bytes 10485760 | tf_op jit(solution)/shard_map/all_gather | solution.py:1844
  71.9 246.0 %all-gather.8.cloned.1.call-start = ((), (), s32[]{:S(2)}) async-start(), calls=%async_computation.7 | async-start | bytes 5242880 | tf_op jit(solution)/shard_map/all_gather | solution.py:1844
  72.7 55.7 %copy-start.6 = (s32[1,20]{1,0:T(1,128)S(1)}, s32[1,20]{1,0:T(1,128)}, u32[]{:S(2)}) copy-start(s32[1,20]{1,0:T(1,128)} %param.27) | copy-start | bytes 244
  72.7 55.7 %copy-start.7 = (s32[1,20]{1,0:T(1,128)S(1)}, s32[1,20]{1,0:T(1,128)}, u32[]{:S(2)}) copy-start(s32[1,20]{1,0:T(1,128)} %param.28) | copy-start | bytes 244
  72.7 395.8 %reduce-scatter.5.cloned.1.call-start = ((), (), s32[]{:S(2)}) async-start(), calls=%async_computation.8 | async-start | bytes 5242880 | tf_op jit(solution)/shard_map/reduce_scatter | solution.py:1939
  124.8 56.8 %collective-permute-start.2 = (bf16[320,2048]{1,0:T(8,128)(2,1)}, bf16[320,2048]{1,0:T(8,128)(2,1)S(1)}, u32[]{:S(2)}, u32[]{:S(2)}) collective-permute-start(bf16[320,2048]{1,0:T(8,128)(2,1)} %get-tuple-element.67), channel_id=1, source_target_pairs={{0,6},{2,4},{4,2},{6,0},{1,7},{3,5},{5,3},{7,1},{8,14},{10,12},{12... | collective-permute-start | bytes 3932168 | tf_op jit(solution)/shard_map/ppermute | solution.py:1907
  126.3 58.9 %collective-permute-start.1 = (bf16[320,2048]{1,0:T(8,128)(2,1)}, bf16[320,2048]{1,0:T(8,128)(2,1)S(1)}, u32[]{:S(2)}, u32[]{:S(2)}) collective-permute-start(bf16[320,2048]{1,0:T(8,128)(2,1)} %get-tuple-element.67), channel_id=1, source_target_pairs={{0,4},{2,6},{4,0},{6,2},{1,5},{3,7},{5,1},{7,3},{8,12},{10,14},{12... | collective-permute-start | bytes 3932168 | tf_op jit(solution)/shard_map/ppermute | solution.py:1907
  127.3 57.9 %collective-permute-start = (bf16[320,2048]{1,0:T(8,128)(2,1)}, bf16[320,2048]{1,0:T(8,128)(2,1)}, u32[]{:S(2)}, u32[]{:S(2)}) collective-permute-start(bf16[320,2048]{1,0:T(8,128)(2,1)} %get-tuple-element.67), channel_id=1, source_target_pairs={{0,2},{2,0},{4,6},{6,4},{1,3},{3,1},{5,7},{7,5},{8,10},{10,8},{12,... | collective-permute-start | bytes 3932168 | tf_op jit(solution)/shard_map/ppermute | solution.py:1907
  181.6 3.6 copy-start.2
  185.2 1.1 copy-start.3
  317.8 208.1 %reduce-scatter.7.cloned.1.call-start = ((), (), s32[]{:S(2)}) async-start(), calls=%async_computation.9 | async-start | bytes 5242880 | tf_op jit(solution)/shard_map/reduce_scatter | solution.py:1939
  402.7 153.7 %reduce-scatter.11.cloned.1.call-start = ((), (), s32[]{:S(2)}) async-start(), calls=%async_computation.11 | async-start | bytes 5242880 | tf_op jit(solution)/shard_map/reduce_scatter | solution.py:1939
  456.8 69.1 %collective-permute-start.3 = (bf16[320,2048]{1,0:T(8,128)(2,1)}, bf16[320,2048]{1,0:T(8,128)(2,1)S(1)}, u32[]{:S(2)}, u32[]{:S(2)}) collective-permute-start(bf16[320,2048]{1,0:T(8,128)(2,1)} %get-tuple-element.83), channel_id=1, source_target_pairs={{0,2},{2,0},{4,6},{6,4},{1,3},{3,1},{5,7},{7,5},{8,10},{10,8},{12,... | collective-permute-start | bytes 3932168 | tf_op jit(solution)/shard_map/ppermute | solution.py:1961
  458.0 67.9 %collective-permute-start.4 = (bf16[320,2048]{1,0:T(8,128)(2,1)}, bf16[320,2048]{1,0:T(8,128)(2,1)}, u32[]{:S(2)}, u32[]{:S(2)}) collective-permute-start(bf16[320,2048]{1,0:T(8,128)(2,1)} %get-tuple-element.84), channel_id=1, source_target_pairs={{0,4},{2,6},{4,0},{6,2},{1,5},{3,7},{5,1},{7,3},{8,12},{10,14},{12... | collective-permute-start | bytes 3932168 | tf_op jit(solution)/shard_map/ppermute | solution.py:1961
  458.9 67.0 %collective-permute-start.5 = (bf16[320,2048]{1,0:T(8,128)(2,1)}, bf16[320,2048]{1,0:T(8,128)(2,1)}, u32[]{:S(2)}, u32[]{:S(2)}) collective-permute-start(bf16[320,2048]{1,0:T(8,128)(2,1)} %get-tuple-element.85), channel_id=1, source_target_pairs={{0,6},{2,4},{4,2},{6,0},{1,7},{3,5},{5,3},{7,1},{8,14},{10,12},{12... | collective-permute-start | bytes 3932168 | tf_op jit(solution)/shard_map/ppermute | solution.py:1961
  468.5 58.5 %all-to-all-start = ((bf16[4,128,1024]{2,1,0:T(8,128)(2,1)}), bf16[4,128,1024]{2,1,0:T(8,128)(2,1)S(1)}, u32[]{:S(2)}, u32[]{:S(2)}) async-start(bf16[4,128,1024]{2,1,0:T(8,128)(2,1)} %bitcast.59), calls=%async_computation.2 | async-start | bytes 2097152 | tf_op jit(solution)/shard_map/all_to_all | solution.py:1942
  472.0 152.0 %reduce-scatter.9.cloned.1.call-start = ((), (), s32[]{:S(2)}) async-start(), calls=%async_computation.10 | async-start | bytes 3276800 | tf_op jit(solution)/shard_map/reduce_scatter | solution.py:1939
  525.9 1.1 copy-start.1
  526.9 1.0 copy-start
Sparse Core Ops, SparseCore 0:
  31.2 52.9 all-gather.3
  85.7 148.3 all-gather.5
  235.7 79.0 all-gather.7
  318.0 74.7 reduce-scatter.4
  402.9 74.0 reduce-scatter.6
  479.1 77.2 reduce-scatter.10
  558.8 52.6 reduce-scatter.8

commit v9 on v8

--- a/solution.py
+++ b/solution.py
@@ -739,45 +739,23 @@
     weights,
     gain,
     tokens,
-    beside,
-    from_x,
-    from_y,
-    from_both,
     hidden,
     middle,
-    beside_out,
     sent,
     landed,
     local,
     residual,
-    held_beside,
-    held_blocks,
     *scratch,
 ):
     p = Plane(sent, landed)
-    blocks = ((from_x, p.at_x), (from_y, p.at_y), (from_both, p.at_both))
-    loads = [pltpu.make_async_copy(beside, held_beside, local.at[0])]
-    for i, (block, rank) in enumerate(blocks):
-        loads.append(pltpu.make_async_copy(block, held_blocks.at[i], local.at[i + 1]))
     share = hidden.shape[0]
     first = pl.ds(pl.multiple_of(p.core * share, SLAB), share)
-    loads.append(pltpu.make_async_copy(tokens.at[first], residual, local.at[4]))
-    for started in loads:
-        started.start()
+    load = pltpu.make_async_copy(tokens.at[first], residual, local)
+    load.start()
     width = attended.shape[3]
     columns = slice(weights.shape[1] - width, weights.shape[1])
     total = Scatter(p, attended, weights, columns, *scratch)
-    kept, across = [], []
-    loads[0].wait()
-    kept.append(pltpu.make_async_copy(held_beside, beside_out.at[p.rank], local.at[0]))
-    kept[0].start()
-    for i, (block, rank) in enumerate(blocks):
-        loads[i + 1].wait()
-        place = beside_out.at[rank, p.core]
-        kept.append(pltpu.make_async_copy(held_blocks.at[i], place, local.at[i + 1]))
-        kept[i + 1].start()
-        across.append(p.send(held_blocks.at[i], place, p.sibling))
-    loads[4].wait()
+    load.wait()
 
     def work(rows):
         value = residual[rows, :].astype(jnp.float32) + residual_scale * total.rows(rows)
@@ -787,31 +765,23 @@
     for h in range(2):
         total.ready(h)
         slabs(h * (share // 2), share // 2, work)
-    for number, rank in zip(across, (p.at_x, p.at_y, p.at_both)):
-        p.arrive(number, beside_out.at[rank, 1 - p.core])
     p.finish()
-    for started in kept:
-        started.wait()
-
-
-def middle_plane(attended, weights, tokens, gain, beside, blocks):
-    share, width = blocks[0].shape
-    full = jax.ShapeDtypeStruct((4, 2, share, width), jnp.bfloat16)
-    hidden, middle, beside_out = pl.pallas_call(
+
+
+def middle_plane(attended, weights, tokens, gain):
+    share, width = tokens.shape[0] // 2, tokens.shape[1]
+    return pl.pallas_call(
         middle_kernel,
         out_shape=[
             jax.ShapeDtypeStruct((share, width), jnp.bfloat16),
             jax.ShapeDtypeStruct((share, width), jnp.float32),
-            full,
         ],
-        in_specs=[VMEM] * 3 + [ANY] * 5,
-        out_specs=[VMEM, VMEM, ANY],
-        scratch_shapes=wires(SCATTER_COPIES + 3)
+        in_specs=[VMEM] * 3 + [ANY],
+        out_specs=[VMEM, VMEM],
+        scratch_shapes=wires(SCATTER_COPIES)
         + [
-            pltpu.SemaphoreType.DMA((5,)),
+            pltpu.SemaphoreType.DMA,
             pltpu.VMEM((share, width), jnp.bfloat16),
-            pltpu.VMEM((2, share, width), jnp.bfloat16),
-            pltpu.VMEM((3, share, width), jnp.bfloat16),
         ]
         + scatter_scratch(share, width),
         compiler_params=pltpu.CompilerParams(
@@ -824,19 +794,21 @@
         weights,
         gain,
         tokens,
-        beside.reshape(2, share, width),
-        *blocks,
     )
-    return hidden, middle, beside_out.reshape(8 * share, width)
 
 
 def ffn_rows_kernel(
     block,
     weights_in,
+    beside,
+    from_x,
+    from_y,
+    from_both,
     out,
     m,
     gate,
     up,
+    beside_out,
     sent,
     landed,
     local,
@@ -847,6 +819,9 @@
     m_held,
     gate_held,
     up_held,
+    wires_beside,
+    held_beside,
+    held_blocks,
 ):
     p = Plane(sent, landed)
     gather = Gather(p, block, out)
@@ -856,6 +831,14 @@
     weights_load.start()
     mine = pltpu.make_async_copy(block, out.at[p.rank, p.core], local.at[1])
     mine.start()
+    blocks = ((from_x, p.at_x), (from_y, p.at_y), (from_both, p.at_both))
+    loads = [pltpu.make_async_copy(beside, held_beside, wires_beside.at[0])]
+    for i, (source, rank) in enumerate(blocks):
+        loads.append(
+            pltpu.make_async_copy(source, held_blocks.at[i], wires_beside.at[i + 1])
+        )
+    for started in loads:
+        started.start()
     units = m.shape[3]
     stores = []
 
@@ -897,6 +880,16 @@
 
     weights_load.wait()
     compute(0, p.rank, p.core, block)
+    kept, shared = [], []
+    loads[0].wait()
+    kept.append(pltpu.make_async_copy(held_beside, beside_out.at[p.rank], wires_beside.at[0]))
+    kept[0].start()
+    for i, (source, rank) in enumerate(blocks):
+        loads[i + 1].wait()
+        place = beside_out.at[rank, p.core]
+        kept.append(pltpu.make_async_copy(held_blocks.at[i], place, wires_beside.at[i + 1]))
+        kept[i + 1].start()
+        shared.append(p.send(held_blocks.at[i], place, p.sibling))
     gather.forward_chunk(0)
     from_sibling(0, p.rank)
     load(1, p.rank, 1 - p.core).start()
@@ -926,14 +919,18 @@
     compute(6, p.at_both, p.core, rows_in.at[0])
     load(7, p.at_both, 1 - p.core).wait()
     compute(7, p.at_both, 1 - p.core, rows_in.at[1])
+    for number, (source, rank) in zip(shared, blocks):
+        p.arrive(number, beside_out.at[rank, 1 - p.core])
     p.finish()
     mine.wait()
+    for started in kept:
+        started.wait()
     for n in (6, 7):
         for started in stores[n]:
             started.wait()
 
 
-def ffn_rows(block, weights):
+def ffn_rows(block, weights, beside, blocks):
     share, width = block.shape
     units = weights.shape[1] // 2
     kind = jnp.bfloat16
@@ -942,10 +939,10 @@
     held = pltpu.VMEM((2, share, units), kind)
     outs = pl.pallas_call(
         ffn_rows_kernel,
-        out_shape=[full, part, part, part],
-        in_specs=[VMEM, ANY],
-        out_specs=[ANY] * 4,
-        scratch_shapes=wires(GATHER_COPIES)
+        out_shape=[full, part, part, part, full],
+        in_specs=[VMEM] + [ANY] * 5,
+        out_specs=[ANY] * 5,
+        scratch_shapes=wires(GATHER_COPIES + 3)
         + [
             pltpu.SemaphoreType.DMA((2,)),
             pltpu.SemaphoreType.DMA((2,)),
@@ -955,13 +952,16 @@
             held,
             held,
             held,
+            pltpu.SemaphoreType.DMA((4,)),
+            pltpu.VMEM((2, share, width), kind),
+            pltpu.VMEM((3, share, width), kind),
         ],
         compiler_params=pltpu.CompilerParams(
             collective_id=11, has_side_effects=True, vmem_limit_bytes=VMEM_LIMIT
         ),
         cost_estimate=lasting(60),
         name="ffn_rows",
-    )(block, weights)
+    )(block, weights, beside.reshape(2, share, width), *blocks)
     return [array.reshape(8 * share, -1) for array in outs]
 
 
@@ -1380,10 +1380,15 @@
         started.start()
     middle, ffn_own, ffn_x, ffn_y, ffn_both, gates, gate, up, residual, grad_middle = landing
     p = Plane(sent, landed, diagonal=True)
+    moves = []
+
+    def hand_back(partner, rank):
+        moves.append((p.send(ups.at[rank], up_out.at[p.rank], partner), up_out.at[rank]))
+
+    hand_back(p.both, p.at_both)
     total = Scatter(p, back, weights, slice(0, back.shape[3]), *scratch)
-    moves = []
-    for partner, rank in ((p.both, p.at_both), (p.x, p.at_x), (p.y, p.at_y)):
-        moves.append((p.send(ups.at[rank], up_out.at[p.rank], partner), up_out.at[rank]))
+    hand_back(p.x, p.at_x)
+    hand_back(p.y, p.at_y)
     up_out[p.rank] = ups[p.rank]
     share = held.shape[0]
 
@@ -1427,8 +1432,10 @@
             total.ready(k // (CHUNKS // 2))
         slabs(k * (share // CHUNKS), share // CHUNKS, work)
         across.append(p.send(held.at[cut], out.at[p.core, cut], p.sibling))
-    kept.append(pltpu.make_async_copy(held, out.at[p.core], local.at[1]))
-    kept[1].start()
+        kept.append(
+            pltpu.make_async_copy(held.at[cut], out.at[p.core, cut], local.at[1 + k])
+        )
+        kept[1 + k].start()
     for number, target in moves:
         p.arrive(number, target)
     slabs(0, gate.shape[0], up_rows)
@@ -1460,7 +1467,7 @@
         out_specs=[ANY, ANY, VMEM, VMEM],
         scratch_shapes=wires(CHUNKS + 5 + SCATTER_COPIES)
         + [
-            pltpu.SemaphoreType.DMA((2,)),
+            pltpu.SemaphoreType.DMA((1 + CHUNKS,)),
             pltpu.SemaphoreType.DMA((LATER,)),
             pltpu.VMEM((share, width), jnp.float32),
             pltpu.VMEM((share, width), jnp.bfloat16),
@@ -1906,9 +1913,7 @@
         ffn_grad_blocks = [
             lax.ppermute(my_ffn_grad, "context", context_pairs(step)) for step in (1, 2, 3)
         ]
-        hidden_block, middle, ffn_grad = middle_plane(
-            attended, packed, tokens, gain_rows, ffn_grad, ffn_grad_blocks
-        )
+        hidden_block, middle = middle_plane(attended, packed, tokens, gain_rows)
     else:
         ffn_grad = gather_rows(my_ffn_grad)
         middle = residual_in + residual_scale * scatter_rows(dot(attended, out_full, LAST))
@@ -1916,7 +1921,9 @@
 
     units = down_full.shape[1]
     if square:
-        hidden_second, hidden, gate_proj, up_proj = ffn_rows(hidden_block, both_full)
+        hidden_second, hidden, gate_proj, up_proj, ffn_grad = ffn_rows(
+            hidden_block, both_full, ffn_grad, ffn_grad_blocks
+        )
     else:
         hidden, gate_proj, up_proj = row_tiles(
             ffn_first_kernel,

time: 667 us -> 660 us (0.990)
  transfers between devices with their start and end apart: 14 -> 14, of which waited for: 3 -> 2; matrix products, arithmetic and copies ran while one was open for 4% -> 4% of each run, Pallas kernels for 83% -> 83%
where the time goes in v9:
time: 660 us; the launch traced here: 650 us
  Pallas kernels  580 us (88%)
  matrix products  25 us (4%)
  between operations  14.8 us (2%)
  starting transfers between devices  11.3 us (2%)
  local copies, waits for them, and re-layouts  10.1 us (2%)
  waiting for transfers between devices  7.48 us (1%)
    pallas_call x1, Pallas kernels, last_plane(): pl.pallas_call(last_kernel, out_shape=[jax.ShapeDtypeStruct((2, share, wi...  64.3 us
    pallas_call x1, Pallas kernels, second_plane(): pl.pallas_call(second_kernel, out_shape=[jax.ShapeDtypeStruct((share, wid...  63.5 us
    pallas_call x1, Pallas kernels, ffn_rows(): pl.pallas_call(ffn_rows_kernel, out_shape=[full, part, part, part, full],...  59 us
    pallas_call x1, Pallas kernels, middle_plane(): pl.pallas_call(middle_kernel, out_shape=[jax.ShapeDtypeStruct((share, wid...  56.1 us
    pallas_call x1, Pallas kernels, spread_plane(): pl.pallas_call(spread_kernel, out_shape=[full] + [jax.ShapeDtypeStruct((s...  54.2 us
    pallas_call x1, Pallas kernels, attention_backward(): pl.pallas_call(attention_backward_kernel, out_shape=jax.ShapeDtypeStruct(...  53.6 us
    pallas_call x1, Pallas kernels, start_plane(): pl.pallas_call(start_kernel, out_shape=[jax.ShapeDtypeStruct((4, 2, share...  52.1 us
    pallas_call x1, Pallas kernels, exchange_columns(): pl.pallas_call(columns_kernel, out_shape=[jax.ShapeDtypeStruct((4, depth,...  39.5 us
  transfers between devices with their start and end apart: 14, of which 2 were waited for; matrix products, arithmetic and copies ran while one was open for 4% of the time, Pallas kernels for 83%

profile of v9, /device:TPU:0, one launch (start us, length us, event | category | flops | bytes accessed | tf_op | source)
XLA Modules:
  0.0 649.6 jit_solution(13051910706985478332)
XLA Ops:
  10.0 1.8 copy.34
  13.1 17.9 %first_exchange.1 = (bf16[4,128,640]{2,1,0:T(8,128)(2,1)}, f32[8,2048]{1,0:T(8,128)}) custom-call(bf16[128,1024]{1,0:T(8,128)(2,1)} %query.3, bf16[128,512]{1,0:T(8,128)(2,1)} %copy.35.pair, bf16[128,1024]{1,0:T(8,128)(2,1)} %bitcast.60, f32[8,128]{1,0:T(8,128)} %pad.4.gains), custom_call_target="tpu_custom_call" | custom-call | bytes 30000000 | tf_op jit(solution)/shard_map/first_exchange/pallas_call | solution.py:646
  32.4 39.5 %exchange_columns.1 = (bf16[4,128,2048]{2,1,0:T(8,128)(2,1)}, bf16[4,128,1024]{2,1,0:T(8,128)(2,1)}) custom-call(bf16[128,4096]{1,0:T(8,128)(2,1)} %rest_6_.1, bf16[128,4096]{1,0:T(8,128)(2,1)} %rest_7_.1, bf16[128,4096]{1,0:T(8,128)(2,1)} %bitcast.53, f32[8,2048]{1,0:T(8,128)} %get-tuple-element.59.early.gains.gain), custom_call_target="tpu_custom_call" | custom-call | bytes 90000000 | tf_op jit(solution)/shard_map/exchange_columns/pallas_call | solution.py:722
  72.7 52.1 %gather_tokens.1 = (bf16[4,2,320,2048]{3,2,1,0:T(8,128)(2,1)}, bf16[640,2048]{1,0:T(8,128)(2,1)}, bf16[320,2048]{1,0:T(8,128)(2,1)}) custom-call(bf16[640,2048]{1,0:T(8,128)(2,1)} %rest_8_.1, bf16[640,2048]{1,0:T(8,128)(2,1)} %cotangent_in.1, bf16[4,128,1024]{2,1,0:T(8,128)(2,1)} %get-tuple-element.60.early), custom_call_target="tpu_custom_call" | custom-call | bytes 180000000 | tf_op jit(solution)/shard_map/gather_tokens/pallas_call | solution.py:689
  124.9 1.5 collective-permute-start.2
  129.0 14.2 %first_rows.1 = (bf16[2560,2048]{1,0:T(8,128)(2,1)}, f32[2560,384]{1,0:T(8,128)}) custom-call(bf16[2560,2048]{1,0:T(8,128)(2,1)} %bitcast.44, f32[8,2048]{1,0:T(8,128)} %get-tuple-element.59.early.gains.gain, bf16[2048,640]{1,0:T(8,128)(2,1)} %all-gather.4.cloned.1.call-done.weight.weights), custom_call_target="tpu_custom_call" | custom-call | bytes 12000000 | tf_op jit(solution)/shard_map/first_rows/pallas_call | solution.py:1685
  143.1 38.5 %attention_forward.1 = (bf16[2560,256]{1,0:T(8,128)(2,1)}, bf16[2560,256]{1,0:T(8,128)(2,1)}, bf16[2560,256]{1,0:T(8,128)(2,1)}, bf16[2560,256]{1,0:T(8,128)(2,1)}, f32[4,1,2560]{2,1,0:T(1,128)}) custom-call(s32[20]{0:T(128)} %compare_select_fusion.1.to_ref, s32[20]{0:T(128)} %bitcast.69, f32[2560,384]{1,0:T(8,128)} %get-tuple-element.64.raw_ref, ...), custom_call_target="tpu_custom_call" | custom-call | flops 5368709120 | bytes 10485760 | tf_op jit(solution)/shard_map/attention_forward/pallas_call | solution.py:313
  181.6 56.1 %middle_rows.1 = (bf16[320,2048]{1,0:T(8,128)(2,1)}, f32[320,2048]{1,0:T(8,128)}) custom-call(bf16[4,2,320,256]{3,2,1,0:T(8,128)(2,1)} %bitcast.52, bf16[2048,640]{1,0:T(8,128)(2,1)} %all-gather.4.cloned.1.call-done.weight.weights, f32[8,2048]{1,0:T(8,128)} %get-tuple-element.59.early.gains.gain, bf16[640,2048]{1,0:T(8,128)(2,1)} %rest_8_.1), custom_call_target="tpu_custom_call" | custom-call | bytes 165000000 | tf_op jit(solution)/shard_map/middle_rows/pallas_call | solution.py:773
  239.2 59.0 %ffn_rows.1 = (bf16[4,2,320,2048]{3,2,1,0:T(8,128)(2,1)}, bf16[4,2,320,1024]{3,2,1,0:T(8,128)(2,1)}, bf16[4,2,320,1024]{3,2,1,0:T(8,128)(2,1)}, bf16[4,2,320,102...) custom-call(bf16[320,2048]{1,0:T(8,128)(2,1)} %get-tuple-element.66.block, ...), custom_call_target="tpu_custom_call" | custom-call | bytes 180000000 | tf_op jit(solution)/shard_map/ffn_rows/pallas_call | solution.py:940
  298.2 16.8 %bitcast_convert_fusion.early = bf16[2048,1024]{1,0:T(8,128)(2,1)} fusion(bf16[4,2,320,2048]{3,2,1,0:T(8,128)(2,1)} %get-tuple-element.70, bf16[4,2,320,1024]{3,2,1,0:T(8,128)(2,1)} %get-tuple-element.73.m), kind=kOutput, calls=%fused_computation | convolution fusion | flops 10739515392 | bytes 19922944 | tf_op jit(solution)/shard_map/dot_general | solution.py:32
  315.1 21.8 %ffn_slopes.1.slopes = bf16[2560,2048]{1,0:T(8,128)(2,1)} custom-call(bf16[2560,2048]{1,0:T(8,128)(2,1)} %bitcast.47, bf16[2560,1024]{1,0:T(8,128)(2,1)} %bitcast.49, bf16[2560,1024]{1,0:T(8,128)(2,1)} %bitcast.50, bf16[2048,1024]{1,0:T(8,128)(2,1)} %all-gather.8.cloned.1.call-done.down_w.down_in, bf16[2048,1024]{1,0:T(8,128)(2,1)} %bitcast_convert_fusion.early), custom_call_target="tpu_custom_call" | custom-call | flops 10737418240 | bytes 26843544 | tf_op jit(solution)/shard_map/ffn_slopes/pallas_call | solution.py:1773
  336.9 63.5 %second_rows.1 = (f32[320,2048]{1,0:T(8,128)}, bf16[320,2048]{1,0:T(8,128)(2,1)}, bf16[2048,1024]{1,0:T(8,128)(2,1)}) custom-call(bf16[2560,2048]{1,0:T(8,128)(2,1)} %ffn_slopes.1.slopes, bf16[2560,2048]{1,0:T(8,128)(2,1)} %bitcast.42, bf16[2048,2048]{1,0:T(8,128)(2,1)} %all-gather.6.cloned.1.call-done.weights_in, ...), custom_call_target="tpu_custom_call" | custom-call | bytes 180000000 | tf_op jit(solution)/shard_map/second_rows/pallas_call | solution.py:1210
  400.6 54.2 %spread_rows.1 = (bf16[4,2,320,2048]{3,2,1,0:T(8,128)(2,1)}, bf16[320,2048]{1,0:T(8,128)(2,1)}, bf16[320,2048]{1,0:T(8,128)(2,1)}, bf16[320,2048]{1,0:T(8,128)(2...) custom-call(bf16[320,2048]{1,0:T(8,128)(2,1)} %get-tuple-element.76.hidden, ...), custom_call_target="tpu_custom_call" | custom-call | bytes 180000000 | tf_op jit(solution)/shard_map/spread_rows/pallas_call | solution.py:1320
  455.5 1.4 collective-permute-start.4
  457.0 1.5 collective-permute-start.5
  458.4 8.2 %convolution_convert_fusion.grad_ref = bf16[2560,256]{1,0:T(8,128)(2,1)} fusion(bf16[2560,2048]{1,0:T(8,128)(2,1)} %bitcast.45, bf16[2048,640]{1,0:T(8,128)(2,1)} %all-gather.4.cloned.1.call-done.weight.weights), kind=kOutput, calls=%fused_computation.1 | convolution fusion | flops 2685009920 | bytes 12845056 | tf_op jit(solution)/shard_map/dot_general | solution.py:32
  466.6 3.5 all-to-all-start
  470.4 53.6 %attention_backward.1.back = bf16[2560,384]{1,0:T(8,128)(2,1)} custom-call(s32[20]{0:T(128)} %compare_select_fusion.1.to_ref, s32[20]{0:T(128)} %bitcast.70, bf16[2560,256]{1,0:T(8,128)(2,1)} %convolution_convert_fusion.grad_ref, bf16[2560,256]{1,0:T(8,128)(2,1)} %get-tuple-element.79.q_ref, bf16[2560,256]{1,0:T(8,128)(2,1)} %get-tuple-element.80.k_ref, ...), custom_call_target="tpu_custom_call" | custom-call | flops 13421772800 | bytes 10485760 | tf_op jit(solution)/shard_map/attention_backward/pallas_call | solution.py:331
  525.6 18.4 %attention_weights.1 = (bf16[2048,640]{1,0:T(8,128)(2,1)}, bf16[4,128,1024]{2,1,0:T(8,128)(2,1)}) custom-call(bf16[2560,2048]{1,0:T(8,128)(2,1)} %get-tuple-element.63.hidden, bf16[2560,384]{1,0:T(8,128)(2,1)} %attention_backward.1.back, bf16[2560,2048]{1,0:T(8,128)(2,1)} %bitcast.46, bf16[2560,256]{1,0:T(8,128)(2,1)} %get-tuple-element.65.attended, ...), custom_call_target="tpu_custom_call" | custom-call | bytes 75000000 | tf_op jit(solution)/shard_map/attention_weights/pallas_call | solution.py:1736
  544.0 4.5 finish_first.1
  548.5 6.1 reduce-scatter.11.cloned.1.call-done
  554.5 64.3 %last_rows.1 = (f32[2,320,2048]{2,1,0:T(8,128)}, bf16[2,320,2048]{2,1,0:T(8,128)(2,1)}, bf16[4,128,1024]{2,1,0:T(8,128)(2,1)}, f32[128,128]{1,0:T(8,128)}) custom-call(bf16[4,2,320,384]{3,2,1,0:T(8,128)(2,1)} %bitcast.48, bf16[2048,640]{1,0:T(8,128)(2,1)} %all-gather.4.cloned.1.call-done.weight.weights, f32[8,2048]{1,0:T(8,128)} %get-tuple-element.59.early.gains.gain, ...), custom_call_target="tpu_custom_call" | custom-call | bytes 210000000 | tf_op jit(solution)/shard_map/last_rows/pallas_call | solution.py:1458
  618.8 14.1 %exchange_blocks.1 = (bf16[4,128,640]{2,1,0:T(8,128)(2,1)}, f32[2,128,128]{2,1,0:T(8,128)}) custom-call(bf16[4,128,640]{2,1,0:T(8,128)(2,1)} %bitcast.63, bf16[128,1024]{1,0:T(8,128)(2,1)} %query.3, bf16[128,512]{1,0:T(8,128)(2,1)} %copy.35.pair, f32[128,128]{1,0:T(8,128)} %get-tuple-element.92.other_sums), custom_call_target="tpu_custom_call" | custom-call | bytes 24000000 | tf_op jit(solution)/shard_map/exchange_blocks/pallas_call | solution.py:1527
  632.9 8.2 %finish.1 = (f32[128,1024]{1,0:T(8,128)}, f32[128,256]{1,0:T(8,128)}, f32[128,256]{1,0:T(8,128)}, f32[1024,128]{1,0:T(8,128)}, f32[128,4096]{1,0:T(8,128)}, /*in...) custom-call(bf16[4,128,640]{2,1,0:T(8,128)(2,1)} %get-tuple-element.93.attn, ...), custom_call_target="tpu_custom_call" | custom-call | bytes 36000000 | tf_op jit(solution)/shard_map/finish/pallas_call | solution.py:1608
  (56 shorter events, 14.3 us)
Async XLA Ops:
  7.2 23.9 %copy-start.4 = (bf16[4096,128]{1,0:T(8,128)(2,1)S(1)}, bf16[4096,128]{1,0:T(8,128)(2,1)}, u32[]{:S(2)}) copy-start(bf16[4096,128]{1,0:T(8,128)(2,1)} %param.26) | copy-start | bytes 3145732
  7.2 121.8 %all-gather.4.cloned.1.call-start = ((), (), s32[]{:S(2)}) async-start(), calls=%async_computation.5 | async-start | bytes 3276800 | tf_op jit(solution)/shard_map/all_gather | solution.py:1851
  12.5 59.4 %copy-start.5 = (f32[2,128]{1,0:T(2,128)}, f32[2,128]{1,0:T(2,128)S(1)}, u32[]{:S(2)}) copy-start(f32[2,128]{1,0:T(2,128)S(1)} %maximum_convert_fusion.gains) | copy-start | bytes 3076
  31.0 206.7 %all-gather.6.cloned.1.call-start = ((), (), s32[]{:S(2)}) async-start(), calls=%async_computation.6 | async-start | bytes 10485760 | tf_op jit(solution)/shard_map/all_gather | solution.py:1851
  71.9 243.1 %all-gather.8.cloned.1.call-start = ((), (), s32[]{:S(2)}) async-start(), calls=%async_computation.7 | async-start | bytes 5242880 | tf_op jit(solution)/shard_map/all_gather | solution.py:1851
  72.7 55.8 %copy-start.6 = (s32[1,20]{1,0:T(1,128)S(1)}, s32[1,20]{1,0:T(1,128)}, u32[]{:S(2)}) copy-start(s32[1,20]{1,0:T(1,128)} %param.27) | copy-start | bytes 244
  72.7 55.7 %copy-start.7 = (s32[1,20]{1,0:T(1,128)S(1)}, s32[1,20]{1,0:T(1,128)}, u32[]{:S(2)}) copy-start(s32[1,20]{1,0:T(1,128)} %param.28) | copy-start | bytes 244
  72.7 393.9 %reduce-scatter.5.cloned.1.call-start = ((), (), s32[]{:S(2)}) async-start(), calls=%async_computation.8 | async-start | bytes 5242880 | tf_op jit(solution)/shard_map/reduce_scatter | solution.py:1946
  124.9 112.8 %collective-permute-start.2 = (bf16[320,2048]{1,0:T(8,128)(2,1)}, bf16[320,2048]{1,0:T(8,128)(2,1)S(1)}, u32[]{:S(2)}, u32[]{:S(2)}) collective-permute-start(bf16[320,2048]{1,0:T(8,128)(2,1)} %get-tuple-element.69), channel_id=1, source_target_pairs={{0,6},{2,4},{4,2},{6,0},{1,7},{3,5},{5,3},{7,1},{8,14},{10,12},{12... | collective-permute-start | bytes 3932168 | tf_op jit(solution)/shard_map/ppermute | solution.py:1914
  126.4 111.3 %collective-permute-start.1 = (bf16[320,2048]{1,0:T(8,128)(2,1)}, bf16[320,2048]{1,0:T(8,128)(2,1)S(1)}, u32[]{:S(2)}, u32[]{:S(2)}) collective-permute-start(bf16[320,2048]{1,0:T(8,128)(2,1)} %get-tuple-element.69), channel_id=1, source_target_pairs={{0,4},{2,6},{4,0},{6,2},{1,5},{3,7},{5,1},{7,3},{8,12},{10,14},{12... | collective-permute-start | bytes 3932168 | tf_op jit(solution)/shard_map/ppermute | solution.py:1914
  127.4 110.3 %collective-permute-start = (bf16[320,2048]{1,0:T(8,128)(2,1)}, bf16[320,2048]{1,0:T(8,128)(2,1)}, u32[]{:S(2)}, u32[]{:S(2)}) collective-permute-start(bf16[320,2048]{1,0:T(8,128)(2,1)} %get-tuple-element.69), channel_id=1, source_target_pairs={{0,2},{2,0},{4,6},{6,4},{1,3},{3,1},{5,7},{7,5},{8,10},{10,8},{12,... | collective-permute-start | bytes 3932168 | tf_op jit(solution)/shard_map/ppermute | solution.py:1914
  237.7 1.1 copy-start.2
  237.7 1.5 copy-start.3
  315.0 209.0 %reduce-scatter.7.cloned.1.call-start = ((), (), s32[]{:S(2)}) async-start(), calls=%async_computation.9 | async-start | bytes 5242880 | tf_op jit(solution)/shard_map/reduce_scatter | solution.py:1946
  400.4 154.1 %reduce-scatter.11.cloned.1.call-start = ((), (), s32[]{:S(2)}) async-start(), calls=%async_computation.11 | async-start | bytes 5242880 | tf_op jit(solution)/shard_map/reduce_scatter | solution.py:1946
  454.9 69.1 %collective-permute-start.3 = (bf16[320,2048]{1,0:T(8,128)(2,1)}, bf16[320,2048]{1,0:T(8,128)(2,1)S(1)}, u32[]{:S(2)}, u32[]{:S(2)}) collective-permute-start(bf16[320,2048]{1,0:T(8,128)(2,1)} %get-tuple-element.83), channel_id=1, source_target_pairs={{0,2},{2,0},{4,6},{6,4},{1,3},{3,1},{5,7},{7,5},{8,10},{10,8},{12,... | collective-permute-start | bytes 3932168 | tf_op jit(solution)/shard_map/ppermute | solution.py:1968
  455.5 68.5 %collective-permute-start.4 = (bf16[320,2048]{1,0:T(8,128)(2,1)}, bf16[320,2048]{1,0:T(8,128)(2,1)}, u32[]{:S(2)}, u32[]{:S(2)}) collective-permute-start(bf16[320,2048]{1,0:T(8,128)(2,1)} %get-tuple-element.84), channel_id=1, source_target_pairs={{0,4},{2,6},{4,0},{6,2},{1,5},{3,7},{5,1},{7,3},{8,12},{10,14},{12... | collective-permute-start | bytes 3932168 | tf_op jit(solution)/shard_map/ppermute | solution.py:1968
  457.0 67.0 %collective-permute-start.5 = (bf16[320,2048]{1,0:T(8,128)(2,1)}, bf16[320,2048]{1,0:T(8,128)(2,1)}, u32[]{:S(2)}, u32[]{:S(2)}) collective-permute-start(bf16[320,2048]{1,0:T(8,128)(2,1)} %get-tuple-element.85), channel_id=1, source_target_pairs={{0,6},{2,4},{4,2},{6,0},{1,7},{3,5},{5,3},{7,1},{8,14},{10,12},{12... | collective-permute-start | bytes 3932168 | tf_op jit(solution)/shard_map/ppermute | solution.py:1968
  466.6 58.0 %all-to-all-start = ((bf16[4,128,1024]{2,1,0:T(8,128)(2,1)}), bf16[4,128,1024]{2,1,0:T(8,128)(2,1)S(1)}, u32[]{:S(2)}, u32[]{:S(2)}) async-start(bf16[4,128,1024]{2,1,0:T(8,128)(2,1)} %bitcast.59), calls=%async_computation.2 | async-start | bytes 2097152 | tf_op jit(solution)/shard_map/all_to_all | solution.py:1949
  470.1 148.7 %reduce-scatter.9.cloned.1.call-start = ((), (), s32[]{:S(2)}) async-start(), calls=%async_computation.10 | async-start | bytes 3276800 | tf_op jit(solution)/shard_map/reduce_scatter | solution.py:1946
  524.0 1.1 copy-start.1
  524.6 1.0 copy-start
Sparse Core Ops, SparseCore 0:
  31.2 52.9 all-gather.3
  85.7 148.3 all-gather.5
  235.7 79.0 all-gather.7
  317.5 75.2 reduce-scatter.4
  400.5 74.5 reduce-scatter.6
  477.2 77.2 reduce-scatter.10
  556.9 52.6 reduce-scatter.8

commit v10 on v9

--- a/solution.py
+++ b/solution.py
@@ -595,7 +595,22 @@
         self.mine.wait()
 
 
-def first_kernel(query, pair, out_turned, gains, packed, gains_out, sent, landed, local, far_sent, far_landed):
+def first_kernel(
+    query,
+    key,
+    value,
+    out_weight,
+    gains,
+    packed,
+    gains_out,
+    pair,
+    sent,
+    landed,
+    local,
+    far_sent,
+    far_landed,
+    out_turned,
+):
     groups = lax.axis_size("fsdp")
     group, rank = lax.axis_index("fsdp"), lax.axis_index("context")
     depth = gains.shape[1]
@@ -610,6 +625,18 @@
     barrier = pltpu.get_barrier_semaphore()
     for i, j in others:
         pl.semaphore_signal(barrier, inc=1, device_id=device(i, j), device_id_type=MESH)
+    for c in range(pair.shape[1] // 128):
+        cut = slice(c // 2 * 128, c // 2 * 128 + 128)
+        keys, values = key[:, cut].astype(jnp.float32), value[:, cut].astype(jnp.float32)
+        if c % 2:
+            keys = pltpu.roll(keys, HEAD, 1)
+        else:
+            values = pltpu.roll(values, HEAD, 1)
+        both = jnp.where(lanes(keys) < HEAD, keys, values)
+        pair[:, c * 128 : c * 128 + 128] = both.astype(jnp.bfloat16)
+    for first in range(0, out_weight.shape[0], 256):
+        block = jnp.transpose(out_weight[first : first + 256, :].astype(jnp.float32))
+        out_turned[:, first : first + 256] = block.astype(jnp.bfloat16)
     pl.semaphore_wait(barrier, len(others))
     p = Plane(sent, landed, entered=True)
     width = query.shape[1] // 4
@@ -639,7 +666,7 @@
     p.finish()
 
 
-def first_exchange(query, pair, out_turned, gains):
+def first_exchange(query, key, value, out_weight, gains):
     depth, columns = query.shape
     groups = lax.axis_size("fsdp")
     far = groups * 4 - 1
@@ -648,14 +675,20 @@
         out_shape=[
             jax.ShapeDtypeStruct((4, depth, columns // 2 + 128), query.dtype),
             jax.ShapeDtypeStruct((8, groups * 4 * depth), jnp.float32),
+            jax.ShapeDtypeStruct((depth, 2 * key.shape[1]), key.dtype),
         ],
-        in_specs=[VMEM] * 4,
-        out_specs=[ANY, VMEM],
-        scratch_shapes=wires(9) + [pltpu.SemaphoreType.DMA((3,))] + wires(far),
-        compiler_params=pltpu.CompilerParams(collective_id=9, has_side_effects=True),
+        in_specs=[VMEM] * 5,
+        out_specs=[ANY, VMEM, VMEM],
+        scratch_shapes=wires(9)
+        + [pltpu.SemaphoreType.DMA((3,))]
+        + wires(far)
+        + [pltpu.VMEM((depth, columns), query.dtype)],
+        compiler_params=pltpu.CompilerParams(
+            collective_id=9, has_side_effects=True, vmem_limit_bytes=VMEM_LIMIT
+        ),
         cost_estimate=lasting(10),
         name="first_exchange",
-    )(query, pair, out_turned, gains)
+    )(query, key, value, out_weight, gains)
 
 
 def start_kernel(tokens, cotangent, early, out, scaled, my_scaled, sent, landed, local):
@@ -1844,7 +1877,7 @@
     square = groups == 4 and cores == 2
     width = w_query.shape[1] // groups
     columns_qkv = width + 2 * HEAD
-    out_turned, down_turned = w_out.T, w_down.T
+    down_turned = w_down.T
     tokens_half, cotangent_half = my_rows(tokens), my_rows(cotangent)
 
     def over_groups(blocks_here):
@@ -1854,10 +1887,7 @@
 
     if square:
         gains = jnp.pad(jnp.stack([attn_gain, ffn_gain]).astype(jnp.float32), ((0, 6), (0, 0)))
-        w_pair = jnp.stack(
-            [w_key.reshape(depth, groups, HEAD), w_value.reshape(depth, groups, HEAD)], axis=2
-        ).reshape(depth, -1)
-        packed, gain_rows = first_exchange(w_query, w_pair, out_turned, gains)
+        packed, gain_rows, w_pair = first_exchange(w_query, w_key, w_value, w_out, gains)
         packed = over_groups(packed)
         both_blocks, down_blocks = exchange_columns(w_gate, w_up, down_turned, gain_rows)
         inputs_full, ffn_grad, my_ffn_grad = start_plane(tokens, cotangent, down_blocks)
@@ -1875,7 +1905,7 @@
                     blocks(w_query),
                     kv_blocks(w_key),
                     kv_blocks(w_value),
-                    blocks(out_turned),
+                    blocks(w_out.T),
                     gains,
                 ],
                 axis=2,

time: 660 us -> 656 us (level)
  no operation moved by 1% of the time
where the time goes in v10:
time: 656 us; the launch traced here: 645 us
  Pallas kernels  579 us (88%)
  matrix products  25 us (4%)
  between operations  14.8 us (2%)
  starting transfers between devices  11.3 us (2%)
  waiting for transfers between devices  7.47 us (1%)
    pallas_call x1, Pallas kernels, last_plane(): pl.pallas_call(last_kernel, out_shape=[jax.ShapeDtypeStruct((2, share, wi...  64.1 us
    pallas_call x1, Pallas kernels, second_plane(): pl.pallas_call(second_kernel, out_shape=[jax.ShapeDtypeStruct((share, wid...  62.5 us
    pallas_call x1, Pallas kernels, ffn_rows(): pl.pallas_call(ffn_rows_kernel, out_shape=[full, part, part, part, full],...  59 us
    pallas_call x1, Pallas kernels, middle_plane(): pl.pallas_call(middle_kernel, out_shape=[jax.ShapeDtypeStruct((share, wid...  56.1 us
    pallas_call x1, Pallas kernels, spread_plane(): pl.pallas_call(spread_kernel, out_shape=[full] + [jax.ShapeDtypeStruct((s...  53.9 us
    pallas_call x1, Pallas kernels, attention_backward(): pl.pallas_call(attention_backward_kernel, out_shape=jax.ShapeDtypeStruct(...  53.6 us
    pallas_call x1, Pallas kernels, start_plane(): pl.pallas_call(start_kernel, out_shape=[jax.ShapeDtypeStruct((4, 2, share...  52.1 us
    pallas_call x1, Pallas kernels, exchange_columns(): pl.pallas_call(columns_kernel, out_shape=[jax.ShapeDtypeStruct((4, depth,...  39.5 us
  transfers between devices with their start and end apart: 14, of which 2 were waited for; matrix products, arithmetic and copies ran while one was open for 4% of the time, Pallas kernels for 83%

profile of v10, /device:TPU:0, one launch (start us, length us, event | category | flops | bytes accessed | tf_op | source)
XLA Modules:
  0.0 644.9 jit_solution(7356521841213986535)
XLA Ops:
  8.5 17.9 %first_exchange.1 = (bf16[4,128,640]{2,1,0:T(8,128)(2,1)}, f32[8,2048]{1,0:T(8,128)}, bf16[128,512]{1,0:T(8,128)(2,1)}) custom-call(bf16[128,1024]{1,0:T(8,128)(2,1)} %query.3, bf16[128,256]{1,0:T(8,128)(2,1)} %key.1, bf16[128,256]{1,0:T(8,128)(2,1)} %value.1, bf16[1024,128]{1,0:T(8,128)(2,1)} %out_weight.1, f32[8,128]{1,0:T(8,128)} %pad.4.gains), custom_call_target="tpu_custom_call" | custom-call | bytes 30000000 | tf_op jit(solution)/shard_map/first_exchange/pallas_call | solution.py:673
  26.5 2.3 copy.26
  28.8 39.5 %exchange_columns.1 = (bf16[4,128,2048]{2,1,0:T(8,128)(2,1)}, bf16[4,128,1024]{2,1,0:T(8,128)(2,1)}) custom-call(bf16[128,4096]{1,0:T(8,128)(2,1)} %rest_6_.1, bf16[128,4096]{1,0:T(8,128)(2,1)} %rest_7_.1, bf16[128,4096]{1,0:T(8,128)(2,1)} %bitcast.49, f32[8,2048]{1,0:T(8,128)} %get-tuple-element.60.early.gains.gain), custom_call_target="tpu_custom_call" | custom-call | bytes 90000000 | tf_op jit(solution)/shard_map/exchange_columns/pallas_call | solution.py:755
  69.1 52.1 %gather_tokens.1 = (bf16[4,2,320,2048]{3,2,1,0:T(8,128)(2,1)}, bf16[640,2048]{1,0:T(8,128)(2,1)}, bf16[320,2048]{1,0:T(8,128)(2,1)}) custom-call(bf16[640,2048]{1,0:T(8,128)(2,1)} %rest_8_.1, bf16[640,2048]{1,0:T(8,128)(2,1)} %cotangent_in.1, bf16[4,128,1024]{2,1,0:T(8,128)(2,1)} %get-tuple-element.61.early), custom_call_target="tpu_custom_call" | custom-call | bytes 180000000 | tf_op jit(solution)/shard_map/gather_tokens/pallas_call | solution.py:722
  121.2 1.5 collective-permute-start.2
  125.3 14.2 %first_rows.1 = (bf16[2560,2048]{1,0:T(8,128)(2,1)}, f32[2560,384]{1,0:T(8,128)}) custom-call(bf16[2560,2048]{1,0:T(8,128)(2,1)} %bitcast.40, f32[8,2048]{1,0:T(8,128)} %get-tuple-element.60.early.gains.gain, bf16[2048,640]{1,0:T(8,128)(2,1)} %all-gather.4.cloned.1.call-done.weight.weights), custom_call_target="tpu_custom_call" | custom-call | bytes 12000000 | tf_op jit(solution)/shard_map/first_rows/pallas_call | solution.py:1718
  139.5 38.5 %attention_forward.1 = (bf16[2560,256]{1,0:T(8,128)(2,1)}, bf16[2560,256]{1,0:T(8,128)(2,1)}, bf16[2560,256]{1,0:T(8,128)(2,1)}, bf16[2560,256]{1,0:T(8,128)(2,1)}, f32[4,1,2560]{2,1,0:T(1,128)}) custom-call(s32[20]{0:T(128)} %compare_select_fusion.1.to_ref, s32[20]{0:T(128)} %bitcast.61, f32[2560,384]{1,0:T(8,128)} %get-tuple-element.65.raw_ref, ...), custom_call_target="tpu_custom_call" | custom-call | flops 5368709120 | bytes 10485760 | tf_op jit(solution)/shard_map/attention_forward/pallas_call | solution.py:313
  178.0 56.1 %middle_rows.1 = (bf16[320,2048]{1,0:T(8,128)(2,1)}, f32[320,2048]{1,0:T(8,128)}) custom-call(bf16[4,2,320,256]{3,2,1,0:T(8,128)(2,1)} %bitcast.48, bf16[2048,640]{1,0:T(8,128)(2,1)} %all-gather.4.cloned.1.call-done.weight.weights, f32[8,2048]{1,0:T(8,128)} %get-tuple-element.60.early.gains.gain, bf16[640,2048]{1,0:T(8,128)(2,1)} %rest_8_.1), custom_call_target="tpu_custom_call" | custom-call | bytes 165000000 | tf_op jit(solution)/shard_map/middle_rows/pallas_call | solution.py:806
  235.6 59.0 %ffn_rows.1 = (bf16[4,2,320,2048]{3,2,1,0:T(8,128)(2,1)}, bf16[4,2,320,1024]{3,2,1,0:T(8,128)(2,1)}, bf16[4,2,320,1024]{3,2,1,0:T(8,128)(2,1)}, bf16[4,2,320,102...) custom-call(bf16[320,2048]{1,0:T(8,128)(2,1)} %get-tuple-element.67.block, ...), custom_call_target="tpu_custom_call" | custom-call | bytes 180000000 | tf_op jit(solution)/shard_map/ffn_rows/pallas_call | solution.py:973
  294.6 16.8 %bitcast_convert_fusion.early = bf16[2048,1024]{1,0:T(8,128)(2,1)} fusion(bf16[4,2,320,2048]{3,2,1,0:T(8,128)(2,1)} %get-tuple-element.71, bf16[4,2,320,1024]{3,2,1,0:T(8,128)(2,1)} %get-tuple-element.74.m), kind=kOutput, calls=%fused_computation | convolution fusion | flops 10739515392 | bytes 19922944 | tf_op jit(solution)/shard_map/dot_general | solution.py:32
  311.5 22.1 %ffn_slopes.1.slopes = bf16[2560,2048]{1,0:T(8,128)(2,1)} custom-call(bf16[2560,2048]{1,0:T(8,128)(2,1)} %bitcast.43, bf16[2560,1024]{1,0:T(8,128)(2,1)} %bitcast.45, bf16[2560,1024]{1,0:T(8,128)(2,1)} %bitcast.46, bf16[2048,1024]{1,0:T(8,128)(2,1)} %all-gather.8.cloned.1.call-done.down_w.down_in, bf16[2048,1024]{1,0:T(8,128)(2,1)} %bitcast_convert_fusion.early), custom_call_target="tpu_custom_call" | custom-call | flops 10737418240 | bytes 26843544 | tf_op jit(solution)/shard_map/ffn_slopes/pallas_call | solution.py:1806
  333.5 62.5 %second_rows.1 = (f32[320,2048]{1,0:T(8,128)}, bf16[320,2048]{1,0:T(8,128)(2,1)}, bf16[2048,1024]{1,0:T(8,128)(2,1)}) custom-call(bf16[2560,2048]{1,0:T(8,128)(2,1)} %ffn_slopes.1.slopes, bf16[2560,2048]{1,0:T(8,128)(2,1)} %bitcast.38, bf16[2048,2048]{1,0:T(8,128)(2,1)} %all-gather.6.cloned.1.call-done.weights_in, ...), custom_call_target="tpu_custom_call" | custom-call | bytes 180000000 | tf_op jit(solution)/shard_map/second_rows/pallas_call | solution.py:1243
  396.3 53.9 %spread_rows.1 = (bf16[4,2,320,2048]{3,2,1,0:T(8,128)(2,1)}, bf16[320,2048]{1,0:T(8,128)(2,1)}, bf16[320,2048]{1,0:T(8,128)(2,1)}, bf16[320,2048]{1,0:T(8,128)(2...) custom-call(bf16[320,2048]{1,0:T(8,128)(2,1)} %get-tuple-element.77.hidden, ...), custom_call_target="tpu_custom_call" | custom-call | bytes 180000000 | tf_op jit(solution)/shard_map/spread_rows/pallas_call | solution.py:1353
  452.4 1.5 collective-permute-start.5
  453.8 8.2 %convolution_convert_fusion.grad_ref = bf16[2560,256]{1,0:T(8,128)(2,1)} fusion(bf16[2560,2048]{1,0:T(8,128)(2,1)} %bitcast.41, bf16[2048,640]{1,0:T(8,128)(2,1)} %all-gather.4.cloned.1.call-done.weight.weights), kind=kOutput, calls=%fused_computation.1 | convolution fusion | flops 2685009920 | bytes 12845056 | tf_op jit(solution)/shard_map/dot_general | solution.py:32
  462.0 3.5 all-to-all-start
  465.8 53.6 %attention_backward.1.back = bf16[2560,384]{1,0:T(8,128)(2,1)} custom-call(s32[20]{0:T(128)} %compare_select_fusion.1.to_ref, s32[20]{0:T(128)} %bitcast.62, bf16[2560,256]{1,0:T(8,128)(2,1)} %convolution_convert_fusion.grad_ref, bf16[2560,256]{1,0:T(8,128)(2,1)} %get-tuple-element.80.q_ref, bf16[2560,256]{1,0:T(8,128)(2,1)} %get-tuple-element.81.k_ref, ...), custom_call_target="tpu_custom_call" | custom-call | flops 13421772800 | bytes 10485760 | tf_op jit(solution)/shard_map/attention_backward/pallas_call | solution.py:331
  520.9 18.4 %attention_weights.1 = (bf16[2048,640]{1,0:T(8,128)(2,1)}, bf16[4,128,1024]{2,1,0:T(8,128)(2,1)}) custom-call(bf16[2560,2048]{1,0:T(8,128)(2,1)} %get-tuple-element.64.hidden, bf16[2560,384]{1,0:T(8,128)(2,1)} %attention_backward.1.back, bf16[2560,2048]{1,0:T(8,128)(2,1)} %bitcast.42, bf16[2560,256]{1,0:T(8,128)(2,1)} %get-tuple-element.66.attended, ...), custom_call_target="tpu_custom_call" | custom-call | bytes 75000000 | tf_op jit(solution)/shard_map/attention_weights/pallas_call | solution.py:1769
  539.4 4.5 finish_first.1
  543.9 6.0 reduce-scatter.11.cloned.1.call-done
  549.9 64.1 %last_rows.1 = (f32[2,320,2048]{2,1,0:T(8,128)}, bf16[2,320,2048]{2,1,0:T(8,128)(2,1)}, bf16[4,128,1024]{2,1,0:T(8,128)(2,1)}, f32[128,128]{1,0:T(8,128)}) custom-call(bf16[4,2,320,384]{3,2,1,0:T(8,128)(2,1)} %bitcast.44, bf16[2048,640]{1,0:T(8,128)(2,1)} %all-gather.4.cloned.1.call-done.weight.weights, f32[8,2048]{1,0:T(8,128)} %get-tuple-element.60.early.gains.gain, ...), custom_call_target="tpu_custom_call" | custom-call | bytes 210000000 | tf_op jit(solution)/shard_map/last_rows/pallas_call | solution.py:1491
  614.0 14.1 %exchange_blocks.1 = (bf16[4,128,640]{2,1,0:T(8,128)(2,1)}, f32[2,128,128]{2,1,0:T(8,128)}) custom-call(bf16[4,128,640]{2,1,0:T(8,128)(2,1)} %bitcast.58, bf16[128,1024]{1,0:T(8,128)(2,1)} %query.3, bf16[128,512]{1,0:T(8,128)(2,1)} %get-tuple-element.88.pair, f32[128,128]{1,0:T(8,128)} %get-tuple-element.94.other_sums), custom_call_target="tpu_custom_call" | custom-call | bytes 24000000 | tf_op jit(solution)/shard_map/exchange_blocks/pallas_call | solution.py:1560
  628.1 8.2 %finish.1 = (f32[128,1024]{1,0:T(8,128)}, f32[128,256]{1,0:T(8,128)}, f32[128,256]{1,0:T(8,128)}, f32[1024,128]{1,0:T(8,128)}, f32[128,4096]{1,0:T(8,128)}, /*in...) custom-call(bf16[4,128,640]{2,1,0:T(8,128)(2,1)} %get-tuple-element.95.attn, ...), custom_call_target="tpu_custom_call" | custom-call | bytes 36000000 | tf_op jit(solution)/shard_map/finish/pallas_call | solution.py:1641
  636.4 1.3 slice_bitcast_fusion
  (48 shorter events, 10.4 us)
Async XLA Ops:
  7.2 118.2 %all-gather.4.cloned.1.call-start = ((), (), s32[]{:S(2)}) async-start(), calls=%async_computation.5 | async-start | bytes 3276800 | tf_op jit(solution)/shard_map/all_gather | solution.py:1884
  7.9 60.4 %copy-start.4 = (f32[2,128]{1,0:T(2,128)}, f32[2,128]{1,0:T(2,128)S(1)}, u32[]{:S(2)}) copy-start(f32[2,128]{1,0:T(2,128)S(1)} %maximum_convert_fusion.gains) | copy-start | bytes 3076
  26.5 207.7 %all-gather.6.cloned.1.call-start = ((), (), s32[]{:S(2)}) async-start(), calls=%async_computation.6 | async-start | bytes 10485760 | tf_op jit(solution)/shard_map/all_gather | solution.py:1884
  68.3 243.2 %all-gather.8.cloned.1.call-start = ((), (), s32[]{:S(2)}) async-start(), calls=%async_computation.7 | async-start | bytes 5242880 | tf_op jit(solution)/shard_map/all_gather | solution.py:1884
  69.0 55.8 %copy-start.5 = (s32[1,20]{1,0:T(1,128)S(1)}, s32[1,20]{1,0:T(1,128)}, u32[]{:S(2)}) copy-start(s32[1,20]{1,0:T(1,128)} %param.27) | copy-start | bytes 244
  69.0 55.8 %copy-start.6 = (s32[1,20]{1,0:T(1,128)S(1)}, s32[1,20]{1,0:T(1,128)}, u32[]{:S(2)}) copy-start(s32[1,20]{1,0:T(1,128)} %param.28) | copy-start | bytes 244
  69.1 392.9 %reduce-scatter.5.cloned.1.call-start = ((), (), s32[]{:S(2)}) async-start(), calls=%async_computation.8 | async-start | bytes 5242880 | tf_op jit(solution)/shard_map/reduce_scatter | solution.py:1976
  121.2 112.9 %collective-permute-start.2 = (bf16[320,2048]{1,0:T(8,128)(2,1)}, bf16[320,2048]{1,0:T(8,128)(2,1)S(1)}, u32[]{:S(2)}, u32[]{:S(2)}) collective-permute-start(bf16[320,2048]{1,0:T(8,128)(2,1)} %get-tuple-element.70), channel_id=1, source_target_pairs={{0,6},{2,4},{4,2},{6,0},{1,7},{3,5},{5,3},{7,1},{8,14},{10,12},{12... | collective-permute-start | bytes 3932168 | tf_op jit(solution)/shard_map/ppermute | solution.py:1944
  122.8 111.4 %collective-permute-start.1 = (bf16[320,2048]{1,0:T(8,128)(2,1)}, bf16[320,2048]{1,0:T(8,128)(2,1)S(1)}, u32[]{:S(2)}, u32[]{:S(2)}) collective-permute-start(bf16[320,2048]{1,0:T(8,128)(2,1)} %get-tuple-element.70), channel_id=1, source_target_pairs={{0,4},{2,6},{4,0},{6,2},{1,5},{3,7},{5,1},{7,3},{8,12},{10,14},{12... | collective-permute-start | bytes 3932168 | tf_op jit(solution)/shard_map/ppermute | solution.py:1944
  123.8 110.4 %collective-permute-start = (bf16[320,2048]{1,0:T(8,128)(2,1)}, bf16[320,2048]{1,0:T(8,128)(2,1)}, u32[]{:S(2)}, u32[]{:S(2)}) collective-permute-start(bf16[320,2048]{1,0:T(8,128)(2,1)} %get-tuple-element.70), channel_id=1, source_target_pairs={{0,2},{2,0},{4,6},{6,4},{1,3},{3,1},{5,7},{7,5},{8,10},{10,8},{12,... | collective-permute-start | bytes 3932168 | tf_op jit(solution)/shard_map/ppermute | solution.py:1944
  234.1 1.1 copy-start.2
  234.1 1.5 copy-start.3
  311.4 208.0 %reduce-scatter.7.cloned.1.call-start = ((), (), s32[]{:S(2)}) async-start(), calls=%async_computation.9 | async-start | bytes 5242880 | tf_op jit(solution)/shard_map/reduce_scatter | solution.py:1976
  396.1 153.8 %reduce-scatter.11.cloned.1.call-start = ((), (), s32[]{:S(2)}) async-start(), calls=%async_computation.11 | async-start | bytes 5242880 | tf_op jit(solution)/shard_map/reduce_scatter | solution.py:1976
  450.3 69.1 %collective-permute-start.3 = (bf16[320,2048]{1,0:T(8,128)(2,1)}, bf16[320,2048]{1,0:T(8,128)(2,1)S(1)}, u32[]{:S(2)}, u32[]{:S(2)}) collective-permute-start(bf16[320,2048]{1,0:T(8,128)(2,1)} %get-tuple-element.84), channel_id=1, source_target_pairs={{0,2},{2,0},{4,6},{6,4},{1,3},{3,1},{5,7},{7,5},{8,10},{10,8},{12,... | collective-permute-start | bytes 3932168 | tf_op jit(solution)/shard_map/ppermute | solution.py:1998
  451.3 68.1 %collective-permute-start.4 = (bf16[320,2048]{1,0:T(8,128)(2,1)}, bf16[320,2048]{1,0:T(8,128)(2,1)}, u32[]{:S(2)}, u32[]{:S(2)}) collective-permute-start(bf16[320,2048]{1,0:T(8,128)(2,1)} %get-tuple-element.85), channel_id=1, source_target_pairs={{0,4},{2,6},{4,0},{6,2},{1,5},{3,7},{5,1},{7,3},{8,12},{10,14},{12... | collective-permute-start | bytes 3932168 | tf_op jit(solution)/shard_map/ppermute | solution.py:1998
  452.4 67.0 %collective-permute-start.5 = (bf16[320,2048]{1,0:T(8,128)(2,1)}, bf16[320,2048]{1,0:T(8,128)(2,1)}, u32[]{:S(2)}, u32[]{:S(2)}) collective-permute-start(bf16[320,2048]{1,0:T(8,128)(2,1)} %get-tuple-element.86), channel_id=1, source_target_pairs={{0,6},{2,4},{4,2},{6,0},{1,7},{3,5},{5,3},{7,1},{8,14},{10,12},{12... | collective-permute-start | bytes 3932168 | tf_op jit(solution)/shard_map/ppermute | solution.py:1998
  462.0 58.0 %all-to-all-start = ((bf16[4,128,1024]{2,1,0:T(8,128)(2,1)}), bf16[4,128,1024]{2,1,0:T(8,128)(2,1)S(1)}, u32[]{:S(2)}, u32[]{:S(2)}) async-start(bf16[4,128,1024]{2,1,0:T(8,128)(2,1)} %bitcast.55), calls=%async_computation.2 | async-start | bytes 2097152 | tf_op jit(solution)/shard_map/all_to_all | solution.py:1979
  465.5 148.5 %reduce-scatter.9.cloned.1.call-start = ((), (), s32[]{:S(2)}) async-start(), calls=%async_computation.10 | async-start | bytes 3276800 | tf_op jit(solution)/shard_map/reduce_scatter | solution.py:1976
  519.4 1.1 copy-start.1
  520.0 1.0 copy-start
Sparse Core Ops, SparseCore 0:
  26.6 52.9 all-gather.3
  81.1 148.3 all-gather.5
  231.1 78.9 all-gather.7
  312.9 75.2 reduce-scatter.4
  396.2 74.1 reduce-scatter.6
  472.6 77.2 reduce-scatter.10
  552.3 52.6 reduce-scatter.8

commit v11 on v10

--- a/solution.py
+++ b/solution.py
@@ -1188,18 +1188,17 @@
         started.start()
     wait_loads((0,))
     unit(0)
+    settle(0)
     wait_loads((1,))
     unit(1)
-    settle(0)
+    settle(1)
     wait_loads((2, 3))
     unit(2)
-    settle(1)
     unit(3)
     settle(2)
+    settle(3)
     wait_loads((4, 5, 6, 7))
     unit(4)
-    tiles.run(0, 2)
-    settle(3)
     unit(5)
     settle(4)
     unit(6)
@@ -1207,7 +1206,7 @@
     unit(7)
     settle(6)
     settle(7)
-    tiles.run(2, tiles.count)
+    tiles.run(0, tiles.count)
 
     def work(rows):
         value = middle[rows, :]

time: 656 us -> 656 us (level)
  transfers between devices with their start and end apart: 14 -> 14, of which waited for: 2 -> 2; matrix products, arithmetic and copies ran while one was open for 4% -> 4% of each run, Pallas kernels for 83% -> 84%
where the time goes in v11:
time: 656 us; the launch traced here: 646 us
  Pallas kernels  580 us (88%)
  matrix products  25 us (4%)
  between operations  14.8 us (2%)
  starting transfers between devices  10.9 us (2%)
  waiting for transfers between devices  7.59 us (1%)
    pallas_call x1, Pallas kernels, last_plane(): pl.pallas_call(last_kernel, out_shape=[jax.ShapeDtypeStruct((2, share, wi...  64.2 us
    pallas_call x1, Pallas kernels, second_plane(): pl.pallas_call(second_kernel, out_shape=[jax.ShapeDtypeStruct((share, wid...  63.3 us
    pallas_call x1, Pallas kernels, ffn_rows(): pl.pallas_call(ffn_rows_kernel, out_shape=[full, part, part, part, full],...  59 us
    pallas_call x1, Pallas kernels, middle_plane(): pl.pallas_call(middle_kernel, out_shape=[jax.ShapeDtypeStruct((share, wid...  56.1 us
    pallas_call x1, Pallas kernels, spread_plane(): pl.pallas_call(spread_kernel, out_shape=[full] + [jax.ShapeDtypeStruct((s...  53.9 us
    pallas_call x1, Pallas kernels, attention_backward(): pl.pallas_call(attention_backward_kernel, out_shape=jax.ShapeDtypeStruct(...  53.8 us
    pallas_call x1, Pallas kernels, start_plane(): pl.pallas_call(start_kernel, out_shape=[jax.ShapeDtypeStruct((4, 2, share...  52.1 us
    pallas_call x1, Pallas kernels, exchange_columns(): pl.pallas_call(columns_kernel, out_shape=[jax.ShapeDtypeStruct((4, depth,...  39.5 us
  transfers between devices with their start and end apart: 14, of which 2 were waited for; matrix products, arithmetic and copies ran while one was open for 4% of the time, Pallas kernels for 84%

profile of v11, /device:TPU:0, one launch (start us, length us, event | category | flops | bytes accessed | tf_op | source)
XLA Modules:
  0.0 645.7 jit_solution(567926123526958871)
XLA Ops:
  8.5 17.9 %first_exchange.1 = (bf16[4,128,640]{2,1,0:T(8,128)(2,1)}, f32[8,2048]{1,0:T(8,128)}, bf16[128,512]{1,0:T(8,128)(2,1)}) custom-call(bf16[128,1024]{1,0:T(8,128)(2,1)} %query.3, bf16[128,256]{1,0:T(8,128)(2,1)} %key.1, bf16[128,256]{1,0:T(8,128)(2,1)} %value.1, bf16[1024,128]{1,0:T(8,128)(2,1)} %out_weight.1, f32[8,128]{1,0:T(8,128)} %pad.4.gains), custom_call_target="tpu_custom_call" | custom-call | bytes 30000000 | tf_op jit(solution)/shard_map/first_exchange/pallas_call | solution.py:673
  26.5 2.3 copy.26
  28.8 39.5 %exchange_columns.1 = (bf16[4,128,2048]{2,1,0:T(8,128)(2,1)}, bf16[4,128,1024]{2,1,0:T(8,128)(2,1)}) custom-call(bf16[128,4096]{1,0:T(8,128)(2,1)} %rest_6_.1, bf16[128,4096]{1,0:T(8,128)(2,1)} %rest_7_.1, bf16[128,4096]{1,0:T(8,128)(2,1)} %bitcast.49, f32[8,2048]{1,0:T(8,128)} %get-tuple-element.60.early.gains.gain), custom_call_target="tpu_custom_call" | custom-call | bytes 90000000 | tf_op jit(solution)/shard_map/exchange_columns/pallas_call | solution.py:755
  69.1 52.1 %gather_tokens.1 = (bf16[4,2,320,2048]{3,2,1,0:T(8,128)(2,1)}, bf16[640,2048]{1,0:T(8,128)(2,1)}, bf16[320,2048]{1,0:T(8,128)(2,1)}) custom-call(bf16[640,2048]{1,0:T(8,128)(2,1)} %rest_8_.1, bf16[640,2048]{1,0:T(8,128)(2,1)} %cotangent_in.1, bf16[4,128,1024]{2,1,0:T(8,128)(2,1)} %get-tuple-element.61.early), custom_call_target="tpu_custom_call" | custom-call | bytes 180000000 | tf_op jit(solution)/shard_map/gather_tokens/pallas_call | solution.py:722
  121.2 1.5 collective-permute-start.2
  125.3 14.2 %first_rows.1 = (bf16[2560,2048]{1,0:T(8,128)(2,1)}, f32[2560,384]{1,0:T(8,128)}) custom-call(bf16[2560,2048]{1,0:T(8,128)(2,1)} %bitcast.40, f32[8,2048]{1,0:T(8,128)} %get-tuple-element.60.early.gains.gain, bf16[2048,640]{1,0:T(8,128)(2,1)} %all-gather.4.cloned.1.call-done.weight.weights), custom_call_target="tpu_custom_call" | custom-call | bytes 12000000 | tf_op jit(solution)/shard_map/first_rows/pallas_call | solution.py:1717
  139.5 38.5 %attention_forward.1 = (bf16[2560,256]{1,0:T(8,128)(2,1)}, bf16[2560,256]{1,0:T(8,128)(2,1)}, bf16[2560,256]{1,0:T(8,128)(2,1)}, bf16[2560,256]{1,0:T(8,128)(2,1)}, f32[4,1,2560]{2,1,0:T(1,128)}) custom-call(s32[20]{0:T(128)} %compare_select_fusion.1.to_ref, s32[20]{0:T(128)} %bitcast.61, f32[2560,384]{1,0:T(8,128)} %get-tuple-element.65.raw_ref, ...), custom_call_target="tpu_custom_call" | custom-call | flops 5368709120 | bytes 10485760 | tf_op jit(solution)/shard_map/attention_forward/pallas_call | solution.py:313
  178.0 56.1 %middle_rows.1 = (bf16[320,2048]{1,0:T(8,128)(2,1)}, f32[320,2048]{1,0:T(8,128)}) custom-call(bf16[4,2,320,256]{3,2,1,0:T(8,128)(2,1)} %bitcast.48, bf16[2048,640]{1,0:T(8,128)(2,1)} %all-gather.4.cloned.1.call-done.weight.weights, f32[8,2048]{1,0:T(8,128)} %get-tuple-element.60.early.gains.gain, bf16[640,2048]{1,0:T(8,128)(2,1)} %rest_8_.1), custom_call_target="tpu_custom_call" | custom-call | bytes 165000000 | tf_op jit(solution)/shard_map/middle_rows/pallas_call | solution.py:806
  235.6 59.0 %ffn_rows.1 = (bf16[4,2,320,2048]{3,2,1,0:T(8,128)(2,1)}, bf16[4,2,320,1024]{3,2,1,0:T(8,128)(2,1)}, bf16[4,2,320,1024]{3,2,1,0:T(8,128)(2,1)}, bf16[4,2,320,102...) custom-call(bf16[320,2048]{1,0:T(8,128)(2,1)} %get-tuple-element.67.block, ...), custom_call_target="tpu_custom_call" | custom-call | bytes 180000000 | tf_op jit(solution)/shard_map/ffn_rows/pallas_call | solution.py:973
  294.6 16.8 %bitcast_convert_fusion.early = bf16[2048,1024]{1,0:T(8,128)(2,1)} fusion(bf16[4,2,320,2048]{3,2,1,0:T(8,128)(2,1)} %get-tuple-element.71, bf16[4,2,320,1024]{3,2,1,0:T(8,128)(2,1)} %get-tuple-element.74.m), kind=kOutput, calls=%fused_computation | convolution fusion | flops 10739515392 | bytes 19922944 | tf_op jit(solution)/shard_map/dot_general | solution.py:32
  311.5 22.1 %ffn_slopes.1.slopes = bf16[2560,2048]{1,0:T(8,128)(2,1)} custom-call(bf16[2560,2048]{1,0:T(8,128)(2,1)} %bitcast.43, bf16[2560,1024]{1,0:T(8,128)(2,1)} %bitcast.45, bf16[2560,1024]{1,0:T(8,128)(2,1)} %bitcast.46, bf16[2048,1024]{1,0:T(8,128)(2,1)} %all-gather.8.cloned.1.call-done.down_w.down_in, bf16[2048,1024]{1,0:T(8,128)(2,1)} %bitcast_convert_fusion.early), custom_call_target="tpu_custom_call" | custom-call | flops 10737418240 | bytes 26843544 | tf_op jit(solution)/shard_map/ffn_slopes/pallas_call | solution.py:1805
  333.5 63.3 %second_rows.1 = (f32[320,2048]{1,0:T(8,128)}, bf16[320,2048]{1,0:T(8,128)(2,1)}, bf16[2048,1024]{1,0:T(8,128)(2,1)}) custom-call(bf16[2560,2048]{1,0:T(8,128)(2,1)} %ffn_slopes.1.slopes, bf16[2560,2048]{1,0:T(8,128)(2,1)} %bitcast.38, bf16[2048,2048]{1,0:T(8,128)(2,1)} %all-gather.6.cloned.1.call-done.weights_in, ...), custom_call_target="tpu_custom_call" | custom-call | bytes 180000000 | tf_op jit(solution)/shard_map/second_rows/pallas_call | solution.py:1242
  396.9 53.9 %spread_rows.1 = (bf16[4,2,320,2048]{3,2,1,0:T(8,128)(2,1)}, bf16[320,2048]{1,0:T(8,128)(2,1)}, bf16[320,2048]{1,0:T(8,128)(2,1)}, bf16[320,2048]{1,0:T(8,128)(2...) custom-call(bf16[320,2048]{1,0:T(8,128)(2,1)} %get-tuple-element.77.hidden, ...), custom_call_target="tpu_custom_call" | custom-call | bytes 180000000 | tf_op jit(solution)/shard_map/spread_rows/pallas_call | solution.py:1352
  452.9 1.5 collective-permute-start.5
  454.4 8.2 %convolution_convert_fusion.grad_ref = bf16[2560,256]{1,0:T(8,128)(2,1)} fusion(bf16[2560,2048]{1,0:T(8,128)(2,1)} %bitcast.41, bf16[2048,640]{1,0:T(8,128)(2,1)} %all-gather.4.cloned.1.call-done.weight.weights), kind=kOutput, calls=%fused_computation.1 | convolution fusion | flops 2685009920 | bytes 12845056 | tf_op jit(solution)/shard_map/dot_general | solution.py:32
  462.6 3.5 all-to-all-start
  466.1 53.8 %attention_backward.1.back = bf16[2560,384]{1,0:T(8,128)(2,1)} custom-call(s32[20]{0:T(128)} %compare_select_fusion.1.to_ref, s32[20]{0:T(128)} %bitcast.62, bf16[2560,256]{1,0:T(8,128)(2,1)} %convolution_convert_fusion.grad_ref, bf16[2560,256]{1,0:T(8,128)(2,1)} %get-tuple-element.80.q_ref, bf16[2560,256]{1,0:T(8,128)(2,1)} %get-tuple-element.81.k_ref, ...), custom_call_target="tpu_custom_call" | custom-call | flops 13421772800 | bytes 10485760 | tf_op jit(solution)/shard_map/attention_backward/pallas_call | solution.py:331
  521.5 18.4 %attention_weights.1 = (bf16[2048,640]{1,0:T(8,128)(2,1)}, bf16[4,128,1024]{2,1,0:T(8,128)(2,1)}) custom-call(bf16[2560,2048]{1,0:T(8,128)(2,1)} %get-tuple-element.64.hidden, bf16[2560,384]{1,0:T(8,128)(2,1)} %attention_backward.1.back, bf16[2560,2048]{1,0:T(8,128)(2,1)} %bitcast.42, bf16[2560,256]{1,0:T(8,128)(2,1)} %get-tuple-element.66.attended, ...), custom_call_target="tpu_custom_call" | custom-call | bytes 75000000 | tf_op jit(solution)/shard_map/attention_weights/pallas_call | solution.py:1768
  539.9 4.5 finish_first.1
  544.4 6.2 reduce-scatter.11.cloned.1.call-done
  550.6 64.2 %last_rows.1 = (f32[2,320,2048]{2,1,0:T(8,128)}, bf16[2,320,2048]{2,1,0:T(8,128)(2,1)}, bf16[4,128,1024]{2,1,0:T(8,128)(2,1)}, f32[128,128]{1,0:T(8,128)}) custom-call(bf16[4,2,320,384]{3,2,1,0:T(8,128)(2,1)} %bitcast.44, bf16[2048,640]{1,0:T(8,128)(2,1)} %all-gather.4.cloned.1.call-done.weight.weights, f32[8,2048]{1,0:T(8,128)} %get-tuple-element.60.early.gains.gain, ...), custom_call_target="tpu_custom_call" | custom-call | bytes 210000000 | tf_op jit(solution)/shard_map/last_rows/pallas_call | solution.py:1490
  614.8 14.1 %exchange_blocks.1 = (bf16[4,128,640]{2,1,0:T(8,128)(2,1)}, f32[2,128,128]{2,1,0:T(8,128)}) custom-call(bf16[4,128,640]{2,1,0:T(8,128)(2,1)} %bitcast.58, bf16[128,1024]{1,0:T(8,128)(2,1)} %query.3, bf16[128,512]{1,0:T(8,128)(2,1)} %get-tuple-element.88.pair, f32[128,128]{1,0:T(8,128)} %get-tuple-element.94.other_sums), custom_call_target="tpu_custom_call" | custom-call | bytes 24000000 | tf_op jit(solution)/shard_map/exchange_blocks/pallas_call | solution.py:1559
  628.9 8.2 %finish.1 = (f32[128,1024]{1,0:T(8,128)}, f32[128,256]{1,0:T(8,128)}, f32[128,256]{1,0:T(8,128)}, f32[1024,128]{1,0:T(8,128)}, f32[128,4096]{1,0:T(8,128)}, /*in...) custom-call(bf16[4,128,640]{2,1,0:T(8,128)(2,1)} %get-tuple-element.95.attn, ...), custom_call_target="tpu_custom_call" | custom-call | bytes 36000000 | tf_op jit(solution)/shard_map/finish/pallas_call | solution.py:1640
  637.1 1.3 slice_bitcast_fusion
  (48 shorter events, 10.0 us)
Async XLA Ops:
  7.2 118.2 %all-gather.4.cloned.1.call-start = ((), (), s32[]{:S(2)}) async-start(), calls=%async_computation.5 | async-start | bytes 3276800 | tf_op jit(solution)/shard_map/all_gather | solution.py:1883
  7.9 60.4 %copy-start.4 = (f32[2,128]{1,0:T(2,128)}, f32[2,128]{1,0:T(2,128)S(1)}, u32[]{:S(2)}) copy-start(f32[2,128]{1,0:T(2,128)S(1)} %maximum_convert_fusion.gains) | copy-start | bytes 3076
  26.5 207.7 %all-gather.6.cloned.1.call-start = ((), (), s32[]{:S(2)}) async-start(), calls=%async_computation.6 | async-start | bytes 10485760 | tf_op jit(solution)/shard_map/all_gather | solution.py:1883
  68.3 243.2 %all-gather.8.cloned.1.call-start = ((), (), s32[]{:S(2)}) async-start(), calls=%async_computation.7 | async-start | bytes 5242880 | tf_op jit(solution)/shard_map/all_gather | solution.py:1883
  69.0 55.8 %copy-start.5 = (s32[1,20]{1,0:T(1,128)S(1)}, s32[1,20]{1,0:T(1,128)}, u32[]{:S(2)}) copy-start(s32[1,20]{1,0:T(1,128)} %param.27) | copy-start | bytes 244
  69.0 55.8 %copy-start.6 = (s32[1,20]{1,0:T(1,128)S(1)}, s32[1,20]{1,0:T(1,128)}, u32[]{:S(2)}) copy-start(s32[1,20]{1,0:T(1,128)} %param.28) | copy-start | bytes 244
  69.1 393.5 %reduce-scatter.5.cloned.1.call-start = ((), (), s32[]{:S(2)}) async-start(), calls=%async_computation.8 | async-start | bytes 5242880 | tf_op jit(solution)/shard_map/reduce_scatter | solution.py:1975
  121.2 112.9 %collective-permute-start.2 = (bf16[320,2048]{1,0:T(8,128)(2,1)}, bf16[320,2048]{1,0:T(8,128)(2,1)S(1)}, u32[]{:S(2)}, u32[]{:S(2)}) collective-permute-start(bf16[320,2048]{1,0:T(8,128)(2,1)} %get-tuple-element.70), channel_id=1, source_target_pairs={{0,6},{2,4},{4,2},{6,0},{1,7},{3,5},{5,3},{7,1},{8,14},{10,12},{12... | collective-permute-start | bytes 3932168 | tf_op jit(solution)/shard_map/ppermute | solution.py:1943
  122.8 111.4 %collective-permute-start.1 = (bf16[320,2048]{1,0:T(8,128)(2,1)}, bf16[320,2048]{1,0:T(8,128)(2,1)S(1)}, u32[]{:S(2)}, u32[]{:S(2)}) collective-permute-start(bf16[320,2048]{1,0:T(8,128)(2,1)} %get-tuple-element.70), channel_id=1, source_target_pairs={{0,4},{2,6},{4,0},{6,2},{1,5},{3,7},{5,1},{7,3},{8,12},{10,14},{12... | collective-permute-start | bytes 3932168 | tf_op jit(solution)/shard_map/ppermute | solution.py:1943
  123.8 110.4 %collective-permute-start = (bf16[320,2048]{1,0:T(8,128)(2,1)}, bf16[320,2048]{1,0:T(8,128)(2,1)}, u32[]{:S(2)}, u32[]{:S(2)}) collective-permute-start(bf16[320,2048]{1,0:T(8,128)(2,1)} %get-tuple-element.70), channel_id=1, source_target_pairs={{0,2},{2,0},{4,6},{6,4},{1,3},{3,1},{5,7},{7,5},{8,10},{10,8},{12,... | collective-permute-start | bytes 3932168 | tf_op jit(solution)/shard_map/ppermute | solution.py:1943
  234.1 1.1 copy-start.2
  234.1 1.5 copy-start.3
  311.4 208.6 %reduce-scatter.7.cloned.1.call-start = ((), (), s32[]{:S(2)}) async-start(), calls=%async_computation.9 | async-start | bytes 5242880 | tf_op jit(solution)/shard_map/reduce_scatter | solution.py:1975
  396.9 153.7 %reduce-scatter.11.cloned.1.call-start = ((), (), s32[]{:S(2)}) async-start(), calls=%async_computation.11 | async-start | bytes 5242880 | tf_op jit(solution)/shard_map/reduce_scatter | solution.py:1975
  450.9 69.1 %collective-permute-start.3 = (bf16[320,2048]{1,0:T(8,128)(2,1)}, bf16[320,2048]{1,0:T(8,128)(2,1)S(1)}, u32[]{:S(2)}, u32[]{:S(2)}) collective-permute-start(bf16[320,2048]{1,0:T(8,128)(2,1)} %get-tuple-element.84), channel_id=1, source_target_pairs={{0,2},{2,0},{4,6},{6,4},{1,3},{3,1},{5,7},{7,5},{8,10},{10,8},{12,... | collective-permute-start | bytes 3932168 | tf_op jit(solution)/shard_map/ppermute | solution.py:1997
  451.8 68.1 %collective-permute-start.4 = (bf16[320,2048]{1,0:T(8,128)(2,1)}, bf16[320,2048]{1,0:T(8,128)(2,1)}, u32[]{:S(2)}, u32[]{:S(2)}) collective-permute-start(bf16[320,2048]{1,0:T(8,128)(2,1)} %get-tuple-element.85), channel_id=1, source_target_pairs={{0,4},{2,6},{4,0},{6,2},{1,5},{3,7},{5,1},{7,3},{8,12},{10,14},{12... | collective-permute-start | bytes 3932168 | tf_op jit(solution)/shard_map/ppermute | solution.py:1997
  452.9 67.0 %collective-permute-start.5 = (bf16[320,2048]{1,0:T(8,128)(2,1)}, bf16[320,2048]{1,0:T(8,128)(2,1)}, u32[]{:S(2)}, u32[]{:S(2)}) collective-permute-start(bf16[320,2048]{1,0:T(8,128)(2,1)} %get-tuple-element.86), channel_id=1, source_target_pairs={{0,6},{2,4},{4,2},{6,0},{1,7},{3,5},{5,3},{7,1},{8,14},{10,12},{12... | collective-permute-start | bytes 3932168 | tf_op jit(solution)/shard_map/ppermute | solution.py:1997
  462.6 58.0 %all-to-all-start = ((bf16[4,128,1024]{2,1,0:T(8,128)(2,1)}), bf16[4,128,1024]{2,1,0:T(8,128)(2,1)S(1)}, u32[]{:S(2)}, u32[]{:S(2)}) async-start(bf16[4,128,1024]{2,1,0:T(8,128)(2,1)} %bitcast.55), calls=%async_computation.2 | async-start | bytes 2097152 | tf_op jit(solution)/shard_map/all_to_all | solution.py:1978
  466.1 148.7 %reduce-scatter.9.cloned.1.call-start = ((), (), s32[]{:S(2)}) async-start(), calls=%async_computation.10 | async-start | bytes 3276800 | tf_op jit(solution)/shard_map/reduce_scatter | solution.py:1975
  520.0 1.1 copy-start.1
  520.6 1.0 copy-start
Sparse Core Ops, SparseCore 0:
  26.6 52.9 all-gather.3
  81.1 148.3 all-gather.5
  231.1 78.9 all-gather.7
  312.9 75.2 reduce-scatter.4
  397.0 74.1 reduce-scatter.6
  473.3 77.2 reduce-scatter.10
  553.0 52.6 reduce-scatter.8
